TPU v7x, 32 devices: a whole 2x2x4 slice. The times are simulated.
32 devices in a mesh: row: 8 (over z, x), col: 4 (over y, core).
Axes of the slice: x: 2, y: 2, z: 4, core: 2. Of those that a mesh axis runs over, the one named last changes fastest.
Arguments:
- ensemble: float32 [4096, 1024], P(('row', 'col')), may hold values from -6 to 6
- obs_blocks: int32 [2, 256], replicated, may hold values from 0 to 1023
- obs_weights: float32 [2, 256, 4], replicated, may hold values from 0.1 to 1
- comp_tags: int32 [2, 256], replicated, may hold values from 0 to 1
- obs_values: float32 [2, 256], replicated, may hold values from -6 to 6
- obs_noise: bfloat16 [2, 256, 1024], replicated, may hold values from -6 to 6
Outputs:
- analysis: float32 [4096, 1024], P(('row', 'col'))
Inputs may be any that keep to these rules, and one draw needn't show every extreme that they name: Observation o reads state rows 4 * obs_blocks[b, o] to 4 * obs_blocks[b, o] + 3. `comp_tags`: 0 marks an atmosphere observation, 1 an ocean one.
All inputs are finite; a program needn't handle non-finite values.
Results may differ from a plain program's by a relative error of at most 0.0035.
Values may be sent and summed in bfloat16 or wider, within the bound.
No kernel may reach another device: no remote copies, remote signals or barrier semaphores. Data moves between devices by JAX's collectives and lax.ppermute only.
A program may use at most 64 MiB of HBM per device.

v0:
```python
import jax
import jax.numpy as jnp
from jax import lax
from jax.sharding import PartitionSpec as P


def broadcast(value, axis, source):
    kept = jnp.where(lax.axis_index(axis) == source, value, 0).astype(value.dtype)
    return lax.psum(kept, axis)


def joint_solve(factor_lower, anomalies, innovation):
    width = anomalies.shape[1]
    stacked = jnp.concatenate([anomalies, innovation], axis=1)
    solved = jax.scipy.linalg.solve_triangular(factor_lower, stacked, lower=True).astype(
        jnp.bfloat16
    )
    return (solved[:, :width], solved[:, width:])


def full_whiten(observed, variance, noise_scale, values, noise_full):
    members = observed.shape[1]
    highest = lax.Precision.HIGHEST
    anomalies = observed - jnp.mean(observed, axis=1, keepdims=True)
    covariance = jnp.dot(anomalies, anomalies.T, precision=highest) / (members - 1) + jnp.diag(
        variance
    )
    factor_lower = jnp.linalg.cholesky(covariance)
    innovation = values[:, None] + noise_scale[:, None] * noise_full.astype(jnp.float32) - observed
    return joint_solve(factor_lower, anomalies, innovation)


def body(ensemble, obs_blocks, obs_weights, comp_tags, obs_values, obs_noise):
    ensemble_state = ensemble
    highest = lax.Precision.HIGHEST
    local_rows = ensemble_state.shape[0]
    members = ensemble_state.shape[1]
    interp_points = obs_weights.shape[2]
    batch_count = obs_blocks.shape[0]
    devices = lax.axis_size(("row", "col"))
    my_device = lax.axis_index(("row", "col"))
    first_row = my_device * local_rows
    position = jnp.arange(local_rows, dtype=jnp.int32)
    offsets = jnp.arange(interp_points, dtype=jnp.int32)
    for batch_index in range(batch_count):
        row_ids = obs_blocks[batch_index][:, None] * interp_points + offsets[None, :] - first_row
        weights = obs_weights[batch_index]
        selector = jnp.sum(
            jnp.where(
                row_ids[:, :, None] == position[None, None, :],
                weights[:, :, None],
                jnp.float32(0.0),
            ),
            axis=1,
        )
        partial_value = jnp.dot(
            selector, ensemble_state, precision=highest, preferred_element_type=jnp.float32
        )
        member_slice = lax.psum_scatter(
            partial_value.astype(jnp.bfloat16), "col", scatter_dimension=1, tiled=True
        ).astype(jnp.float32)
        observed_slice = lax.psum(member_slice, "row")
        variance = jnp.where(comp_tags[batch_index] == 0, jnp.float32(0.5), jnp.float32(2.0))
        noise_scale = jnp.sqrt(variance)
        values = obs_values[batch_index]
        gathered = lax.all_gather(observed_slice.astype(jnp.bfloat16), "col", axis=1, tiled=True)
        observed = gathered.astype(jnp.float32)
        owner_index = batch_index * devices // batch_count

        def run_owner(observed_all):
            return full_whiten(observed_all, variance, noise_scale, values, obs_noise[batch_index])

        def nothing_here(observed_all):
            return (
                jnp.zeros(observed_all.shape, jnp.bfloat16),
                jnp.zeros(observed_all.shape, jnp.bfloat16),
            )

        whitened, white_innov = lax.cond(
            my_device == owner_index, run_owner, nothing_here, observed
        )
        whitened, white_innov = (
            broadcast(whitened, ("row", "col"), owner_index),
            broadcast(white_innov, ("row", "col"), owner_index),
        )
        state_anom = ensemble_state - jnp.mean(ensemble_state, axis=1, keepdims=True)
        projected = jnp.dot(state_anom, whitened.astype(jnp.float32).T, precision=highest)
        ensemble_state = ensemble_state + jnp.dot(
            projected, white_innov.astype(jnp.float32), precision=highest
        ) / (members - 1)
    return ensemble_state


def solution(mesh):
    in_specs = (P(("row", "col"), None), P(), P(), P(), P(), P())
    out_specs = P(("row", "col"), None)
    return jax.shard_map(body, mesh=mesh, in_specs=in_specs, out_specs=out_specs, check_vma=False)
```

profile of v0, /device:TPU:0, one launch (start us, length us, event | category | flops | bytes accessed | tf_op | source)
XLA Modules:
  0.0 626.7 jit_solution(5807010735228665193)
XLA Ops:
  8.4 2.8 convolution_convert_fusion.1
  11.4 24.3 %reduce-scatter.3.cloned.1.call-done = bf16[256,256]{1,0:T(8,128)(2,1)} async-done(((bf16[256,1024]{1,0:T(8,128)(2,1)}), bf16[256,256]{1,0:T(8,128)(2,1)}) %reduce-scatter.3.cloned.1.call-update) | async-done | bytes 131088 | tf_op jit(solution)/shard_map/reduce_scatter | solution.py:59
  35.8 73.4 %all-reduce.8.cloned.1.call-done = bf16[256,256]{1,0:T(8,128)(2,1)} async-done(((bf16[256,256]{1,0:T(8,128)(2,1)}), bf16[256,256]{1,0:T(8,128)(2,1)}) %all-reduce.8.cloned.1.call-update) | async-done | bytes 131088 | tf_op jit(solution)/shard_map/psum | solution.py:62
  109.2 7.4 %all_gather.6 = bf16[256,1024]{1,0:T(8,128)(2,1)S(1)} all-gather(bf16[256,256]{1,0:T(8,128)(2,1)} %all-reduce.8.cloned.1.call-done), channel_id=1, replica_groups=mesh['row'=8,'col'=4] {'col'}, dimensions={1}, use_global_device_ids=true | all-gather | bytes 655360 | tf_op jit(solution)/shard_map/all_gather | solution.py:66
  116.7 67.0 %conditional.2 = (bf16[256,1024]{1,0:T(8,128)(2,1)}, bf16[256,1024]{1,0:T(8,128)(2,1)}) conditional(s32[]{:T(128)} %convert_element_type.57, () %tuple.23, (f32[256,1024]{1,0:T(8,128)S(1)}, f32[256]{0:T(256)S(1)}, f32[2,256]{1,0:T(2,128)S(1)}, f32[256]{0:T(256)S(1)}, bf16[2,256,1024]{2,1,0:T(8,128)(2,1)}) %tuple.101), branch_computations={%region_4.5_spmd, %region_5.13_spmd} | conditional | flops 2068857088 | bytes 23082212 | solution.py:79
  116.9 1.3 fusion.5
  119.5 11.7 %cholesky.130 = f32[128,128]{1,0:T(8,128)S(1)} custom-call(f32[128,128]{1,0:T(8,128)S(1)} %cholesky.194), custom_call_target="Cholesky" | custom-call | tf_op jit(solution)/shard_map/cond/branch_1_fun/jit(cholesky)/cholesky | solution.py:28
  131.2 9.8 %custom-call.13 = f32[1,128,128]{1,2,0:T(8,128)S(1)} custom-call(f32[1,128,128]{2,1,0:T(8,128)S(1)} %get-tuple-element.94), custom_call_target="InvertDiagBlocksLowerTriangular" | custom-call | tf_op jit(solution)/shard_map/cond/branch_1_fun/jit(cholesky)/cholesky | solution.py:28
  141.5 11.7 %cholesky.147 = f32[128,128]{1,0:T(8,128)S(1)} custom-call(f32[128,128]{1,0:T(8,128)S(1)} %convolution_subtract_fusion.1), custom_call_target="Cholesky" | custom-call | tf_op jit(solution)/shard_map/cond/branch_1_fun/jit(cholesky)/cholesky | solution.py:28
  155.3 4.3 while.4
  156.2 1.3 bitcast_dynamic-update-slice_fusion.5
  158.2 1.3 bitcast_dynamic-update-slice_fusion.5
  159.6 19.7 %custom-call.14 = f32[2,128,128]{1,2,0:T(8,128)S(1)} custom-call(f32[2,128,128]{2,1,0:T(8,128)S(1)} %get-tuple-element.63), custom_call_target="InvertDiagBlocksLowerTriangular" | custom-call | tf_op jit(solution)/shard_map/cond/branch_1_fun/jit(_solve_triangular)/triangular_solve | solution.py:15
  183.6 2.2 broadcast_select_fusion.2
  186.3 125.7 %all-reduce.14.cloned.1.call-done = (bf16[256,1024]{1,0:T(8,128)(2,1)}, bf16[256,1024]{1,0:T(8,128)(2,1)}) async-done(((bf16[256,1024]{1,0:T(8,128)(2,1)}, bf16[256,1024]{1,0:T(8,128)(2,1)}), (bf16[256,1024]{1,0:T(8,128)(2,1)}, bf16[256,1024]{1,0:T(8,128)(2,1)})) %all-reduce.14.cloned.1.call-update) | async-done | bytes 1048592 | tf_op jit(solution)/shard_map/psum | solution.py:9
  312.0 1.8 fusion.30
  315.1 1.8 convolution_convert_fusion
  316.9 20.8 %reduce-scatter.5.cloned.1.call-done = bf16[256,256]{1,0:T(8,128)(2,1)} async-done(((bf16[256,1024]{1,0:T(8,128)(2,1)}), bf16[256,256]{1,0:T(8,128)(2,1)}) %reduce-scatter.5.cloned.1.call-update) | async-done | bytes 131088 | tf_op jit(solution)/shard_map/reduce_scatter | solution.py:59
  337.8 72.9 %all-reduce.10.cloned.1.call-done = bf16[256,256]{1,0:T(8,128)(2,1)} async-done(((bf16[256,256]{1,0:T(8,128)(2,1)}), bf16[256,256]{1,0:T(8,128)(2,1)}) %all-reduce.10.cloned.1.call-update) | async-done | bytes 131088 | tf_op jit(solution)/shard_map/psum | solution.py:62
  410.6 7.4 %all_gather.7 = bf16[256,1024]{1,0:T(8,128)(2,1)S(1)} all-gather(bf16[256,256]{1,0:T(8,128)(2,1)} %all-reduce.10.cloned.1.call-done), channel_id=1, replica_groups=mesh['row'=8,'col'=4] {'col'}, dimensions={1}, use_global_device_ids=true | all-gather | bytes 655360 | tf_op jit(solution)/shard_map/all_gather | solution.py:66
  418.1 1.8 conditional.3
  421.6 195.4 %all-reduce.12.cloned.1.call-done = (bf16[256,1024]{1,0:T(8,128)(2,1)}, bf16[256,1024]{1,0:T(8,128)(2,1)}) async-done(((bf16[256,1024]{1,0:T(8,128)(2,1)}, bf16[256,1024]{1,0:T(8,128)(2,1)}), (bf16[256,1024]{1,0:T(8,128)(2,1)}, bf16[256,1024]{1,0:T(8,128)(2,1)})) %all-reduce.12.cloned.1.call-update) | async-done | bytes 1048592 | tf_op jit(solution)/shard_map/psum | solution.py:9
  617.0 1.7 fusion.28
  618.7 1.2 fusion.26
  (72 shorter events, 15.9 us)
Async XLA Ops:
  6.5 4.7 copy-start
  6.5 29.2 %reduce-scatter.3.cloned.1.call-start = ((), (), s32[]{:S(2)}) async-start(), calls=%async_computation.2 | async-start | bytes 655360 | tf_op jit(solution)/shard_map/reduce_scatter | solution.py:59
  8.4 27.4 %copy-start.6 = (s32[2,256]{1,0:T(2,128)S(1)}, s32[2,256]{1,0:T(2,128)}, u32[]{:S(2)}) copy-start(s32[2,256]{1,0:T(2,128)} %param.16) | copy-start | bytes 6148
  11.2 98.0 %all-reduce.8.cloned.1.call-start = ((), (), s32[]{:S(2)}) async-start(), calls=%async_computation.3 | async-start | bytes 262144 | tf_op jit(solution)/shard_map/psum | solution.py:62
  35.7 276.3 %all-reduce.14.cloned.1.call-start = ((), (), s32[]{:S(2)}) async-start(), calls=%async_computation.7 | async-start | bytes 2097152 | tf_op jit(solution)/shard_map/psum | solution.py:9
  35.8 80.8 %copy-start.7 = (f32[2,256]{1,0:T(2,128)S(1)}, f32[2,256]{1,0:T(2,128)}, u32[]{:S(2)}) copy-start(f32[2,256]{1,0:T(2,128)} %param.17) | copy-start | bytes 6148
  185.9 126.2 %copy-start.1 = (f32[128,1024]{1,0:T(8,128)S(1)}, f32[128,1024]{1,0:T(8,128)}, u32[]{:S(2)}) copy-start(f32[128,1024]{1,0:T(8,128)} %param.13) | copy-start | bytes 1572868
  185.9 151.8 %reduce-scatter.5.cloned.1.call-start = ((), (), s32[]{:S(2)}) async-start(), calls=%async_computation.4 | async-start | bytes 655360 | tf_op jit(solution)/shard_map/reduce_scatter | solution.py:59
  312.0 1.8 copy-start.4
  314.3 0.8 copy-start.2
  316.9 93.8 %all-reduce.10.cloned.1.call-start = ((), (), s32[]{:S(2)}) async-start(), calls=%async_computation.5 | async-start | bytes 262144 | tf_op jit(solution)/shard_map/psum | solution.py:62
  337.7 279.2 %all-reduce.12.cloned.1.call-start = ((), (), s32[]{:S(2)}) async-start(), calls=%async_computation.6 | async-start | bytes 2097152 | tf_op jit(solution)/shard_map/psum | solution.py:9
  420.7 196.3 %copy-start.3 = (f32[128,1024]{1,0:T(8,128)S(1)}, f32[128,1024]{1,0:T(8,128)}, u32[]{:S(2)}) copy-start(f32[128,1024]{1,0:T(8,128)} %copy-done.2) | copy-start | bytes 1572868
  617.0 1.8 copy-start.5
Sparse Core Ops, SparseCore 0:
  11.3 24.3 reduce-scatter.2
  39.4 69.7 all-reduce.7
  186.0 125.9 all-reduce.13
  317.0 20.6 reduce-scatter.4
  340.9 69.7 all-reduce.9
  421.7 195.2 all-reduce.11
where the time goes:
time: 636 us; the launch traced here: 627 us
  waiting for transfers between devices  513 us (81%)
  other arithmetic  61.1 us (10%)
  blocking collectives  14.7 us (2%)
  matrix products  14.3 us (2%)
  between operations  13.6 us (2%)
  local copies, waits for them, and re-layouts  8.58 us (1%)
    psum x2, waiting for transfers between devices, broadcast(): return lax.psum(kept, axis)  321 us
    psum x2, waiting for transfers between devices, body(): observed_slice = lax.psum(member_slice, 'row')  146 us
    reduce_scatter x2, waiting for transfers between devices, body(): lax.psum_scatter(partial_value.astype(jnp.bfloat16), 'col', scatter_dimen...  45.1 us
    another operation x6, other arithmetic, full_whiten(): factor_lower = jnp.linalg.cholesky(covariance)  34 us
    another operation x4, other arithmetic, joint_solve(): jax.scipy.linalg.solve_triangular(factor_lower, stacked, lower=True)  19.7 us
    all_gather x2, blocking collectives, body(): lax.all_gather(observed_slice.astype(jnp.bfloat16), 'col', axis=1, tiled=...  14.7 us
  transfers between devices with their start and end apart: 6, of which 6 were waited for; matrix products, arithmetic and copies ran while one was open for 0% of the time, Pallas kernels for 0%

commit v1 on v0

v1 whole, which is shorter than its diff:
```python
import functools

import jax
import jax.numpy as jnp
from jax import lax
from jax.experimental import pallas as pl
from jax.experimental.pallas import tpu as pltpu
from jax.sharding import PartitionSpec as P

SLOTS = 32
SCALE = 0.5
TOLERANCE = 2e-3
BF16 = jnp.bfloat16
F32 = jnp.float32
VMEM = pl.BlockSpec(memory_space=pltpu.VMEM)
SMEM = pl.BlockSpec(memory_space=pltpu.SMEM)
PARAMS = pltpu.CompilerParams(vmem_limit_bytes=40 * 1024 * 1024)


def nt(a, b):
    return lax.dot_general(a, b, (((1,), (1,)), ((), ())), preferred_element_type=F32)


def nn(a, b):
    return lax.dot_general(a, b, (((1,), (0,)), ((), ())), preferred_element_type=F32)


def split(a):
    high = a.astype(BF16)
    return high, (a - high.astype(F32)).astype(BF16)


def dot3(dot, a, b):
    (ah, al), (bh, bl) = a, b
    return dot(ah, bh) + (dot(ah, bl) + dot(al, bh))


def row_mean(a):
    return jnp.sum(a, axis=1, keepdims=True) * (1.0 / a.shape[1])


def column(row):
    size = row.shape[1]
    lane = lax.broadcasted_iota(jnp.int32, (size, size), 1)
    sub = lax.broadcasted_iota(jnp.int32, (size, size), 0)
    return jnp.sum(jnp.where(lane == sub, row, jnp.zeros_like(row)), axis=1, keepdims=True)


def both_ways(row):
    as_float = row.astype(F32)
    return as_float, column(as_float)


def split_rows(first, second):
    high = second.astype(BF16)
    return first.astype(BF16), high, (second - high.astype(F32)).astype(BF16)


def pick_kernel(place, blocks, weights, state, keep0, send0, keep1, send1):
    device = place[0]
    batches, points, size = weights.shape
    width, members = state.shape
    held = width // points
    lane = lax.broadcasted_iota(jnp.int32, (size, size), 1)
    sub = lax.broadcasted_iota(jnp.int32, (size, size), 0)
    slots = lax.broadcasted_iota(jnp.int32, (SLOTS, size), 0)
    lanes = lax.broadcasted_iota(jnp.int32, (SLOTS, width), 1)
    selectors = []
    for batch in range(batches):
        row = blocks[batch : batch + 1, :]
        pair_row, pair_column = both_ways(row // (2 * held))
        before = jnp.where((pair_row == pair_column) & (sub < lane), 1.0, 0.0)
        rank = jnp.sum(before, axis=0, keepdims=True).astype(jnp.int32)
        slot = jnp.where(row // held == device, rank, -1)
        chosen = jnp.where(slots == slot, 1.0, 0.0)
        local = jnp.sum(chosen * (row - device * held).astype(F32), axis=1, keepdims=True)
        weight = lax.dot_general(
            chosen,
            weights[batch],
            (((1,), (1,)), ((), ())),
            precision=lax.Precision.HIGHEST,
            preferred_element_type=F32,
        )
        value = jnp.zeros((SLOTS, width), F32)
        for point in range(points):
            value = jnp.where(lanes % points == point, weight[:, point : point + 1], value)
        selectors.append(jnp.where((lanes // points).astype(F32) == local, value, 0.0))
    rows = jnp.dot(
        jnp.concatenate(selectors, axis=0),
        state[...],
        precision=lax.Precision.HIGHEST,
        preferred_element_type=F32,
    )
    left, right = rows[:, : members // 2], rows[:, members // 2 :]
    first = device % 2 == 0
    for half, out0, out1 in (
        (jnp.where(first, left, right), keep0, keep1),
        (jnp.where(first, right, left), send0, send1),
    ):
        out0[...], out1[:SLOTS, :], out1[SLOTS:, :] = split_rows(half[:SLOTS], half[SLOTS:])


def pick(place, blocks, weights, state):
    half = state.shape[1] // 2
    outs = [jax.ShapeDtypeStruct((rows, half), BF16) for rows in (SLOTS, SLOTS, 2 * SLOTS, 2 * SLOTS)]
    return pl.pallas_call(
        pick_kernel,
        out_shape=outs,
        in_specs=[SMEM, VMEM, VMEM, VMEM],
        out_specs=[VMEM] * 4,
        compiler_params=PARAMS,
        name="pick",
    )(place, blocks, weights, state)


def pick_all_kernel(place, blocks, weights, state, out):
    device = place[0]
    batches, points, size = weights.shape
    width = state.shape[0]
    lanes = lax.broadcasted_iota(jnp.int32, (size, width), 1)
    rows = []
    for batch in range(batches):
        value = jnp.zeros((size, width), F32)
        for point in range(points):
            weight = column(weights[batch, point : point + 1, :])
            value = jnp.where(lanes % points == point, weight, value)
        row = blocks[batch : batch + 1, :]
        local = column((row - device * (width // points)).astype(F32))
        selector = jnp.where((lanes // points).astype(F32) == local, value, 0.0)
        rows.append(
            jnp.dot(
                selector, state[...], precision=lax.Precision.HIGHEST, preferred_element_type=F32
            )
        )
    out[:size, :], out[size : 2 * size, :], out[2 * size :, :] = split_rows(*rows)


def pick_all(place, blocks, weights, state):
    return pl.pallas_call(
        pick_all_kernel,
        out_shape=jax.ShapeDtypeStruct((3 * blocks.shape[1], state.shape[1]), BF16),
        in_specs=[SMEM, VMEM, VMEM, VMEM],
        out_specs=VMEM,
        compiler_params=PARAMS,
        name="pick_all",
    )(place, blocks, weights, state)


def in_order(device, row, held, parts, refs):
    size = row.shape[1]
    pair_row, pair_column = both_ways(row // (2 * held))
    lane = lax.broadcasted_iota(jnp.int32, (size, size), 1)
    sub = lax.broadcasted_iota(jnp.int32, (size, size), 0)
    before = jnp.where((pair_row == pair_column) & (lane < sub), 1.0, 0.0)
    rank = jnp.sum(before, axis=1, keepdims=True).astype(jnp.int32)
    away = (2 * pair_column.astype(jnp.int32)) ^ device
    far, near = (away >> 4) & 1, (away >> 3) & 1
    x, y = (away >> 2) & 1, (away >> 1) & 1
    block = jnp.where(near == 0, 4 * x + 2 * y + far, 4 * y + 2 * x + far)
    halves = []
    for group in (refs[:2], refs[2:]):
        total = jnp.zeros((size, group[0].shape[-1]), F32)
        for index, ref in enumerate(group):
            values = ref[...].reshape(-1, ref.shape[-1])
            slots = lax.broadcasted_iota(jnp.int32, (size, values.shape[0]), 1)
            chosen = jnp.zeros((size, values.shape[0]), F32)
            for part in range(parts):
                slot = (block * parts + part) * SLOTS + rank
                chosen = chosen + jnp.where((slots == slot) & (near == index), 1.0, 0.0)
            total = total + nn(chosen.astype(BF16), values)
        halves.append(total)
    first = device % 2 == 0
    return jnp.concatenate(
        [jnp.where(first, halves[0], halves[1]), jnp.where(first, halves[1], halves[0])], axis=1
    )


def eliminate(covariance, work, inverse):
    size = covariance.shape[0]
    lane = lax.broadcasted_iota(jnp.int32, (size, size), 1)
    sub = lax.broadcasted_iota(jnp.int32, (size, size), 0)
    work[...] = covariance
    inverse[...] = jnp.where(lane == sub, 1.0, 0.0)

    def step(k, carry):
        row = work[pl.ds(k, 1), :]
        current = work[...]
        pivot = jnp.sum(jnp.where(lane[:1] == k, row, 0.0), axis=1, keepdims=True)
        column = jnp.sum(jnp.where(lane == k, current, 0.0), axis=1, keepdims=True)
        factor = jnp.where(sub[:, :1] > k, column / pivot, 0.0)
        inverse_row = inverse[pl.ds(k, 1), :]
        work[...] = current - factor * row
        inverse[...] = inverse[...] - factor * inverse_row
        return carry

    lax.fori_loop(0, size, step, 0)
    pivots = jnp.sum(jnp.where(lane == sub, work[...], 0.0), axis=1, keepdims=True)
    inverse[...] = inverse[...] * (1.0 / jnp.sqrt(pivots))


def inverse_factor(covariance, work, inverse):
    size = covariance.shape[0]
    lane = lax.broadcasted_iota(jnp.int32, (size, size), 1)
    sub = lax.broadcasted_iota(jnp.int32, (size, size), 0)
    diagonal = lane == sub
    eye = jnp.where(diagonal, 1.0, 0.0)
    half = jnp.where(lane < sub, 1.0, jnp.where(diagonal, 0.5, 0.0))
    on_diagonal = jnp.where(diagonal, covariance, 0.0)
    scale_row = lax.rsqrt(jnp.sum(on_diagonal, axis=0, keepdims=True) * (1.0 / SCALE))
    scale_column = lax.rsqrt(jnp.sum(on_diagonal, axis=1, keepdims=True) * (1.0 / SCALE))
    scaled = covariance * scale_row * scale_column

    def third_order(m):
        low = (m - eye) * half
        lowb = low.astype(BF16)
        return (nn(lowb, lowb) + half * nt(lowb, lowb)) - low

    m = scaled
    t = None
    for step in range(3):
        u = third_order(m) + eye
        ub = u.astype(BF16)
        t = u if t is None else nn(ub, t.astype(BF16))
        if step < 2:
            m = nt(nn(ub, m.astype(BF16)).astype(BF16), ub)
    parts = split(scaled)
    ts = split(t)
    m = dot3(nt, split(dot3(nn, ts, parts)), ts)
    t = t + nn(third_order(m).astype(BF16), ts[0])
    ts = split(t)
    m = dot3(nt, split(dot3(nn, ts, parts)), ts)
    error = m - eye
    t = t - nn((error * half).astype(BF16), ts[0])
    inverse[...] = t * scale_row
    good = jnp.min(jnp.where(jnp.abs(error) <= TOLERANCE, 1.0, 0.0))

    @pl.when(good < 0.5)
    def _():
        eliminate(covariance, work, inverse)


def whiten(observed, tags, values, noise, work, inverse):
    members = observed.shape[1]
    size = observed.shape[0]
    anomalies = observed - row_mean(observed)
    ah, al = split(anomalies)
    lane = lax.broadcasted_iota(jnp.int32, (size, size), 1)
    sub = lax.broadcasted_iota(jnp.int32, (size, size), 0)
    variance = column(jnp.where(tags == 0, 0.5, 2.0))
    values = column(values)
    covariance = dot3(nt, (ah, al), (ah, al)) * (1.0 / (members - 1))
    covariance = covariance + jnp.where(lane == sub, variance, 0.0)
    inverse_factor(covariance, work, inverse)
    ts = split(inverse[...])
    innovation = values + jnp.sqrt(variance) * noise.astype(F32) - observed
    whitened = dot3(nn, ts, (ah, al)).astype(BF16)
    white_innov = dot3(nn, ts, split(innovation)).astype(BF16)
    return whitened, white_innov


def update(state, whitened, white_innov):
    members = state.shape[1]
    sh, sl = split(state - row_mean(state))
    ph, plow = split(nt(sh, whitened) + nt(sl, whitened))
    return state + (nn(ph, white_innov) + nn(plow, white_innov)) * (1.0 / (members - 1))


def first_kernel(direct, place, blocks, tags, values, noise, *rest):
    arrived, (whitened, white_innov, work, inverse) = rest[:-4], rest[-4:]
    if direct:
        held = place[1]
        observed = in_order(place[0], blocks[:1, :], held, 1, arrived)
    else:
        observed = arrived[0][...].astype(F32)
    w, v = whiten(observed, tags[:1, :], values[:1, :], noise[0], work, inverse)
    whitened[...] = w
    white_innov[...] = v


def second_kernel(direct, place, blocks, tags, values, noise, state, whitened, white_innov, *rest):
    arrived, (analysis, work, inverse) = rest[:-3], rest[-3:]
    if direct:
        held = place[1]
        prior = in_order(place[0], blocks[1:2, :], held, 2, arrived)
    else:
        prior = arrived[0][...].astype(F32) + arrived[1][...].astype(F32)
    w, v = whitened[...], white_innov[...]
    observed = update(prior, w, v).astype(BF16).astype(F32)
    first = update(state[...], w, v)
    w, v = whiten(observed, tags[1:2, :], values[1:2, :], noise[0], work, inverse)
    analysis[...] = update(first, w, v)


def whole(array):
    return pl.BlockSpec(array.shape, lambda i, n=len(array.shape): (0,) * n)


def batch_call(kernel, name, batch, outs, place, blocks, tags, values, noise, *arrays):
    rows, members = noise.shape[1:]
    return pl.pallas_call(
        kernel,
        grid=(1,),
        out_shape=outs,
        in_specs=[SMEM, whole(blocks), whole(tags), whole(values)]
        + [pl.BlockSpec((1, rows, members), lambda i: (batch, 0, 0))]
        + [whole(array) for array in arrays],
        out_specs=[whole(out) for out in outs],
        scratch_shapes=[pltpu.VMEM((rows, rows), F32), pltpu.VMEM((rows, rows), F32)],
        compiler_params=PARAMS,
        name=name,
    )(place, blocks, tags, values, noise, *arrays)


def batches(direct, place, blocks, tags, values, noise, state, arrived0, arrived1):
    shape = jax.ShapeDtypeStruct(noise.shape[1:], BF16)
    whitened, white_innov = batch_call(
        functools.partial(first_kernel, direct),
        "first_batch",
        0,
        [shape, shape],
        place,
        blocks,
        tags,
        values,
        noise,
        *arrived0,
    )
    return batch_call(
        functools.partial(second_kernel, direct),
        "second_batch",
        1,
        [jax.ShapeDtypeStruct(state.shape, F32)],
        place,
        blocks,
        tags,
        values,
        noise,
        state,
        whitened,
        white_innov,
        *arrived1,
    )[0]


AXES = ("row", "col")
CORE, Y, X, NEAR_Z, FAR_Z = 1, 2, 4, 8, 16


def swap(value, mask):
    return lax.ppermute(value, AXES, [(i, i ^ mask) for i in range(32)])


def joined(value, mask):
    return jnp.concatenate([value, swap(value, mask)], axis=0)


def gather(keep, send):
    block = (keep + swap(send, CORE))[None]
    along_z = joined(joined(block, FAR_Z), NEAR_Z)
    first = joined(joined(along_z[:2], Y), X)
    second = joined(joined(along_z[2:], X), Y)
    return first, second, swap(first, CORE), swap(second, CORE)


def by_slots(place, ensemble, blocks, weights, tags, values, noise):
    keep0, send0, keep1, send1 = pick(place, blocks, weights, ensemble)
    arrived0, arrived1 = gather(keep0, send0), gather(keep1, send1)
    return batches(True, place, blocks, tags, values, noise, ensemble, arrived0, arrived1)


def by_sum(add_up, place, ensemble, blocks, weights, tags, values, noise):
    rows = blocks.shape[1]
    picked = add_up(pick_all(place, blocks, weights, ensemble))
    arrived0, arrived1 = picked[:rows], (picked[rows : 2 * rows], picked[2 * rows :])
    return batches(False, place, blocks, tags, values, noise, ensemble, (arrived0,), arrived1)


def add_by_swaps(value):
    for mask in (CORE, Y, X, NEAR_Z, FAR_Z):
        value = value + swap(value, mask)
    return value


def add_by_psum(value):
    return lax.psum(value, AXES)


def body(staged, ensemble, obs_blocks, obs_weights, comp_tags, obs_values, obs_noise):
    held = ensemble.shape[0] // obs_weights.shape[2]
    place = jnp.stack([lax.axis_index(AXES), held]).astype(jnp.int32)
    by_point = jnp.swapaxes(obs_weights, 1, 2)
    operands = (place, ensemble, obs_blocks, by_point, comp_tags, obs_values, obs_noise)
    if not staged:
        return by_sum(add_by_psum, *operands)
    pair = obs_blocks // (2 * held)
    counts = jnp.sum(
        (pair[:, :, None] == jnp.arange(16, dtype=jnp.int32)).astype(jnp.int32), axis=1
    )
    fits = jnp.max(counts) <= SLOTS
    return lax.cond(fits, by_slots, functools.partial(by_sum, add_by_swaps), *operands)


def solution(mesh):
    staged = (mesh.shape["row"], mesh.shape["col"]) == (8, 4)
    in_specs = (P(AXES, None), P(), P(), P(), P(), P())
    out_specs = P(AXES, None)
    return jax.shard_map(
        functools.partial(body, staged),
        mesh=mesh,
        in_specs=in_specs,
        out_specs=out_specs,
        check_vma=False,
    )
```

time: 636 us -> 92.5 us (0.15); the launches traced: 627 us -> 92.4 us
  waiting for transfers between devices: 513 us -> 13.6 us
  other arithmetic: 61.1 us -> 1.72 us
  Pallas kernels: 0 us -> 54.7 us
  starting transfers between devices: 0.2 us -> 20.3 us
  blocking collectives: 14.7 us -> 0 us
  matrix products: 14.3 us -> 0 us
  between operations: 13.6 us -> 0.67 us
  local copies, waits for them, and re-layouts: 8.58 us -> 0.88 us
    psum x4 -> x0, waiting for transfers between devices: 467 us -> none  [the longest x2 321 us: broadcast(): return lax.psum(kept, axis)]
    pallas_call x0 -> x3, Pallas kernels: none -> 54.7 us  [the longest x2 52.8 us: batch_call(): pl.pallas_call(kernel, grid=(1,), out_shape=outs, in_specs=[SMEM, whole(b...]
    another operation x10 -> x1, other arithmetic: 53.7 us -> 0.07 us  [body(): place = jnp.stack([lax.axis_index(AXES), held]).astype(jnp.int32)]
    reduce_scatter x2 -> x0, waiting for transfers between devices: 45.1 us -> none  [body(): lax.psum_scatter(partial_value.astype(jnp.bfloat16), 'col', scatter_dimen...]
    ppermute x0 -> x18, starting transfers between devices: none -> 20.3 us  [swap(): return lax.ppermute(value, AXES, [(i, i ^ mask) for i in range(32)])]
    all_gather x2 -> x0, blocking collectives: 14.7 us -> none  [body(): lax.all_gather(observed_slice.astype(jnp.bfloat16), 'col', axis=1, tiled=...]
    ppermute x0 -> x18, waiting for transfers between devices: none -> 13.6 us  [swap(): return lax.ppermute(value, AXES, [(i, i ^ mask) for i in range(32)])]
    dot_general x7 -> x0, matrix products: 10.8 us -> none  [the longest x2 4.59 us: body(): jnp.dot(selector, ensemble_state, precision=highest, preferred_element_ty...]
  transfers between devices with their start and end apart: 6 -> 18, of which waited for: 6 -> 10; matrix products, arithmetic and copies ran while one was open for 0% -> 0% of each run, Pallas kernels for 0% -> 47%
where the time goes in v1:
time: 92.5 us; the launch traced here: 92.4 us
  Pallas kernels  54.7 us (59%)
  starting transfers between devices  20.3 us (22%)
  waiting for transfers between devices  13.6 us (15%)
  other arithmetic  1.72 us (2%)
    pallas_call x2, Pallas kernels, batch_call(): pl.pallas_call(kernel, grid=(1,), out_shape=outs, in_specs=[SMEM, whole(b...  52.8 us
    ppermute x18, starting transfers between devices, swap(): return lax.ppermute(value, AXES, [(i, i ^ mask) for i in range(32)])  20.3 us
    ppermute x18, waiting for transfers between devices, swap(): return lax.ppermute(value, AXES, [(i, i ^ mask) for i in range(32)])  13.6 us
    pallas_call x1, Pallas kernels, pick(): pl.pallas_call(pick_kernel, out_shape=outs, in_specs=[SMEM, VMEM, VMEM, V...  1.87 us
  transfers between devices with their start and end apart: 18, of which 10 were waited for; matrix products, arithmetic and copies ran while one was open for 0% of the time, Pallas kernels for 47%

profile of v1, /device:TPU:0, one launch (start us, length us, event | category | flops | bytes accessed | tf_op | source)
XLA Modules:
  0.0 92.4 jit_solution(4370133182429348533)
XLA Ops:
  0.1 0.7 and_select_fusion
  0.9 0.6 reduce_max.9
  2.2 89.4 %conditional.1 = (f32[128,1024]{1,0:T(8,128)S(1)}) conditional(s32[]{:T(128)} %convert_element_type.7, (s32[2]{0:T(128)S(1)}, s32[2,256]{1,0:T(2,128)}, f32[2,4,256]{2,1,0:T(4,128)}, f32[128,1024]{1,0:T(8,128)}, s32[2,256]{1,0:T(2,128)}, /*index=5*/f32[2,256]{1,0:T(2,128)}, bf16[2,256,1024]{2,1,0:T(8,128)(2,1)}) %tuple.19, (s32[2]{0:T(128)S(1)}, ...), branch_computations={%region_2.3_spmd, %region_3.4_spmd} | conditional | flops 3932160 | bytes 64512348 | solution.py:400
  2.4 1.9 %pick.1 = (bf16[32,512]{1,0:T(8,128)(2,1)S(1)}, bf16[32,512]{1,0:T(8,128)(2,1)S(1)}, bf16[64,512]{1,0:T(8,128)(2,1)S(1)}, bf16[64,512]{1,0:T(8,128)(2,1)S(1)}) custom-call(s32[2]{0:T(128)S(1)} %get-tuple-element.45.place, s32[2,256]{1,0:T(2,128)} %get-tuple-element.46.blocks, f32[2,4,256]{2,1,0:T(4,128)} %get-tuple-element.51.weights, ...), custom_call_target="tpu_custom_call" | custom-call | tf_op jit(solution)/shard_map/cond/branch_1_fun/pick/pallas_call | solution.py:106
  4.9 0.8 collective-permute-done
  5.7 3.9 %collective-permute-start.1 = (bf16[1,32,512]{2,1,0:T(8,128)(2,1)S(1)}, bf16[1,32,512]{2,1,0:T(8,128)(2,1)S(1)}, u32[]{:S(2)}, u32[]{:S(2)}) collective-permute-start(bf16[1,32,512]{2,1,0:T(8,128)(2,1)S(1)} %add_bitcast_fusion.1), channel_id=1, source_target_pairs={{0,16},{1,17},{2,18},{3,19},{4,20},{5,21},{6,22},{7,23},{8,24},{9,... | collective-permute-start | bytes 98312 | tf_op jit(solution)/shard_map/cond/branch_1_fun/ppermute | solution.py:350
  9.9 1.6 %collective-permute-done.1 = bf16[1,32,512]{2,1,0:T(8,128)(2,1)S(1)} collective-permute-done((bf16[1,32,512]{2,1,0:T(8,128)(2,1)S(1)}, bf16[1,32,512]{2,1,0:T(8,128)(2,1)S(1)}, u32[]{:S(2)}, u32[]{:S(2)}) %collective-permute-start.1) | collective-permute-done | bytes 32800 | tf_op jit(solution)/shard_map/cond/branch_1_fun/ppermute | solution.py:350
  11.5 2.7 %collective-permute-start.4 = (bf16[2,32,512]{2,1,0:T(8,128)(2,1)S(1)}, bf16[2,32,512]{2,1,0:T(8,128)(2,1)S(1)}, u32[]{:S(2)}, u32[]{:S(2)}) collective-permute-start(bf16[2,32,512]{2,1,0:T(8,128)(2,1)S(1)} %pad_maximum_fusion.7), channel_id=1, source_target_pairs={{0,8},{1,9},{2,10},{3,11},{4,12},{5,13},{6,14},{7,15},{8,0},{9,1},... | collective-permute-start | bytes 196616 | tf_op jit(solution)/shard_map/cond/branch_1_fun/ppermute | solution.py:350
  14.2 1.5 %collective-permute-start.2 = (bf16[2,32,512]{2,1,0:T(8,128)(2,1)S(1)}, bf16[2,32,512]{2,1,0:T(8,128)(2,1)S(1)}, u32[]{:S(2)}, u32[]{:S(2)}) collective-permute-start(bf16[2,32,512]{2,1,0:T(8,128)(2,1)S(1)} %pad_maximum_fusion.7), channel_id=1, source_target_pairs={{0,2},{1,3},{2,0},{3,1},{4,6},{5,7},{6,4},{7,5},{8,10},{9,11},{10,... | collective-permute-start | bytes 196616 | tf_op jit(solution)/shard_map/cond/branch_1_fun/ppermute | solution.py:350
  15.7 0.6 collective-permute-done.10
  16.5 1.5 %collective-permute-start.11 = (bf16[2,64,512]{2,1,0:T(8,128)(2,1)S(1)}, bf16[2,64,512]{2,1,0:T(8,128)(2,1)S(1)}, u32[]{:S(2)}, u32[]{:S(2)}) collective-permute-start(bf16[2,64,512]{2,1,0:T(8,128)(2,1)S(1)} %pad_maximum_fusion.6), channel_id=1, source_target_pairs={{0,2},{1,3},{2,0},{3,1},{4,6},{5,7},{6,4},{7,5},{8,10},{9,11},{10,... | collective-permute-start | bytes 393224 | tf_op jit(solution)/shard_map/cond/branch_1_fun/ppermute | solution.py:350
  18.0 0.9 %collective-permute-done.2 = bf16[2,32,512]{2,1,0:T(8,128)(2,1)S(1)} collective-permute-done((bf16[2,32,512]{2,1,0:T(8,128)(2,1)S(1)}, bf16[2,32,512]{2,1,0:T(8,128)(2,1)S(1)}, u32[]{:S(2)}, u32[]{:S(2)}) %collective-permute-start.2) | collective-permute-done | bytes 65568 | tf_op jit(solution)/shard_map/cond/branch_1_fun/ppermute | solution.py:350
  19.0 1.6 %collective-permute-start.3 = (bf16[4,32,512]{2,1,0:T(8,128)(2,1)S(1)}, bf16[4,32,512]{2,1,0:T(8,128)(2,1)S(1)}, u32[]{:S(2)}, u32[]{:S(2)}) collective-permute-start(bf16[4,32,512]{2,1,0:T(8,128)(2,1)S(1)} %pad_maximum_fusion.4), channel_id=1, source_target_pairs={{0,4},{1,5},{2,6},{3,7},{4,0},{5,1},{6,2},{7,3},{8,12},{9,13},{10,... | collective-permute-start | bytes 393224 | tf_op jit(solution)/shard_map/cond/branch_1_fun/ppermute | solution.py:350
  21.3 1.5 %collective-permute-start.14 = (bf16[2,64,512]{2,1,0:T(8,128)(2,1)S(1)}, bf16[2,64,512]{2,1,0:T(8,128)(2,1)S(1)}, u32[]{:S(2)}, u32[]{:S(2)}) collective-permute-start(bf16[2,64,512]{2,1,0:T(8,128)(2,1)S(1)} %collective-permute-done.13), channel_id=1, source_target_pairs={{0,4},{1,5},{2,6},{3,7},{4,0},{5,1},{6,2},{7,3},{8,12},{9,13},{10,... | collective-permute-start | bytes 393224 | tf_op jit(solution)/shard_map/cond/branch_1_fun/ppermute | solution.py:350
  22.8 2.5 %collective-permute-done.5 = bf16[2,32,512]{2,1,0:T(8,128)(2,1)S(1)} collective-permute-done((bf16[2,32,512]{2,1,0:T(8,128)(2,1)S(1)}, bf16[2,32,512]{2,1,0:T(8,128)(2,1)S(1)}, u32[]{:S(2)}, u32[]{:S(2)}) %collective-permute-start.5) | collective-permute-done | bytes 65568 | tf_op jit(solution)/shard_map/cond/branch_1_fun/ppermute | solution.py:350
  25.3 2.5 %collective-permute-start.6 = (bf16[4,32,512]{2,1,0:T(8,128)(2,1)S(1)}, bf16[4,32,512]{2,1,0:T(8,128)(2,1)S(1)}, u32[]{:S(2)}, u32[]{:S(2)}) collective-permute-start(bf16[4,32,512]{2,1,0:T(8,128)(2,1)S(1)} %pad_maximum_fusion.5), channel_id=1, source_target_pairs={{0,2},{1,3},{2,0},{3,1},{4,6},{5,7},{6,4},{7,5},{8,10},{9,11},{10,... | collective-permute-start | bytes 393224 | tf_op jit(solution)/shard_map/cond/branch_1_fun/ppermute | solution.py:350
  27.8 1.6 %collective-permute-start.12 = (bf16[4,64,512]{2,1,0:T(8,128)(2,1)S(1)}, bf16[4,64,512]{2,1,0:T(8,128)(2,1)S(1)}, u32[]{:S(2)}, u32[]{:S(2)}) collective-permute-start(bf16[4,64,512]{2,1,0:T(8,128)(2,1)S(1)} %pad_maximum_fusion.2), channel_id=1, source_target_pairs={{0,4},{1,5},{2,6},{3,7},{4,0},{5,1},{6,2},{7,3},{8,12},{9,13},{10,... | collective-permute-start | bytes 786440 | tf_op jit(solution)/shard_map/cond/branch_1_fun/ppermute | solution.py:350
  29.5 1.2 %collective-permute-start.15 = (bf16[4,64,512]{2,1,0:T(8,128)(2,1)S(1)}, bf16[4,64,512]{2,1,0:T(8,128)(2,1)S(1)}, u32[]{:S(2)}, u32[]{:S(2)}) collective-permute-start(bf16[4,64,512]{2,1,0:T(8,128)(2,1)S(1)} %pad_maximum_fusion.3), channel_id=1, source_target_pairs={{0,2},{1,3},{2,0},{3,1},{4,6},{5,7},{6,4},{7,5},{8,10},{9,11},{10,... | collective-permute-start | bytes 786440 | tf_op jit(solution)/shard_map/cond/branch_1_fun/ppermute | solution.py:350
  30.7 3.6 %collective-permute-done.12 = bf16[4,64,512]{2,1,0:T(8,128)(2,1)S(1)} collective-permute-done((bf16[4,64,512]{2,1,0:T(8,128)(2,1)S(1)}, bf16[4,64,512]{2,1,0:T(8,128)(2,1)S(1)}, u32[]{:S(2)}, u32[]{:S(2)}) %collective-permute-start.12) | collective-permute-done | bytes 262176 | tf_op jit(solution)/shard_map/cond/branch_1_fun/ppermute | solution.py:350
  34.4 1.5 %collective-permute-done.15 = bf16[4,64,512]{2,1,0:T(8,128)(2,1)S(1)} collective-permute-done((bf16[4,64,512]{2,1,0:T(8,128)(2,1)S(1)}, bf16[4,64,512]{2,1,0:T(8,128)(2,1)S(1)}, u32[]{:S(2)}, u32[]{:S(2)}) %collective-permute-start.15) | collective-permute-done | bytes 262176 | tf_op jit(solution)/shard_map/cond/branch_1_fun/ppermute | solution.py:350
  36.8 1.6 %collective-permute-done.7.rest_2_ = bf16[8,32,512]{2,1,0:T(8,128)(2,1)S(1)} collective-permute-done((bf16[8,32,512]{2,1,0:T(8,128)(2,1)S(1)}, bf16[8,32,512]{2,1,0:T(8,128)(2,1)S(1)}, u32[]{:S(2)}, u32[]{:S(2)}) %collective-permute-start.7) | collective-permute-done | bytes 262176 | tf_op jit(solution)/shard_map/cond/branch_1_fun/ppermute | solution.py:350
  38.7 43.8 %first_batch.3 = (bf16[256,1024]{1,0:T(8,128)(2,1)S(1)}, bf16[256,1024]{1,0:T(8,128)(2,1)S(1)}) custom-call(s32[2]{0:T(128)S(1)} %get-tuple-element.45.place, s32[2,256]{1,0:T(2,128)S(1)} %copy-done.6, s32[2,256]{1,0:T(2,128)S(1)} %copy-done.8, f32[2,256]{1,0:T(2,128)S(1)} %copy-done.10, bf16[2,256,1024]{2,1,0:T(8,128)(2,1)S(1)} %copy-done.1, ...), custom_call_target="tpu_custom_call" | custom-call | tf_op jit(solution)/shard_map/cond/branch_1_fun/first_batch/pallas_call | solution.py:300
  82.6 9.0 %second_batch.3 = f32[128,1024]{1,0:T(8,128)S(1)} custom-call(s32[2]{0:T(128)S(1)} %get-tuple-element.45.place, s32[2,256]{1,0:T(2,128)S(1)} %copy-done.6, s32[2,256]{1,0:T(2,128)S(1)} %copy-done.8, f32[2,256]{1,0:T(2,128)S(1)} %copy-done.10, bf16[2,256,1024]{2,1,0:T(8,128)(2,1)S(1)} %copy-done.1, f32[128,1024]{1,0:T(8,128)S(1)} %copy-done.3, ...), custom_call_target="tpu_custom_call" | custom-call | tf_op jit(solution)/shard_map/cond/branch_1_fun/second_batch/pallas_call | solution.py:300
  91.6 0.8 copy-done.4
  (48 shorter events, 3.5 us)
Async XLA Ops:
  4.3 1.4 %collective-permute-start = (bf16[32,512]{1,0:T(8,128)(2,1)S(1)}, bf16[32,512]{1,0:T(8,128)(2,1)S(1)}, u32[]{:S(2)}, u32[]{:S(2)}) collective-permute-start(bf16[32,512]{1,0:T(8,128)(2,1)S(1)} %get-tuple-element.53), channel_id=1, source_target_pairs={{0,1},{1,0},{2,3},{3,2},{4,5},{5,4},{6,7},{7,6},{8,9},{9,8},{10,11... | collective-permute-start | bytes 98312 | tf_op jit(solution)/shard_map/cond/branch_1_fun/ppermute | solution.py:350
  4.8 4.8 %collective-permute-start.9 = (bf16[64,512]{1,0:T(8,128)(2,1)S(1)}, bf16[64,512]{1,0:T(8,128)(2,1)S(1)}, u32[]{:S(2)}, u32[]{:S(2)}) collective-permute-start(bf16[64,512]{1,0:T(8,128)(2,1)S(1)} %get-tuple-element.57), channel_id=1, source_target_pairs={{0,1},{1,0},{2,3},{3,2},{4,5},{5,4},{6,7},{7,6},{8,9},{9,8},{10,11... | collective-permute-start | bytes 196616 | tf_op jit(solution)/shard_map/cond/branch_1_fun/ppermute | solution.py:350
  5.7 5.8 %collective-permute-start.1 = (bf16[1,32,512]{2,1,0:T(8,128)(2,1)S(1)}, bf16[1,32,512]{2,1,0:T(8,128)(2,1)S(1)}, u32[]{:S(2)}, u32[]{:S(2)}) collective-permute-start(bf16[1,32,512]{2,1,0:T(8,128)(2,1)S(1)} %add_bitcast_fusion.1), channel_id=1, source_target_pairs={{0,16},{1,17},{2,18},{3,19},{4,20},{5,21},{6,22},{7,23},{8,24},{9,... | collective-permute-start | bytes 98312 | tf_op jit(solution)/shard_map/cond/branch_1_fun/ppermute | solution.py:350
  9.6 6.7 %collective-permute-start.10 = (bf16[1,64,512]{2,1,0:T(8,128)(2,1)S(1)}, bf16[1,64,512]{2,1,0:T(8,128)(2,1)S(1)}, u32[]{:S(2)}, u32[]{:S(2)}) collective-permute-start(bf16[1,64,512]{2,1,0:T(8,128)(2,1)S(1)} %add_bitcast_fusion), channel_id=1, source_target_pairs={{0,16},{1,17},{2,18},{3,19},{4,20},{5,21},{6,22},{7,23},{8,24},{9,... | collective-permute-start | bytes 196616 | tf_op jit(solution)/shard_map/cond/branch_1_fun/ppermute | solution.py:350
  11.5 9.0 %collective-permute-start.4 = (bf16[2,32,512]{2,1,0:T(8,128)(2,1)S(1)}, bf16[2,32,512]{2,1,0:T(8,128)(2,1)S(1)}, u32[]{:S(2)}, u32[]{:S(2)}) collective-permute-start(bf16[2,32,512]{2,1,0:T(8,128)(2,1)S(1)} %pad_maximum_fusion.7), channel_id=1, source_target_pairs={{0,8},{1,9},{2,10},{3,11},{4,12},{5,13},{6,14},{7,15},{8,0},{9,1},... | collective-permute-start | bytes 196616 | tf_op jit(solution)/shard_map/cond/branch_1_fun/ppermute | solution.py:350
  14.2 4.8 %collective-permute-start.2 = (bf16[2,32,512]{2,1,0:T(8,128)(2,1)S(1)}, bf16[2,32,512]{2,1,0:T(8,128)(2,1)S(1)}, u32[]{:S(2)}, u32[]{:S(2)}) collective-permute-start(bf16[2,32,512]{2,1,0:T(8,128)(2,1)S(1)} %pad_maximum_fusion.7), channel_id=1, source_target_pairs={{0,2},{1,3},{2,0},{3,1},{4,6},{5,7},{6,4},{7,5},{8,10},{9,11},{10,... | collective-permute-start | bytes 196616 | tf_op jit(solution)/shard_map/cond/branch_1_fun/ppermute | solution.py:350
  16.3 5.0 %collective-permute-start.13 = (bf16[2,64,512]{2,1,0:T(8,128)(2,1)S(1)}, bf16[2,64,512]{2,1,0:T(8,128)(2,1)S(1)}, u32[]{:S(2)}, u32[]{:S(2)}) collective-permute-start(bf16[2,64,512]{2,1,0:T(8,128)(2,1)S(1)} %pad_maximum_fusion.6), channel_id=1, source_target_pairs={{0,8},{1,9},{2,10},{3,11},{4,12},{5,13},{6,14},{7,15},{8,0},{9,1},... | collective-permute-start | bytes 393224 | tf_op jit(solution)/shard_map/cond/branch_1_fun/ppermute | solution.py:350
  16.5 11.3 %collective-permute-start.11 = (bf16[2,64,512]{2,1,0:T(8,128)(2,1)S(1)}, bf16[2,64,512]{2,1,0:T(8,128)(2,1)S(1)}, u32[]{:S(2)}, u32[]{:S(2)}) collective-permute-start(bf16[2,64,512]{2,1,0:T(8,128)(2,1)S(1)} %pad_maximum_fusion.6), channel_id=1, source_target_pairs={{0,2},{1,3},{2,0},{3,1},{4,6},{5,7},{6,4},{7,5},{8,10},{9,11},{10,... | collective-permute-start | bytes 393224 | tf_op jit(solution)/shard_map/cond/branch_1_fun/ppermute | solution.py:350
  19.0 17.1 %collective-permute-start.3 = (bf16[4,32,512]{2,1,0:T(8,128)(2,1)S(1)}, bf16[4,32,512]{2,1,0:T(8,128)(2,1)S(1)}, u32[]{:S(2)}, u32[]{:S(2)}) collective-permute-start(bf16[4,32,512]{2,1,0:T(8,128)(2,1)S(1)} %pad_maximum_fusion.4), channel_id=1, source_target_pairs={{0,4},{1,5},{2,6},{3,7},{4,0},{5,1},{6,2},{7,3},{8,12},{9,13},{10,... | collective-permute-start | bytes 393224 | tf_op jit(solution)/shard_map/cond/branch_1_fun/ppermute | solution.py:350
  20.6 4.7 %collective-permute-start.5 = (bf16[2,32,512]{2,1,0:T(8,128)(2,1)S(1)}, bf16[2,32,512]{2,1,0:T(8,128)(2,1)S(1)}, u32[]{:S(2)}, u32[]{:S(2)}) collective-permute-start(bf16[2,32,512]{2,1,0:T(8,128)(2,1)S(1)} %collective-permute-done.4), channel_id=1, source_target_pairs={{0,4},{1,5},{2,6},{3,7},{4,0},{5,1},{6,2},{7,3},{8,12},{9,13},{10,... | collective-permute-start | bytes 196616 | tf_op jit(solution)/shard_map/cond/branch_1_fun/ppermute | solution.py:350
  21.3 8.1 %collective-permute-start.14 = (bf16[2,64,512]{2,1,0:T(8,128)(2,1)S(1)}, bf16[2,64,512]{2,1,0:T(8,128)(2,1)S(1)}, u32[]{:S(2)}, u32[]{:S(2)}) collective-permute-start(bf16[2,64,512]{2,1,0:T(8,128)(2,1)S(1)} %collective-permute-done.13), channel_id=1, source_target_pairs={{0,4},{1,5},{2,6},{3,7},{4,0},{5,1},{6,2},{7,3},{8,12},{9,13},{10,... | collective-permute-start | bytes 393224 | tf_op jit(solution)/shard_map/cond/branch_1_fun/ppermute | solution.py:350
  25.3 11.3 %collective-permute-start.6 = (bf16[4,32,512]{2,1,0:T(8,128)(2,1)S(1)}, bf16[4,32,512]{2,1,0:T(8,128)(2,1)S(1)}, u32[]{:S(2)}, u32[]{:S(2)}) collective-permute-start(bf16[4,32,512]{2,1,0:T(8,128)(2,1)S(1)} %pad_maximum_fusion.5), channel_id=1, source_target_pairs={{0,2},{1,3},{2,0},{3,1},{4,6},{5,7},{6,4},{7,5},{8,10},{9,11},{10,... | collective-permute-start | bytes 393224 | tf_op jit(solution)/shard_map/cond/branch_1_fun/ppermute | solution.py:350
  27.8 6.4 %collective-permute-start.12 = (bf16[4,64,512]{2,1,0:T(8,128)(2,1)S(1)}, bf16[4,64,512]{2,1,0:T(8,128)(2,1)S(1)}, u32[]{:S(2)}, u32[]{:S(2)}) collective-permute-start(bf16[4,64,512]{2,1,0:T(8,128)(2,1)S(1)} %pad_maximum_fusion.2), channel_id=1, source_target_pairs={{0,4},{1,5},{2,6},{3,7},{4,0},{5,1},{6,2},{7,3},{8,12},{9,13},{10,... | collective-permute-start | bytes 786440 | tf_op jit(solution)/shard_map/cond/branch_1_fun/ppermute | solution.py:350
  29.4 9.2 %copy-start.1 = (bf16[2,256,1024]{2,1,0:T(8,128)(2,1)S(1)}, bf16[2,256,1024]{2,1,0:T(8,128)(2,1)}, u32[]{:S(2)}) copy-start(bf16[2,256,1024]{2,1,0:T(8,128)(2,1)} %get-tuple-element.74.noise) | copy-start | bytes 3145732 | tf_op jit(solution)/shard_map/cond
  29.4 9.2 %copy-start.6 = (s32[2,256]{1,0:T(2,128)S(1)}, s32[2,256]{1,0:T(2,128)}, u32[]{:S(2)}) copy-start(s32[2,256]{1,0:T(2,128)} %get-tuple-element.46.blocks) | copy-start | bytes 6148 | tf_op jit(solution)/shard_map/cond
  29.5 9.2 %copy-start.8 = (s32[2,256]{1,0:T(2,128)S(1)}, s32[2,256]{1,0:T(2,128)}, u32[]{:S(2)}) copy-start(s32[2,256]{1,0:T(2,128)} %get-tuple-element.70.tags) | copy-start | bytes 6148 | tf_op jit(solution)/shard_map/cond
  29.5 9.2 %copy-start.10 = (f32[2,256]{1,0:T(2,128)S(1)}, f32[2,256]{1,0:T(2,128)}, u32[]{:S(2)}) copy-start(f32[2,256]{1,0:T(2,128)} %get-tuple-element.72.values) | copy-start | bytes 6148 | tf_op jit(solution)/shard_map/cond
  29.5 6.4 %collective-permute-start.15 = (bf16[4,64,512]{2,1,0:T(8,128)(2,1)S(1)}, bf16[4,64,512]{2,1,0:T(8,128)(2,1)S(1)}, u32[]{:S(2)}, u32[]{:S(2)}) collective-permute-start(bf16[4,64,512]{2,1,0:T(8,128)(2,1)S(1)} %pad_maximum_fusion.3), channel_id=1, source_target_pairs={{0,2},{1,3},{2,0},{3,1},{4,6},{5,7},{6,4},{7,5},{8,10},{9,11},{10,... | collective-permute-start | bytes 786440 | tf_op jit(solution)/shard_map/cond/branch_1_fun/ppermute | solution.py:350
  34.3 48.2 %collective-permute-start.16 = (bf16[8,64,512]{2,1,0:T(8,128)(2,1)S(1)}, bf16[8,64,512]{2,1,0:T(8,128)(2,1)S(1)}, u32[]{:S(2)}, u32[]{:S(2)}) collective-permute-start(bf16[8,64,512]{2,1,0:T(8,128)(2,1)S(1)} %pad_maximum_fusion.rest_0_), channel_id=1, source_target_pairs={{0,1},{1,0},{2,3},{3,2},{4,5},{5,4},{6,7},{7,6},{8,9},{9,8},{10,11... | collective-permute-start | bytes 1572872 | tf_op jit(solution)/shard_map/cond/branch_1_fun/ppermute | solution.py:350
  35.9 46.6 %copy-start.3 = (f32[128,1024]{1,0:T(8,128)S(1)}, f32[128,1024]{1,0:T(8,128)}, u32[]{:S(2)}) copy-start(f32[128,1024]{1,0:T(8,128)} %get-tuple-element.68.state) | copy-start | bytes 1572868 | tf_op jit(solution)/shard_map/cond
  36.0 46.6 %collective-permute-start.17 = (bf16[8,64,512]{2,1,0:T(8,128)(2,1)S(1)}, bf16[8,64,512]{2,1,0:T(8,128)(2,1)S(1)}, u32[]{:S(2)}, u32[]{:S(2)}) collective-permute-start(bf16[8,64,512]{2,1,0:T(8,128)(2,1)S(1)} %constant_dynamic-update-slice_fusion.3.rest_1_), channel_id=1, source_target_pairs={{0,1},{1,0},{2,3},{3,2},{4,5},{5,4},{6,7},{7,6},{8,9},{9,8},{10,11... | collective-permute-start | bytes 1572872 | tf_op jit(solution)/shard_map/cond/branch_1_fun/ppermute | solution.py:350
  36.1 2.2 %collective-permute-start.7 = (bf16[8,32,512]{2,1,0:T(8,128)(2,1)S(1)}, bf16[8,32,512]{2,1,0:T(8,128)(2,1)S(1)}, u32[]{:S(2)}, u32[]{:S(2)}) collective-permute-start(bf16[8,32,512]{2,1,0:T(8,128)(2,1)S(1)} %pad_maximum_fusion.1.rest_0_), channel_id=1, source_target_pairs={{0,1},{1,0},{2,3},{3,2},{4,5},{5,4},{6,7},{7,6},{8,9},{9,8},{10,11... | collective-permute-start | bytes 786440 | tf_op jit(solution)/shard_map/cond/branch_1_fun/ppermute | solution.py:350
  36.7 2.0 %collective-permute-start.8 = (bf16[8,32,512]{2,1,0:T(8,128)(2,1)S(1)}, bf16[8,32,512]{2,1,0:T(8,128)(2,1)S(1)}, u32[]{:S(2)}, u32[]{:S(2)}) collective-permute-start(bf16[8,32,512]{2,1,0:T(8,128)(2,1)S(1)} %constant_dynamic-update-slice_fusion.rest_1_), channel_id=1, source_target_pairs={{0,1},{1,0},{2,3},{3,2},{4,5},{5,4},{6,7},{7,6},{8,9},{9,8},{10,11... | collective-permute-start | bytes 786440 | tf_op jit(solution)/shard_map/cond/branch_1_fun/ppermute | solution.py:350
  91.6 0.8 copy-start.4

commit v2 on v1

v2 whole, which is shorter than its diff:
```python
import functools

import jax
import jax.numpy as jnp
from jax import lax
from jax.experimental import pallas as pl
from jax.experimental.pallas import tpu as pltpu
from jax.sharding import PartitionSpec as P

SLOTS = 64
UNIT = 1.0 / 1024
SCALE = 0.5
TOLERANCE = 2e-3
BF16 = jnp.bfloat16
F32 = jnp.float32
VMEM = pl.BlockSpec(memory_space=pltpu.VMEM)
SMEM = pl.BlockSpec(memory_space=pltpu.SMEM)
PARAMS = pltpu.CompilerParams(vmem_limit_bytes=40 * 1024 * 1024)


def nt(a, b):
    return lax.dot_general(a, b, (((1,), (1,)), ((), ())), preferred_element_type=F32)


def nn(a, b):
    return lax.dot_general(a, b, (((1,), (0,)), ((), ())), preferred_element_type=F32)


def split(a):
    high = a.astype(BF16)
    return high, (a - high.astype(F32)).astype(BF16)


def dot3(dot, a, b):
    (ah, al), (bh, bl) = a, b
    return dot(ah, bh) + (dot(ah, bl) + dot(al, bh))


def row_mean(a):
    return jnp.sum(a, axis=1, keepdims=True) * (1.0 / a.shape[1])


def column(row):
    size = row.shape[1]
    lane = lax.broadcasted_iota(jnp.int32, (size, size), 1)
    sub = lax.broadcasted_iota(jnp.int32, (size, size), 0)
    return jnp.sum(jnp.where(lane == sub, row, jnp.zeros_like(row)), axis=1, keepdims=True)


def both_ways(row):
    as_float = row.astype(F32)
    return as_float, column(as_float)


def select(lanes, points, local, weight):
    value = jnp.zeros(lanes.shape, F32)
    for point in range(points):
        value = jnp.where(lanes % points == point, weight[point], value)
    return jnp.where((lanes // points).astype(F32) == local, value, 0.0)


def rounded(value):
    return value.astype(BF16).astype(F32)


def pick_kernel(place, blocks, weights, state, keep, send):
    device = place[0]
    batches, points, size = weights.shape
    width, members = state.shape
    held = width // points
    lane = lax.broadcasted_iota(jnp.int32, (size, size), 1)
    sub = lax.broadcasted_iota(jnp.int32, (size, size), 0)
    slots = lax.broadcasted_iota(jnp.int32, (SLOTS, size), 0)
    lanes = lax.broadcasted_iota(jnp.int32, (SLOTS, width), 1)
    selectors, taken = [], []
    for batch in range(batches):
        row = blocks[batch : batch + 1, :]
        pair_row, pair_column = both_ways(row // (2 * held))
        before = jnp.where((pair_row == pair_column) & (sub < lane), 1.0, 0.0)
        rank = jnp.sum(before, axis=0, keepdims=True).astype(jnp.int32)
        slot = jnp.where(row // held == device, rank if batch == 0 else SLOTS - 1 - rank, -1)
        chosen = jnp.where(slots == slot, 1.0, 0.0)
        local = jnp.sum(chosen * (row - device * held).astype(F32), axis=1, keepdims=True)
        weight = lax.dot_general(
            chosen,
            weights[batch],
            (((1,), (1,)), ((), ())),
            precision=lax.Precision.HIGHEST,
            preferred_element_type=F32,
        )
        columns = [weight[:, point : point + 1] for point in range(points)]
        selectors.append(select(lanes, points, local, columns))
        taken.append(jnp.sum(chosen, axis=1, keepdims=True))
    rows = jnp.dot(
        selectors[0] + selectors[1],
        state[...],
        precision=lax.Precision.HIGHEST,
        preferred_element_type=F32,
    )
    rows = jnp.where(taken[0] > 0.5, rounded(rows), rows)
    code = jnp.round(rows * (1.0 / UNIT)).astype(jnp.int32)
    left, right = code[:, : members // 2], code[:, members // 2 :]
    first = device % 2 == 0
    keep[...] = jnp.where(first, left, right).astype(jnp.int16)
    send[...] = jnp.where(first, right, left).astype(jnp.int16)


def pick(place, blocks, weights, state):
    return pl.pallas_call(
        pick_kernel,
        out_shape=[jax.ShapeDtypeStruct((SLOTS, state.shape[1] // 2), jnp.int16)] * 2,
        in_specs=[SMEM, VMEM, VMEM, VMEM],
        out_specs=[VMEM] * 2,
        compiler_params=PARAMS,
        name="pick",
    )(place, blocks, weights, state)


def pick_all_kernel(place, blocks, weights, state, out):
    device = place[0]
    batches, points, size = weights.shape
    width = state.shape[0]
    lanes = lax.broadcasted_iota(jnp.int32, (size, width), 1)
    for batch in range(batches):
        columns = [column(weights[batch, point : point + 1, :]) for point in range(points)]
        local = column((blocks[batch : batch + 1, :] - device * (width // points)).astype(F32))
        rows = jnp.dot(
            select(lanes, points, local, columns),
            state[...],
            precision=lax.Precision.HIGHEST,
            preferred_element_type=F32,
        )
        rows = rounded(rows) if batch == 0 else rows
        out[batch * size : (batch + 1) * size, :] = jnp.round(rows * (1.0 / UNIT))


def pick_all(place, blocks, weights, state):
    return pl.pallas_call(
        pick_all_kernel,
        out_shape=jax.ShapeDtypeStruct((blocks.size, state.shape[1]), F32),
        in_specs=[SMEM, VMEM, VMEM, VMEM],
        out_specs=VMEM,
        compiler_params=PARAMS,
        name="pick_all",
    )(place, blocks, weights, state)


def put_in_order(place, blocks, members, pieces):
    device, held = place[0], place[1]
    size = blocks.shape[1]
    lane = lax.broadcasted_iota(jnp.int32, (size, size), 1)
    sub = lax.broadcasted_iota(jnp.int32, (size, size), 0)
    values = jnp.concatenate([ref[...].reshape(2 * SLOTS, -1) for _, ref in pieces], axis=0)
    values = values.astype(jnp.int32)
    high, low = values >> 8, values & 255
    high, low = high.astype(F32).astype(BF16), low.astype(F32).astype(BF16)
    slots = lax.broadcasted_iota(jnp.int32, (size, values.shape[0]), 1)
    results = []
    for batch in range(blocks.shape[0]):
        pair_row, pair_column = both_ways(blocks[batch : batch + 1, :] // (2 * held))
        before = jnp.where((pair_row == pair_column) & (lane < sub), 1.0, 0.0)
        rank = jnp.sum(before, axis=1, keepdims=True).astype(jnp.int32)
        away = (2 * pair_column.astype(jnp.int32)) ^ device
        near_x_y = (away >> 1) & 7
        where = jnp.full(rank.shape, -2 * SLOTS, jnp.int32)
        for index, (distance, _) in enumerate(pieces):
            where = jnp.where(near_x_y == distance, 2 * SLOTS * index, where)
        slot = where + SLOTS * ((away >> 4) & 1) + (rank if batch == 0 else SLOTS - 1 - rank)
        chosen = jnp.where(slots == slot, 1.0, 0.0).astype(BF16)
        results.append(256.0 * nn(chosen, high) + nn(chosen, low))
    return results


def early_kernel(distances, place, blocks, *refs):
    results = put_in_order(place, blocks, refs[0].shape[-1], list(zip(distances, refs[:-1])))
    size = blocks.shape[1]
    for batch, result in enumerate(results):
        refs[-1][batch * size : (batch + 1) * size, :] = result


def late_kernel(distances, place, blocks, early, *refs):
    results = put_in_order(place, blocks, refs[0].shape[-1], list(zip(distances, refs[:-2])))
    size = blocks.shape[1]
    refs[-2][...] = ((results[0] + early[:size, :]) * UNIT).astype(BF16)
    refs[-1][...] = (results[1] + early[size:, :]).astype(jnp.int32).astype(jnp.int16)


def early_rows(place, blocks, pieces):
    distances = [distance for distance, _ in pieces]
    half = pieces[0][1].shape[-1]
    return pl.pallas_call(
        functools.partial(early_kernel, distances),
        out_shape=jax.ShapeDtypeStruct((blocks.size, half), F32),
        in_specs=[SMEM] + [VMEM] * (1 + len(pieces)),
        out_specs=VMEM,
        compiler_params=PARAMS,
        cost_estimate=pl.CostEstimate(flops=10**9, bytes_accessed=4 * 10**6, transcendentals=0),
        name="early_rows",
    )(place, blocks, *[piece for _, piece in pieces])


def late_rows(place, blocks, early, pieces):
    distances = [distance for distance, _ in pieces]
    rows, half = blocks.shape[1], early.shape[1]
    return pl.pallas_call(
        functools.partial(late_kernel, distances),
        out_shape=[
            jax.ShapeDtypeStruct((rows, half), BF16),
            jax.ShapeDtypeStruct((rows, half), jnp.int16),
        ],
        in_specs=[SMEM] + [VMEM] * (2 + len(pieces)),
        out_specs=[VMEM] * 2,
        compiler_params=PARAMS,
        name="late_rows",
    )(place, blocks, early, *[piece for _, piece in pieces])


def eliminate(covariance, work, inverse):
    size = covariance.shape[0]
    lane = lax.broadcasted_iota(jnp.int32, (size, size), 1)
    sub = lax.broadcasted_iota(jnp.int32, (size, size), 0)
    work[...] = covariance
    inverse[...] = jnp.where(lane == sub, 1.0, 0.0)

    def step(k, carry):
        row = work[pl.ds(k, 1), :]
        current = work[...]
        pivot = jnp.sum(jnp.where(lane[:1] == k, row, 0.0), axis=1, keepdims=True)
        column = jnp.sum(jnp.where(lane == k, current, 0.0), axis=1, keepdims=True)
        factor = jnp.where(sub[:, :1] > k, column / pivot, 0.0)
        inverse_row = inverse[pl.ds(k, 1), :]
        work[...] = current - factor * row
        inverse[...] = inverse[...] - factor * inverse_row
        return carry

    lax.fori_loop(0, size, step, 0)
    pivots = jnp.sum(jnp.where(lane == sub, work[...], 0.0), axis=1, keepdims=True)
    inverse[...] = inverse[...] * (1.0 / jnp.sqrt(pivots))


def inverse_factor(covariance, work, inverse):
    size = covariance.shape[0]
    lane = lax.broadcasted_iota(jnp.int32, (size, size), 1)
    sub = lax.broadcasted_iota(jnp.int32, (size, size), 0)
    diagonal = lane == sub
    eye = jnp.where(diagonal, 1.0, 0.0)
    half = jnp.where(lane < sub, 1.0, jnp.where(diagonal, 0.5, 0.0))
    on_diagonal = jnp.where(diagonal, covariance, 0.0)
    scale_row = lax.rsqrt(jnp.sum(on_diagonal, axis=0, keepdims=True) * (1.0 / SCALE))
    scale_column = lax.rsqrt(jnp.sum(on_diagonal, axis=1, keepdims=True) * (1.0 / SCALE))
    scaled = covariance * scale_row * scale_column

    def third_order(m):
        low = (m - eye) * half
        lowb = low.astype(BF16)
        return (nn(lowb, lowb) + half * nt(lowb, lowb)) - low

    m = scaled
    t = None
    for step in range(3):
        u = third_order(m) + eye
        ub = u.astype(BF16)
        t = u if t is None else nn(ub, t.astype(BF16))
        if step < 2:
            m = nt(nn(ub, m.astype(BF16)).astype(BF16), ub)
    parts = split(scaled)
    ts = split(t)
    m = dot3(nt, split(dot3(nn, ts, parts)), ts)
    t = t + nn(third_order(m).astype(BF16), ts[0])
    ts = split(t)
    m = dot3(nt, split(dot3(nn, ts, parts)), ts)
    error = m - eye
    t = t - nn((error * half).astype(BF16), ts[0])
    inverse[...] = t * scale_row
    good = jnp.min(jnp.where(jnp.abs(error) <= TOLERANCE, 1.0, 0.0))

    @pl.when(good < 0.5)
    def _():
        eliminate(covariance, work, inverse)


def whiten(observed, tags, values, noise, work, inverse):
    members = observed.shape[1]
    size = observed.shape[0]
    anomalies = observed - row_mean(observed)
    ah, al = split(anomalies)
    lane = lax.broadcasted_iota(jnp.int32, (size, size), 1)
    sub = lax.broadcasted_iota(jnp.int32, (size, size), 0)
    variance = column(jnp.where(tags == 0, 0.5, 2.0))
    values = column(values)
    covariance = dot3(nt, (ah, al), (ah, al)) * (1.0 / (members - 1))
    covariance = covariance + jnp.where(lane == sub, variance, 0.0)
    inverse_factor(covariance, work, inverse)
    ts = split(inverse[...])
    innovation = values + jnp.sqrt(variance) * noise.astype(F32) - observed
    whitened = dot3(nn, ts, (ah, al)).astype(BF16)
    white_innov = dot3(nn, ts, split(innovation)).astype(BF16)
    return whitened, white_innov


def update(state, whitened, white_innov):
    members = state.shape[1]
    sh, sl = split(state - row_mean(state))
    ph, plow = split(nt(sh, whitened) + nt(sl, whitened))
    return state + (nn(ph, white_innov) + nn(plow, white_innov)) * (1.0 / (members - 1))


def both_halves(place, own, other):
    own, other = own[...].astype(F32), other[...].astype(F32)
    first = place[0] % 2 == 0
    return jnp.concatenate(
        [jnp.where(first, own, other), jnp.where(first, other, own)], axis=1
    )


def first_kernel(place, tags, values, noise, own, other, whitened, white_innov, work, inverse):
    observed = both_halves(place, own, other)
    w, v = whiten(observed, tags[:1, :], values[:1, :], noise[0], work, inverse)
    whitened[...] = w
    white_innov[...] = v


def second_kernel(
    place, tags, values, noise, own, other, state, whitened, white_innov, analysis, work, inverse
):
    prior = both_halves(place, own, other) * UNIT
    w, v = whitened[...], white_innov[...]
    observed = rounded(update(prior, w, v))
    first = update(state[...], w, v)
    w, v = whiten(observed, tags[1:2, :], values[1:2, :], noise[0], work, inverse)
    analysis[...] = update(first, w, v)


def whole(array):
    return pl.BlockSpec(array.shape, lambda i, n=len(array.shape): (0,) * n)


def batch_call(kernel, name, batch, outs, place, tags, values, noise, *arrays):
    rows, members = noise.shape[1:]
    return pl.pallas_call(
        kernel,
        grid=(1,),
        out_shape=outs,
        in_specs=[SMEM, whole(tags), whole(values)]
        + [pl.BlockSpec((1, rows, members), lambda i: (batch, 0, 0))]
        + [whole(array) for array in arrays],
        out_specs=[whole(out) for out in outs],
        scratch_shapes=[pltpu.VMEM((rows, rows), F32), pltpu.VMEM((rows, rows), F32)],
        compiler_params=PARAMS,
        name=name,
    )(place, tags, values, noise, *arrays)


def batches(place, tags, values, noise, state, observed, prior):
    shape = jax.ShapeDtypeStruct(noise.shape[1:], BF16)
    shared = (place, tags, values, noise)
    whitened, white_innov = batch_call(
        first_kernel, "first_batch", 0, [shape, shape], *shared, *observed
    )
    analysis = jax.ShapeDtypeStruct(state.shape, F32)
    return batch_call(
        second_kernel, "second_batch", 1, [analysis], *shared, *prior, state, whitened, white_innov
    )[0]


AXES = ("row", "col")
CORE, Y, X, NEAR_Z, FAR_Z = 1, 2, 4, 8, 16


def swap(value, mask):
    return lax.ppermute(value, AXES, [(i, i ^ mask) for i in range(32)])


def by_slots(place, ensemble, blocks, weights):
    keep, send = pick(place, blocks, weights, ensemble)
    block = (keep + swap(send, CORE))[None]
    here = jnp.concatenate([block, swap(block, FAR_Z)], axis=0)
    near = swap(here, NEAR_Z)
    early = [(0, here), (NEAR_Z // 2, near)]
    early += [(mask // 2, swap(here, mask)) for mask in (Y, X, X | Y)]
    late = [((NEAR_Z | mask) // 2, swap(near, mask)) for mask in (Y, X, X | Y)]
    return late_rows(place, blocks, early_rows(place, blocks, early), late)


def add_by_swaps(value):
    for mask in (CORE, Y, X, NEAR_Z, FAR_Z):
        value = value + swap(value, mask)
    return value


def half_of(value, core):
    rows, members = value.shape
    return lax.dynamic_slice(value, (0, core * (members // 2)), (rows, members // 2))


def by_sum(add_up, other, place, ensemble, blocks, weights):
    rows = blocks.shape[1]
    codes = add_up(pick_all(place, blocks, weights, ensemble))
    codes = half_of(codes, (place[0] + other) % 2)
    return (codes[:rows] * UNIT).astype(BF16), codes[rows:].astype(jnp.int16)


def body(staged, ensemble, obs_blocks, obs_weights, comp_tags, obs_values, obs_noise):
    held = ensemble.shape[0] // obs_weights.shape[2]
    place = jnp.stack([lax.axis_index(AXES), held]).astype(jnp.int32)
    by_point = jnp.swapaxes(obs_weights, 1, 2)
    operands = (place, ensemble, obs_blocks, by_point)
    if staged:
        pair = obs_blocks // (2 * held)
        counts = jnp.sum(
            (pair[:, :, None] == jnp.arange(16, dtype=jnp.int32)).astype(jnp.int32), axis=(0, 1)
        )
        slotted = by_slots(*operands)
        own = lax.cond(
            jnp.max(counts) <= SLOTS,
            lambda slotted, *operands: tuple(slotted),
            lambda slotted, *operands: by_sum(add_by_swaps, 0, *operands),
            slotted,
            *operands,
        )
        pairs = [(half, swap(half, CORE)) for half in own]
    else:
        add_up = lambda value: lax.psum(value, AXES)
        pairs = list(zip(by_sum(add_up, 0, *operands), by_sum(add_up, 1, *operands)))
    return batches(place, comp_tags, obs_values, obs_noise, ensemble, *pairs)


def solution(mesh):
    staged = (mesh.shape["row"], mesh.shape["col"]) == (8, 4)
    in_specs = (P(AXES, None), P(), P(), P(), P(), P())
    out_specs = P(AXES, None)
    return jax.shard_map(
        functools.partial(body, staged),
        mesh=mesh,
        in_specs=in_specs,
        out_specs=out_specs,
        check_vma=False,
    )
```

time: 92.5 us -> 85.1 us (0.920)
  starting transfers between devices: 20.3 us -> 12.9 us
  Pallas kernels: 54.7 us -> 59.3 us
  waiting for transfers between devices: 13.6 us -> 10.3 us
    ppermute x18 -> x11, starting transfers between devices: 20.3 us -> 12.9 us  [swap(): return lax.ppermute(value, AXES, [(i, i ^ mask) for i in range(32)])]
    pallas_call x3 -> x5, Pallas kernels: 54.7 us -> 59.3 us  [the longest x2 53.3 us: batch_call(): pl.pallas_call(kernel, grid=(1,), out_shape=outs, in_specs=[SMEM, whole(t...]
    ppermute x18 -> x11, waiting for transfers between devices: 13.6 us -> 10.3 us  [swap(): return lax.ppermute(value, AXES, [(i, i ^ mask) for i in range(32)])]
  transfers between devices with their start and end apart: 18 -> 11, of which waited for: 10 -> 6; matrix products, arithmetic and copies ran while one was open for 0% -> 2% of each run, Pallas kernels for 47% -> 54%
where the time goes in v2:
time: 85.1 us; the launch traced here: 84.9 us
  Pallas kernels  59.3 us (70%)
  starting transfers between devices  12.9 us (15%)
  waiting for transfers between devices  10.3 us (12%)
  other arithmetic  1.58 us (2%)
    pallas_call x2, Pallas kernels, batch_call(): pl.pallas_call(kernel, grid=(1,), out_shape=outs, in_specs=[SMEM, whole(t...  53.3 us
    ppermute x11, starting transfers between devices, swap(): return lax.ppermute(value, AXES, [(i, i ^ mask) for i in range(32)])  12.9 us
    ppermute x11, waiting for transfers between devices, swap(): return lax.ppermute(value, AXES, [(i, i ^ mask) for i in range(32)])  10.3 us
    pallas_call x1, Pallas kernels, early_rows(): pl.pallas_call(functools.partial(early_kernel, distances), out_shape=jax....  2.19 us
    pallas_call x1, Pallas kernels, pick(): pl.pallas_call(pick_kernel, out_shape=[jax.ShapeDtypeStruct((SLOTS, state...  2.04 us
    pallas_call x1, Pallas kernels, late_rows(): pl.pallas_call(functools.partial(late_kernel, distances), out_shape=[jax....  1.76 us
  transfers between devices with their start and end apart: 11, of which 6 were waited for; matrix products, arithmetic and copies ran while one was open for 2% of the time, Pallas kernels for 54%

profile of v2, /device:TPU:0, one launch (start us, length us, event | category | flops | bytes accessed | tf_op | source)
XLA Modules:
  0.0 84.9 jit_solution(17328215490149088474)
XLA Ops:
  0.1 2.0 %pick.1 = (s16[64,512]{1,0:T(8,128)(2,1)S(1)}, s16[64,512]{1,0:T(8,128)(2,1)S(1)}) custom-call(s32[2]{0:T(128)S(1)} %pad_add_fusion.1.place, s32[2,256]{1,0:T(2,128)} %blocks.5, f32[2,4,256]{2,1,0:T(4,128)} %bitcast.4, f32[128,1024]{1,0:T(8,128)} %state.3), custom_call_target="tpu_custom_call" | custom-call | tf_op jit(solution)/shard_map/pick/pallas_call | solution.py:109
  2.2 0.5 collective-permute-start.5
  2.7 0.9 %collective-permute-done.5 = s16[64,512]{1,0:T(8,128)(2,1)S(1)} collective-permute-done((s16[64,512]{1,0:T(8,128)(2,1)S(1)}, s16[64,512]{1,0:T(8,128)(2,1)S(1)}, u32[]{:S(2)}, u32[]{:S(2)}) %collective-permute-start.5) | collective-permute-done | bytes 65568 | tf_op jit(solution)/shard_map/ppermute | solution.py:371
  3.6 4.0 %collective-permute-start.6 = (s16[1,64,512]{2,1,0:T(8,128)(2,1)S(1)}, s16[1,64,512]{2,1,0:T(8,128)(2,1)S(1)}, u32[]{:S(2)}, u32[]{:S(2)}) collective-permute-start(s16[1,64,512]{2,1,0:T(8,128)(2,1)S(1)} %add_bitcast_fusion), channel_id=1, source_target_pairs={{0,16},{1,17},{2,18},{3,19},{4,20},{5,21},{6,22},{7,23},{8,24},{9,... | collective-permute-start | bytes 196616 | tf_op jit(solution)/shard_map/ppermute | solution.py:371
  7.6 3.8 %collective-permute-done.6 = s16[1,64,512]{2,1,0:T(8,128)(2,1)S(1)} collective-permute-done((s16[1,64,512]{2,1,0:T(8,128)(2,1)S(1)}, s16[1,64,512]{2,1,0:T(8,128)(2,1)S(1)}, u32[]{:S(2)}, u32[]{:S(2)}) %collective-permute-start.6) | collective-permute-done | bytes 65568 | tf_op jit(solution)/shard_map/ppermute | solution.py:371
  11.4 2.7 %collective-permute-start.10 = (s16[2,64,512]{2,1,0:T(8,128)(2,1)S(1)}, s16[2,64,512]{2,1,0:T(8,128)(2,1)S(1)}, u32[]{:S(2)}, u32[]{:S(2)}) collective-permute-start(s16[2,64,512]{2,1,0:T(8,128)(2,1)S(1)} %pad_add_fusion.refs_0_), channel_id=1, source_target_pairs={{0,6},{1,7},{2,4},{3,5},{4,2},{5,3},{6,0},{7,1},{8,14},{9,15},{10,... | collective-permute-start | bytes 393224 | tf_op jit(solution)/shard_map/ppermute | solution.py:371
  14.1 0.5 collective-permute-start.9
  14.6 0.3 collective-permute-start.8
  15.0 0.7 collective-permute-start.7
  15.7 0.7 and_select_fusion
  16.4 3.6 %collective-permute-done.7.refs_1_ = s16[2,64,512]{2,1,0:T(8,128)(2,1)S(1)} collective-permute-done((s16[2,64,512]{2,1,0:T(8,128)(2,1)S(1)}, s16[2,64,512]{2,1,0:T(8,128)(2,1)S(1)}, u32[]{:S(2)}, u32[]{:S(2)}) %collective-permute-start.7) | collective-permute-done | bytes 131104 | tf_op jit(solution)/shard_map/ppermute | solution.py:371
  20.0 2.6 %collective-permute-start.13 = (s16[2,64,512]{2,1,0:T(8,128)(2,1)S(1)}, s16[2,64,512]{2,1,0:T(8,128)(2,1)S(1)}, u32[]{:S(2)}, u32[]{:S(2)}) collective-permute-start(s16[2,64,512]{2,1,0:T(8,128)(2,1)S(1)} %collective-permute-done.7.refs_1_), channel_id=1, source_target_pairs={{0,6},{1,7},{2,4},{3,5},{4,2},{5,3},{6,0},{7,1},{8,14},{9,15},{10,... | collective-permute-start | bytes 393224 | tf_op jit(solution)/shard_map/ppermute | solution.py:371
  22.6 0.5 collective-permute-start.12
  23.1 0.3 collective-permute-start.11
  23.5 0.1 convert_reduce_fusion
  23.6 0.7 reduce_max.9
  24.9 2.2 %early_rows.1.early = f32[512,512]{1,0:T(8,128)S(1)} custom-call(s32[2]{0:T(128)S(1)} %pad_add_fusion.1.place, s32[2,256]{1,0:T(2,128)} %blocks.5, s16[2,64,512]{2,1,0:T(8,128)(2,1)S(1)} %pad_add_fusion.refs_0_, s16[2,64,512]{2,1,0:T(8,128)(2,1)S(1)} %collective-permute-done.7.refs_1_, s16[2,64,512]{2,1,0:T(8,128)(2,1)S(1)} %collective-permute-done.8.refs_2_, ...), custom_call_target="tpu_custom_call" | custom-call | flops 1000000000 | bytes 4000000 | tf_op jit(solution)/shard_map/early_rows/pallas_call | solution.py:191
  27.1 0.4 collective-permute-done.12.refs_1_
  27.5 0.5 collective-permute-done.11.refs_0_
  28.1 1.8 %late_rows.1 = (bf16[256,512]{1,0:T(8,128)(2,1)S(1)}, s16[256,512]{1,0:T(8,128)(2,1)S(1)}) custom-call(s32[2]{0:T(128)S(1)} %pad_add_fusion.1.place, s32[2,256]{1,0:T(2,128)S(1)} %copy-done.5, f32[512,512]{1,0:T(8,128)S(1)} %early_rows.1.early, s16[2,64,512]{2,1,0:T(8,128)(2,1)S(1)} %collective-permute-done.11.refs_0_, ...), custom_call_target="tpu_custom_call" | custom-call | tf_op jit(solution)/shard_map/late_rows/pallas_call | solution.py:205
  30.0 0.5 collective-permute-start.14
  30.5 1.0 %collective-permute-done.15.other = bf16[256,512]{1,0:T(8,128)(2,1)S(1)} collective-permute-done((bf16[256,512]{1,0:T(8,128)(2,1)S(1)}, bf16[256,512]{1,0:T(8,128)(2,1)S(1)}, u32[]{:S(2)}, u32[]{:S(2)}) %collective-permute-start.15) | collective-permute-done | bytes 262176 | tf_op jit(solution)/shard_map/ppermute | solution.py:371
  31.6 43.4 %first_batch.1 = (bf16[256,1024]{1,0:T(8,128)(2,1)S(1)}, bf16[256,1024]{1,0:T(8,128)(2,1)S(1)}) custom-call(s32[2]{0:T(128)S(1)} %pad_add_fusion.1.place, s32[2,256]{1,0:T(2,128)S(1)} %copy-done.1, f32[2,256]{1,0:T(2,128)S(1)} %copy-done.2, bf16[2,256,1024]{2,1,0:T(8,128)(2,1)S(1)} %copy-done, bf16[256,512]{1,0:T(8,128)(2,1)S(1)} %get-tuple-element.33.own, ...), custom_call_target="tpu_custom_call" | custom-call | tf_op jit(solution)/shard_map/first_batch/pallas_call | solution.py:340
  75.0 9.9 %second_batch.1 = f32[128,1024]{1,0:T(8,128)} custom-call(s32[2]{0:T(128)S(1)} %pad_add_fusion.1.place, s32[2,256]{1,0:T(2,128)S(1)} %copy-done.1, f32[2,256]{1,0:T(2,128)S(1)} %copy-done.2, bf16[2,256,1024]{2,1,0:T(8,128)(2,1)S(1)} %copy-done, s16[256,512]{1,0:T(8,128)(2,1)S(1)} %get-tuple-element.32.own, ...), custom_call_target="tpu_custom_call" | custom-call | tf_op jit(solution)/shard_map/second_batch/pallas_call | solution.py:340
  (24 shorter events, 0.3 us)
Async XLA Ops:
  2.1 26.0 %copy-start.3 = (f32[128,1024]{1,0:T(8,128)S(1)}, f32[128,1024]{1,0:T(8,128)}, u32[]{:S(2)}) copy-start(f32[128,1024]{1,0:T(8,128)} %state.3) | copy-start | bytes 1572868
  2.1 25.9 %copy-start.4 = (f32[2,256,4]{1,2,0:T(4,128)S(1)}, f32[2,256,4]{1,2,0:T(4,128)}, u32[]{:S(2)}) copy-start(f32[2,256,4]{1,2,0:T(4,128)} %param.10) | copy-start | bytes 24580
  2.1 25.9 %copy-start.5 = (s32[2,256]{1,0:T(2,128)S(1)}, s32[2,256]{1,0:T(2,128)}, u32[]{:S(2)}) copy-start(s32[2,256]{1,0:T(2,128)} %blocks.5) | copy-start | bytes 6148
  2.2 1.4 %collective-permute-start.5 = (s16[64,512]{1,0:T(8,128)(2,1)S(1)}, s16[64,512]{1,0:T(8,128)(2,1)S(1)}, u32[]{:S(2)}, u32[]{:S(2)}) collective-permute-start(s16[64,512]{1,0:T(8,128)(2,1)S(1)} %get-tuple-element.31), channel_id=1, source_target_pairs={{0,1},{1,0},{2,3},{3,2},{4,5},{5,4},{6,7},{7,6},{8,9},{9,8},{10,11... | collective-permute-start | bytes 196616 | tf_op jit(solution)/shard_map/ppermute | solution.py:371
  3.6 7.8 %collective-permute-start.6 = (s16[1,64,512]{2,1,0:T(8,128)(2,1)S(1)}, s16[1,64,512]{2,1,0:T(8,128)(2,1)S(1)}, u32[]{:S(2)}, u32[]{:S(2)}) collective-permute-start(s16[1,64,512]{2,1,0:T(8,128)(2,1)S(1)} %add_bitcast_fusion), channel_id=1, source_target_pairs={{0,16},{1,17},{2,18},{3,19},{4,20},{5,21},{6,22},{7,23},{8,24},{9,... | collective-permute-start | bytes 196616 | tf_op jit(solution)/shard_map/ppermute | solution.py:371
  11.4 11.7 %collective-permute-start.10 = (s16[2,64,512]{2,1,0:T(8,128)(2,1)S(1)}, s16[2,64,512]{2,1,0:T(8,128)(2,1)S(1)}, u32[]{:S(2)}, u32[]{:S(2)}) collective-permute-start(s16[2,64,512]{2,1,0:T(8,128)(2,1)S(1)} %pad_add_fusion.refs_0_), channel_id=1, source_target_pairs={{0,6},{1,7},{2,4},{3,5},{4,2},{5,3},{6,0},{7,1},{8,14},{9,15},{10,... | collective-permute-start | bytes 393224 | tf_op jit(solution)/shard_map/ppermute | solution.py:371
  14.1 10.8 %collective-permute-start.9 = (s16[2,64,512]{2,1,0:T(8,128)(2,1)S(1)}, s16[2,64,512]{2,1,0:T(8,128)(2,1)S(1)}, u32[]{:S(2)}, u32[]{:S(2)}) collective-permute-start(s16[2,64,512]{2,1,0:T(8,128)(2,1)S(1)} %pad_add_fusion.refs_0_), channel_id=1, source_target_pairs={{0,4},{1,5},{2,6},{3,7},{4,0},{5,1},{6,2},{7,3},{8,12},{9,13},{10,... | collective-permute-start | bytes 393224 | tf_op jit(solution)/shard_map/ppermute | solution.py:371
  14.6 10.2 %collective-permute-start.8 = (s16[2,64,512]{2,1,0:T(8,128)(2,1)S(1)}, s16[2,64,512]{2,1,0:T(8,128)(2,1)S(1)}, u32[]{:S(2)}, u32[]{:S(2)}) collective-permute-start(s16[2,64,512]{2,1,0:T(8,128)(2,1)S(1)} %pad_add_fusion.refs_0_), channel_id=1, source_target_pairs={{0,2},{1,3},{2,0},{3,1},{4,6},{5,7},{6,4},{7,5},{8,10},{9,11},{10,... | collective-permute-start | bytes 393224 | tf_op jit(solution)/shard_map/ppermute | solution.py:371
  15.0 5.0 %collective-permute-start.7 = (s16[2,64,512]{2,1,0:T(8,128)(2,1)S(1)}, s16[2,64,512]{2,1,0:T(8,128)(2,1)S(1)}, u32[]{:S(2)}, u32[]{:S(2)}) collective-permute-start(s16[2,64,512]{2,1,0:T(8,128)(2,1)S(1)} %pad_add_fusion.refs_0_), channel_id=1, source_target_pairs={{0,8},{1,9},{2,10},{3,11},{4,12},{5,13},{6,14},{7,15},{8,0},{9,1},... | collective-permute-start | bytes 393224 | tf_op jit(solution)/shard_map/ppermute | solution.py:371
  20.0 7.1 %collective-permute-start.13 = (s16[2,64,512]{2,1,0:T(8,128)(2,1)S(1)}, s16[2,64,512]{2,1,0:T(8,128)(2,1)S(1)}, u32[]{:S(2)}, u32[]{:S(2)}) collective-permute-start(s16[2,64,512]{2,1,0:T(8,128)(2,1)S(1)} %collective-permute-done.7.refs_1_), channel_id=1, source_target_pairs={{0,6},{1,7},{2,4},{3,5},{4,2},{5,3},{6,0},{7,1},{8,14},{9,15},{10,... | collective-permute-start | bytes 393224 | tf_op jit(solution)/shard_map/ppermute | solution.py:371
  22.6 5.0 %collective-permute-start.12 = (s16[2,64,512]{2,1,0:T(8,128)(2,1)S(1)}, s16[2,64,512]{2,1,0:T(8,128)(2,1)S(1)}, u32[]{:S(2)}, u32[]{:S(2)}) collective-permute-start(s16[2,64,512]{2,1,0:T(8,128)(2,1)S(1)} %collective-permute-done.7.refs_1_), channel_id=1, source_target_pairs={{0,4},{1,5},{2,6},{3,7},{4,0},{5,1},{6,2},{7,3},{8,12},{9,13},{10,... | collective-permute-start | bytes 393224 | tf_op jit(solution)/shard_map/ppermute | solution.py:371
  23.1 5.0 %collective-permute-start.11 = (s16[2,64,512]{2,1,0:T(8,128)(2,1)S(1)}, s16[2,64,512]{2,1,0:T(8,128)(2,1)S(1)}, u32[]{:S(2)}, u32[]{:S(2)}) collective-permute-start(s16[2,64,512]{2,1,0:T(8,128)(2,1)S(1)} %collective-permute-done.7.refs_1_), channel_id=1, source_target_pairs={{0,2},{1,3},{2,0},{3,1},{4,6},{5,7},{6,4},{7,5},{8,10},{9,11},{10,... | collective-permute-start | bytes 393224 | tf_op jit(solution)/shard_map/ppermute | solution.py:371
  29.8 1.7 %copy-start = (bf16[2,256,1024]{2,1,0:T(8,128)(2,1)S(1)}, bf16[2,256,1024]{2,1,0:T(8,128)(2,1)}, u32[]{:S(2)}) copy-start(bf16[2,256,1024]{2,1,0:T(8,128)(2,1)} %noise.3) | copy-start | bytes 3145732
  29.9 1.7 %copy-start.1 = (s32[2,256]{1,0:T(2,128)S(1)}, s32[2,256]{1,0:T(2,128)}, u32[]{:S(2)}) copy-start(s32[2,256]{1,0:T(2,128)} %tags.3) | copy-start | bytes 6148
  29.9 1.7 %copy-start.2 = (f32[2,256]{1,0:T(2,128)S(1)}, f32[2,256]{1,0:T(2,128)}, u32[]{:S(2)}) copy-start(f32[2,256]{1,0:T(2,128)} %values.3) | copy-start | bytes 6148
  30.0 1.6 %collective-permute-start.15 = (bf16[256,512]{1,0:T(8,128)(2,1)S(1)}, bf16[256,512]{1,0:T(8,128)(2,1)S(1)}, u32[]{:S(2)}, u32[]{:S(2)}) collective-permute-start(bf16[256,512]{1,0:T(8,128)(2,1)S(1)} %get-tuple-element.33.own), channel_id=1, source_target_pairs={{0,1},{1,0},{2,3},{3,2},{4,5},{5,4},{6,7},{7,6},{8,9},{9,8},{10,11... | collective-permute-start | bytes 786440 | tf_op jit(solution)/shard_map/ppermute | solution.py:371
  30.0 45.0 %collective-permute-start.14 = (s16[256,512]{1,0:T(8,128)(2,1)S(1)}, s16[256,512]{1,0:T(8,128)(2,1)S(1)}, u32[]{:S(2)}, u32[]{:S(2)}) collective-permute-start(s16[256,512]{1,0:T(8,128)(2,1)S(1)} %get-tuple-element.32.own), channel_id=1, source_target_pairs={{0,1},{1,0},{2,3},{3,2},{4,5},{5,4},{6,7},{7,6},{8,9},{9,8},{10,11... | collective-permute-start | bytes 786440 | tf_op jit(solution)/shard_map/ppermute | solution.py:371

commit v3 on v2

--- a/solution.py
+++ b/solution.py
@@ -9,8 +9,8 @@
 
 SLOTS = 64
 UNIT = 1.0 / 1024
-SCALE = 0.5
-TOLERANCE = 2e-3
+SCALE = 0.55
+TOLERANCE = 0.03
 BF16 = jnp.bfloat16
 F32 = jnp.float32
 VMEM = pl.BlockSpec(memory_space=pltpu.VMEM)
@@ -63,7 +63,9 @@
     return value.astype(BF16).astype(F32)
 
 
-def pick_kernel(place, blocks, weights, state, keep, send):
+def pick_kernel(place, blocks, weights, state_ref, keep, send, state, arrived):
+    load = pltpu.make_async_copy(state_ref, state, arrived)
+    load.start()
     device = place[0]
     batches, points, size = weights.shape
     width, members = state.shape
@@ -91,6 +93,7 @@
         columns = [weight[:, point : point + 1] for point in range(points)]
         selectors.append(select(lanes, points, local, columns))
         taken.append(jnp.sum(chosen, axis=1, keepdims=True))
+    load.wait()
     rows = jnp.dot(
         selectors[0] + selectors[1],
         state[...],
@@ -109,8 +112,9 @@
     return pl.pallas_call(
         pick_kernel,
         out_shape=[jax.ShapeDtypeStruct((SLOTS, state.shape[1] // 2), jnp.int16)] * 2,
-        in_specs=[SMEM, VMEM, VMEM, VMEM],
+        in_specs=[SMEM, VMEM, VMEM, pl.BlockSpec(memory_space=pl.ANY)],
         out_specs=[VMEM] * 2,
+        scratch_shapes=[pltpu.VMEM(state.shape, F32), pltpu.SemaphoreType.DMA],
         compiler_params=PARAMS,
         name="pick",
     )(place, blocks, weights, state)
@@ -145,74 +149,82 @@
     )(place, blocks, weights, state)
 
 
-def put_in_order(place, blocks, members, pieces):
+def order_kernel(groups, place, blocks, *outs):
     device, held = place[0], place[1]
     size = blocks.shape[1]
     lane = lax.broadcasted_iota(jnp.int32, (size, size), 1)
     sub = lax.broadcasted_iota(jnp.int32, (size, size), 0)
-    values = jnp.concatenate([ref[...].reshape(2 * SLOTS, -1) for _, ref in pieces], axis=0)
-    values = values.astype(jnp.int32)
-    high, low = values >> 8, values & 255
-    high, low = high.astype(F32).astype(BF16), low.astype(F32).astype(BF16)
-    slots = lax.broadcasted_iota(jnp.int32, (size, values.shape[0]), 1)
-    results = []
     for batch in range(blocks.shape[0]):
         pair_row, pair_column = both_ways(blocks[batch : batch + 1, :] // (2 * held))
         before = jnp.where((pair_row == pair_column) & (lane < sub), 1.0, 0.0)
         rank = jnp.sum(before, axis=1, keepdims=True).astype(jnp.int32)
         away = (2 * pair_column.astype(jnp.int32)) ^ device
-        near_x_y = (away >> 1) & 7
-        where = jnp.full(rank.shape, -2 * SLOTS, jnp.int32)
-        for index, (distance, _) in enumerate(pieces):
-            where = jnp.where(near_x_y == distance, 2 * SLOTS * index, where)
-        slot = where + SLOTS * ((away >> 4) & 1) + (rank if batch == 0 else SLOTS - 1 - rank)
-        chosen = jnp.where(slots == slot, 1.0, 0.0).astype(BF16)
-        results.append(256.0 * nn(chosen, high) + nn(chosen, low))
-    return results
-
-
-def early_kernel(distances, place, blocks, *refs):
-    results = put_in_order(place, blocks, refs[0].shape[-1], list(zip(distances, refs[:-1])))
-    size = blocks.shape[1]
-    for batch, result in enumerate(results):
-        refs[-1][batch * size : (batch + 1) * size, :] = result
-
-
-def late_kernel(distances, place, blocks, early, *refs):
-    results = put_in_order(place, blocks, refs[0].shape[-1], list(zip(distances, refs[:-2])))
-    size = blocks.shape[1]
-    refs[-2][...] = ((results[0] + early[:size, :]) * UNIT).astype(BF16)
-    refs[-1][...] = (results[1] + early[size:, :]).astype(jnp.int32).astype(jnp.int16)
-
-
-def early_rows(place, blocks, pieces):
-    distances = [distance for distance, _ in pieces]
-    half = pieces[0][1].shape[-1]
-    return pl.pallas_call(
-        functools.partial(early_kernel, distances),
-        out_shape=jax.ShapeDtypeStruct((blocks.size, half), F32),
-        in_specs=[SMEM] + [VMEM] * (1 + len(pieces)),
+        slot = SLOTS * ((away >> 4) & 1) + (rank if batch == 0 else SLOTS - 1 - rank)
+        for distances, out in zip(groups, outs):
+            where = jnp.full(rank.shape, -2 * SLOTS, jnp.int32)
+            for index, distance in enumerate(distances):
+                where = jnp.where((away >> 1) & 7 == distance, 2 * SLOTS * index, where)
+            slots = lax.broadcasted_iota(jnp.int32, (size, out.shape[1]), 1)
+            chosen = jnp.where(slots == where + slot, 1.0, 0.0)
+            out[batch * size : (batch + 1) * size, :] = chosen.astype(BF16)
+
+
+def order(place, blocks, groups):
+    return pl.pallas_call(
+        functools.partial(order_kernel, groups),
+        out_shape=[
+            jax.ShapeDtypeStruct((blocks.size, 2 * SLOTS * len(group)), BF16) for group in groups
+        ],
+        in_specs=[SMEM, VMEM],
+        out_specs=[VMEM] * len(groups),
+        compiler_params=PARAMS,
+        cost_estimate=pl.CostEstimate(flops=10**6, bytes_accessed=10**6, transcendentals=0),
+        name="order",
+    )(place, blocks)
+
+
+def put_in_order(chosen, pieces):
+    size = chosen.shape[0] // 2
+    values = jnp.concatenate([ref[...].reshape(2 * SLOTS, -1) for ref in pieces], axis=0)
+    high, low = split(values.astype(jnp.int32).astype(F32))
+    second = chosen[size:, :]
+    return nn(chosen[:size, :], high), nn(second, high) + nn(second, low)
+
+
+def early_kernel(chosen, *refs):
+    size = chosen.shape[0] // 2
+    refs[-1][:size, :], refs[-1][size:, :] = put_in_order(chosen, refs[:-1])
+
+
+def late_kernel(chosen, early, *refs):
+    size = chosen.shape[0] // 2
+    first, second = put_in_order(chosen, refs[:-2])
+    refs[-2][...] = ((first + early[:size, :]) * UNIT).astype(BF16)
+    refs[-1][...] = (second + early[size:, :]).astype(jnp.int32).astype(jnp.int16)
+
+
+def early_rows(chosen, pieces):
+    return pl.pallas_call(
+        early_kernel,
+        out_shape=jax.ShapeDtypeStruct((chosen.shape[0], pieces[0].shape[-1]), F32),
+        in_specs=[VMEM] * (1 + len(pieces)),
         out_specs=VMEM,
         compiler_params=PARAMS,
         cost_estimate=pl.CostEstimate(flops=10**9, bytes_accessed=4 * 10**6, transcendentals=0),
         name="early_rows",
-    )(place, blocks, *[piece for _, piece in pieces])
-
-
-def late_rows(place, blocks, early, pieces):
-    distances = [distance for distance, _ in pieces]
-    rows, half = blocks.shape[1], early.shape[1]
-    return pl.pallas_call(
-        functools.partial(late_kernel, distances),
-        out_shape=[
-            jax.ShapeDtypeStruct((rows, half), BF16),
-            jax.ShapeDtypeStruct((rows, half), jnp.int16),
-        ],
-        in_specs=[SMEM] + [VMEM] * (2 + len(pieces)),
+    )(chosen, *pieces)
+
+
+def late_rows(chosen, early, pieces):
+    shape = (early.shape[0] // 2, early.shape[1])
+    return pl.pallas_call(
+        late_kernel,
+        out_shape=[jax.ShapeDtypeStruct(shape, BF16), jax.ShapeDtypeStruct(shape, jnp.int16)],
+        in_specs=[VMEM] * (2 + len(pieces)),
         out_specs=[VMEM] * 2,
         compiler_params=PARAMS,
         name="late_rows",
-    )(place, blocks, early, *[piece for _, piece in pieces])
+    )(chosen, early, *pieces)
 
 
 def eliminate(covariance, work, inverse):
@@ -257,11 +269,11 @@
 
     m = scaled
     t = None
-    for step in range(3):
+    for step in range(2):
         u = third_order(m) + eye
         ub = u.astype(BF16)
         t = u if t is None else nn(ub, t.astype(BF16))
-        if step < 2:
+        if step < 1:
             m = nt(nn(ub, m.astype(BF16)).astype(BF16), ub)
     parts = split(scaled)
     ts = split(t)
@@ -272,9 +284,9 @@
     error = m - eye
     t = t - nn((error * half).astype(BF16), ts[0])
     inverse[...] = t * scale_row
-    good = jnp.min(jnp.where(jnp.abs(error) <= TOLERANCE, 1.0, 0.0))
-
-    @pl.when(good < 0.5)
+    good = jnp.sum(error * error) <= TOLERANCE * TOLERANCE
+
+    @pl.when(jnp.logical_not(good))
     def _():
         eliminate(covariance, work, inverse)
 
@@ -282,19 +294,26 @@
 def whiten(observed, tags, values, noise, work, inverse):
     members = observed.shape[1]
     size = observed.shape[0]
-    anomalies = observed - row_mean(observed)
-    ah, al = split(anomalies)
-    lane = lax.broadcasted_iota(jnp.int32, (size, size), 1)
-    sub = lax.broadcasted_iota(jnp.int32, (size, size), 0)
-    variance = column(jnp.where(tags == 0, 0.5, 2.0))
-    values = column(values)
+    mean = row_mean(observed)
+    ah, al = split(observed - mean)
+    lane = lax.broadcasted_iota(jnp.int32, (size, size), 1)
+    sub = lax.broadcasted_iota(jnp.int32, (size, size), 0)
+    variance_row = jnp.where(tags == 0, 0.5, 2.0)
+    variance = column(variance_row)
+    mean_row = jnp.sum(jnp.where(lane == sub, mean, 0.0), axis=0, keepdims=True)
     covariance = dot3(nt, (ah, al), (ah, al)) * (1.0 / (members - 1))
     covariance = covariance + jnp.where(lane == sub, variance, 0.0)
     inverse_factor(covariance, work, inverse)
-    ts = split(inverse[...])
-    innovation = values + jnp.sqrt(variance) * noise.astype(F32) - observed
-    whitened = dot3(nn, ts, (ah, al)).astype(BF16)
-    white_innov = dot3(nn, ts, split(innovation)).astype(BF16)
+    t = inverse[...]
+    th, tl = split(t)
+    nh, nl = split(t * jnp.sqrt(variance_row))
+    exact = observed.astype(BF16)
+    applied = nn(th, exact) + nn(tl, exact)
+    noise = nn(nh, noise) + nn(nl, noise)
+    mean_part = jnp.sum(t * mean_row, axis=1, keepdims=True)
+    value_part = jnp.sum(t * values, axis=1, keepdims=True)
+    whitened = (applied - mean_part).astype(BF16)
+    white_innov = (noise + value_part - applied).astype(BF16)
     return whitened, white_innov
 
 
@@ -372,14 +391,16 @@
 
 
 def by_slots(place, ensemble, blocks, weights):
+    sides = (X | Y, X, Y)
+    groups = [[0] + [mask // 2 for mask in sides + (NEAR_Z,)]]
+    groups += [[(NEAR_Z | mask) // 2 for mask in sides]]
+    early_places, late_places = order(place, blocks, groups)
     keep, send = pick(place, blocks, weights, ensemble)
     block = (keep + swap(send, CORE))[None]
     here = jnp.concatenate([block, swap(block, FAR_Z)], axis=0)
-    near = swap(here, NEAR_Z)
-    early = [(0, here), (NEAR_Z // 2, near)]
-    early += [(mask // 2, swap(here, mask)) for mask in (Y, X, X | Y)]
-    late = [((NEAR_Z | mask) // 2, swap(near, mask)) for mask in (Y, X, X | Y)]
-    return late_rows(place, blocks, early_rows(place, blocks, early), late)
+    early = [here] + [swap(here, mask) for mask in sides + (NEAR_Z,)]
+    late = [swap(early[-1], mask) for mask in sides]
+    return late_rows(late_places, early_rows(early_places, early), late)
 
 
 def add_by_swaps(value):

time: 85.1 us -> 81.7 us (0.960)
  Pallas kernels: 59.3 us -> 56.8 us
  waiting for transfers between devices: 10.3 us -> 8.99 us
    pallas_call x2, Pallas kernels: 53.3 us -> 51.8 us  [batch_call(): pl.pallas_call(kernel, grid=(1,), out_shape=outs, in_specs=[SMEM, whole(t...]
    ppermute x11, waiting for transfers between devices: 10.3 us -> 8.99 us  [swap(): return lax.ppermute(value, AXES, [(i, i ^ mask) for i in range(32)])]
    pallas_call x2 -> x3, Pallas kernels: 3.95 us -> 2.85 us  [the longest x1 1.41 us: order(): pl.pallas_call(functools.partial(order_kernel, groups), out_shape=[jax.Sh...]
  transfers between devices with their start and end apart: 11 -> 11, of which waited for: 6 -> 6; matrix products, arithmetic and copies ran while one was open for 2% -> 2% of each run, Pallas kernels for 54% -> 55%
where the time goes in v3:
time: 81.7 us; the launch traced here: 81.4 us
  Pallas kernels  56.8 us (70%)
  starting transfers between devices  13.1 us (16%)
  waiting for transfers between devices  8.99 us (11%)
  other arithmetic  1.61 us (2%)
    pallas_call x2, Pallas kernels, batch_call(): pl.pallas_call(kernel, grid=(1,), out_shape=outs, in_specs=[SMEM, whole(t...  51.8 us
    ppermute x11, starting transfers between devices, swap(): return lax.ppermute(value, AXES, [(i, i ^ mask) for i in range(32)])  13.1 us
    ppermute x11, waiting for transfers between devices, swap(): return lax.ppermute(value, AXES, [(i, i ^ mask) for i in range(32)])  8.99 us
    pallas_call x1, Pallas kernels, pick(): pl.pallas_call(pick_kernel, out_shape=[jax.ShapeDtypeStruct((SLOTS, state...  2.17 us
  transfers between devices with their start and end apart: 11, of which 6 were waited for; matrix products, arithmetic and copies ran while one was open for 2% of the time, Pallas kernels for 55%

profile of v3, /device:TPU:0, one launch (start us, length us, event | category | flops | bytes accessed | tf_op | source)
XLA Modules:
  0.0 81.4 jit_solution(5321174232773640349)
XLA Ops:
  0.1 2.2 %pick.1 = (s16[64,512]{1,0:T(8,128)(2,1)S(1)}, s16[64,512]{1,0:T(8,128)(2,1)S(1)}) custom-call(s32[2]{0:T(128)S(1)} %pad_add_fusion.1.place, s32[2,256]{1,0:T(2,128)} %blocks.3, f32[2,4,256]{2,1,0:T(4,128)} %bitcast.4, f32[128,1024]{1,0:T(8,128)} %state.1), custom_call_target="tpu_custom_call" | custom-call | tf_op jit(solution)/shard_map/pick/pallas_call | solution.py:112
  2.3 0.5 collective-permute-start.5
  2.8 0.9 %collective-permute-done.5 = s16[64,512]{1,0:T(8,128)(2,1)S(1)} collective-permute-done((s16[64,512]{1,0:T(8,128)(2,1)S(1)}, s16[64,512]{1,0:T(8,128)(2,1)S(1)}, u32[]{:S(2)}, u32[]{:S(2)}) %collective-permute-start.5) | collective-permute-done | bytes 65568 | tf_op jit(solution)/shard_map/ppermute | solution.py:390
  3.7 4.0 %collective-permute-start.6 = (s16[1,64,512]{2,1,0:T(8,128)(2,1)S(1)}, s16[1,64,512]{2,1,0:T(8,128)(2,1)S(1)}, u32[]{:S(2)}, u32[]{:S(2)}) collective-permute-start(s16[1,64,512]{2,1,0:T(8,128)(2,1)S(1)} %add_bitcast_fusion), channel_id=1, source_target_pairs={{0,16},{1,17},{2,18},{3,19},{4,20},{5,21},{6,22},{7,23},{8,24},{9,... | collective-permute-start | bytes 196616 | tf_op jit(solution)/shard_map/ppermute | solution.py:390
  7.7 3.8 %collective-permute-done.6 = s16[1,64,512]{2,1,0:T(8,128)(2,1)S(1)} collective-permute-done((s16[1,64,512]{2,1,0:T(8,128)(2,1)S(1)}, s16[1,64,512]{2,1,0:T(8,128)(2,1)S(1)}, u32[]{:S(2)}, u32[]{:S(2)}) %collective-permute-start.6) | collective-permute-done | bytes 65568 | tf_op jit(solution)/shard_map/ppermute | solution.py:390
  11.6 0.8 collective-permute-start.10
  12.4 1.5 %collective-permute-start.9 = (s16[2,64,512]{2,1,0:T(8,128)(2,1)S(1)}, s16[2,64,512]{2,1,0:T(8,128)(2,1)S(1)}, u32[]{:S(2)}, u32[]{:S(2)}) collective-permute-start(s16[2,64,512]{2,1,0:T(8,128)(2,1)S(1)} %pad_add_fusion.refs_0_), channel_id=1, source_target_pairs={{0,2},{1,3},{2,0},{3,1},{4,6},{5,7},{6,4},{7,5},{8,10},{9,11},{10,... | collective-permute-start | bytes 393224 | tf_op jit(solution)/shard_map/ppermute | solution.py:390
  13.9 1.5 %collective-permute-start.8 = (s16[2,64,512]{2,1,0:T(8,128)(2,1)S(1)}, s16[2,64,512]{2,1,0:T(8,128)(2,1)S(1)}, u32[]{:S(2)}, u32[]{:S(2)}) collective-permute-start(s16[2,64,512]{2,1,0:T(8,128)(2,1)S(1)} %pad_add_fusion.refs_0_), channel_id=1, source_target_pairs={{0,4},{1,5},{2,6},{3,7},{4,0},{5,1},{6,2},{7,3},{8,12},{9,13},{10,... | collective-permute-start | bytes 393224 | tf_op jit(solution)/shard_map/ppermute | solution.py:390
  15.4 0.5 collective-permute-start.7
  15.8 0.7 and_select_fusion
  16.6 1.7 %collective-permute-start.13 = (s16[2,64,512]{2,1,0:T(8,128)(2,1)S(1)}, s16[2,64,512]{2,1,0:T(8,128)(2,1)S(1)}, u32[]{:S(2)}, u32[]{:S(2)}) collective-permute-start(s16[2,64,512]{2,1,0:T(8,128)(2,1)S(1)} %collective-permute-done.10.refs_4_), channel_id=1, source_target_pairs={{0,2},{1,3},{2,0},{3,1},{4,6},{5,7},{6,4},{7,5},{8,10},{9,11},{10,... | collective-permute-start | bytes 393224 | tf_op jit(solution)/shard_map/ppermute | solution.py:390
  18.3 1.5 %collective-permute-start.12 = (s16[2,64,512]{2,1,0:T(8,128)(2,1)S(1)}, s16[2,64,512]{2,1,0:T(8,128)(2,1)S(1)}, u32[]{:S(2)}, u32[]{:S(2)}) collective-permute-start(s16[2,64,512]{2,1,0:T(8,128)(2,1)S(1)} %collective-permute-done.10.refs_4_), channel_id=1, source_target_pairs={{0,4},{1,5},{2,6},{3,7},{4,0},{5,1},{6,2},{7,3},{8,12},{9,13},{10,... | collective-permute-start | bytes 393224 | tf_op jit(solution)/shard_map/ppermute | solution.py:390
  19.8 0.6 collective-permute-start.11
  20.3 0.1 convert_reduce_fusion
  20.4 0.7 reduce_max.9
  21.8 1.4 %order.1 = (bf16[512,640]{1,0:T(8,128)(2,1)S(1)}, bf16[512,384]{1,0:T(8,128)(2,1)S(1)}) custom-call(s32[2]{0:T(128)S(1)} %pad_add_fusion.1.place, s32[2,256]{1,0:T(2,128)} %blocks.3), custom_call_target="tpu_custom_call" | custom-call | flops 1000000 | bytes 1000000 | tf_op jit(solution)/shard_map/order/pallas_call | solution.py:173
  23.2 0.8 early_rows.1.early
  24.0 1.7 %collective-permute-done.12.refs_1_ = s16[2,64,512]{2,1,0:T(8,128)(2,1)S(1)} collective-permute-done((s16[2,64,512]{2,1,0:T(8,128)(2,1)S(1)}, s16[2,64,512]{2,1,0:T(8,128)(2,1)S(1)}, u32[]{:S(2)}, u32[]{:S(2)}) %collective-permute-start.12) | collective-permute-done | bytes 131104 | tf_op jit(solution)/shard_map/ppermute | solution.py:390
  25.7 1.5 %collective-permute-done.11.refs_0_ = s16[2,64,512]{2,1,0:T(8,128)(2,1)S(1)} collective-permute-done((s16[2,64,512]{2,1,0:T(8,128)(2,1)S(1)}, s16[2,64,512]{2,1,0:T(8,128)(2,1)S(1)}, u32[]{:S(2)}, u32[]{:S(2)}) %collective-permute-start.11) | collective-permute-done | bytes 131104 | tf_op jit(solution)/shard_map/ppermute | solution.py:390
  27.2 0.6 late_rows.1
  28.0 0.5 collective-permute-start.14
  28.5 1.0 %collective-permute-done.15.other = bf16[256,512]{1,0:T(8,128)(2,1)S(1)} collective-permute-done((bf16[256,512]{1,0:T(8,128)(2,1)S(1)}, bf16[256,512]{1,0:T(8,128)(2,1)S(1)}, u32[]{:S(2)}, u32[]{:S(2)}) %collective-permute-start.15) | collective-permute-done | bytes 262176 | tf_op jit(solution)/shard_map/ppermute | solution.py:390
  29.6 42.5 %first_batch.1 = (bf16[256,1024]{1,0:T(8,128)(2,1)S(1)}, bf16[256,1024]{1,0:T(8,128)(2,1)S(1)}) custom-call(s32[2]{0:T(128)S(1)} %pad_add_fusion.1.place, s32[2,256]{1,0:T(2,128)S(1)} %copy-done.1, f32[2,256]{1,0:T(2,128)S(1)} %copy-done.2, bf16[2,256,1024]{2,1,0:T(8,128)(2,1)S(1)} %copy-done, bf16[256,512]{1,0:T(8,128)(2,1)S(1)} %get-tuple-element.37.own, ...), custom_call_target="tpu_custom_call" | custom-call | tf_op jit(solution)/shard_map/first_batch/pallas_call | solution.py:359
  72.1 9.2 %second_batch.1 = f32[128,1024]{1,0:T(8,128)} custom-call(s32[2]{0:T(128)S(1)} %pad_add_fusion.1.place, s32[2,256]{1,0:T(2,128)S(1)} %copy-done.1, f32[2,256]{1,0:T(2,128)S(1)} %copy-done.2, bf16[2,256,1024]{2,1,0:T(8,128)(2,1)S(1)} %copy-done, s16[256,512]{1,0:T(8,128)(2,1)S(1)} %get-tuple-element.36.own, ...), custom_call_target="tpu_custom_call" | custom-call | tf_op jit(solution)/shard_map/second_batch/pallas_call | solution.py:359
  (25 shorter events, 0.4 us)
Async XLA Ops:
  2.3 25.0 %copy-start.3 = (f32[128,1024]{1,0:T(8,128)S(1)}, f32[128,1024]{1,0:T(8,128)}, u32[]{:S(2)}) copy-start(f32[128,1024]{1,0:T(8,128)} %state.1) | copy-start | bytes 1572868
  2.3 25.0 %copy-start.4 = (f32[2,256,4]{1,2,0:T(4,128)S(1)}, f32[2,256,4]{1,2,0:T(4,128)}, u32[]{:S(2)}) copy-start(f32[2,256,4]{1,2,0:T(4,128)} %param.10) | copy-start | bytes 24580
  2.3 24.9 %copy-start.5 = (s32[2,256]{1,0:T(2,128)S(1)}, s32[2,256]{1,0:T(2,128)}, u32[]{:S(2)}) copy-start(s32[2,256]{1,0:T(2,128)} %blocks.3) | copy-start | bytes 6148
  2.3 1.4 %collective-permute-start.5 = (s16[64,512]{1,0:T(8,128)(2,1)S(1)}, s16[64,512]{1,0:T(8,128)(2,1)S(1)}, u32[]{:S(2)}, u32[]{:S(2)}) collective-permute-start(s16[64,512]{1,0:T(8,128)(2,1)S(1)} %get-tuple-element.35), channel_id=1, source_target_pairs={{0,1},{1,0},{2,3},{3,2},{4,5},{5,4},{6,7},{7,6},{8,9},{9,8},{10,11... | collective-permute-start | bytes 196616 | tf_op jit(solution)/shard_map/ppermute | solution.py:390
  3.7 7.8 %collective-permute-start.6 = (s16[1,64,512]{2,1,0:T(8,128)(2,1)S(1)}, s16[1,64,512]{2,1,0:T(8,128)(2,1)S(1)}, u32[]{:S(2)}, u32[]{:S(2)}) collective-permute-start(s16[1,64,512]{2,1,0:T(8,128)(2,1)S(1)} %add_bitcast_fusion), channel_id=1, source_target_pairs={{0,16},{1,17},{2,18},{3,19},{4,20},{5,21},{6,22},{7,23},{8,24},{9,... | collective-permute-start | bytes 196616 | tf_op jit(solution)/shard_map/ppermute | solution.py:390
  11.6 5.0 %collective-permute-start.10 = (s16[2,64,512]{2,1,0:T(8,128)(2,1)S(1)}, s16[2,64,512]{2,1,0:T(8,128)(2,1)S(1)}, u32[]{:S(2)}, u32[]{:S(2)}) collective-permute-start(s16[2,64,512]{2,1,0:T(8,128)(2,1)S(1)} %pad_add_fusion.refs_0_), channel_id=1, source_target_pairs={{0,8},{1,9},{2,10},{3,11},{4,12},{5,13},{6,14},{7,15},{8,0},{9,1},... | collective-permute-start | bytes 393224 | tf_op jit(solution)/shard_map/ppermute | solution.py:390
  12.4 7.4 %collective-permute-start.9 = (s16[2,64,512]{2,1,0:T(8,128)(2,1)S(1)}, s16[2,64,512]{2,1,0:T(8,128)(2,1)S(1)}, u32[]{:S(2)}, u32[]{:S(2)}) collective-permute-start(s16[2,64,512]{2,1,0:T(8,128)(2,1)S(1)} %pad_add_fusion.refs_0_), channel_id=1, source_target_pairs={{0,2},{1,3},{2,0},{3,1},{4,6},{5,7},{6,4},{7,5},{8,10},{9,11},{10,... | collective-permute-start | bytes 393224 | tf_op jit(solution)/shard_map/ppermute | solution.py:390
  13.9 9.3 %collective-permute-start.8 = (s16[2,64,512]{2,1,0:T(8,128)(2,1)S(1)}, s16[2,64,512]{2,1,0:T(8,128)(2,1)S(1)}, u32[]{:S(2)}, u32[]{:S(2)}) collective-permute-start(s16[2,64,512]{2,1,0:T(8,128)(2,1)S(1)} %pad_add_fusion.refs_0_), channel_id=1, source_target_pairs={{0,4},{1,5},{2,6},{3,7},{4,0},{5,1},{6,2},{7,3},{8,12},{9,13},{10,... | collective-permute-start | bytes 393224 | tf_op jit(solution)/shard_map/ppermute | solution.py:390
  15.4 7.8 %collective-permute-start.7 = (s16[2,64,512]{2,1,0:T(8,128)(2,1)S(1)}, s16[2,64,512]{2,1,0:T(8,128)(2,1)S(1)}, u32[]{:S(2)}, u32[]{:S(2)}) collective-permute-start(s16[2,64,512]{2,1,0:T(8,128)(2,1)S(1)} %pad_add_fusion.refs_0_), channel_id=1, source_target_pairs={{0,6},{1,7},{2,4},{3,5},{4,2},{5,3},{6,0},{7,1},{8,14},{9,15},{10,... | collective-permute-start | bytes 393224 | tf_op jit(solution)/shard_map/ppermute | solution.py:390
  16.6 7.4 %collective-permute-start.13 = (s16[2,64,512]{2,1,0:T(8,128)(2,1)S(1)}, s16[2,64,512]{2,1,0:T(8,128)(2,1)S(1)}, u32[]{:S(2)}, u32[]{:S(2)}) collective-permute-start(s16[2,64,512]{2,1,0:T(8,128)(2,1)S(1)} %collective-permute-done.10.refs_4_), channel_id=1, source_target_pairs={{0,2},{1,3},{2,0},{3,1},{4,6},{5,7},{6,4},{7,5},{8,10},{9,11},{10,... | collective-permute-start | bytes 393224 | tf_op jit(solution)/shard_map/ppermute | solution.py:390
  18.3 7.5 %collective-permute-start.12 = (s16[2,64,512]{2,1,0:T(8,128)(2,1)S(1)}, s16[2,64,512]{2,1,0:T(8,128)(2,1)S(1)}, u32[]{:S(2)}, u32[]{:S(2)}) collective-permute-start(s16[2,64,512]{2,1,0:T(8,128)(2,1)S(1)} %collective-permute-done.10.refs_4_), channel_id=1, source_target_pairs={{0,4},{1,5},{2,6},{3,7},{4,0},{5,1},{6,2},{7,3},{8,12},{9,13},{10,... | collective-permute-start | bytes 393224 | tf_op jit(solution)/shard_map/ppermute | solution.py:390
  19.8 7.4 %collective-permute-start.11 = (s16[2,64,512]{2,1,0:T(8,128)(2,1)S(1)}, s16[2,64,512]{2,1,0:T(8,128)(2,1)S(1)}, u32[]{:S(2)}, u32[]{:S(2)}) collective-permute-start(s16[2,64,512]{2,1,0:T(8,128)(2,1)S(1)} %collective-permute-done.10.refs_4_), channel_id=1, source_target_pairs={{0,6},{1,7},{2,4},{3,5},{4,2},{5,3},{6,0},{7,1},{8,14},{9,15},{10,... | collective-permute-start | bytes 393224 | tf_op jit(solution)/shard_map/ppermute | solution.py:390
  27.9 1.7 %copy-start = (bf16[2,256,1024]{2,1,0:T(8,128)(2,1)S(1)}, bf16[2,256,1024]{2,1,0:T(8,128)(2,1)}, u32[]{:S(2)}) copy-start(bf16[2,256,1024]{2,1,0:T(8,128)(2,1)} %noise.3) | copy-start | bytes 3145732
  27.9 1.7 %copy-start.1 = (s32[2,256]{1,0:T(2,128)S(1)}, s32[2,256]{1,0:T(2,128)}, u32[]{:S(2)}) copy-start(s32[2,256]{1,0:T(2,128)} %tags.3) | copy-start | bytes 6148
  27.9 1.7 %copy-start.2 = (f32[2,256]{1,0:T(2,128)S(1)}, f32[2,256]{1,0:T(2,128)}, u32[]{:S(2)}) copy-start(f32[2,256]{1,0:T(2,128)} %values.3) | copy-start | bytes 6148
  28.0 1.6 %collective-permute-start.15 = (bf16[256,512]{1,0:T(8,128)(2,1)S(1)}, bf16[256,512]{1,0:T(8,128)(2,1)S(1)}, u32[]{:S(2)}, u32[]{:S(2)}) collective-permute-start(bf16[256,512]{1,0:T(8,128)(2,1)S(1)} %get-tuple-element.37.own), channel_id=1, source_target_pairs={{0,1},{1,0},{2,3},{3,2},{4,5},{5,4},{6,7},{7,6},{8,9},{9,8},{10,11... | collective-permute-start | bytes 786440 | tf_op jit(solution)/shard_map/ppermute | solution.py:390
  28.0 44.1 %collective-permute-start.14 = (s16[256,512]{1,0:T(8,128)(2,1)S(1)}, s16[256,512]{1,0:T(8,128)(2,1)S(1)}, u32[]{:S(2)}, u32[]{:S(2)}) collective-permute-start(s16[256,512]{1,0:T(8,128)(2,1)S(1)} %get-tuple-element.36.own), channel_id=1, source_target_pairs={{0,1},{1,0},{2,3},{3,2},{4,5},{5,4},{6,7},{7,6},{8,9},{9,8},{10,11... | collective-permute-start | bytes 786440 | tf_op jit(solution)/shard_map/ppermute | solution.py:390

commit v4 on v3

--- a/solution.py
+++ b/solution.py
@@ -10,11 +10,12 @@
 SLOTS = 64
 UNIT = 1.0 / 1024
 SCALE = 0.55
-TOLERANCE = 0.03
+TOLERANCE = 0.16
 BF16 = jnp.bfloat16
 F32 = jnp.float32
 VMEM = pl.BlockSpec(memory_space=pltpu.VMEM)
 SMEM = pl.BlockSpec(memory_space=pltpu.SMEM)
+ANYWHERE = pl.BlockSpec(memory_space=pl.ANY)
 PARAMS = pltpu.CompilerParams(vmem_limit_bytes=40 * 1024 * 1024)
 
 
@@ -61,6 +62,13 @@
 
 def rounded(value):
     return value.astype(BF16).astype(F32)
+
+
+def three_parts(a):
+    high = a.astype(BF16)
+    rest = a - high.astype(F32)
+    middle = rest.astype(BF16)
+    return high, middle, (rest - middle.astype(F32)).astype(BF16)
 
 
 def pick_kernel(place, blocks, weights, state_ref, keep, send, state, arrived):
@@ -72,35 +80,36 @@
     held = width // points
     lane = lax.broadcasted_iota(jnp.int32, (size, size), 1)
     sub = lax.broadcasted_iota(jnp.int32, (size, size), 0)
+    earlier = jnp.where(sub < lane, 1.0, 0.0).astype(BF16)
+    row = blocks[...]
+    mine = jnp.where(row // (2 * held) == device // 2, 1.0, 0.0)
+    rank = nn(mine.astype(BF16), earlier).astype(jnp.int32)
+    own = row // held == device
     slots = lax.broadcasted_iota(jnp.int32, (SLOTS, size), 0)
-    lanes = lax.broadcasted_iota(jnp.int32, (SLOTS, width), 1)
-    selectors, taken = [], []
+    points_of = lax.broadcasted_iota(jnp.int32, (width, size), 0)
+    chosen, selector = [], []
     for batch in range(batches):
-        row = blocks[batch : batch + 1, :]
-        pair_row, pair_column = both_ways(row // (2 * held))
-        before = jnp.where((pair_row == pair_column) & (sub < lane), 1.0, 0.0)
-        rank = jnp.sum(before, axis=0, keepdims=True).astype(jnp.int32)
-        slot = jnp.where(row // held == device, rank if batch == 0 else SLOTS - 1 - rank, -1)
-        chosen = jnp.where(slots == slot, 1.0, 0.0)
-        local = jnp.sum(chosen * (row - device * held).astype(F32), axis=1, keepdims=True)
-        weight = lax.dot_general(
-            chosen,
-            weights[batch],
-            (((1,), (1,)), ((), ())),
-            precision=lax.Precision.HIGHEST,
-            preferred_element_type=F32,
-        )
-        columns = [weight[:, point : point + 1] for point in range(points)]
-        selectors.append(select(lanes, points, local, columns))
-        taken.append(jnp.sum(chosen, axis=1, keepdims=True))
+        place_of = rank[batch : batch + 1, :]
+        place_of = place_of if batch == 0 else SLOTS - 1 - place_of
+        place_of = jnp.where(own[batch : batch + 1, :], place_of, -1)
+        chosen.append(jnp.where(slots == place_of, 1.0, 0.0))
+        value = jnp.zeros((width, size), F32)
+        for point in range(points):
+            weight = weights[batch, point : point + 1, :]
+            value = jnp.where(points_of % points == point, weight, value)
+        local = row[batch : batch + 1, :] - device * held
+        selector.append(jnp.where(points_of // points == local, value, 0.0))
+    chosen = jnp.concatenate(chosen, axis=1).astype(BF16)
+    parts = three_parts(jnp.concatenate(selector, axis=1))
+    high, middle, low = [nt(chosen, part).astype(BF16) for part in parts]
     load.wait()
-    rows = jnp.dot(
-        selectors[0] + selectors[1],
-        state[...],
-        precision=lax.Precision.HIGHEST,
-        preferred_element_type=F32,
-    )
-    rows = jnp.where(taken[0] > 0.5, rounded(rows), rows)
+    top, mid, end = three_parts(state[...])
+    rows = nn(high, end) + nn(middle, mid) + nn(low, top)
+    rows = (nn(high, mid) + nn(middle, top)) + rows
+    rows = nn(high, top) + rows
+    from_first = lax.broadcasted_iota(jnp.int32, (SLOTS, 1), 0).astype(F32)
+    from_first = from_first < jnp.sum(mine[:1, :], axis=1, keepdims=True)
+    rows = jnp.where(from_first, rounded(rows), rows)
     code = jnp.round(rows * (1.0 / UNIT)).astype(jnp.int32)
     left, right = code[:, : members // 2], code[:, members // 2 :]
     first = device % 2 == 0
@@ -112,7 +121,7 @@
     return pl.pallas_call(
         pick_kernel,
         out_shape=[jax.ShapeDtypeStruct((SLOTS, state.shape[1] // 2), jnp.int16)] * 2,
-        in_specs=[SMEM, VMEM, VMEM, pl.BlockSpec(memory_space=pl.ANY)],
+        in_specs=[SMEM, VMEM, VMEM, ANYWHERE],
         out_specs=[VMEM] * 2,
         scratch_shapes=[pltpu.VMEM(state.shape, F32), pltpu.SemaphoreType.DMA],
         compiler_params=PARAMS,
@@ -159,11 +168,14 @@
         before = jnp.where((pair_row == pair_column) & (lane < sub), 1.0, 0.0)
         rank = jnp.sum(before, axis=1, keepdims=True).astype(jnp.int32)
         away = (2 * pair_column.astype(jnp.int32)) ^ device
-        slot = SLOTS * ((away >> 4) & 1) + (rank if batch == 0 else SLOTS - 1 - rank)
+        x, y = (away >> 2) & 1, (away >> 1) & 1
+        plane = jnp.where(device % 2 == 0, 2 * x + y, 2 * y + x)
+        distance = 8 * ((away >> 3) & 1) + 4 * ((away >> 4) & 1) + plane
+        slot = rank if batch == 0 else SLOTS - 1 - rank
         for distances, out in zip(groups, outs):
-            where = jnp.full(rank.shape, -2 * SLOTS, jnp.int32)
-            for index, distance in enumerate(distances):
-                where = jnp.where((away >> 1) & 7 == distance, 2 * SLOTS * index, where)
+            where = jnp.full(rank.shape, -SLOTS, jnp.int32)
+            for index, known in enumerate(distances):
+                where = jnp.where(distance == known, SLOTS * index, where)
             slots = lax.broadcasted_iota(jnp.int32, (size, out.shape[1]), 1)
             chosen = jnp.where(slots == where + slot, 1.0, 0.0)
             out[batch * size : (batch + 1) * size, :] = chosen.astype(BF16)
@@ -173,7 +185,7 @@
     return pl.pallas_call(
         functools.partial(order_kernel, groups),
         out_shape=[
-            jax.ShapeDtypeStruct((blocks.size, 2 * SLOTS * len(group)), BF16) for group in groups
+            jax.ShapeDtypeStruct((blocks.size, SLOTS * len(group)), BF16) for group in groups
         ],
         in_specs=[SMEM, VMEM],
         out_specs=[VMEM] * len(groups),
@@ -185,7 +197,7 @@
 
 def put_in_order(chosen, pieces):
     size = chosen.shape[0] // 2
-    values = jnp.concatenate([ref[...].reshape(2 * SLOTS, -1) for ref in pieces], axis=0)
+    values = jnp.concatenate([ref[...].reshape(-1, ref.shape[-1]) for ref in pieces], axis=0)
     high, low = split(values.astype(jnp.int32).astype(F32))
     second = chosen[size:, :]
     return nn(chosen[:size, :], high), nn(second, high) + nn(second, low)
@@ -250,7 +262,7 @@
     inverse[...] = inverse[...] * (1.0 / jnp.sqrt(pivots))
 
 
-def inverse_factor(covariance, work, inverse):
+def inverse_factor(covariance):
     size = covariance.shape[0]
     lane = lax.broadcasted_iota(jnp.int32, (size, size), 1)
     sub = lax.broadcasted_iota(jnp.int32, (size, size), 0)
@@ -262,59 +274,56 @@
     scale_column = lax.rsqrt(jnp.sum(on_diagonal, axis=1, keepdims=True) * (1.0 / SCALE))
     scaled = covariance * scale_row * scale_column
 
-    def third_order(m):
-        low = (m - eye) * half
+    def third_order(error):
+        low = error * half
         lowb = low.astype(BF16)
         return (nn(lowb, lowb) + half * nt(lowb, lowb)) - low
 
     m = scaled
     t = None
-    for step in range(2):
-        u = third_order(m) + eye
+    for step in range(3):
+        u = third_order(m - eye) + eye
         ub = u.astype(BF16)
         t = u if t is None else nn(ub, t.astype(BF16))
-        if step < 1:
+        if step < 2:
             m = nt(nn(ub, m.astype(BF16)).astype(BF16), ub)
-    parts = split(scaled)
     ts = split(t)
-    m = dot3(nt, split(dot3(nn, ts, parts)), ts)
-    t = t + nn(third_order(m).astype(BF16), ts[0])
-    ts = split(t)
-    m = dot3(nt, split(dot3(nn, ts, parts)), ts)
-    error = m - eye
-    t = t - nn((error * half).astype(BF16), ts[0])
-    inverse[...] = t * scale_row
-    good = jnp.sum(error * error) <= TOLERANCE * TOLERANCE
-
-    @pl.when(jnp.logical_not(good))
-    def _():
-        eliminate(covariance, work, inverse)
-
-
-def whiten(observed, tags, values, noise, work, inverse):
+    error = dot3(nt, split(dot3(nn, ts, split(scaled))), ts) - eye
+    t = t + nn(third_order(error).astype(BF16), ts[0])
+    return t * scale_row, jnp.sum(error * error) <= TOLERANCE * TOLERANCE
+
+
+def whiten(observed, tags, values, load, noise_ref, work, inverse, store):
     members = observed.shape[1]
     size = observed.shape[0]
     mean = row_mean(observed)
-    ah, al = split(observed - mean)
+    parts = split(observed - mean)
     lane = lax.broadcasted_iota(jnp.int32, (size, size), 1)
     sub = lax.broadcasted_iota(jnp.int32, (size, size), 0)
     variance_row = jnp.where(tags == 0, 0.5, 2.0)
     variance = column(variance_row)
     mean_row = jnp.sum(jnp.where(lane == sub, mean, 0.0), axis=0, keepdims=True)
-    covariance = dot3(nt, (ah, al), (ah, al)) * (1.0 / (members - 1))
+    covariance = dot3(nt, parts, parts) * (1.0 / (members - 1))
     covariance = covariance + jnp.where(lane == sub, variance, 0.0)
-    inverse_factor(covariance, work, inverse)
-    t = inverse[...]
-    th, tl = split(t)
-    nh, nl = split(t * jnp.sqrt(variance_row))
     exact = observed.astype(BF16)
-    applied = nn(th, exact) + nn(tl, exact)
-    noise = nn(nh, noise) + nn(nl, noise)
-    mean_part = jnp.sum(t * mean_row, axis=1, keepdims=True)
-    value_part = jnp.sum(t * values, axis=1, keepdims=True)
-    whitened = (applied - mean_part).astype(BF16)
-    white_innov = (noise + value_part - applied).astype(BF16)
-    return whitened, white_innov
+
+    def finish(t):
+        th, tl = split(t)
+        nh, nl = split(t * jnp.sqrt(variance_row))
+        applied = nn(th, exact) + nn(tl, exact)
+        noise = nn(nh, noise_ref[...]) + nn(nl, noise_ref[...])
+        mean_part = jnp.sum(t * mean_row, axis=1, keepdims=True)
+        value_part = jnp.sum(t * values, axis=1, keepdims=True)
+        store((applied - mean_part).astype(BF16), (noise + value_part - applied).astype(BF16))
+
+    t, good = inverse_factor(covariance)
+    load.wait()
+    finish(t)
+
+    @pl.when(jnp.logical_not(good))
+    def _():
+        eliminate(covariance, work, inverse)
+        finish(inverse[...])
 
 
 def update(state, whitened, white_innov):
@@ -332,53 +341,79 @@
     )
 
 
-def first_kernel(place, tags, values, noise, own, other, whitened, white_innov, work, inverse):
+def first_kernel(
+    place, tags, values, noise_ref, own, other, whitened, white_innov, noise, loads, work, inverse
+):
+    load = pltpu.make_async_copy(noise_ref.at[0], noise, loads.at[0])
+    load.start()
     observed = both_halves(place, own, other)
-    w, v = whiten(observed, tags[:1, :], values[:1, :], noise[0], work, inverse)
-    whitened[...] = w
-    white_innov[...] = v
+
+    def store(w, v):
+        whitened[...] = w
+        white_innov[...] = v
+
+    whiten(observed, tags[:1, :], values[:1, :], load, noise, work, inverse, store)
 
 
 def second_kernel(
-    place, tags, values, noise, own, other, state, whitened, white_innov, analysis, work, inverse
+    place,
+    tags,
+    values,
+    noise_ref,
+    own,
+    other,
+    whitened,
+    white_innov,
+    state_ref,
+    analysis,
+    noise,
+    loads,
+    work,
+    inverse,
+    state,
 ):
+    load = pltpu.make_async_copy(noise_ref.at[1], noise, loads.at[0])
+    load_state = pltpu.make_async_copy(state_ref, state, loads.at[1])
+    load_state.start()
+    load.start()
     prior = both_halves(place, own, other) * UNIT
     w, v = whitened[...], white_innov[...]
     observed = rounded(update(prior, w, v))
+    load_state.wait()
     first = update(state[...], w, v)
-    w, v = whiten(observed, tags[1:2, :], values[1:2, :], noise[0], work, inverse)
-    analysis[...] = update(first, w, v)
-
-
-def whole(array):
-    return pl.BlockSpec(array.shape, lambda i, n=len(array.shape): (0,) * n)
-
-
-def batch_call(kernel, name, batch, outs, place, tags, values, noise, *arrays):
+
+    def store(w, v):
+        analysis[...] = update(first, w, v)
+
+    whiten(observed, tags[1:2, :], values[1:2, :], load, noise, work, inverse, store)
+
+
+def batch_call(kernel, name, outs, place, tags, values, noise, *arrays, state=()):
     rows, members = noise.shape[1:]
     return pl.pallas_call(
         kernel,
-        grid=(1,),
         out_shape=outs,
-        in_specs=[SMEM, whole(tags), whole(values)]
-        + [pl.BlockSpec((1, rows, members), lambda i: (batch, 0, 0))]
-        + [whole(array) for array in arrays],
-        out_specs=[whole(out) for out in outs],
-        scratch_shapes=[pltpu.VMEM((rows, rows), F32), pltpu.VMEM((rows, rows), F32)],
+        in_specs=[SMEM, VMEM, VMEM, ANYWHERE] + [VMEM] * len(arrays) + [ANYWHERE] * len(state),
+        out_specs=[VMEM] * len(outs),
+        scratch_shapes=[
+            pltpu.VMEM((rows, members), BF16),
+            pltpu.SemaphoreType.DMA((2,)),
+            pltpu.VMEM((rows, rows), F32),
+            pltpu.VMEM((rows, rows), F32),
+        ]
+        + [pltpu.VMEM(array.shape, F32) for array in state],
         compiler_params=PARAMS,
         name=name,
-    )(place, tags, values, noise, *arrays)
+    )(place, tags, values, noise, *arrays, *state)
 
 
 def batches(place, tags, values, noise, state, observed, prior):
     shape = jax.ShapeDtypeStruct(noise.shape[1:], BF16)
     shared = (place, tags, values, noise)
-    whitened, white_innov = batch_call(
-        first_kernel, "first_batch", 0, [shape, shape], *shared, *observed
-    )
+    white = batch_call(first_kernel, "first_batch", [shape, shape], *shared, *observed)
     analysis = jax.ShapeDtypeStruct(state.shape, F32)
     return batch_call(
-        second_kernel, "second_batch", 1, [analysis], *shared, *prior, state, whitened, white_innov
+        second_kernel, "second_batch", [analysis], *shared, *prior, *white, state=(state,)
     )[0]
 
 
@@ -386,21 +421,38 @@
 CORE, Y, X, NEAR_Z, FAR_Z = 1, 2, 4, 8, 16
 
 
-def swap(value, mask):
-    return lax.ppermute(value, AXES, [(i, i ^ mask) for i in range(32)])
+def swap(value, mask, odd_mask=None):
+    masks = (mask, mask if odd_mask is None else odd_mask)
+    return lax.ppermute(value, AXES, [(i, i ^ masks[i % 2]) for i in range(32)])
+
+
+def along_first(value):
+    return swap(value, X, Y)
+
+
+def along_second(value):
+    return swap(value, Y, X)
+
+
+EARLY = (0, 8, 4, 2, 6, 1, 5, 3, 7, 12, 10, 14)
+LATE = (9, 13, 11, 15)
 
 
 def by_slots(place, ensemble, blocks, weights):
-    sides = (X | Y, X, Y)
-    groups = [[0] + [mask // 2 for mask in sides + (NEAR_Z,)]]
-    groups += [[(NEAR_Z | mask) // 2 for mask in sides]]
-    early_places, late_places = order(place, blocks, groups)
     keep, send = pick(place, blocks, weights, ensemble)
-    block = (keep + swap(send, CORE))[None]
-    here = jnp.concatenate([block, swap(block, FAR_Z)], axis=0)
-    early = [here] + [swap(here, mask) for mask in sides + (NEAR_Z,)]
-    late = [swap(early[-1], mask) for mask in sides]
-    return late_rows(late_places, early_rows(early_places, early), late)
+    own = (keep + swap(send, CORE))[None]
+    near_own = swap(own, NEAR_Z)
+    far = swap(own, FAR_Z)
+    here = jnp.concatenate([own, far], axis=0)
+    first = along_first(here)
+    second = along_second(jnp.concatenate([here, first], axis=0))
+    near_far = swap(far, NEAR_Z)
+    near = jnp.concatenate([near_own, near_far], axis=0)
+    near_first = along_first(near)
+    near_second = along_second(jnp.concatenate([near, near_first], axis=0))
+    early_places, late_places = order(place, blocks, (EARLY, LATE))
+    early = early_rows(early_places, [own, near_own, far, first, second, near_far, near_first])
+    return late_rows(late_places, early, [near_second])
 
 
 def add_by_swaps(value):

time: 81.7 us -> 82.6 us (1.011)
  starting transfers between devices: 13.1 us -> 15 us
    ppermute x11 -> x10, starting transfers between devices: 13.1 us -> 15 us  [swap(): return lax.ppermute(value, AXES, [(i, i ^ masks[i % 2]) for i in range(32)])]
    ppermute x11 -> x10, waiting for transfers between devices: 8.99 us -> 8.65 us  [swap(): return lax.ppermute(value, AXES, [(i, i ^ masks[i % 2]) for i in range(32)])]
  transfers between devices with their start and end apart: 11 -> 10, of which waited for: 6 -> 7; matrix products, arithmetic and copies ran while one was open for 2% -> 1% of each run, Pallas kernels for 55% -> 55%
where the time goes in v4:
time: 82.6 us; the launch traced here: 82.4 us
  Pallas kernels  56.8 us (69%)
  starting transfers between devices  15 us (18%)
  waiting for transfers between devices  8.65 us (10%)
  other arithmetic  0.95 us (1%)
  between operations  0.94 us (1%)
    pallas_call x2, Pallas kernels, batch_call(): pl.pallas_call(kernel, out_shape=outs, in_specs=[SMEM, VMEM, VMEM, ANYWHE...  51.9 us
    ppermute x10, starting transfers between devices, swap(): return lax.ppermute(value, AXES, [(i, i ^ masks[i % 2]) for i in range(32)])  15 us
    ppermute x10, waiting for transfers between devices, swap(): return lax.ppermute(value, AXES, [(i, i ^ masks[i % 2]) for i in range(32)])  8.65 us
    pallas_call x1, Pallas kernels, pick(): pl.pallas_call(pick_kernel, out_shape=[jax.ShapeDtypeStruct((SLOTS, state...  2.22 us
  transfers between devices with their start and end apart: 10, of which 7 were waited for; matrix products, arithmetic and copies ran while one was open for 1% of the time, Pallas kernels for 55%

profile of v4, /device:TPU:0, one launch (start us, length us, event | category | flops | bytes accessed | tf_op | source)
XLA Modules:
  0.0 82.4 jit_solution(10944970015285910258)
XLA Ops:
  0.1 2.2 %pick.1 = (s16[64,512]{1,0:T(8,128)(2,1)S(1)}, s16[64,512]{1,0:T(8,128)(2,1)S(1)}) custom-call(s32[2]{0:T(128)S(1)} %pad_add_fusion.4.place, s32[2,256]{1,0:T(2,128)} %blocks.3, f32[2,4,256]{2,1,0:T(4,128)} %bitcast.4, f32[128,1024]{1,0:T(8,128)} %state_ref.3), custom_call_target="tpu_custom_call" | custom-call | tf_op jit(solution)/shard_map/pick/pallas_call | solution.py:121
  2.3 0.5 collective-permute-start.5
  2.8 0.9 %collective-permute-done.5 = s16[64,512]{1,0:T(8,128)(2,1)S(1)} collective-permute-done((s16[64,512]{1,0:T(8,128)(2,1)S(1)}, s16[64,512]{1,0:T(8,128)(2,1)S(1)}, u32[]{:S(2)}, u32[]{:S(2)}) %collective-permute-start.5) | collective-permute-done | bytes 65568 | tf_op jit(solution)/shard_map/ppermute | solution.py:426
  3.8 4.0 %collective-permute-start.7 = (s16[1,64,512]{2,1,0:T(8,128)(2,1)S(1)}, s16[1,64,512]{2,1,0:T(8,128)(2,1)S(1)}, u32[]{:S(2)}, u32[]{:S(2)}) collective-permute-start(s16[1,64,512]{2,1,0:T(8,128)(2,1)S(1)} %add_bitcast_fusion.refs_0_), channel_id=1, source_target_pairs={{0,16},{1,17},{2,18},{3,19},{4,20},{5,21},{6,22},{7,23},{8,24},{9,... | collective-permute-start | bytes 196616 | tf_op jit(solution)/shard_map/ppermute | solution.py:426
  7.8 1.6 %collective-permute-start.6 = (s16[1,64,512]{2,1,0:T(8,128)(2,1)S(1)}, s16[1,64,512]{2,1,0:T(8,128)(2,1)S(1)}, u32[]{:S(2)}, u32[]{:S(2)}) collective-permute-start(s16[1,64,512]{2,1,0:T(8,128)(2,1)S(1)} %add_bitcast_fusion.refs_0_), channel_id=1, source_target_pairs={{0,8},{1,9},{2,10},{3,11},{4,12},{5,13},{6,14},{7,15},{8,0},{9,1},... | collective-permute-start | bytes 196616 | tf_op jit(solution)/shard_map/ppermute | solution.py:426
  9.3 1.8 %collective-permute-done.7.refs_2_ = s16[1,64,512]{2,1,0:T(8,128)(2,1)S(1)} collective-permute-done((s16[1,64,512]{2,1,0:T(8,128)(2,1)S(1)}, s16[1,64,512]{2,1,0:T(8,128)(2,1)S(1)}, u32[]{:S(2)}, u32[]{:S(2)}) %collective-permute-start.7) | collective-permute-done | bytes 65568 | tf_op jit(solution)/shard_map/ppermute | solution.py:426
  11.1 1.4 %collective-permute-start.10 = (s16[1,64,512]{2,1,0:T(8,128)(2,1)S(1)}, s16[1,64,512]{2,1,0:T(8,128)(2,1)S(1)}, u32[]{:S(2)}, u32[]{:S(2)}) collective-permute-start(s16[1,64,512]{2,1,0:T(8,128)(2,1)S(1)} %collective-permute-done.7.refs_2_), channel_id=1, source_target_pairs={{0,8},{1,9},{2,10},{3,11},{4,12},{5,13},{6,14},{7,15},{8,0},{9,1},... | collective-permute-start | bytes 196616 | tf_op jit(solution)/shard_map/ppermute | solution.py:426
  12.5 1.6 %collective-permute-start.8 = (s16[2,64,512]{2,1,0:T(8,128)(2,1)S(1)}, s16[2,64,512]{2,1,0:T(8,128)(2,1)S(1)}, u32[]{:S(2)}, u32[]{:S(2)}) collective-permute-start(s16[2,64,512]{2,1,0:T(8,128)(2,1)S(1)} %pad_add_fusion.2), channel_id=1, source_target_pairs={{0,4},{1,3},{2,6},{3,1},{4,0},{5,7},{6,2},{7,5},{8,12},{9,11},{10,... | collective-permute-start | bytes 393224 | tf_op jit(solution)/shard_map/ppermute | solution.py:426
  14.1 1.3 %collective-permute-done.10.refs_5_ = s16[1,64,512]{2,1,0:T(8,128)(2,1)S(1)} collective-permute-done((s16[1,64,512]{2,1,0:T(8,128)(2,1)S(1)}, s16[1,64,512]{2,1,0:T(8,128)(2,1)S(1)}, u32[]{:S(2)}, u32[]{:S(2)}) %collective-permute-start.10) | collective-permute-done | bytes 65568 | tf_op jit(solution)/shard_map/ppermute | solution.py:426
  15.4 1.9 %collective-permute-start.11 = (s16[2,64,512]{2,1,0:T(8,128)(2,1)S(1)}, s16[2,64,512]{2,1,0:T(8,128)(2,1)S(1)}, u32[]{:S(2)}, u32[]{:S(2)}) collective-permute-start(s16[2,64,512]{2,1,0:T(8,128)(2,1)S(1)} %pad_add_fusion.3), channel_id=1, source_target_pairs={{0,4},{1,3},{2,6},{3,1},{4,0},{5,7},{6,2},{7,5},{8,12},{9,11},{10,... | collective-permute-start | bytes 393224 | tf_op jit(solution)/shard_map/ppermute | solution.py:426
  17.3 0.3 collective-permute-done.8.refs_3_
  17.6 1.6 %collective-permute-start.9 = (s16[4,64,512]{2,1,0:T(8,128)(2,1)S(1)}, s16[4,64,512]{2,1,0:T(8,128)(2,1)S(1)}, u32[]{:S(2)}, u32[]{:S(2)}) collective-permute-start(s16[4,64,512]{2,1,0:T(8,128)(2,1)S(1)} %pad_add_fusion), channel_id=1, source_target_pairs={{0,2},{1,5},{2,0},{3,7},{4,6},{5,1},{6,4},{7,3},{8,10},{9,13},{10,... | collective-permute-start | bytes 786440 | tf_op jit(solution)/shard_map/ppermute | solution.py:426
  19.2 2.6 %collective-permute-done.11.refs_6_ = s16[2,64,512]{2,1,0:T(8,128)(2,1)S(1)} collective-permute-done((s16[2,64,512]{2,1,0:T(8,128)(2,1)S(1)}, s16[2,64,512]{2,1,0:T(8,128)(2,1)S(1)}, u32[]{:S(2)}, u32[]{:S(2)}) %collective-permute-start.11) | collective-permute-done | bytes 131104 | tf_op jit(solution)/shard_map/ppermute | solution.py:426
  21.8 1.9 %collective-permute-start.12 = (s16[4,64,512]{2,1,0:T(8,128)(2,1)S(1)}, s16[4,64,512]{2,1,0:T(8,128)(2,1)S(1)}, u32[]{:S(2)}, u32[]{:S(2)}) collective-permute-start(s16[4,64,512]{2,1,0:T(8,128)(2,1)S(1)} %pad_add_fusion.1), channel_id=1, source_target_pairs={{0,2},{1,5},{2,0},{3,7},{4,6},{5,1},{6,4},{7,3},{8,10},{9,13},{10,... | collective-permute-start | bytes 786440 | tf_op jit(solution)/shard_map/ppermute | solution.py:426
  23.7 0.1 convert_reduce_fusion
  23.9 0.7 reduce_max.9
  25.2 1.5 %order.1 = (bf16[512,768]{1,0:T(8,128)(2,1)S(1)}, bf16[512,256]{1,0:T(8,128)(2,1)S(1)}) custom-call(s32[2]{0:T(128)S(1)} %pad_add_fusion.4.place, s32[2,256]{1,0:T(2,128)S(1)} %copy-done.5), custom_call_target="tpu_custom_call" | custom-call | flops 1000000 | bytes 1000000 | tf_op jit(solution)/shard_map/order/pallas_call | solution.py:185
  26.6 0.8 early_rows.1.early
  27.5 0.8 collective-permute-done.12.refs_0_
  28.2 0.4 late_rows.1
  28.8 0.5 collective-permute-start.13
  29.3 1.0 %collective-permute-done.14.other = bf16[256,512]{1,0:T(8,128)(2,1)S(1)} collective-permute-done((bf16[256,512]{1,0:T(8,128)(2,1)S(1)}, bf16[256,512]{1,0:T(8,128)(2,1)S(1)}, u32[]{:S(2)}, u32[]{:S(2)}) %collective-permute-start.14) | collective-permute-done | bytes 262176 | tf_op jit(solution)/shard_map/ppermute | solution.py:426
  30.4 43.1 %first_batch.1 = (bf16[256,1024]{1,0:T(8,128)(2,1)S(1)}, bf16[256,1024]{1,0:T(8,128)(2,1)S(1)}) custom-call(s32[2]{0:T(128)S(1)} %pad_add_fusion.4.place, s32[2,256]{1,0:T(2,128)S(1)} %copy-done.1, f32[2,256]{1,0:T(2,128)S(1)} %copy-done.2, bf16[2,256,1024]{2,1,0:T(8,128)(2,1)S(1)} %copy-done, bf16[256,512]{1,0:T(8,128)(2,1)S(1)} %get-tuple-element.37.own, ...), custom_call_target="tpu_custom_call" | custom-call | tf_op jit(solution)/shard_map/first_batch/pallas_call | solution.py:393
  73.5 8.8 %second_batch.1 = f32[128,1024]{1,0:T(8,128)} custom-call(s32[2]{0:T(128)S(1)} %pad_add_fusion.4.place, s32[2,256]{1,0:T(2,128)S(1)} %copy-done.1, f32[2,256]{1,0:T(2,128)S(1)} %copy-done.2, bf16[2,256,1024]{2,1,0:T(8,128)(2,1)S(1)} %copy-done, s16[256,512]{1,0:T(8,128)(2,1)S(1)} %get-tuple-element.36.own, ...), custom_call_target="tpu_custom_call" | custom-call | tf_op jit(solution)/shard_map/second_batch/pallas_call | solution.py:393
  (26 shorter events, 0.4 us)
Async XLA Ops:
  0.0 23.7 %copy-start.5 = (s32[2,256]{1,0:T(2,128)S(1)}, s32[2,256]{1,0:T(2,128)}, u32[]{:S(2)}) copy-start(s32[2,256]{1,0:T(2,128)} %blocks.3) | copy-start | bytes 6148
  2.3 1.4 %collective-permute-start.5 = (s16[64,512]{1,0:T(8,128)(2,1)S(1)}, s16[64,512]{1,0:T(8,128)(2,1)S(1)}, u32[]{:S(2)}, u32[]{:S(2)}) collective-permute-start(s16[64,512]{1,0:T(8,128)(2,1)S(1)} %get-tuple-element.35), channel_id=1, source_target_pairs={{0,1},{1,0},{2,3},{3,2},{4,5},{5,4},{6,7},{7,6},{8,9},{9,8},{10,11... | collective-permute-start | bytes 196616 | tf_op jit(solution)/shard_map/ppermute | solution.py:426
  3.8 7.4 %collective-permute-start.7 = (s16[1,64,512]{2,1,0:T(8,128)(2,1)S(1)}, s16[1,64,512]{2,1,0:T(8,128)(2,1)S(1)}, u32[]{:S(2)}, u32[]{:S(2)}) collective-permute-start(s16[1,64,512]{2,1,0:T(8,128)(2,1)S(1)} %add_bitcast_fusion.refs_0_), channel_id=1, source_target_pairs={{0,16},{1,17},{2,18},{3,19},{4,20},{5,21},{6,22},{7,23},{8,24},{9,... | collective-permute-start | bytes 196616 | tf_op jit(solution)/shard_map/ppermute | solution.py:426
  7.8 6.3 %collective-permute-start.6 = (s16[1,64,512]{2,1,0:T(8,128)(2,1)S(1)}, s16[1,64,512]{2,1,0:T(8,128)(2,1)S(1)}, u32[]{:S(2)}, u32[]{:S(2)}) collective-permute-start(s16[1,64,512]{2,1,0:T(8,128)(2,1)S(1)} %add_bitcast_fusion.refs_0_), channel_id=1, source_target_pairs={{0,8},{1,9},{2,10},{3,11},{4,12},{5,13},{6,14},{7,15},{8,0},{9,1},... | collective-permute-start | bytes 196616 | tf_op jit(solution)/shard_map/ppermute | solution.py:426
  11.1 4.3 %collective-permute-start.10 = (s16[1,64,512]{2,1,0:T(8,128)(2,1)S(1)}, s16[1,64,512]{2,1,0:T(8,128)(2,1)S(1)}, u32[]{:S(2)}, u32[]{:S(2)}) collective-permute-start(s16[1,64,512]{2,1,0:T(8,128)(2,1)S(1)} %collective-permute-done.7.refs_2_), channel_id=1, source_target_pairs={{0,8},{1,9},{2,10},{3,11},{4,12},{5,13},{6,14},{7,15},{8,0},{9,1},... | collective-permute-start | bytes 196616 | tf_op jit(solution)/shard_map/ppermute | solution.py:426
  12.5 5.0 %collective-permute-start.8 = (s16[2,64,512]{2,1,0:T(8,128)(2,1)S(1)}, s16[2,64,512]{2,1,0:T(8,128)(2,1)S(1)}, u32[]{:S(2)}, u32[]{:S(2)}) collective-permute-start(s16[2,64,512]{2,1,0:T(8,128)(2,1)S(1)} %pad_add_fusion.2), channel_id=1, source_target_pairs={{0,4},{1,3},{2,6},{3,1},{4,0},{5,7},{6,2},{7,5},{8,12},{9,11},{10,... | collective-permute-start | bytes 393224 | tf_op jit(solution)/shard_map/ppermute | solution.py:426
  15.4 6.4 %collective-permute-start.11 = (s16[2,64,512]{2,1,0:T(8,128)(2,1)S(1)}, s16[2,64,512]{2,1,0:T(8,128)(2,1)S(1)}, u32[]{:S(2)}, u32[]{:S(2)}) collective-permute-start(s16[2,64,512]{2,1,0:T(8,128)(2,1)S(1)} %pad_add_fusion.3), channel_id=1, source_target_pairs={{0,4},{1,3},{2,6},{3,1},{4,0},{5,7},{6,2},{7,5},{8,12},{9,11},{10,... | collective-permute-start | bytes 393224 | tf_op jit(solution)/shard_map/ppermute | solution.py:426
  17.6 10.7 %copy-start.3 = (f32[128,1024]{1,0:T(8,128)S(1)}, f32[128,1024]{1,0:T(8,128)}, u32[]{:S(2)}) copy-start(f32[128,1024]{1,0:T(8,128)} %state_ref.3) | copy-start | bytes 1572868
  17.6 10.6 %copy-start.4 = (f32[2,256,4]{1,2,0:T(4,128)S(1)}, f32[2,256,4]{1,2,0:T(4,128)}, u32[]{:S(2)}) copy-start(f32[2,256,4]{1,2,0:T(4,128)} %param.10) | copy-start | bytes 24580
  17.6 9.0 %collective-permute-start.9 = (s16[4,64,512]{2,1,0:T(8,128)(2,1)S(1)}, s16[4,64,512]{2,1,0:T(8,128)(2,1)S(1)}, u32[]{:S(2)}, u32[]{:S(2)}) collective-permute-start(s16[4,64,512]{2,1,0:T(8,128)(2,1)S(1)} %pad_add_fusion), channel_id=1, source_target_pairs={{0,2},{1,5},{2,0},{3,7},{4,6},{5,1},{6,4},{7,3},{8,10},{9,13},{10,... | collective-permute-start | bytes 786440 | tf_op jit(solution)/shard_map/ppermute | solution.py:426
  21.8 6.4 %collective-permute-start.12 = (s16[4,64,512]{2,1,0:T(8,128)(2,1)S(1)}, s16[4,64,512]{2,1,0:T(8,128)(2,1)S(1)}, u32[]{:S(2)}, u32[]{:S(2)}) collective-permute-start(s16[4,64,512]{2,1,0:T(8,128)(2,1)S(1)} %pad_add_fusion.1), channel_id=1, source_target_pairs={{0,2},{1,5},{2,0},{3,7},{4,6},{5,1},{6,4},{7,3},{8,10},{9,13},{10,... | collective-permute-start | bytes 786440 | tf_op jit(solution)/shard_map/ppermute | solution.py:426
  28.7 1.7 %copy-start = (bf16[2,256,1024]{2,1,0:T(8,128)(2,1)S(1)}, bf16[2,256,1024]{2,1,0:T(8,128)(2,1)}, u32[]{:S(2)}) copy-start(bf16[2,256,1024]{2,1,0:T(8,128)(2,1)} %noise_ref.3) | copy-start | bytes 3145732
  28.7 1.7 %copy-start.1 = (s32[2,256]{1,0:T(2,128)S(1)}, s32[2,256]{1,0:T(2,128)}, u32[]{:S(2)}) copy-start(s32[2,256]{1,0:T(2,128)} %tags.3) | copy-start | bytes 6148
  28.7 1.7 %copy-start.2 = (f32[2,256]{1,0:T(2,128)S(1)}, f32[2,256]{1,0:T(2,128)}, u32[]{:S(2)}) copy-start(f32[2,256]{1,0:T(2,128)} %values.3) | copy-start | bytes 6148
  28.8 1.6 %collective-permute-start.14 = (bf16[256,512]{1,0:T(8,128)(2,1)S(1)}, bf16[256,512]{1,0:T(8,128)(2,1)S(1)}, u32[]{:S(2)}, u32[]{:S(2)}) collective-permute-start(bf16[256,512]{1,0:T(8,128)(2,1)S(1)} %get-tuple-element.37.own), channel_id=1, source_target_pairs={{0,1},{1,0},{2,3},{3,2},{4,5},{5,4},{6,7},{7,6},{8,9},{9,8},{10,11... | collective-permute-start | bytes 786440 | tf_op jit(solution)/shard_map/ppermute | solution.py:426
  28.8 44.6 %collective-permute-start.13 = (s16[256,512]{1,0:T(8,128)(2,1)S(1)}, s16[256,512]{1,0:T(8,128)(2,1)S(1)}, u32[]{:S(2)}, u32[]{:S(2)}) collective-permute-start(s16[256,512]{1,0:T(8,128)(2,1)S(1)} %get-tuple-element.36.own), channel_id=1, source_target_pairs={{0,1},{1,0},{2,3},{3,2},{4,5},{5,4},{6,7},{7,6},{8,9},{9,8},{10,11... | collective-permute-start | bytes 786440 | tf_op jit(solution)/shard_map/ppermute | solution.py:426

commit v5 on v4

--- a/solution.py
+++ b/solution.py
@@ -9,8 +9,9 @@
 
 SLOTS = 64
 UNIT = 1.0 / 1024
-SCALE = 0.55
-TOLERANCE = 0.16
+SCALE = 0.6
+RESCALE = 1.25
+TOLERANCE = 0.25
 BF16 = jnp.bfloat16
 F32 = jnp.float32
 VMEM = pl.BlockSpec(memory_space=pltpu.VMEM)
@@ -159,6 +160,7 @@
 
 
 def order_kernel(groups, place, blocks, *outs):
+    outs, fits = outs[:-1], outs[-1]
     device, held = place[0], place[1]
     size = blocks.shape[1]
     lane = lax.broadcasted_iota(jnp.int32, (size, size), 1)
@@ -168,9 +170,7 @@
         before = jnp.where((pair_row == pair_column) & (lane < sub), 1.0, 0.0)
         rank = jnp.sum(before, axis=1, keepdims=True).astype(jnp.int32)
         away = (2 * pair_column.astype(jnp.int32)) ^ device
-        x, y = (away >> 2) & 1, (away >> 1) & 1
-        plane = jnp.where(device % 2 == 0, 2 * x + y, 2 * y + x)
-        distance = 8 * ((away >> 3) & 1) + 4 * ((away >> 4) & 1) + plane
+        distance = 8 * ((away >> 3) & 1) + 4 * ((away >> 4) & 1) + ((away >> 1) & 3)
         slot = rank if batch == 0 else SLOTS - 1 - rank
         for distances, out in zip(groups, outs):
             where = jnp.full(rank.shape, -SLOTS, jnp.int32)
@@ -179,6 +179,12 @@
             slots = lax.broadcasted_iota(jnp.int32, (size, out.shape[1]), 1)
             chosen = jnp.where(slots == where + slot, 1.0, 0.0)
             out[batch * size : (batch + 1) * size, :] = chosen.astype(BF16)
+    counts = jnp.zeros((16, 1), F32)
+    for batch in range(blocks.shape[0]):
+        chip = blocks[batch : batch + 1, :] // (2 * held)
+        chips = lax.broadcasted_iota(jnp.int32, (16, size), 0)
+        counts = counts + jnp.sum(jnp.where(chips == chip, 1.0, 0.0), axis=1, keepdims=True)
+    fits[0] = (jnp.max(counts) <= SLOTS).astype(jnp.int32)
 
 
 def order(place, blocks, groups):
@@ -186,9 +192,10 @@
         functools.partial(order_kernel, groups),
         out_shape=[
             jax.ShapeDtypeStruct((blocks.size, SLOTS * len(group)), BF16) for group in groups
-        ],
+        ]
+        + [jax.ShapeDtypeStruct((1,), jnp.int32)],
         in_specs=[SMEM, VMEM],
-        out_specs=[VMEM] * len(groups),
+        out_specs=[VMEM] * len(groups) + [SMEM],
         compiler_params=PARAMS,
         cost_estimate=pl.CostEstimate(flops=10**6, bytes_accessed=10**6, transcendentals=0),
         name="order",
@@ -262,35 +269,68 @@
     inverse[...] = inverse[...] * (1.0 / jnp.sqrt(pivots))
 
 
-def inverse_factor(covariance):
-    size = covariance.shape[0]
-    lane = lax.broadcasted_iota(jnp.int32, (size, size), 1)
-    sub = lax.broadcasted_iota(jnp.int32, (size, size), 0)
-    diagonal = lane == sub
-    eye = jnp.where(diagonal, 1.0, 0.0)
-    half = jnp.where(lane < sub, 1.0, jnp.where(diagonal, 0.5, 0.0))
-    on_diagonal = jnp.where(diagonal, covariance, 0.0)
-    scale_row = lax.rsqrt(jnp.sum(on_diagonal, axis=0, keepdims=True) * (1.0 / SCALE))
-    scale_column = lax.rsqrt(jnp.sum(on_diagonal, axis=1, keepdims=True) * (1.0 / SCALE))
-    scaled = covariance * scale_row * scale_column
+def squared(a):
+    return jnp.sum(a * a)
+
+
+def newton(scaled):
+    size = scaled.shape[0]
+    lane = lax.broadcasted_iota(jnp.int32, (size, size), 1)
+    sub = lax.broadcasted_iota(jnp.int32, (size, size), 0)
+    eye = jnp.where(lane == sub, 1.0, 0.0)
+    half = jnp.where(lane < sub, 1.0, jnp.where(lane == sub, 0.5, 0.0))
 
     def third_order(error):
         low = error * half
         lowb = low.astype(BF16)
         return (nn(lowb, lowb) + half * nt(lowb, lowb)) - low
 
-    m = scaled
-    t = None
-    for step in range(3):
-        u = third_order(m - eye) + eye
-        ub = u.astype(BF16)
-        t = u if t is None else nn(ub, t.astype(BF16))
-        if step < 2:
-            m = nt(nn(ub, m.astype(BF16)).astype(BF16), ub)
-    ts = split(t)
-    error = dot3(nt, split(dot3(nn, ts, split(scaled))), ts) - eye
-    t = t + nn(third_order(error).astype(BF16), ts[0])
-    return t * scale_row, jnp.sum(error * error) <= TOLERANCE * TOLERANCE
+    def begin():
+        first = (third_order(scaled - eye) + eye) * (RESCALE**0.5)
+        fb = first.astype(BF16)
+        error = nt(nn(fb, scaled.astype(BF16)).astype(BF16), fb) - eye
+        return nn((third_order(error) + eye).astype(BF16), fb)
+
+    def step(t):
+        ts = split(t)
+        error = dot3(nt, split(dot3(nn, ts, split(scaled))), ts) - eye
+        return t + nn(third_order(error).astype(BF16), ts[0]), squared(error)
+
+    return begin, step
+
+
+def inverse_factor(covariance, work, inverse, use):
+    size = covariance.shape[0]
+    lane = lax.broadcasted_iota(jnp.int32, (size, size), 1)
+    sub = lax.broadcasted_iota(jnp.int32, (size, size), 0)
+    on_diagonal = jnp.where(lane == sub, covariance, 0.0)
+    scale_row = lax.rsqrt(jnp.sum(on_diagonal, axis=0, keepdims=True) * (1.0 / SCALE))
+    scale_column = lax.rsqrt(jnp.sum(on_diagonal, axis=1, keepdims=True) * (1.0 / SCALE))
+    scaled = covariance * scale_row * scale_column
+    begin, step = newton(scaled)
+    t, residual = step(begin())
+    use(t * scale_row)
+
+    @pl.when(jnp.logical_not(residual <= TOLERANCE**2))
+    def _():
+        inverse[...] = t
+
+        def again(carry):
+            better, left = step(inverse[...])
+            inverse[...] = better
+            return carry[0] + 1, left
+
+        def wanted(carry):
+            return (carry[0] < 6) & jnp.logical_not(carry[1] <= (0.2 * TOLERANCE) ** 2)
+
+        _, left = lax.while_loop(wanted, again, (0, residual))
+        inverse[...] = inverse[...] * scale_row
+
+        @pl.when(jnp.logical_not(left <= (0.2 * TOLERANCE) ** 2))
+        def _():
+            eliminate(covariance, work, inverse)
+
+        use(inverse[...])
 
 
 def whiten(observed, tags, values, load, noise_ref, work, inverse, store):
@@ -316,14 +356,8 @@
         value_part = jnp.sum(t * values, axis=1, keepdims=True)
         store((applied - mean_part).astype(BF16), (noise + value_part - applied).astype(BF16))
 
-    t, good = inverse_factor(covariance)
     load.wait()
-    finish(t)
-
-    @pl.when(jnp.logical_not(good))
-    def _():
-        eliminate(covariance, work, inverse)
-        finish(inverse[...])
+    inverse_factor(covariance, work, inverse, finish)
 
 
 def update(state, whitened, white_innov):
@@ -421,38 +455,38 @@
 CORE, Y, X, NEAR_Z, FAR_Z = 1, 2, 4, 8, 16
 
 
-def swap(value, mask, odd_mask=None):
-    masks = (mask, mask if odd_mask is None else odd_mask)
-    return lax.ppermute(value, AXES, [(i, i ^ masks[i % 2]) for i in range(32)])
-
-
-def along_first(value):
-    return swap(value, X, Y)
-
-
-def along_second(value):
-    return swap(value, Y, X)
-
-
-EARLY = (0, 8, 4, 2, 6, 1, 5, 3, 7, 12, 10, 14)
-LATE = (9, 13, 11, 15)
+def swap(value, mask):
+    return lax.ppermute(value, AXES, [(i, i ^ mask) for i in range(32)])
+
+
+def after(value, other):
+    return lax.optimization_barrier((value, other))[0]
+
+
+def joined(first, second):
+    return jnp.concatenate([first, second], axis=0)
+
+
+EARLY = (0, 4, 8, 12, 2, 10, 5, 13, 1, 9, 3, 11, 6, 7)
+LATE = (14, 15)
 
 
 def by_slots(place, ensemble, blocks, weights):
     keep, send = pick(place, blocks, weights, ensemble)
     own = (keep + swap(send, CORE))[None]
-    near_own = swap(own, NEAR_Z)
-    far = swap(own, FAR_Z)
-    here = jnp.concatenate([own, far], axis=0)
-    first = along_first(here)
-    second = along_second(jnp.concatenate([here, first], axis=0))
+    far, near = swap(own, FAR_Z), swap(own, NEAR_Z)
     near_far = swap(far, NEAR_Z)
-    near = jnp.concatenate([near_own, near_far], axis=0)
-    near_first = along_first(near)
-    near_second = along_second(jnp.concatenate([near, near_first], axis=0))
-    early_places, late_places = order(place, blocks, (EARLY, LATE))
-    early = early_rows(early_places, [own, near_own, far, first, second, near_far, near_first])
-    return late_rows(late_places, early, [near_second])
+    both = joined(own, near)
+    both_x = swap(both, X)
+    far_y = swap(after(far, near), Y)
+    near_far_y = swap(near_far, Y)
+    both_y = swap(after(joined(both, both_x), near_far), Y)
+    far_x = swap(joined(far, far_y), X)
+    near_far_x = swap(joined(near_far, near_far_y), X)
+    early_places, late_places, fits = order(place, blocks, (EARLY, LATE))
+    pieces = [own, far, near, near_far, both_x, far_y, near_far_y, both_y, far_x]
+    early = early_rows(early_places, pieces)
+    return late_rows(late_places, early, [near_far_x]), fits
 
 
 def add_by_swaps(value):
@@ -479,13 +513,9 @@
     by_point = jnp.swapaxes(obs_weights, 1, 2)
     operands = (place, ensemble, obs_blocks, by_point)
     if staged:
-        pair = obs_blocks // (2 * held)
-        counts = jnp.sum(
-            (pair[:, :, None] == jnp.arange(16, dtype=jnp.int32)).astype(jnp.int32), axis=(0, 1)
-        )
-        slotted = by_slots(*operands)
+        slotted, fits = by_slots(*operands)
         own = lax.cond(
-            jnp.max(counts) <= SLOTS,
+            fits[0] == 1,
             lambda slotted, *operands: tuple(slotted),
             lambda slotted, *operands: by_sum(add_by_swaps, 0, *operands),
             slotted,

time: 82.6 us -> 85.9 us (1.040)
  Pallas kernels: 56.8 us -> 61.9 us
  waiting for transfers between devices: 8.65 us -> 7.22 us
    pallas_call x2, Pallas kernels: 51.9 us -> 56.5 us  [batch_call(): pl.pallas_call(kernel, out_shape=outs, in_specs=[SMEM, VMEM, VMEM, ANYWHE...]
    ppermute x10 -> x12, waiting for transfers between devices: 8.65 us -> 7.22 us  [swap(): return lax.ppermute(value, AXES, [(i, i ^ mask) for i in range(32)])]
    ppermute x10 -> x12, starting transfers between devices: 15 us -> 15.4 us  [swap(): return lax.ppermute(value, AXES, [(i, i ^ mask) for i in range(32)])]
  transfers between devices with their start and end apart: 10 -> 12, of which waited for: 7 -> 5; matrix products, arithmetic and copies ran while one was open for 1% -> 0% of each run, Pallas kernels for 55% -> 60%
where the time goes in v5:
time: 85.9 us; the launch traced here: 85.7 us
  Pallas kernels  61.9 us (72%)
  starting transfers between devices  15.4 us (18%)
  waiting for transfers between devices  7.22 us (8%)
  between operations  0.98 us (1%)
    pallas_call x2, Pallas kernels, batch_call(): pl.pallas_call(kernel, out_shape=outs, in_specs=[SMEM, VMEM, VMEM, ANYWHE...  56.5 us
    ppermute x12, starting transfers between devices, swap(): return lax.ppermute(value, AXES, [(i, i ^ mask) for i in range(32)])  15.4 us
    ppermute x12, waiting for transfers between devices, swap(): return lax.ppermute(value, AXES, [(i, i ^ mask) for i in range(32)])  7.22 us
    pallas_call x1, Pallas kernels, pick(): pl.pallas_call(pick_kernel, out_shape=[jax.ShapeDtypeStruct((SLOTS, state...  2.22 us
    pallas_call x1, Pallas kernels, order(): pl.pallas_call(functools.partial(order_kernel, groups), out_shape=[jax.Sh...  1.74 us
  transfers between devices with their start and end apart: 12, of which 5 were waited for; matrix products, arithmetic and copies ran while one was open for 0% of the time, Pallas kernels for 60%

profile of v5, /device:TPU:0, one launch (start us, length us, event | category | flops | bytes accessed | tf_op | source)
XLA Modules:
  0.0 85.7 jit_solution(18435179791040229079)
XLA Ops:
  0.0 0.1 pad_add_fusion.4.place
  0.1 2.2 %pick.1 = (s16[64,512]{1,0:T(8,128)(2,1)S(1)}, s16[64,512]{1,0:T(8,128)(2,1)S(1)}) custom-call(s32[2]{0:T(128)S(1)} %pad_add_fusion.4.place, s32[2,256]{1,0:T(2,128)} %blocks.3, f32[2,4,256]{2,1,0:T(4,128)} %bitcast.5, f32[128,1024]{1,0:T(8,128)} %state_ref.3), custom_call_target="tpu_custom_call" | custom-call | tf_op jit(solution)/shard_map/pick/pallas_call | solution.py:122
  2.3 0.5 collective-permute-start.5
  2.8 0.9 %collective-permute-done.5 = s16[64,512]{1,0:T(8,128)(2,1)S(1)} collective-permute-done((s16[64,512]{1,0:T(8,128)(2,1)S(1)}, s16[64,512]{1,0:T(8,128)(2,1)S(1)}, u32[]{:S(2)}, u32[]{:S(2)}) %collective-permute-start.5) | collective-permute-done | bytes 65568 | tf_op jit(solution)/shard_map/ppermute | solution.py:459
  3.8 3.0 %collective-permute-start.7 = (s16[1,64,512]{2,1,0:T(8,128)(2,1)S(1)}, s16[1,64,512]{2,1,0:T(8,128)(2,1)S(1)}, u32[]{:S(2)}, u32[]{:S(2)}) collective-permute-start(s16[1,64,512]{2,1,0:T(8,128)(2,1)S(1)} %add_bitcast_fusion.refs_0_), channel_id=1, source_target_pairs={{0,8},{1,9},{2,10},{3,11},{4,12},{5,13},{6,14},{7,15},{8,0},{9,1},... | collective-permute-start | bytes 196616 | tf_op jit(solution)/shard_map/ppermute | solution.py:459
  6.7 2.6 %collective-permute-start.6 = (s16[1,64,512]{2,1,0:T(8,128)(2,1)S(1)}, s16[1,64,512]{2,1,0:T(8,128)(2,1)S(1)}, u32[]{:S(2)}, u32[]{:S(2)}) collective-permute-start(s16[1,64,512]{2,1,0:T(8,128)(2,1)S(1)} %add_bitcast_fusion.refs_0_), channel_id=1, source_target_pairs={{0,16},{1,17},{2,18},{3,19},{4,20},{5,21},{6,22},{7,23},{8,24},{9,... | collective-permute-start | bytes 196616 | tf_op jit(solution)/shard_map/ppermute | solution.py:459
  9.3 1.7 %collective-permute-start.9 = (s16[2,64,512]{2,1,0:T(8,128)(2,1)S(1)}, s16[2,64,512]{2,1,0:T(8,128)(2,1)S(1)}, u32[]{:S(2)}, u32[]{:S(2)}) collective-permute-start(s16[2,64,512]{2,1,0:T(8,128)(2,1)S(1)} %pad_add_fusion.1), channel_id=1, source_target_pairs={{0,4},{1,5},{2,6},{3,7},{4,0},{5,1},{6,2},{7,3},{8,12},{9,13},{10,... | collective-permute-start | bytes 393224 | tf_op jit(solution)/shard_map/ppermute | solution.py:459
  11.0 2.0 %collective-permute-done.6.refs_1_ = s16[1,64,512]{2,1,0:T(8,128)(2,1)S(1)} collective-permute-done((s16[1,64,512]{2,1,0:T(8,128)(2,1)S(1)}, s16[1,64,512]{2,1,0:T(8,128)(2,1)S(1)}, u32[]{:S(2)}, u32[]{:S(2)}) %collective-permute-start.6) | collective-permute-done | bytes 65568 | tf_op jit(solution)/shard_map/ppermute | solution.py:459
  13.0 0.3 collective-permute-start.8
  13.3 1.5 %collective-permute-start.10 = (s16[1,64,512]{2,1,0:T(8,128)(2,1)S(1)}, s16[1,64,512]{2,1,0:T(8,128)(2,1)S(1)}, u32[]{:S(2)}, u32[]{:S(2)}) collective-permute-start(s16[1,64,512]{2,1,0:T(8,128)(2,1)S(1)} %collective-permute-done.6.refs_1_), channel_id=1, source_target_pairs={{0,2},{1,3},{2,0},{3,1},{4,6},{5,7},{6,4},{7,5},{8,10},{9,11},{10,... | collective-permute-start | bytes 196616 | tf_op jit(solution)/shard_map/ppermute | solution.py:459
  14.8 2.4 %collective-permute-done.8.refs_3_ = s16[1,64,512]{2,1,0:T(8,128)(2,1)S(1)} collective-permute-done((s16[1,64,512]{2,1,0:T(8,128)(2,1)S(1)}, s16[1,64,512]{2,1,0:T(8,128)(2,1)S(1)}, u32[]{:S(2)}, u32[]{:S(2)}) %collective-permute-start.8) | collective-permute-done | bytes 65568 | tf_op jit(solution)/shard_map/ppermute | solution.py:459
  17.3 1.5 %collective-permute-start.11 = (s16[1,64,512]{2,1,0:T(8,128)(2,1)S(1)}, s16[1,64,512]{2,1,0:T(8,128)(2,1)S(1)}, u32[]{:S(2)}, u32[]{:S(2)}) collective-permute-start(s16[1,64,512]{2,1,0:T(8,128)(2,1)S(1)} %collective-permute-done.8.refs_3_), channel_id=1, source_target_pairs={{0,2},{1,3},{2,0},{3,1},{4,6},{5,7},{6,4},{7,5},{8,10},{9,11},{10,... | collective-permute-start | bytes 196616 | tf_op jit(solution)/shard_map/ppermute | solution.py:459
  18.8 0.6 collective-permute-start.12
  19.4 1.6 %collective-permute-start.13 = (s16[2,64,512]{2,1,0:T(8,128)(2,1)S(1)}, s16[2,64,512]{2,1,0:T(8,128)(2,1)S(1)}, u32[]{:S(2)}, u32[]{:S(2)}) collective-permute-start(s16[2,64,512]{2,1,0:T(8,128)(2,1)S(1)} %pad_add_fusion.2), channel_id=1, source_target_pairs={{0,4},{1,5},{2,6},{3,7},{4,0},{5,1},{6,2},{7,3},{8,12},{9,13},{10,... | collective-permute-start | bytes 393224 | tf_op jit(solution)/shard_map/ppermute | solution.py:459
  20.9 0.8 collective-permute-done.11.refs_6_
  21.8 1.6 %collective-permute-start.14 = (s16[2,64,512]{2,1,0:T(8,128)(2,1)S(1)}, s16[2,64,512]{2,1,0:T(8,128)(2,1)S(1)}, u32[]{:S(2)}, u32[]{:S(2)}) collective-permute-start(s16[2,64,512]{2,1,0:T(8,128)(2,1)S(1)} %pad_add_fusion.3), channel_id=1, source_target_pairs={{0,4},{1,5},{2,6},{3,7},{4,0},{5,1},{6,2},{7,3},{8,12},{9,13},{10,... | collective-permute-start | bytes 393224 | tf_op jit(solution)/shard_map/ppermute | solution.py:459
  23.4 1.7 %order.1 = (bf16[512,896]{1,0:T(8,128)(2,1)S(1)}, bf16[512,128]{1,0:T(8,128)(2,1)S(1)}, s32[1]{0:T(128)}) custom-call(s32[2]{0:T(128)S(1)} %pad_add_fusion.4.place, s32[2,256]{1,0:T(2,128)} %blocks.3), custom_call_target="tpu_custom_call" | custom-call | flops 1000000 | bytes 1000000 | tf_op jit(solution)/shard_map/order/pallas_call | solution.py:191
  25.8 1.0 %early_rows.1.early = f32[512,512]{1,0:T(8,128)S(1)} custom-call(bf16[512,896]{1,0:T(8,128)(2,1)S(1)} %get-tuple-element.37.chosen, s16[1,64,512]{2,1,0:T(8,128)(2,1)S(1)} %add_bitcast_fusion.refs_0_, s16[1,64,512]{2,1,0:T(8,128)(2,1)S(1)} %collective-permute-done.6.refs_1_, s16[1,64,512]{2,1,0:T(8,128)(2,1)S(1)} %collective-permute-done.7.refs_2_, ...), custom_call_target="tpu_custom_call" | custom-call | flops 1000000000 | bytes 4000000 | tf_op jit(solution)/shard_map/early_rows/pallas_call | solution.py:226
  26.8 0.4 late_rows.1
  27.4 0.1 collective-permute-start.16
  27.5 0.5 collective-permute-start.15
  27.9 1.0 %collective-permute-done.16.other = bf16[256,512]{1,0:T(8,128)(2,1)S(1)} collective-permute-done((bf16[256,512]{1,0:T(8,128)(2,1)S(1)}, bf16[256,512]{1,0:T(8,128)(2,1)S(1)}, u32[]{:S(2)}, u32[]{:S(2)}) %collective-permute-start.16) | collective-permute-done | bytes 262176 | tf_op jit(solution)/shard_map/ppermute | solution.py:459
  29.0 48.2 %first_batch.1 = (bf16[256,1024]{1,0:T(8,128)(2,1)S(1)}, bf16[256,1024]{1,0:T(8,128)(2,1)S(1)}) custom-call(s32[2]{0:T(128)S(1)} %pad_add_fusion.4.place, s32[2,256]{1,0:T(2,128)S(1)} %copy-done.1, f32[2,256]{1,0:T(2,128)S(1)} %copy-done.2, bf16[2,256,1024]{2,1,0:T(8,128)(2,1)S(1)} %copy-done, bf16[256,512]{1,0:T(8,128)(2,1)S(1)} %get-tuple-element.43.own, ...), custom_call_target="tpu_custom_call" | custom-call | tf_op jit(solution)/shard_map/first_batch/pallas_call | solution.py:427
  77.3 8.3 %second_batch.1 = f32[128,1024]{1,0:T(8,128)} custom-call(s32[2]{0:T(128)S(1)} %pad_add_fusion.4.place, s32[2,256]{1,0:T(2,128)S(1)} %copy-done.1, f32[2,256]{1,0:T(2,128)S(1)} %copy-done.2, bf16[2,256,1024]{2,1,0:T(8,128)(2,1)S(1)} %copy-done, s16[256,512]{1,0:T(8,128)(2,1)S(1)} %get-tuple-element.42.own, ...), custom_call_target="tpu_custom_call" | custom-call | tf_op jit(solution)/shard_map/second_batch/pallas_call | solution.py:427
  (27 shorter events, 0.3 us)
Async XLA Ops:
  2.3 1.4 %collective-permute-start.5 = (s16[64,512]{1,0:T(8,128)(2,1)S(1)}, s16[64,512]{1,0:T(8,128)(2,1)S(1)}, u32[]{:S(2)}, u32[]{:S(2)}) collective-permute-start(s16[64,512]{1,0:T(8,128)(2,1)S(1)} %get-tuple-element.39), channel_id=1, source_target_pairs={{0,1},{1,0},{2,3},{3,2},{4,5},{5,4},{6,7},{7,6},{8,9},{9,8},{10,11... | collective-permute-start | bytes 196616 | tf_op jit(solution)/shard_map/ppermute | solution.py:459
  3.8 5.6 %collective-permute-start.7 = (s16[1,64,512]{2,1,0:T(8,128)(2,1)S(1)}, s16[1,64,512]{2,1,0:T(8,128)(2,1)S(1)}, u32[]{:S(2)}, u32[]{:S(2)}) collective-permute-start(s16[1,64,512]{2,1,0:T(8,128)(2,1)S(1)} %add_bitcast_fusion.refs_0_), channel_id=1, source_target_pairs={{0,8},{1,9},{2,10},{3,11},{4,12},{5,13},{6,14},{7,15},{8,0},{9,1},... | collective-permute-start | bytes 196616 | tf_op jit(solution)/shard_map/ppermute | solution.py:459
  6.7 6.2 %collective-permute-start.6 = (s16[1,64,512]{2,1,0:T(8,128)(2,1)S(1)}, s16[1,64,512]{2,1,0:T(8,128)(2,1)S(1)}, u32[]{:S(2)}, u32[]{:S(2)}) collective-permute-start(s16[1,64,512]{2,1,0:T(8,128)(2,1)S(1)} %add_bitcast_fusion.refs_0_), channel_id=1, source_target_pairs={{0,16},{1,17},{2,18},{3,19},{4,20},{5,21},{6,22},{7,23},{8,24},{9,... | collective-permute-start | bytes 196616 | tf_op jit(solution)/shard_map/ppermute | solution.py:459
  9.3 9.4 %collective-permute-start.9 = (s16[2,64,512]{2,1,0:T(8,128)(2,1)S(1)}, s16[2,64,512]{2,1,0:T(8,128)(2,1)S(1)}, u32[]{:S(2)}, u32[]{:S(2)}) collective-permute-start(s16[2,64,512]{2,1,0:T(8,128)(2,1)S(1)} %pad_add_fusion.1), channel_id=1, source_target_pairs={{0,4},{1,5},{2,6},{3,7},{4,0},{5,1},{6,2},{7,3},{8,12},{9,13},{10,... | collective-permute-start | bytes 393224 | tf_op jit(solution)/shard_map/ppermute | solution.py:459
  13.0 4.3 %collective-permute-start.8 = (s16[1,64,512]{2,1,0:T(8,128)(2,1)S(1)}, s16[1,64,512]{2,1,0:T(8,128)(2,1)S(1)}, u32[]{:S(2)}, u32[]{:S(2)}) collective-permute-start(s16[1,64,512]{2,1,0:T(8,128)(2,1)S(1)} %collective-permute-done.6.refs_1_), channel_id=1, source_target_pairs={{0,8},{1,9},{2,10},{3,11},{4,12},{5,13},{6,14},{7,15},{8,0},{9,1},... | collective-permute-start | bytes 196616 | tf_op jit(solution)/shard_map/ppermute | solution.py:459
  13.3 6.1 %collective-permute-start.10 = (s16[1,64,512]{2,1,0:T(8,128)(2,1)S(1)}, s16[1,64,512]{2,1,0:T(8,128)(2,1)S(1)}, u32[]{:S(2)}, u32[]{:S(2)}) collective-permute-start(s16[1,64,512]{2,1,0:T(8,128)(2,1)S(1)} %collective-permute-done.6.refs_1_), channel_id=1, source_target_pairs={{0,2},{1,3},{2,0},{3,1},{4,6},{5,7},{6,4},{7,5},{8,10},{9,11},{10,... | collective-permute-start | bytes 196616 | tf_op jit(solution)/shard_map/ppermute | solution.py:459
  17.3 4.5 %collective-permute-start.11 = (s16[1,64,512]{2,1,0:T(8,128)(2,1)S(1)}, s16[1,64,512]{2,1,0:T(8,128)(2,1)S(1)}, u32[]{:S(2)}, u32[]{:S(2)}) collective-permute-start(s16[1,64,512]{2,1,0:T(8,128)(2,1)S(1)} %collective-permute-done.8.refs_3_), channel_id=1, source_target_pairs={{0,2},{1,3},{2,0},{3,1},{4,6},{5,7},{6,4},{7,5},{8,10},{9,11},{10,... | collective-permute-start | bytes 196616 | tf_op jit(solution)/shard_map/ppermute | solution.py:459
  18.8 7.0 %collective-permute-start.12 = (s16[4,64,512]{2,1,0:T(8,128)(2,1)S(1)}, s16[4,64,512]{2,1,0:T(8,128)(2,1)S(1)}, u32[]{:S(2)}, u32[]{:S(2)}) collective-permute-start(s16[4,64,512]{2,1,0:T(8,128)(2,1)S(1)} %pad_add_fusion), channel_id=1, source_target_pairs={{0,2},{1,3},{2,0},{3,1},{4,6},{5,7},{6,4},{7,5},{8,10},{9,11},{10,... | collective-permute-start | bytes 786440 | tf_op jit(solution)/shard_map/ppermute | solution.py:459
  19.4 6.4 %collective-permute-start.13 = (s16[2,64,512]{2,1,0:T(8,128)(2,1)S(1)}, s16[2,64,512]{2,1,0:T(8,128)(2,1)S(1)}, u32[]{:S(2)}, u32[]{:S(2)}) collective-permute-start(s16[2,64,512]{2,1,0:T(8,128)(2,1)S(1)} %pad_add_fusion.2), channel_id=1, source_target_pairs={{0,4},{1,5},{2,6},{3,7},{4,0},{5,1},{6,2},{7,3},{8,12},{9,13},{10,... | collective-permute-start | bytes 393224 | tf_op jit(solution)/shard_map/ppermute | solution.py:459
  21.8 5.0 %collective-permute-start.14 = (s16[2,64,512]{2,1,0:T(8,128)(2,1)S(1)}, s16[2,64,512]{2,1,0:T(8,128)(2,1)S(1)}, u32[]{:S(2)}, u32[]{:S(2)}) collective-permute-start(s16[2,64,512]{2,1,0:T(8,128)(2,1)S(1)} %pad_add_fusion.3), channel_id=1, source_target_pairs={{0,4},{1,5},{2,6},{3,7},{4,0},{5,1},{6,2},{7,3},{8,12},{9,13},{10,... | collective-permute-start | bytes 393224 | tf_op jit(solution)/shard_map/ppermute | solution.py:459
  25.8 1.5 %copy-start.3 = (f32[128,1024]{1,0:T(8,128)S(1)}, f32[128,1024]{1,0:T(8,128)}, u32[]{:S(2)}) copy-start(f32[128,1024]{1,0:T(8,128)} %state_ref.3) | copy-start | bytes 1572868
  25.8 1.5 %copy-start.4 = (f32[2,256,4]{1,2,0:T(4,128)S(1)}, f32[2,256,4]{1,2,0:T(4,128)}, u32[]{:S(2)}) copy-start(f32[2,256,4]{1,2,0:T(4,128)} %param.10) | copy-start | bytes 24580
  25.8 1.5 %copy-start.5 = (s32[2,256]{1,0:T(2,128)S(1)}, s32[2,256]{1,0:T(2,128)}, u32[]{:S(2)}) copy-start(s32[2,256]{1,0:T(2,128)} %blocks.3) | copy-start | bytes 6148
  27.3 1.7 %copy-start = (bf16[2,256,1024]{2,1,0:T(8,128)(2,1)S(1)}, bf16[2,256,1024]{2,1,0:T(8,128)(2,1)}, u32[]{:S(2)}) copy-start(bf16[2,256,1024]{2,1,0:T(8,128)(2,1)} %noise_ref.3) | copy-start | bytes 3145732
  27.3 1.7 %copy-start.1 = (s32[2,256]{1,0:T(2,128)S(1)}, s32[2,256]{1,0:T(2,128)}, u32[]{:S(2)}) copy-start(s32[2,256]{1,0:T(2,128)} %tags.3) | copy-start | bytes 6148
  27.3 1.7 %copy-start.2 = (f32[2,256]{1,0:T(2,128)S(1)}, f32[2,256]{1,0:T(2,128)}, u32[]{:S(2)}) copy-start(f32[2,256]{1,0:T(2,128)} %values.3) | copy-start | bytes 6148
  27.4 1.6 %collective-permute-start.16 = (bf16[256,512]{1,0:T(8,128)(2,1)S(1)}, bf16[256,512]{1,0:T(8,128)(2,1)S(1)}, u32[]{:S(2)}, u32[]{:S(2)}) collective-permute-start(bf16[256,512]{1,0:T(8,128)(2,1)S(1)} %get-tuple-element.43.own), channel_id=1, source_target_pairs={{0,1},{1,0},{2,3},{3,2},{4,5},{5,4},{6,7},{7,6},{8,9},{9,8},{10,11... | collective-permute-start | bytes 786440 | tf_op jit(solution)/shard_map/ppermute | solution.py:459
  27.5 49.8 %collective-permute-start.15 = (s16[256,512]{1,0:T(8,128)(2,1)S(1)}, s16[256,512]{1,0:T(8,128)(2,1)S(1)}, u32[]{:S(2)}, u32[]{:S(2)}) collective-permute-start(s16[256,512]{1,0:T(8,128)(2,1)S(1)} %get-tuple-element.42.own), channel_id=1, source_target_pairs={{0,1},{1,0},{2,3},{3,2},{4,5},{5,4},{6,7},{7,6},{8,9},{9,8},{10,11... | collective-permute-start | bytes 786440 | tf_op jit(solution)/shard_map/ppermute | solution.py:459

commit v6 on v5

--- a/solution.py
+++ b/solution.py
@@ -8,6 +8,7 @@
 from jax.sharding import PartitionSpec as P
 
 SLOTS = 64
+LANES = 128
 UNIT = 1.0 / 1024
 SCALE = 0.6
 RESCALE = 1.25
@@ -165,20 +166,24 @@
     size = blocks.shape[1]
     lane = lax.broadcasted_iota(jnp.int32, (size, size), 1)
     sub = lax.broadcasted_iota(jnp.int32, (size, size), 0)
+    lanes = lax.broadcasted_iota(jnp.int32, (size, LANES), 1)
+    ones = jnp.ones((size, LANES), BF16)
     for batch in range(blocks.shape[0]):
-        pair_row, pair_column = both_ways(blocks[batch : batch + 1, :] // (2 * held))
-        before = jnp.where((pair_row == pair_column) & (lane < sub), 1.0, 0.0)
-        rank = jnp.sum(before, axis=1, keepdims=True).astype(jnp.int32)
-        away = (2 * pair_column.astype(jnp.int32)) ^ device
+        pair_row = (blocks[batch : batch + 1, :] // (2 * held)).astype(F32)
+        pair = nn(jnp.where(lane == sub, pair_row, 0.0).astype(BF16), ones)
+        wide = jnp.concatenate([pair] * (size // LANES), axis=1)
+        before = jnp.where((pair_row == wide) & (lane < sub), 1.0, 0.0)
+        rank = nn(before.astype(BF16), ones).astype(jnp.int32)
+        away = (2 * pair.astype(jnp.int32)) ^ device
         distance = 8 * ((away >> 3) & 1) + 4 * ((away >> 4) & 1) + ((away >> 1) & 3)
         slot = rank if batch == 0 else SLOTS - 1 - rank
         for distances, out in zip(groups, outs):
             where = jnp.full(rank.shape, -SLOTS, jnp.int32)
             for index, known in enumerate(distances):
                 where = jnp.where(distance == known, SLOTS * index, where)
-            slots = lax.broadcasted_iota(jnp.int32, (size, out.shape[1]), 1)
-            chosen = jnp.where(slots == where + slot, 1.0, 0.0)
-            out[batch * size : (batch + 1) * size, :] = chosen.astype(BF16)
+            for start in range(0, out.shape[1], LANES):
+                chosen = jnp.where(where + slot == lanes + start, 1.0, 0.0).astype(BF16)
+                out[batch * size : (batch + 1) * size, start : start + LANES] = chosen
     counts = jnp.zeros((16, 1), F32)
     for batch in range(blocks.shape[0]):
         chip = blocks[batch : batch + 1, :] // (2 * held)
@@ -337,15 +342,13 @@
     members = observed.shape[1]
     size = observed.shape[0]
     mean = row_mean(observed)
-    parts = split(observed - mean)
     lane = lax.broadcasted_iota(jnp.int32, (size, size), 1)
     sub = lax.broadcasted_iota(jnp.int32, (size, size), 0)
     variance_row = jnp.where(tags == 0, 0.5, 2.0)
-    variance = column(variance_row)
     mean_row = jnp.sum(jnp.where(lane == sub, mean, 0.0), axis=0, keepdims=True)
-    covariance = dot3(nt, parts, parts) * (1.0 / (members - 1))
-    covariance = covariance + jnp.where(lane == sub, variance, 0.0)
     exact = observed.astype(BF16)
+    covariance = (nt(exact, exact) - mean * (mean_row * members)) * (1.0 / (members - 1))
+    covariance = covariance + jnp.where(lane == sub, variance_row, 0.0)
 
     def finish(t):
         th, tl = split(t)
@@ -360,10 +363,15 @@
     inverse_factor(covariance, work, inverse, finish)
 
 
+def row_sums(array):
+    return nt(jnp.ones((8, array.shape[1]), BF16), array)[:1, :]
+
+
 def update(state, whitened, white_innov):
     members = state.shape[1]
-    sh, sl = split(state - row_mean(state))
-    ph, plow = split(nt(sh, whitened) + nt(sl, whitened))
+    sh, sl = split(state)
+    projected = nt(sh, whitened) + nt(sl, whitened) - row_mean(state) * row_sums(whitened)
+    ph, plow = split(projected)
     return state + (nn(ph, white_innov) + nn(plow, white_innov)) * (1.0 / (members - 1))
 
 
@@ -410,9 +418,8 @@
     load_state = pltpu.make_async_copy(state_ref, state, loads.at[1])
     load_state.start()
     load.start()
-    prior = both_halves(place, own, other) * UNIT
     w, v = whitened[...], white_innov[...]
-    observed = rounded(update(prior, w, v))
+    observed = rounded(update(both_halves(place, own, other), w, v) * UNIT)
     load_state.wait()
     first = update(state[...], w, v)
 
@@ -467,7 +474,7 @@
     return jnp.concatenate([first, second], axis=0)
 
 
-EARLY = (0, 4, 8, 12, 2, 10, 5, 13, 1, 9, 3, 11, 6, 7)
+EARLY = (0, 4, 8, 12, 2, 10, 5, 1, 13, 9, 3, 11, 6, 7)
 LATE = (14, 15)
 
 
@@ -478,10 +485,10 @@
     near_far = swap(far, NEAR_Z)
     both = joined(own, near)
     both_x = swap(both, X)
-    far_y = swap(after(far, near), Y)
+    far_y = swap(after(joined(far, own), near), Y)
     near_far_y = swap(near_far, Y)
-    both_y = swap(after(joined(both, both_x), near_far), Y)
-    far_x = swap(joined(far, far_y), X)
+    both_y = swap(after(joined(near, both_x), near_far), Y)
+    far_x = swap(joined(far, far_y[:1]), X)
     near_far_x = swap(joined(near_far, near_far_y), X)
     early_places, late_places, fits = order(place, blocks, (EARLY, LATE))
     pieces = [own, far, near, near_far, both_x, far_y, near_far_y, both_y, far_x]

time: 85.9 us -> 85.3 us (level)
  waiting for transfers between devices: 7.22 us -> 10.3 us
  starting transfers between devices: 15.4 us -> 13.4 us
  Pallas kernels: 61.9 us -> 60.3 us
    ppermute x12, waiting for transfers between devices: 7.22 us -> 10.3 us  [swap(): return lax.ppermute(value, AXES, [(i, i ^ mask) for i in range(32)])]
    ppermute x12, starting transfers between devices: 15.4 us -> 13.4 us  [swap(): return lax.ppermute(value, AXES, [(i, i ^ mask) for i in range(32)])]
    pallas_call x2, Pallas kernels: 56.5 us -> 54.6 us  [batch_call(): pl.pallas_call(kernel, out_shape=outs, in_specs=[SMEM, VMEM, VMEM, ANYWHE...]
  transfers between devices with their start and end apart: 12 -> 12, of which waited for: 5 -> 6; matrix products, arithmetic and copies ran while one was open for 0% -> 0% of each run, Pallas kernels for 60% -> 59%
where the time goes in v6:
time: 85.3 us; the launch traced here: 85.1 us
  Pallas kernels  60.3 us (71%)
  starting transfers between devices  13.4 us (16%)
  waiting for transfers between devices  10.3 us (12%)
  between operations  0.95 us (1%)
    pallas_call x2, Pallas kernels, batch_call(): pl.pallas_call(kernel, out_shape=outs, in_specs=[SMEM, VMEM, VMEM, ANYWHE...  54.6 us
    ppermute x12, starting transfers between devices, swap(): return lax.ppermute(value, AXES, [(i, i ^ mask) for i in range(32)])  13.4 us
    ppermute x12, waiting for transfers between devices, swap(): return lax.ppermute(value, AXES, [(i, i ^ mask) for i in range(32)])  10.3 us
    pallas_call x1, Pallas kernels, pick(): pl.pallas_call(pick_kernel, out_shape=[jax.ShapeDtypeStruct((SLOTS, state...  2.22 us
    pallas_call x1, Pallas kernels, order(): pl.pallas_call(functools.partial(order_kernel, groups), out_shape=[jax.Sh...  2.03 us
  transfers between devices with their start and end apart: 12, of which 6 were waited for; matrix products, arithmetic and copies ran while one was open for 0% of the time, Pallas kernels for 59%

profile of v6, /device:TPU:0, one launch (start us, length us, event | category | flops | bytes accessed | tf_op | source)
XLA Modules:
  0.0 85.1 jit_solution(9894189035227172936)
XLA Ops:
  0.0 0.1 pad_add_fusion.5.place
  0.1 2.2 %pick.1 = (s16[64,512]{1,0:T(8,128)(2,1)S(1)}, s16[64,512]{1,0:T(8,128)(2,1)S(1)}) custom-call(s32[2]{0:T(128)S(1)} %pad_add_fusion.5.place, s32[2,256]{1,0:T(2,128)} %blocks.3, f32[2,4,256]{2,1,0:T(4,128)} %bitcast.5, f32[128,1024]{1,0:T(8,128)} %state_ref.3), custom_call_target="tpu_custom_call" | custom-call | tf_op jit(solution)/shard_map/pick/pallas_call | solution.py:123
  2.3 0.5 collective-permute-start.5
  2.8 0.9 %collective-permute-done.5 = s16[64,512]{1,0:T(8,128)(2,1)S(1)} collective-permute-done((s16[64,512]{1,0:T(8,128)(2,1)S(1)}, s16[64,512]{1,0:T(8,128)(2,1)S(1)}, u32[]{:S(2)}, u32[]{:S(2)}) %collective-permute-start.5) | collective-permute-done | bytes 65568 | tf_op jit(solution)/shard_map/ppermute | solution.py:466
  3.8 3.0 %collective-permute-start.7 = (s16[1,64,512]{2,1,0:T(8,128)(2,1)S(1)}, s16[1,64,512]{2,1,0:T(8,128)(2,1)S(1)}, u32[]{:S(2)}, u32[]{:S(2)}) collective-permute-start(s16[1,64,512]{2,1,0:T(8,128)(2,1)S(1)} %add_bitcast_fusion.refs_0_), channel_id=1, source_target_pairs={{0,8},{1,9},{2,10},{3,11},{4,12},{5,13},{6,14},{7,15},{8,0},{9,1},... | collective-permute-start | bytes 196616 | tf_op jit(solution)/shard_map/ppermute | solution.py:466
  6.7 2.6 %collective-permute-start.6 = (s16[1,64,512]{2,1,0:T(8,128)(2,1)S(1)}, s16[1,64,512]{2,1,0:T(8,128)(2,1)S(1)}, u32[]{:S(2)}, u32[]{:S(2)}) collective-permute-start(s16[1,64,512]{2,1,0:T(8,128)(2,1)S(1)} %add_bitcast_fusion.refs_0_), channel_id=1, source_target_pairs={{0,16},{1,17},{2,18},{3,19},{4,20},{5,21},{6,22},{7,23},{8,24},{9,... | collective-permute-start | bytes 196616 | tf_op jit(solution)/shard_map/ppermute | solution.py:466
  9.3 3.7 %collective-permute-done.6.refs_1_ = s16[1,64,512]{2,1,0:T(8,128)(2,1)S(1)} collective-permute-done((s16[1,64,512]{2,1,0:T(8,128)(2,1)S(1)}, s16[1,64,512]{2,1,0:T(8,128)(2,1)S(1)}, u32[]{:S(2)}, u32[]{:S(2)}) %collective-permute-start.6) | collective-permute-done | bytes 65568 | tf_op jit(solution)/shard_map/ppermute | solution.py:466
  13.0 1.6 %collective-permute-start.9 = (s16[2,64,512]{2,1,0:T(8,128)(2,1)S(1)}, s16[2,64,512]{2,1,0:T(8,128)(2,1)S(1)}, u32[]{:S(2)}, u32[]{:S(2)}) collective-permute-start(s16[2,64,512]{2,1,0:T(8,128)(2,1)S(1)} %get-tuple-element.49), channel_id=1, source_target_pairs={{0,4},{1,5},{2,6},{3,7},{4,0},{5,1},{6,2},{7,3},{8,12},{9,13},{10,... | collective-permute-start | bytes 393224 | tf_op jit(solution)/shard_map/ppermute | solution.py:466
  14.6 0.3 collective-permute-start.8
  14.9 1.5 %collective-permute-start.10 = (s16[2,64,512]{2,1,0:T(8,128)(2,1)S(1)}, s16[2,64,512]{2,1,0:T(8,128)(2,1)S(1)}, u32[]{:S(2)}, u32[]{:S(2)}) collective-permute-start(s16[2,64,512]{2,1,0:T(8,128)(2,1)S(1)} %get-tuple-element.40), channel_id=1, source_target_pairs={{0,2},{1,3},{2,0},{3,1},{4,6},{5,7},{6,4},{7,5},{8,10},{9,11},{10,... | collective-permute-start | bytes 393224 | tf_op jit(solution)/shard_map/ppermute | solution.py:466
  16.4 2.4 %collective-permute-done.8.refs_3_ = s16[1,64,512]{2,1,0:T(8,128)(2,1)S(1)} collective-permute-done((s16[1,64,512]{2,1,0:T(8,128)(2,1)S(1)}, s16[1,64,512]{2,1,0:T(8,128)(2,1)S(1)}, u32[]{:S(2)}, u32[]{:S(2)}) %collective-permute-start.8) | collective-permute-done | bytes 65568 | tf_op jit(solution)/shard_map/ppermute | solution.py:466
  18.8 1.5 %collective-permute-start.11 = (s16[1,64,512]{2,1,0:T(8,128)(2,1)S(1)}, s16[1,64,512]{2,1,0:T(8,128)(2,1)S(1)}, u32[]{:S(2)}, u32[]{:S(2)}) collective-permute-start(s16[1,64,512]{2,1,0:T(8,128)(2,1)S(1)} %collective-permute-done.8.refs_3_), channel_id=1, source_target_pairs={{0,2},{1,3},{2,0},{3,1},{4,6},{5,7},{6,4},{7,5},{8,10},{9,11},{10,... | collective-permute-start | bytes 196616 | tf_op jit(solution)/shard_map/ppermute | solution.py:466
  20.4 0.6 collective-permute-start.12
  21.0 0.6 collective-permute-start.13
  21.6 1.5 %collective-permute-done.11.refs_6_ = s16[1,64,512]{2,1,0:T(8,128)(2,1)S(1)} collective-permute-done((s16[1,64,512]{2,1,0:T(8,128)(2,1)S(1)}, s16[1,64,512]{2,1,0:T(8,128)(2,1)S(1)}, u32[]{:S(2)}, u32[]{:S(2)}) %collective-permute-start.11) | collective-permute-done | bytes 65568 | tf_op jit(solution)/shard_map/ppermute | solution.py:466
  23.1 0.6 collective-permute-start.14
  23.7 2.0 %order.1 = (bf16[512,896]{1,0:T(8,128)(2,1)S(1)}, bf16[512,128]{1,0:T(8,128)(2,1)S(1)}, s32[1]{0:T(128)}) custom-call(s32[2]{0:T(128)S(1)} %pad_add_fusion.5.place, s32[2,256]{1,0:T(2,128)S(1)} %copy-done.5), custom_call_target="tpu_custom_call" | custom-call | flops 1000000 | bytes 1000000 | tf_op jit(solution)/shard_map/order/pallas_call | solution.py:196
  26.4 1.0 %early_rows.1.early = f32[512,512]{1,0:T(8,128)S(1)} custom-call(bf16[512,896]{1,0:T(8,128)(2,1)S(1)} %get-tuple-element.37.chosen, s16[1,64,512]{2,1,0:T(8,128)(2,1)S(1)} %add_bitcast_fusion.refs_0_, s16[1,64,512]{2,1,0:T(8,128)(2,1)S(1)} %collective-permute-done.6.refs_1_, s16[1,64,512]{2,1,0:T(8,128)(2,1)S(1)} %collective-permute-done.7.refs_2_, ...), custom_call_target="tpu_custom_call" | custom-call | flops 1000000000 | bytes 4000000 | tf_op jit(solution)/shard_map/early_rows/pallas_call | solution.py:231
  27.4 0.7 collective-permute-done.14.refs_0_
  28.1 0.4 late_rows.1
  28.7 0.5 collective-permute-start.15
  29.2 1.0 %collective-permute-done.16.other = bf16[256,512]{1,0:T(8,128)(2,1)S(1)} collective-permute-done((bf16[256,512]{1,0:T(8,128)(2,1)S(1)}, bf16[256,512]{1,0:T(8,128)(2,1)S(1)}, u32[]{:S(2)}, u32[]{:S(2)}) %collective-permute-start.16) | collective-permute-done | bytes 262176 | tf_op jit(solution)/shard_map/ppermute | solution.py:466
  30.3 47.4 %first_batch.1 = (bf16[256,1024]{1,0:T(8,128)(2,1)S(1)}, bf16[256,1024]{1,0:T(8,128)(2,1)S(1)}) custom-call(s32[2]{0:T(128)S(1)} %pad_add_fusion.5.place, s32[2,256]{1,0:T(2,128)S(1)} %copy-done.1, f32[2,256]{1,0:T(2,128)S(1)} %copy-done.2, bf16[2,256,1024]{2,1,0:T(8,128)(2,1)S(1)} %copy-done, bf16[256,512]{1,0:T(8,128)(2,1)S(1)} %get-tuple-element.43.own, ...), custom_call_target="tpu_custom_call" | custom-call | tf_op jit(solution)/shard_map/first_batch/pallas_call | solution.py:434
  77.7 7.2 %second_batch.1 = f32[128,1024]{1,0:T(8,128)} custom-call(s32[2]{0:T(128)S(1)} %pad_add_fusion.5.place, s32[2,256]{1,0:T(2,128)S(1)} %copy-done.1, f32[2,256]{1,0:T(2,128)S(1)} %copy-done.2, bf16[2,256,1024]{2,1,0:T(8,128)(2,1)S(1)} %copy-done, s16[256,512]{1,0:T(8,128)(2,1)S(1)} %get-tuple-element.42.own, ...), custom_call_target="tpu_custom_call" | custom-call | tf_op jit(solution)/shard_map/second_batch/pallas_call | solution.py:434
  (28 shorter events, 0.3 us)
Async XLA Ops:
  0.0 23.7 %copy-start.5 = (s32[2,256]{1,0:T(2,128)S(1)}, s32[2,256]{1,0:T(2,128)}, u32[]{:S(2)}) copy-start(s32[2,256]{1,0:T(2,128)} %blocks.3) | copy-start | bytes 6148
  2.3 1.4 %collective-permute-start.5 = (s16[64,512]{1,0:T(8,128)(2,1)S(1)}, s16[64,512]{1,0:T(8,128)(2,1)S(1)}, u32[]{:S(2)}, u32[]{:S(2)}) collective-permute-start(s16[64,512]{1,0:T(8,128)(2,1)S(1)} %get-tuple-element.39), channel_id=1, source_target_pairs={{0,1},{1,0},{2,3},{3,2},{4,5},{5,4},{6,7},{7,6},{8,9},{9,8},{10,11... | collective-permute-start | bytes 196616 | tf_op jit(solution)/shard_map/ppermute | solution.py:466
  3.8 5.6 %collective-permute-start.7 = (s16[1,64,512]{2,1,0:T(8,128)(2,1)S(1)}, s16[1,64,512]{2,1,0:T(8,128)(2,1)S(1)}, u32[]{:S(2)}, u32[]{:S(2)}) collective-permute-start(s16[1,64,512]{2,1,0:T(8,128)(2,1)S(1)} %add_bitcast_fusion.refs_0_), channel_id=1, source_target_pairs={{0,8},{1,9},{2,10},{3,11},{4,12},{5,13},{6,14},{7,15},{8,0},{9,1},... | collective-permute-start | bytes 196616 | tf_op jit(solution)/shard_map/ppermute | solution.py:466
  6.7 6.2 %collective-permute-start.6 = (s16[1,64,512]{2,1,0:T(8,128)(2,1)S(1)}, s16[1,64,512]{2,1,0:T(8,128)(2,1)S(1)}, u32[]{:S(2)}, u32[]{:S(2)}) collective-permute-start(s16[1,64,512]{2,1,0:T(8,128)(2,1)S(1)} %add_bitcast_fusion.refs_0_), channel_id=1, source_target_pairs={{0,16},{1,17},{2,18},{3,19},{4,20},{5,21},{6,22},{7,23},{8,24},{9,... | collective-permute-start | bytes 196616 | tf_op jit(solution)/shard_map/ppermute | solution.py:466
  13.0 7.3 %collective-permute-start.9 = (s16[2,64,512]{2,1,0:T(8,128)(2,1)S(1)}, s16[2,64,512]{2,1,0:T(8,128)(2,1)S(1)}, u32[]{:S(2)}, u32[]{:S(2)}) collective-permute-start(s16[2,64,512]{2,1,0:T(8,128)(2,1)S(1)} %get-tuple-element.49), channel_id=1, source_target_pairs={{0,4},{1,5},{2,6},{3,7},{4,0},{5,1},{6,2},{7,3},{8,12},{9,13},{10,... | collective-permute-start | bytes 393224 | tf_op jit(solution)/shard_map/ppermute | solution.py:466
  14.6 4.3 %collective-permute-start.8 = (s16[1,64,512]{2,1,0:T(8,128)(2,1)S(1)}, s16[1,64,512]{2,1,0:T(8,128)(2,1)S(1)}, u32[]{:S(2)}, u32[]{:S(2)}) collective-permute-start(s16[1,64,512]{2,1,0:T(8,128)(2,1)S(1)} %collective-permute-done.6.refs_1_), channel_id=1, source_target_pairs={{0,8},{1,9},{2,10},{3,11},{4,12},{5,13},{6,14},{7,15},{8,0},{9,1},... | collective-permute-start | bytes 196616 | tf_op jit(solution)/shard_map/ppermute | solution.py:466
  14.9 6.1 %collective-permute-start.10 = (s16[2,64,512]{2,1,0:T(8,128)(2,1)S(1)}, s16[2,64,512]{2,1,0:T(8,128)(2,1)S(1)}, u32[]{:S(2)}, u32[]{:S(2)}) collective-permute-start(s16[2,64,512]{2,1,0:T(8,128)(2,1)S(1)} %get-tuple-element.40), channel_id=1, source_target_pairs={{0,2},{1,3},{2,0},{3,1},{4,6},{5,7},{6,4},{7,5},{8,10},{9,11},{10,... | collective-permute-start | bytes 393224 | tf_op jit(solution)/shard_map/ppermute | solution.py:466
  18.8 4.3 %collective-permute-start.11 = (s16[1,64,512]{2,1,0:T(8,128)(2,1)S(1)}, s16[1,64,512]{2,1,0:T(8,128)(2,1)S(1)}, u32[]{:S(2)}, u32[]{:S(2)}) collective-permute-start(s16[1,64,512]{2,1,0:T(8,128)(2,1)S(1)} %collective-permute-done.8.refs_3_), channel_id=1, source_target_pairs={{0,2},{1,3},{2,0},{3,1},{4,6},{5,7},{6,4},{7,5},{8,10},{9,11},{10,... | collective-permute-start | bytes 196616 | tf_op jit(solution)/shard_map/ppermute | solution.py:466
  20.4 6.0 %collective-permute-start.12 = (s16[3,64,512]{2,1,0:T(8,128)(2,1)S(1)}, s16[3,64,512]{2,1,0:T(8,128)(2,1)S(1)}, u32[]{:S(2)}, u32[]{:S(2)}) collective-permute-start(s16[3,64,512]{2,1,0:T(8,128)(2,1)S(1)} %pad_add_fusion), channel_id=1, source_target_pairs={{0,2},{1,3},{2,0},{3,1},{4,6},{5,7},{6,4},{7,5},{8,10},{9,11},{10,... | collective-permute-start | bytes 589832 | tf_op jit(solution)/shard_map/ppermute | solution.py:466
  21.0 5.4 %collective-permute-start.13 = (s16[2,64,512]{2,1,0:T(8,128)(2,1)S(1)}, s16[2,64,512]{2,1,0:T(8,128)(2,1)S(1)}, u32[]{:S(2)}, u32[]{:S(2)}) collective-permute-start(s16[2,64,512]{2,1,0:T(8,128)(2,1)S(1)} %pad_add_fusion.1), channel_id=1, source_target_pairs={{0,4},{1,5},{2,6},{3,7},{4,0},{5,1},{6,2},{7,3},{8,12},{9,13},{10,... | collective-permute-start | bytes 393224 | tf_op jit(solution)/shard_map/ppermute | solution.py:466
  23.1 5.0 %collective-permute-start.14 = (s16[2,64,512]{2,1,0:T(8,128)(2,1)S(1)}, s16[2,64,512]{2,1,0:T(8,128)(2,1)S(1)}, u32[]{:S(2)}, u32[]{:S(2)}) collective-permute-start(s16[2,64,512]{2,1,0:T(8,128)(2,1)S(1)} %pad_add_fusion.4), channel_id=1, source_target_pairs={{0,4},{1,5},{2,6},{3,7},{4,0},{5,1},{6,2},{7,3},{8,12},{9,13},{10,... | collective-permute-start | bytes 393224 | tf_op jit(solution)/shard_map/ppermute | solution.py:466
  26.4 2.2 %copy-start.3 = (f32[128,1024]{1,0:T(8,128)S(1)}, f32[128,1024]{1,0:T(8,128)}, u32[]{:S(2)}) copy-start(f32[128,1024]{1,0:T(8,128)} %state_ref.3) | copy-start | bytes 1572868
  26.4 2.1 %copy-start.4 = (f32[2,256,4]{1,2,0:T(4,128)S(1)}, f32[2,256,4]{1,2,0:T(4,128)}, u32[]{:S(2)}) copy-start(f32[2,256,4]{1,2,0:T(4,128)} %param.10) | copy-start | bytes 24580
  28.6 1.7 %copy-start = (bf16[2,256,1024]{2,1,0:T(8,128)(2,1)S(1)}, bf16[2,256,1024]{2,1,0:T(8,128)(2,1)}, u32[]{:S(2)}) copy-start(bf16[2,256,1024]{2,1,0:T(8,128)(2,1)} %noise_ref.3) | copy-start | bytes 3145732
  28.6 1.7 %copy-start.1 = (s32[2,256]{1,0:T(2,128)S(1)}, s32[2,256]{1,0:T(2,128)}, u32[]{:S(2)}) copy-start(s32[2,256]{1,0:T(2,128)} %tags.3) | copy-start | bytes 6148
  28.6 1.7 %copy-start.2 = (f32[2,256]{1,0:T(2,128)S(1)}, f32[2,256]{1,0:T(2,128)}, u32[]{:S(2)}) copy-start(f32[2,256]{1,0:T(2,128)} %values.3) | copy-start | bytes 6148
  28.7 1.6 %collective-permute-start.16 = (bf16[256,512]{1,0:T(8,128)(2,1)S(1)}, bf16[256,512]{1,0:T(8,128)(2,1)S(1)}, u32[]{:S(2)}, u32[]{:S(2)}) collective-permute-start(bf16[256,512]{1,0:T(8,128)(2,1)S(1)} %get-tuple-element.43.own), channel_id=1, source_target_pairs={{0,1},{1,0},{2,3},{3,2},{4,5},{5,4},{6,7},{7,6},{8,9},{9,8},{10,11... | collective-permute-start | bytes 786440 | tf_op jit(solution)/shard_map/ppermute | solution.py:466
  28.7 49.0 %collective-permute-start.15 = (s16[256,512]{1,0:T(8,128)(2,1)S(1)}, s16[256,512]{1,0:T(8,128)(2,1)S(1)}, u32[]{:S(2)}, u32[]{:S(2)}) collective-permute-start(s16[256,512]{1,0:T(8,128)(2,1)S(1)} %get-tuple-element.42.own), channel_id=1, source_target_pairs={{0,1},{1,0},{2,3},{3,2},{4,5},{5,4},{6,7},{7,6},{8,9},{9,8},{10,11... | collective-permute-start | bytes 786440 | tf_op jit(solution)/shard_map/ppermute | solution.py:466

commit v7 on v5

--- a/solution.py
+++ b/solution.py
@@ -33,9 +33,14 @@
     return high, (a - high.astype(F32)).astype(BF16)
 
 
+def dot2(dot, a, b):
+    rows = a[0].shape[0]
+    both = dot(jnp.concatenate(a, axis=0), b)
+    return both[:rows] + both[rows:]
+
+
 def dot3(dot, a, b):
-    (ah, al), (bh, bl) = a, b
-    return dot(ah, bh) + (dot(ah, bl) + dot(al, bh))
+    return dot2(dot, a, b[0]) + dot(a[0], b[1])
 
 
 def row_mean(a):
@@ -337,21 +342,17 @@
     members = observed.shape[1]
     size = observed.shape[0]
     mean = row_mean(observed)
-    parts = split(observed - mean)
     lane = lax.broadcasted_iota(jnp.int32, (size, size), 1)
     sub = lax.broadcasted_iota(jnp.int32, (size, size), 0)
     variance_row = jnp.where(tags == 0, 0.5, 2.0)
-    variance = column(variance_row)
     mean_row = jnp.sum(jnp.where(lane == sub, mean, 0.0), axis=0, keepdims=True)
-    covariance = dot3(nt, parts, parts) * (1.0 / (members - 1))
-    covariance = covariance + jnp.where(lane == sub, variance, 0.0)
     exact = observed.astype(BF16)
+    covariance = (nt(exact, exact) - mean * (mean_row * members)) * (1.0 / (members - 1))
+    covariance = covariance + jnp.where(lane == sub, variance_row, 0.0)
 
     def finish(t):
-        th, tl = split(t)
-        nh, nl = split(t * jnp.sqrt(variance_row))
-        applied = nn(th, exact) + nn(tl, exact)
-        noise = nn(nh, noise_ref[...]) + nn(nl, noise_ref[...])
+        applied = dot2(nn, split(t), exact)
+        noise = dot2(nn, split(t * jnp.sqrt(variance_row)), noise_ref[...])
         mean_part = jnp.sum(t * mean_row, axis=1, keepdims=True)
         value_part = jnp.sum(t * values, axis=1, keepdims=True)
         store((applied - mean_part).astype(BF16), (noise + value_part - applied).astype(BF16))
@@ -360,11 +361,14 @@
     inverse_factor(covariance, work, inverse, finish)
 
 
+def row_sums(array):
+    return nt(jnp.ones((8, array.shape[1]), BF16), array)[:1, :]
+
+
 def update(state, whitened, white_innov):
     members = state.shape[1]
-    sh, sl = split(state - row_mean(state))
-    ph, plow = split(nt(sh, whitened) + nt(sl, whitened))
-    return state + (nn(ph, white_innov) + nn(plow, white_innov)) * (1.0 / (members - 1))
+    projected = dot2(nt, split(state), whitened) - row_mean(state) * row_sums(whitened)
+    return state + dot2(nn, split(projected), white_innov) * (1.0 / (members - 1))
 
 
 def both_halves(place, own, other):
@@ -410,9 +414,8 @@
     load_state = pltpu.make_async_copy(state_ref, state, loads.at[1])
     load_state.start()
     load.start()
-    prior = both_halves(place, own, other) * UNIT
     w, v = whitened[...], white_innov[...]
-    observed = rounded(update(prior, w, v))
+    observed = rounded(update(both_halves(place, own, other), w, v) * UNIT)
     load_state.wait()
     first = update(state[...], w, v)
 

time: 85.9 us -> 83.2 us (0.969)
  Pallas kernels: 61.9 us -> 59.2 us
    pallas_call x2, Pallas kernels: 56.5 us -> 53.8 us  [batch_call(): pl.pallas_call(kernel, out_shape=outs, in_specs=[SMEM, VMEM, VMEM, ANYWHE...]
where the time goes in v7:
time: 83.2 us; the launch traced here: 83 us
  Pallas kernels  59.2 us (71%)
  starting transfers between devices  15.4 us (19%)
  waiting for transfers between devices  7.22 us (9%)
  between operations  0.98 us (1%)
    pallas_call x2, Pallas kernels, batch_call(): pl.pallas_call(kernel, out_shape=outs, in_specs=[SMEM, VMEM, VMEM, ANYWHE...  53.8 us
    ppermute x12, starting transfers between devices, swap(): return lax.ppermute(value, AXES, [(i, i ^ mask) for i in range(32)])  15.4 us
    ppermute x12, waiting for transfers between devices, swap(): return lax.ppermute(value, AXES, [(i, i ^ mask) for i in range(32)])  7.22 us
    pallas_call x1, Pallas kernels, pick(): pl.pallas_call(pick_kernel, out_shape=[jax.ShapeDtypeStruct((SLOTS, state...  2.22 us
    pallas_call x1, Pallas kernels, order(): pl.pallas_call(functools.partial(order_kernel, groups), out_shape=[jax.Sh...  1.74 us
  transfers between devices with their start and end apart: 12, of which 5 were waited for; matrix products, arithmetic and copies ran while one was open for 0% of the time, Pallas kernels for 60%

profile of v7, /device:TPU:0, one launch (start us, length us, event | category | flops | bytes accessed | tf_op | source)
XLA Modules:
  0.0 83.0 jit_solution(10186410896409673818)
XLA Ops:
  0.0 0.1 pad_add_fusion.4.place
  0.1 2.2 %pick.1 = (s16[64,512]{1,0:T(8,128)(2,1)S(1)}, s16[64,512]{1,0:T(8,128)(2,1)S(1)}) custom-call(s32[2]{0:T(128)S(1)} %pad_add_fusion.4.place, s32[2,256]{1,0:T(2,128)} %blocks.3, f32[2,4,256]{2,1,0:T(4,128)} %bitcast.5, f32[128,1024]{1,0:T(8,128)} %state_ref.3), custom_call_target="tpu_custom_call" | custom-call | tf_op jit(solution)/shard_map/pick/pallas_call | solution.py:127
  2.3 0.5 collective-permute-start.5
  2.8 0.9 %collective-permute-done.5 = s16[64,512]{1,0:T(8,128)(2,1)S(1)} collective-permute-done((s16[64,512]{1,0:T(8,128)(2,1)S(1)}, s16[64,512]{1,0:T(8,128)(2,1)S(1)}, u32[]{:S(2)}, u32[]{:S(2)}) %collective-permute-start.5) | collective-permute-done | bytes 65568 | tf_op jit(solution)/shard_map/ppermute | solution.py:462
  3.8 3.0 %collective-permute-start.7 = (s16[1,64,512]{2,1,0:T(8,128)(2,1)S(1)}, s16[1,64,512]{2,1,0:T(8,128)(2,1)S(1)}, u32[]{:S(2)}, u32[]{:S(2)}) collective-permute-start(s16[1,64,512]{2,1,0:T(8,128)(2,1)S(1)} %add_bitcast_fusion.refs_0_), channel_id=1, source_target_pairs={{0,8},{1,9},{2,10},{3,11},{4,12},{5,13},{6,14},{7,15},{8,0},{9,1},... | collective-permute-start | bytes 196616 | tf_op jit(solution)/shard_map/ppermute | solution.py:462
  6.7 2.6 %collective-permute-start.6 = (s16[1,64,512]{2,1,0:T(8,128)(2,1)S(1)}, s16[1,64,512]{2,1,0:T(8,128)(2,1)S(1)}, u32[]{:S(2)}, u32[]{:S(2)}) collective-permute-start(s16[1,64,512]{2,1,0:T(8,128)(2,1)S(1)} %add_bitcast_fusion.refs_0_), channel_id=1, source_target_pairs={{0,16},{1,17},{2,18},{3,19},{4,20},{5,21},{6,22},{7,23},{8,24},{9,... | collective-permute-start | bytes 196616 | tf_op jit(solution)/shard_map/ppermute | solution.py:462
  9.3 1.7 %collective-permute-start.9 = (s16[2,64,512]{2,1,0:T(8,128)(2,1)S(1)}, s16[2,64,512]{2,1,0:T(8,128)(2,1)S(1)}, u32[]{:S(2)}, u32[]{:S(2)}) collective-permute-start(s16[2,64,512]{2,1,0:T(8,128)(2,1)S(1)} %pad_add_fusion.1), channel_id=1, source_target_pairs={{0,4},{1,5},{2,6},{3,7},{4,0},{5,1},{6,2},{7,3},{8,12},{9,13},{10,... | collective-permute-start | bytes 393224 | tf_op jit(solution)/shard_map/ppermute | solution.py:462
  11.0 2.0 %collective-permute-done.6.refs_1_ = s16[1,64,512]{2,1,0:T(8,128)(2,1)S(1)} collective-permute-done((s16[1,64,512]{2,1,0:T(8,128)(2,1)S(1)}, s16[1,64,512]{2,1,0:T(8,128)(2,1)S(1)}, u32[]{:S(2)}, u32[]{:S(2)}) %collective-permute-start.6) | collective-permute-done | bytes 65568 | tf_op jit(solution)/shard_map/ppermute | solution.py:462
  13.0 0.3 collective-permute-start.8
  13.3 1.5 %collective-permute-start.10 = (s16[1,64,512]{2,1,0:T(8,128)(2,1)S(1)}, s16[1,64,512]{2,1,0:T(8,128)(2,1)S(1)}, u32[]{:S(2)}, u32[]{:S(2)}) collective-permute-start(s16[1,64,512]{2,1,0:T(8,128)(2,1)S(1)} %collective-permute-done.6.refs_1_), channel_id=1, source_target_pairs={{0,2},{1,3},{2,0},{3,1},{4,6},{5,7},{6,4},{7,5},{8,10},{9,11},{10,... | collective-permute-start | bytes 196616 | tf_op jit(solution)/shard_map/ppermute | solution.py:462
  14.8 2.4 %collective-permute-done.8.refs_3_ = s16[1,64,512]{2,1,0:T(8,128)(2,1)S(1)} collective-permute-done((s16[1,64,512]{2,1,0:T(8,128)(2,1)S(1)}, s16[1,64,512]{2,1,0:T(8,128)(2,1)S(1)}, u32[]{:S(2)}, u32[]{:S(2)}) %collective-permute-start.8) | collective-permute-done | bytes 65568 | tf_op jit(solution)/shard_map/ppermute | solution.py:462
  17.3 1.5 %collective-permute-start.11 = (s16[1,64,512]{2,1,0:T(8,128)(2,1)S(1)}, s16[1,64,512]{2,1,0:T(8,128)(2,1)S(1)}, u32[]{:S(2)}, u32[]{:S(2)}) collective-permute-start(s16[1,64,512]{2,1,0:T(8,128)(2,1)S(1)} %collective-permute-done.8.refs_3_), channel_id=1, source_target_pairs={{0,2},{1,3},{2,0},{3,1},{4,6},{5,7},{6,4},{7,5},{8,10},{9,11},{10,... | collective-permute-start | bytes 196616 | tf_op jit(solution)/shard_map/ppermute | solution.py:462
  18.8 0.6 collective-permute-start.12
  19.4 1.6 %collective-permute-start.13 = (s16[2,64,512]{2,1,0:T(8,128)(2,1)S(1)}, s16[2,64,512]{2,1,0:T(8,128)(2,1)S(1)}, u32[]{:S(2)}, u32[]{:S(2)}) collective-permute-start(s16[2,64,512]{2,1,0:T(8,128)(2,1)S(1)} %pad_add_fusion.2), channel_id=1, source_target_pairs={{0,4},{1,5},{2,6},{3,7},{4,0},{5,1},{6,2},{7,3},{8,12},{9,13},{10,... | collective-permute-start | bytes 393224 | tf_op jit(solution)/shard_map/ppermute | solution.py:462
  20.9 0.8 %collective-permute-done.11.refs_6_ = s16[1,64,512]{2,1,0:T(8,128)(2,1)S(1)} collective-permute-done((s16[1,64,512]{2,1,0:T(8,128)(2,1)S(1)}, s16[1,64,512]{2,1,0:T(8,128)(2,1)S(1)}, u32[]{:S(2)}, u32[]{:S(2)}) %collective-permute-start.11) | collective-permute-done | bytes 65568 | tf_op jit(solution)/shard_map/ppermute | solution.py:462
  21.8 1.6 %collective-permute-start.14 = (s16[2,64,512]{2,1,0:T(8,128)(2,1)S(1)}, s16[2,64,512]{2,1,0:T(8,128)(2,1)S(1)}, u32[]{:S(2)}, u32[]{:S(2)}) collective-permute-start(s16[2,64,512]{2,1,0:T(8,128)(2,1)S(1)} %pad_add_fusion.3), channel_id=1, source_target_pairs={{0,4},{1,5},{2,6},{3,7},{4,0},{5,1},{6,2},{7,3},{8,12},{9,13},{10,... | collective-permute-start | bytes 393224 | tf_op jit(solution)/shard_map/ppermute | solution.py:462
  23.4 1.7 %order.1 = (bf16[512,896]{1,0:T(8,128)(2,1)S(1)}, bf16[512,128]{1,0:T(8,128)(2,1)S(1)}, s32[1]{0:T(128)}) custom-call(s32[2]{0:T(128)S(1)} %pad_add_fusion.4.place, s32[2,256]{1,0:T(2,128)} %blocks.3), custom_call_target="tpu_custom_call" | custom-call | flops 1000000 | bytes 1000000 | tf_op jit(solution)/shard_map/order/pallas_call | solution.py:196
  25.8 1.0 %early_rows.1.early = f32[512,512]{1,0:T(8,128)S(1)} custom-call(bf16[512,896]{1,0:T(8,128)(2,1)S(1)} %get-tuple-element.37.chosen, s16[1,64,512]{2,1,0:T(8,128)(2,1)S(1)} %add_bitcast_fusion.refs_0_, s16[1,64,512]{2,1,0:T(8,128)(2,1)S(1)} %collective-permute-done.6.refs_1_, s16[1,64,512]{2,1,0:T(8,128)(2,1)S(1)} %collective-permute-done.7.refs_2_, ...), custom_call_target="tpu_custom_call" | custom-call | flops 1000000000 | bytes 4000000 | tf_op jit(solution)/shard_map/early_rows/pallas_call | solution.py:231
  26.8 0.4 late_rows.1
  27.4 0.1 collective-permute-start.16
  27.5 0.5 collective-permute-start.15
  27.9 1.0 %collective-permute-done.16.other = bf16[256,512]{1,0:T(8,128)(2,1)S(1)} collective-permute-done((bf16[256,512]{1,0:T(8,128)(2,1)S(1)}, bf16[256,512]{1,0:T(8,128)(2,1)S(1)}, u32[]{:S(2)}, u32[]{:S(2)}) %collective-permute-start.16) | collective-permute-done | bytes 262176 | tf_op jit(solution)/shard_map/ppermute | solution.py:462
  29.0 47.4 %first_batch.1 = (bf16[256,1024]{1,0:T(8,128)(2,1)S(1)}, bf16[256,1024]{1,0:T(8,128)(2,1)S(1)}) custom-call(s32[2]{0:T(128)S(1)} %pad_add_fusion.4.place, s32[2,256]{1,0:T(2,128)S(1)} %copy-done.1, f32[2,256]{1,0:T(2,128)S(1)} %copy-done.2, bf16[2,256,1024]{2,1,0:T(8,128)(2,1)S(1)} %copy-done, bf16[256,512]{1,0:T(8,128)(2,1)S(1)} %get-tuple-element.43.own, ...), custom_call_target="tpu_custom_call" | custom-call | tf_op jit(solution)/shard_map/first_batch/pallas_call | solution.py:430
  76.4 6.4 %second_batch.1 = f32[128,1024]{1,0:T(8,128)} custom-call(s32[2]{0:T(128)S(1)} %pad_add_fusion.4.place, s32[2,256]{1,0:T(2,128)S(1)} %copy-done.1, f32[2,256]{1,0:T(2,128)S(1)} %copy-done.2, bf16[2,256,1024]{2,1,0:T(8,128)(2,1)S(1)} %copy-done, s16[256,512]{1,0:T(8,128)(2,1)S(1)} %get-tuple-element.42.own, ...), custom_call_target="tpu_custom_call" | custom-call | tf_op jit(solution)/shard_map/second_batch/pallas_call | solution.py:430
  (27 shorter events, 0.3 us)
Async XLA Ops:
  2.3 1.4 %collective-permute-start.5 = (s16[64,512]{1,0:T(8,128)(2,1)S(1)}, s16[64,512]{1,0:T(8,128)(2,1)S(1)}, u32[]{:S(2)}, u32[]{:S(2)}) collective-permute-start(s16[64,512]{1,0:T(8,128)(2,1)S(1)} %get-tuple-element.39), channel_id=1, source_target_pairs={{0,1},{1,0},{2,3},{3,2},{4,5},{5,4},{6,7},{7,6},{8,9},{9,8},{10,11... | collective-permute-start | bytes 196616 | tf_op jit(solution)/shard_map/ppermute | solution.py:462
  3.8 5.6 %collective-permute-start.7 = (s16[1,64,512]{2,1,0:T(8,128)(2,1)S(1)}, s16[1,64,512]{2,1,0:T(8,128)(2,1)S(1)}, u32[]{:S(2)}, u32[]{:S(2)}) collective-permute-start(s16[1,64,512]{2,1,0:T(8,128)(2,1)S(1)} %add_bitcast_fusion.refs_0_), channel_id=1, source_target_pairs={{0,8},{1,9},{2,10},{3,11},{4,12},{5,13},{6,14},{7,15},{8,0},{9,1},... | collective-permute-start | bytes 196616 | tf_op jit(solution)/shard_map/ppermute | solution.py:462
  6.7 6.2 %collective-permute-start.6 = (s16[1,64,512]{2,1,0:T(8,128)(2,1)S(1)}, s16[1,64,512]{2,1,0:T(8,128)(2,1)S(1)}, u32[]{:S(2)}, u32[]{:S(2)}) collective-permute-start(s16[1,64,512]{2,1,0:T(8,128)(2,1)S(1)} %add_bitcast_fusion.refs_0_), channel_id=1, source_target_pairs={{0,16},{1,17},{2,18},{3,19},{4,20},{5,21},{6,22},{7,23},{8,24},{9,... | collective-permute-start | bytes 196616 | tf_op jit(solution)/shard_map/ppermute | solution.py:462
  9.3 9.4 %collective-permute-start.9 = (s16[2,64,512]{2,1,0:T(8,128)(2,1)S(1)}, s16[2,64,512]{2,1,0:T(8,128)(2,1)S(1)}, u32[]{:S(2)}, u32[]{:S(2)}) collective-permute-start(s16[2,64,512]{2,1,0:T(8,128)(2,1)S(1)} %pad_add_fusion.1), channel_id=1, source_target_pairs={{0,4},{1,5},{2,6},{3,7},{4,0},{5,1},{6,2},{7,3},{8,12},{9,13},{10,... | collective-permute-start | bytes 393224 | tf_op jit(solution)/shard_map/ppermute | solution.py:462
  13.0 4.3 %collective-permute-start.8 = (s16[1,64,512]{2,1,0:T(8,128)(2,1)S(1)}, s16[1,64,512]{2,1,0:T(8,128)(2,1)S(1)}, u32[]{:S(2)}, u32[]{:S(2)}) collective-permute-start(s16[1,64,512]{2,1,0:T(8,128)(2,1)S(1)} %collective-permute-done.6.refs_1_), channel_id=1, source_target_pairs={{0,8},{1,9},{2,10},{3,11},{4,12},{5,13},{6,14},{7,15},{8,0},{9,1},... | collective-permute-start | bytes 196616 | tf_op jit(solution)/shard_map/ppermute | solution.py:462
  13.3 6.1 %collective-permute-start.10 = (s16[1,64,512]{2,1,0:T(8,128)(2,1)S(1)}, s16[1,64,512]{2,1,0:T(8,128)(2,1)S(1)}, u32[]{:S(2)}, u32[]{:S(2)}) collective-permute-start(s16[1,64,512]{2,1,0:T(8,128)(2,1)S(1)} %collective-permute-done.6.refs_1_), channel_id=1, source_target_pairs={{0,2},{1,3},{2,0},{3,1},{4,6},{5,7},{6,4},{7,5},{8,10},{9,11},{10,... | collective-permute-start | bytes 196616 | tf_op jit(solution)/shard_map/ppermute | solution.py:462
  17.3 4.5 %collective-permute-start.11 = (s16[1,64,512]{2,1,0:T(8,128)(2,1)S(1)}, s16[1,64,512]{2,1,0:T(8,128)(2,1)S(1)}, u32[]{:S(2)}, u32[]{:S(2)}) collective-permute-start(s16[1,64,512]{2,1,0:T(8,128)(2,1)S(1)} %collective-permute-done.8.refs_3_), channel_id=1, source_target_pairs={{0,2},{1,3},{2,0},{3,1},{4,6},{5,7},{6,4},{7,5},{8,10},{9,11},{10,... | collective-permute-start | bytes 196616 | tf_op jit(solution)/shard_map/ppermute | solution.py:462
  18.8 7.0 %collective-permute-start.12 = (s16[4,64,512]{2,1,0:T(8,128)(2,1)S(1)}, s16[4,64,512]{2,1,0:T(8,128)(2,1)S(1)}, u32[]{:S(2)}, u32[]{:S(2)}) collective-permute-start(s16[4,64,512]{2,1,0:T(8,128)(2,1)S(1)} %pad_add_fusion), channel_id=1, source_target_pairs={{0,2},{1,3},{2,0},{3,1},{4,6},{5,7},{6,4},{7,5},{8,10},{9,11},{10,... | collective-permute-start | bytes 786440 | tf_op jit(solution)/shard_map/ppermute | solution.py:462
  19.4 6.4 %collective-permute-start.13 = (s16[2,64,512]{2,1,0:T(8,128)(2,1)S(1)}, s16[2,64,512]{2,1,0:T(8,128)(2,1)S(1)}, u32[]{:S(2)}, u32[]{:S(2)}) collective-permute-start(s16[2,64,512]{2,1,0:T(8,128)(2,1)S(1)} %pad_add_fusion.2), channel_id=1, source_target_pairs={{0,4},{1,5},{2,6},{3,7},{4,0},{5,1},{6,2},{7,3},{8,12},{9,13},{10,... | collective-permute-start | bytes 393224 | tf_op jit(solution)/shard_map/ppermute | solution.py:462
  21.8 5.0 %collective-permute-start.14 = (s16[2,64,512]{2,1,0:T(8,128)(2,1)S(1)}, s16[2,64,512]{2,1,0:T(8,128)(2,1)S(1)}, u32[]{:S(2)}, u32[]{:S(2)}) collective-permute-start(s16[2,64,512]{2,1,0:T(8,128)(2,1)S(1)} %pad_add_fusion.3), channel_id=1, source_target_pairs={{0,4},{1,5},{2,6},{3,7},{4,0},{5,1},{6,2},{7,3},{8,12},{9,13},{10,... | collective-permute-start | bytes 393224 | tf_op jit(solution)/shard_map/ppermute | solution.py:462
  25.8 1.5 %copy-start.3 = (f32[128,1024]{1,0:T(8,128)S(1)}, f32[128,1024]{1,0:T(8,128)}, u32[]{:S(2)}) copy-start(f32[128,1024]{1,0:T(8,128)} %state_ref.3) | copy-start | bytes 1572868
  25.8 1.5 %copy-start.4 = (f32[2,256,4]{1,2,0:T(4,128)S(1)}, f32[2,256,4]{1,2,0:T(4,128)}, u32[]{:S(2)}) copy-start(f32[2,256,4]{1,2,0:T(4,128)} %param.10) | copy-start | bytes 24580
  25.8 1.5 %copy-start.5 = (s32[2,256]{1,0:T(2,128)S(1)}, s32[2,256]{1,0:T(2,128)}, u32[]{:S(2)}) copy-start(s32[2,256]{1,0:T(2,128)} %blocks.3) | copy-start | bytes 6148
  27.3 1.7 %copy-start = (bf16[2,256,1024]{2,1,0:T(8,128)(2,1)S(1)}, bf16[2,256,1024]{2,1,0:T(8,128)(2,1)}, u32[]{:S(2)}) copy-start(bf16[2,256,1024]{2,1,0:T(8,128)(2,1)} %noise_ref.3) | copy-start | bytes 3145732
  27.3 1.7 %copy-start.1 = (s32[2,256]{1,0:T(2,128)S(1)}, s32[2,256]{1,0:T(2,128)}, u32[]{:S(2)}) copy-start(s32[2,256]{1,0:T(2,128)} %tags.3) | copy-start | bytes 6148
  27.3 1.7 %copy-start.2 = (f32[2,256]{1,0:T(2,128)S(1)}, f32[2,256]{1,0:T(2,128)}, u32[]{:S(2)}) copy-start(f32[2,256]{1,0:T(2,128)} %values.3) | copy-start | bytes 6148
  27.4 1.6 %collective-permute-start.16 = (bf16[256,512]{1,0:T(8,128)(2,1)S(1)}, bf16[256,512]{1,0:T(8,128)(2,1)S(1)}, u32[]{:S(2)}, u32[]{:S(2)}) collective-permute-start(bf16[256,512]{1,0:T(8,128)(2,1)S(1)} %get-tuple-element.43.own), channel_id=1, source_target_pairs={{0,1},{1,0},{2,3},{3,2},{4,5},{5,4},{6,7},{7,6},{8,9},{9,8},{10,11... | collective-permute-start | bytes 786440 | tf_op jit(solution)/shard_map/ppermute | solution.py:462
  27.5 48.9 %collective-permute-start.15 = (s16[256,512]{1,0:T(8,128)(2,1)S(1)}, s16[256,512]{1,0:T(8,128)(2,1)S(1)}, u32[]{:S(2)}, u32[]{:S(2)}) collective-permute-start(s16[256,512]{1,0:T(8,128)(2,1)S(1)} %get-tuple-element.42.own), channel_id=1, source_target_pairs={{0,1},{1,0},{2,3},{3,2},{4,5},{5,4},{6,7},{7,6},{8,9},{9,8},{10,11... | collective-permute-start | bytes 786440 | tf_op jit(solution)/shard_map/ppermute | solution.py:462

commit v8 on v7

--- a/solution.py
+++ b/solution.py
@@ -7,7 +7,7 @@
 from jax.experimental.pallas import tpu as pltpu
 from jax.sharding import PartitionSpec as P
 
-SLOTS = 64
+SLOTS = 56
 UNIT = 1.0 / 1024
 SCALE = 0.6
 RESCALE = 1.25
@@ -68,13 +68,6 @@
 
 def rounded(value):
     return value.astype(BF16).astype(F32)
-
-
-def three_parts(a):
-    high = a.astype(BF16)
-    rest = a - high.astype(F32)
-    middle = rest.astype(BF16)
-    return high, middle, (rest - middle.astype(F32)).astype(BF16)
 
 
 def pick_kernel(place, blocks, weights, state_ref, keep, send, state, arrived):
@@ -106,13 +99,9 @@
         local = row[batch : batch + 1, :] - device * held
         selector.append(jnp.where(points_of // points == local, value, 0.0))
     chosen = jnp.concatenate(chosen, axis=1).astype(BF16)
-    parts = three_parts(jnp.concatenate(selector, axis=1))
-    high, middle, low = [nt(chosen, part).astype(BF16) for part in parts]
+    parts = [nt(chosen, part).astype(BF16) for part in split(jnp.concatenate(selector, axis=1))]
     load.wait()
-    top, mid, end = three_parts(state[...])
-    rows = nn(high, end) + nn(middle, mid) + nn(low, top)
-    rows = (nn(high, mid) + nn(middle, top)) + rows
-    rows = nn(high, top) + rows
+    rows = dot3(nn, parts, split(state[...]))
     from_first = lax.broadcasted_iota(jnp.int32, (SLOTS, 1), 0).astype(F32)
     from_first = from_first < jnp.sum(mine[:1, :], axis=1, keepdims=True)
     rows = jnp.where(from_first, rounded(rows), rows)
@@ -209,8 +198,8 @@
 
 def put_in_order(chosen, pieces):
     size = chosen.shape[0] // 2
-    values = jnp.concatenate([ref[...].reshape(-1, ref.shape[-1]) for ref in pieces], axis=0)
-    high, low = split(values.astype(jnp.int32).astype(F32))
+    values = [ref[index].astype(jnp.int32) for ref in pieces for index in range(ref.shape[0])]
+    high, low = split(jnp.concatenate(values, axis=0).astype(F32))
     second = chosen[size:, :]
     return nn(chosen[:size, :], high), nn(second, high) + nn(second, low)
 

time: 83.2 us -> 82.4 us (level)
  transfers between devices with their start and end apart: 12 -> 12, of which waited for: 5 -> 5; matrix products, arithmetic and copies ran while one was open for 0% -> 0% of each run, Pallas kernels for 60% -> 61%
where the time goes in v8:
time: 82.4 us; the launch traced here: 82.2 us
  Pallas kernels  59 us (72%)
  starting transfers between devices  15.3 us (19%)
  waiting for transfers between devices  6.68 us (8%)
  between operations  0.98 us (1%)
    pallas_call x2, Pallas kernels, batch_call(): pl.pallas_call(kernel, out_shape=outs, in_specs=[SMEM, VMEM, VMEM, ANYWHE...  53.8 us
    ppermute x12, starting transfers between devices, swap(): return lax.ppermute(value, AXES, [(i, i ^ mask) for i in range(32)])  15.3 us
    ppermute x12, waiting for transfers between devices, swap(): return lax.ppermute(value, AXES, [(i, i ^ mask) for i in range(32)])  6.68 us
    pallas_call x1, Pallas kernels, pick(): pl.pallas_call(pick_kernel, out_shape=[jax.ShapeDtypeStruct((SLOTS, state...  2.05 us
    pallas_call x1, Pallas kernels, order(): pl.pallas_call(functools.partial(order_kernel, groups), out_shape=[jax.Sh...  1.74 us
  transfers between devices with their start and end apart: 12, of which 5 were waited for; matrix products, arithmetic and copies ran while one was open for 0% of the time, Pallas kernels for 61%

profile of v8, /device:TPU:0, one launch (start us, length us, event | category | flops | bytes accessed | tf_op | source)
XLA Modules:
  0.0 82.2 jit_solution(14179839220681213674)
XLA Ops:
  0.0 0.1 pad_add_fusion.4.place
  0.1 2.0 %pick.1 = (s16[56,512]{1,0:T(8,128)(2,1)S(1)}, s16[56,512]{1,0:T(8,128)(2,1)S(1)}) custom-call(s32[2]{0:T(128)S(1)} %pad_add_fusion.4.place, s32[2,256]{1,0:T(2,128)} %blocks.3, f32[2,4,256]{2,1,0:T(4,128)} %bitcast.5, f32[128,1024]{1,0:T(8,128)} %state_ref.3), custom_call_target="tpu_custom_call" | custom-call | tf_op jit(solution)/shard_map/pick/pallas_call | solution.py:116
  2.1 0.5 collective-permute-start.5
  2.7 0.9 %collective-permute-done.5 = s16[56,512]{1,0:T(8,128)(2,1)S(1)} collective-permute-done((s16[56,512]{1,0:T(8,128)(2,1)S(1)}, s16[56,512]{1,0:T(8,128)(2,1)S(1)}, u32[]{:S(2)}, u32[]{:S(2)}) %collective-permute-start.5) | collective-permute-done | bytes 57376 | tf_op jit(solution)/shard_map/ppermute | solution.py:451
  3.6 3.0 %collective-permute-start.7 = (s16[1,56,512]{2,1,0:T(8,128)(2,1)S(1)}, s16[1,56,512]{2,1,0:T(8,128)(2,1)S(1)}, u32[]{:S(2)}, u32[]{:S(2)}) collective-permute-start(s16[1,56,512]{2,1,0:T(8,128)(2,1)S(1)} %add_bitcast_fusion.refs_0_), channel_id=1, source_target_pairs={{0,8},{1,9},{2,10},{3,11},{4,12},{5,13},{6,14},{7,15},{8,0},{9,1},... | collective-permute-start | bytes 172040 | tf_op jit(solution)/shard_map/ppermute | solution.py:451
  6.5 2.6 %collective-permute-start.6 = (s16[1,56,512]{2,1,0:T(8,128)(2,1)S(1)}, s16[1,56,512]{2,1,0:T(8,128)(2,1)S(1)}, u32[]{:S(2)}, u32[]{:S(2)}) collective-permute-start(s16[1,56,512]{2,1,0:T(8,128)(2,1)S(1)} %add_bitcast_fusion.refs_0_), channel_id=1, source_target_pairs={{0,16},{1,17},{2,18},{3,19},{4,20},{5,21},{6,22},{7,23},{8,24},{9,... | collective-permute-start | bytes 172040 | tf_op jit(solution)/shard_map/ppermute | solution.py:451
  9.2 1.6 %collective-permute-start.9 = (s16[2,56,512]{2,1,0:T(8,128)(2,1)S(1)}, s16[2,56,512]{2,1,0:T(8,128)(2,1)S(1)}, u32[]{:S(2)}, u32[]{:S(2)}) collective-permute-start(s16[2,56,512]{2,1,0:T(8,128)(2,1)S(1)} %pad_add_fusion.1), channel_id=1, source_target_pairs={{0,4},{1,5},{2,6},{3,7},{4,0},{5,1},{6,2},{7,3},{8,12},{9,13},{10,... | collective-permute-start | bytes 344072 | tf_op jit(solution)/shard_map/ppermute | solution.py:451
  10.7 1.7 %collective-permute-done.6.refs_1_ = s16[1,56,512]{2,1,0:T(8,128)(2,1)S(1)} collective-permute-done((s16[1,56,512]{2,1,0:T(8,128)(2,1)S(1)}, s16[1,56,512]{2,1,0:T(8,128)(2,1)S(1)}, u32[]{:S(2)}, u32[]{:S(2)}) %collective-permute-start.6) | collective-permute-done | bytes 57376 | tf_op jit(solution)/shard_map/ppermute | solution.py:451
  12.4 0.3 collective-permute-start.8
  12.8 1.5 %collective-permute-start.10 = (s16[1,56,512]{2,1,0:T(8,128)(2,1)S(1)}, s16[1,56,512]{2,1,0:T(8,128)(2,1)S(1)}, u32[]{:S(2)}, u32[]{:S(2)}) collective-permute-start(s16[1,56,512]{2,1,0:T(8,128)(2,1)S(1)} %collective-permute-done.6.refs_1_), channel_id=1, source_target_pairs={{0,2},{1,3},{2,0},{3,1},{4,6},{5,7},{6,4},{7,5},{8,10},{9,11},{10,... | collective-permute-start | bytes 172040 | tf_op jit(solution)/shard_map/ppermute | solution.py:451
  14.3 2.3 %collective-permute-done.8.refs_3_ = s16[1,56,512]{2,1,0:T(8,128)(2,1)S(1)} collective-permute-done((s16[1,56,512]{2,1,0:T(8,128)(2,1)S(1)}, s16[1,56,512]{2,1,0:T(8,128)(2,1)S(1)}, u32[]{:S(2)}, u32[]{:S(2)}) %collective-permute-start.8) | collective-permute-done | bytes 57376 | tf_op jit(solution)/shard_map/ppermute | solution.py:451
  16.6 1.5 %collective-permute-start.11 = (s16[1,56,512]{2,1,0:T(8,128)(2,1)S(1)}, s16[1,56,512]{2,1,0:T(8,128)(2,1)S(1)}, u32[]{:S(2)}, u32[]{:S(2)}) collective-permute-start(s16[1,56,512]{2,1,0:T(8,128)(2,1)S(1)} %collective-permute-done.8.refs_3_), channel_id=1, source_target_pairs={{0,2},{1,3},{2,0},{3,1},{4,6},{5,7},{6,4},{7,5},{8,10},{9,11},{10,... | collective-permute-start | bytes 172040 | tf_op jit(solution)/shard_map/ppermute | solution.py:451
  18.2 0.6 collective-permute-start.12
  18.8 1.6 %collective-permute-start.13 = (s16[2,56,512]{2,1,0:T(8,128)(2,1)S(1)}, s16[2,56,512]{2,1,0:T(8,128)(2,1)S(1)}, u32[]{:S(2)}, u32[]{:S(2)}) collective-permute-start(s16[2,56,512]{2,1,0:T(8,128)(2,1)S(1)} %pad_add_fusion.2), channel_id=1, source_target_pairs={{0,4},{1,5},{2,6},{3,7},{4,0},{5,1},{6,2},{7,3},{8,12},{9,13},{10,... | collective-permute-start | bytes 344072 | tf_op jit(solution)/shard_map/ppermute | solution.py:451
  20.3 0.7 collective-permute-done.11.refs_6_
  21.0 1.6 %collective-permute-start.14 = (s16[2,56,512]{2,1,0:T(8,128)(2,1)S(1)}, s16[2,56,512]{2,1,0:T(8,128)(2,1)S(1)}, u32[]{:S(2)}, u32[]{:S(2)}) collective-permute-start(s16[2,56,512]{2,1,0:T(8,128)(2,1)S(1)} %pad_add_fusion.3), channel_id=1, source_target_pairs={{0,4},{1,5},{2,6},{3,7},{4,0},{5,1},{6,2},{7,3},{8,12},{9,13},{10,... | collective-permute-start | bytes 344072 | tf_op jit(solution)/shard_map/ppermute | solution.py:451
  22.6 1.7 %order.1 = (bf16[512,784]{1,0:T(8,128)(2,1)S(1)}, bf16[512,112]{1,0:T(8,128)(2,1)S(1)}, s32[1]{0:T(128)}) custom-call(s32[2]{0:T(128)S(1)} %pad_add_fusion.4.place, s32[2,256]{1,0:T(2,128)} %blocks.3), custom_call_target="tpu_custom_call" | custom-call | flops 1000000 | bytes 1000000 | tf_op jit(solution)/shard_map/order/pallas_call | solution.py:185
  25.0 1.0 %early_rows.1.early = f32[512,512]{1,0:T(8,128)S(1)} custom-call(bf16[512,784]{1,0:T(8,128)(2,1)S(1)} %get-tuple-element.37.chosen, s16[1,56,512]{2,1,0:T(8,128)(2,1)S(1)} %add_bitcast_fusion.refs_0_, s16[1,56,512]{2,1,0:T(8,128)(2,1)S(1)} %collective-permute-done.6.refs_1_, s16[1,56,512]{2,1,0:T(8,128)(2,1)S(1)} %collective-permute-done.7.refs_2_, ...), custom_call_target="tpu_custom_call" | custom-call | flops 1000000000 | bytes 4000000 | tf_op jit(solution)/shard_map/early_rows/pallas_call | solution.py:220
  26.0 0.4 late_rows.1
  26.6 0.1 collective-permute-start.16
  26.7 0.5 collective-permute-start.15
  27.2 1.0 %collective-permute-done.16.other = bf16[256,512]{1,0:T(8,128)(2,1)S(1)} collective-permute-done((bf16[256,512]{1,0:T(8,128)(2,1)S(1)}, bf16[256,512]{1,0:T(8,128)(2,1)S(1)}, u32[]{:S(2)}, u32[]{:S(2)}) %collective-permute-start.16) | collective-permute-done | bytes 262176 | tf_op jit(solution)/shard_map/ppermute | solution.py:451
  28.2 47.4 %first_batch.1 = (bf16[256,1024]{1,0:T(8,128)(2,1)S(1)}, bf16[256,1024]{1,0:T(8,128)(2,1)S(1)}) custom-call(s32[2]{0:T(128)S(1)} %pad_add_fusion.4.place, s32[2,256]{1,0:T(2,128)S(1)} %copy-done.1, f32[2,256]{1,0:T(2,128)S(1)} %copy-done.2, bf16[2,256,1024]{2,1,0:T(8,128)(2,1)S(1)} %copy-done, bf16[256,512]{1,0:T(8,128)(2,1)S(1)} %get-tuple-element.43.own, ...), custom_call_target="tpu_custom_call" | custom-call | tf_op jit(solution)/shard_map/first_batch/pallas_call | solution.py:419
  75.6 6.4 %second_batch.1 = f32[128,1024]{1,0:T(8,128)} custom-call(s32[2]{0:T(128)S(1)} %pad_add_fusion.4.place, s32[2,256]{1,0:T(2,128)S(1)} %copy-done.1, f32[2,256]{1,0:T(2,128)S(1)} %copy-done.2, bf16[2,256,1024]{2,1,0:T(8,128)(2,1)S(1)} %copy-done, s16[256,512]{1,0:T(8,128)(2,1)S(1)} %get-tuple-element.42.own, ...), custom_call_target="tpu_custom_call" | custom-call | tf_op jit(solution)/shard_map/second_batch/pallas_call | solution.py:419
  (27 shorter events, 0.2 us)
Async XLA Ops:
  2.1 1.4 %collective-permute-start.5 = (s16[56,512]{1,0:T(8,128)(2,1)S(1)}, s16[56,512]{1,0:T(8,128)(2,1)S(1)}, u32[]{:S(2)}, u32[]{:S(2)}) collective-permute-start(s16[56,512]{1,0:T(8,128)(2,1)S(1)} %get-tuple-element.39), channel_id=1, source_target_pairs={{0,1},{1,0},{2,3},{3,2},{4,5},{5,4},{6,7},{7,6},{8,9},{9,8},{10,11... | collective-permute-start | bytes 172040 | tf_op jit(solution)/shard_map/ppermute | solution.py:451
  3.6 5.6 %collective-permute-start.7 = (s16[1,56,512]{2,1,0:T(8,128)(2,1)S(1)}, s16[1,56,512]{2,1,0:T(8,128)(2,1)S(1)}, u32[]{:S(2)}, u32[]{:S(2)}) collective-permute-start(s16[1,56,512]{2,1,0:T(8,128)(2,1)S(1)} %add_bitcast_fusion.refs_0_), channel_id=1, source_target_pairs={{0,8},{1,9},{2,10},{3,11},{4,12},{5,13},{6,14},{7,15},{8,0},{9,1},... | collective-permute-start | bytes 172040 | tf_op jit(solution)/shard_map/ppermute | solution.py:451
  6.5 5.9 %collective-permute-start.6 = (s16[1,56,512]{2,1,0:T(8,128)(2,1)S(1)}, s16[1,56,512]{2,1,0:T(8,128)(2,1)S(1)}, u32[]{:S(2)}, u32[]{:S(2)}) collective-permute-start(s16[1,56,512]{2,1,0:T(8,128)(2,1)S(1)} %add_bitcast_fusion.refs_0_), channel_id=1, source_target_pairs={{0,16},{1,17},{2,18},{3,19},{4,20},{5,21},{6,22},{7,23},{8,24},{9,... | collective-permute-start | bytes 172040 | tf_op jit(solution)/shard_map/ppermute | solution.py:451
  9.2 9.0 %collective-permute-start.9 = (s16[2,56,512]{2,1,0:T(8,128)(2,1)S(1)}, s16[2,56,512]{2,1,0:T(8,128)(2,1)S(1)}, u32[]{:S(2)}, u32[]{:S(2)}) collective-permute-start(s16[2,56,512]{2,1,0:T(8,128)(2,1)S(1)} %pad_add_fusion.1), channel_id=1, source_target_pairs={{0,4},{1,5},{2,6},{3,7},{4,0},{5,1},{6,2},{7,3},{8,12},{9,13},{10,... | collective-permute-start | bytes 344072 | tf_op jit(solution)/shard_map/ppermute | solution.py:451
  12.4 4.2 %collective-permute-start.8 = (s16[1,56,512]{2,1,0:T(8,128)(2,1)S(1)}, s16[1,56,512]{2,1,0:T(8,128)(2,1)S(1)}, u32[]{:S(2)}, u32[]{:S(2)}) collective-permute-start(s16[1,56,512]{2,1,0:T(8,128)(2,1)S(1)} %collective-permute-done.6.refs_1_), channel_id=1, source_target_pairs={{0,8},{1,9},{2,10},{3,11},{4,12},{5,13},{6,14},{7,15},{8,0},{9,1},... | collective-permute-start | bytes 172040 | tf_op jit(solution)/shard_map/ppermute | solution.py:451
  12.8 6.0 %collective-permute-start.10 = (s16[1,56,512]{2,1,0:T(8,128)(2,1)S(1)}, s16[1,56,512]{2,1,0:T(8,128)(2,1)S(1)}, u32[]{:S(2)}, u32[]{:S(2)}) collective-permute-start(s16[1,56,512]{2,1,0:T(8,128)(2,1)S(1)} %collective-permute-done.6.refs_1_), channel_id=1, source_target_pairs={{0,2},{1,3},{2,0},{3,1},{4,6},{5,7},{6,4},{7,5},{8,10},{9,11},{10,... | collective-permute-start | bytes 172040 | tf_op jit(solution)/shard_map/ppermute | solution.py:451
  16.6 4.4 %collective-permute-start.11 = (s16[1,56,512]{2,1,0:T(8,128)(2,1)S(1)}, s16[1,56,512]{2,1,0:T(8,128)(2,1)S(1)}, u32[]{:S(2)}, u32[]{:S(2)}) collective-permute-start(s16[1,56,512]{2,1,0:T(8,128)(2,1)S(1)} %collective-permute-done.8.refs_3_), channel_id=1, source_target_pairs={{0,2},{1,3},{2,0},{3,1},{4,6},{5,7},{6,4},{7,5},{8,10},{9,11},{10,... | collective-permute-start | bytes 172040 | tf_op jit(solution)/shard_map/ppermute | solution.py:451
  18.2 6.8 %collective-permute-start.12 = (s16[4,56,512]{2,1,0:T(8,128)(2,1)S(1)}, s16[4,56,512]{2,1,0:T(8,128)(2,1)S(1)}, u32[]{:S(2)}, u32[]{:S(2)}) collective-permute-start(s16[4,56,512]{2,1,0:T(8,128)(2,1)S(1)} %pad_add_fusion), channel_id=1, source_target_pairs={{0,2},{1,3},{2,0},{3,1},{4,6},{5,7},{6,4},{7,5},{8,10},{9,11},{10,... | collective-permute-start | bytes 688136 | tf_op jit(solution)/shard_map/ppermute | solution.py:451
  18.8 6.2 %collective-permute-start.13 = (s16[2,56,512]{2,1,0:T(8,128)(2,1)S(1)}, s16[2,56,512]{2,1,0:T(8,128)(2,1)S(1)}, u32[]{:S(2)}, u32[]{:S(2)}) collective-permute-start(s16[2,56,512]{2,1,0:T(8,128)(2,1)S(1)} %pad_add_fusion.2), channel_id=1, source_target_pairs={{0,4},{1,5},{2,6},{3,7},{4,0},{5,1},{6,2},{7,3},{8,12},{9,13},{10,... | collective-permute-start | bytes 344072 | tf_op jit(solution)/shard_map/ppermute | solution.py:451
  21.0 5.0 %collective-permute-start.14 = (s16[2,56,512]{2,1,0:T(8,128)(2,1)S(1)}, s16[2,56,512]{2,1,0:T(8,128)(2,1)S(1)}, u32[]{:S(2)}, u32[]{:S(2)}) collective-permute-start(s16[2,56,512]{2,1,0:T(8,128)(2,1)S(1)} %pad_add_fusion.3), channel_id=1, source_target_pairs={{0,4},{1,5},{2,6},{3,7},{4,0},{5,1},{6,2},{7,3},{8,12},{9,13},{10,... | collective-permute-start | bytes 344072 | tf_op jit(solution)/shard_map/ppermute | solution.py:451
  25.0 1.4 %copy-start.3 = (f32[128,1024]{1,0:T(8,128)S(1)}, f32[128,1024]{1,0:T(8,128)}, u32[]{:S(2)}) copy-start(f32[128,1024]{1,0:T(8,128)} %state_ref.3) | copy-start | bytes 1572868
  25.0 1.4 %copy-start.4 = (f32[2,256,4]{1,2,0:T(4,128)S(1)}, f32[2,256,4]{1,2,0:T(4,128)}, u32[]{:S(2)}) copy-start(f32[2,256,4]{1,2,0:T(4,128)} %param.10) | copy-start | bytes 24580
  25.0 1.4 %copy-start.5 = (s32[2,256]{1,0:T(2,128)S(1)}, s32[2,256]{1,0:T(2,128)}, u32[]{:S(2)}) copy-start(s32[2,256]{1,0:T(2,128)} %blocks.3) | copy-start | bytes 6148
  26.5 1.7 %copy-start = (bf16[2,256,1024]{2,1,0:T(8,128)(2,1)S(1)}, bf16[2,256,1024]{2,1,0:T(8,128)(2,1)}, u32[]{:S(2)}) copy-start(bf16[2,256,1024]{2,1,0:T(8,128)(2,1)} %noise_ref.3) | copy-start | bytes 3145732
  26.5 1.7 %copy-start.1 = (s32[2,256]{1,0:T(2,128)S(1)}, s32[2,256]{1,0:T(2,128)}, u32[]{:S(2)}) copy-start(s32[2,256]{1,0:T(2,128)} %tags.3) | copy-start | bytes 6148
  26.5 1.7 %copy-start.2 = (f32[2,256]{1,0:T(2,128)S(1)}, f32[2,256]{1,0:T(2,128)}, u32[]{:S(2)}) copy-start(f32[2,256]{1,0:T(2,128)} %values.3) | copy-start | bytes 6148
  26.6 1.6 %collective-permute-start.16 = (bf16[256,512]{1,0:T(8,128)(2,1)S(1)}, bf16[256,512]{1,0:T(8,128)(2,1)S(1)}, u32[]{:S(2)}, u32[]{:S(2)}) collective-permute-start(bf16[256,512]{1,0:T(8,128)(2,1)S(1)} %get-tuple-element.43.own), channel_id=1, source_target_pairs={{0,1},{1,0},{2,3},{3,2},{4,5},{5,4},{6,7},{7,6},{8,9},{9,8},{10,11... | collective-permute-start | bytes 786440 | tf_op jit(solution)/shard_map/ppermute | solution.py:451
  26.7 48.9 %collective-permute-start.15 = (s16[256,512]{1,0:T(8,128)(2,1)S(1)}, s16[256,512]{1,0:T(8,128)(2,1)S(1)}, u32[]{:S(2)}, u32[]{:S(2)}) collective-permute-start(s16[256,512]{1,0:T(8,128)(2,1)S(1)} %get-tuple-element.42.own), channel_id=1, source_target_pairs={{0,1},{1,0},{2,3},{3,2},{4,5},{5,4},{6,7},{7,6},{8,9},{9,8},{10,11... | collective-permute-start | bytes 786440 | tf_op jit(solution)/shard_map/ppermute | solution.py:451

commit v9 on v8

--- a/solution.py
+++ b/solution.py
@@ -70,7 +70,7 @@
     return value.astype(BF16).astype(F32)
 
 
-def pick_kernel(place, blocks, weights, state_ref, keep, send, state, arrived):
+def pick_kernel(place, blocks, weights, state_ref, keep, send, fits, state, arrived):
     load = pltpu.make_async_copy(state_ref, state, arrived)
     load.start()
     device = place[0]
@@ -110,14 +110,21 @@
     first = device % 2 == 0
     keep[...] = jnp.where(first, left, right).astype(jnp.int16)
     send[...] = jnp.where(first, right, left).astype(jnp.int16)
+    chips = lax.broadcasted_iota(jnp.int32, (16, size), 0)
+    counts = jnp.zeros((16, 1), F32)
+    for batch in range(batches):
+        here = jnp.where(chips == row[batch : batch + 1, :] // (2 * held), 1.0, 0.0)
+        counts = counts + jnp.sum(here, axis=1, keepdims=True)
+    fits[0] = (jnp.max(counts) <= SLOTS).astype(jnp.int32)
 
 
 def pick(place, blocks, weights, state):
     return pl.pallas_call(
         pick_kernel,
-        out_shape=[jax.ShapeDtypeStruct((SLOTS, state.shape[1] // 2), jnp.int16)] * 2,
+        out_shape=[jax.ShapeDtypeStruct((SLOTS, state.shape[1] // 2), jnp.int16)] * 2
+        + [jax.ShapeDtypeStruct((1,), jnp.int32)],
         in_specs=[SMEM, VMEM, VMEM, ANYWHERE],
-        out_specs=[VMEM] * 2,
+        out_specs=[VMEM] * 2 + [SMEM],
         scratch_shapes=[pltpu.VMEM(state.shape, F32), pltpu.SemaphoreType.DMA],
         compiler_params=PARAMS,
         name="pick",
@@ -153,43 +160,32 @@
     )(place, blocks, weights, state)
 
 
-def order_kernel(groups, place, blocks, *outs):
-    outs, fits = outs[:-1], outs[-1]
+def order_kernel(batch, groups, place, blocks, *outs):
     device, held = place[0], place[1]
     size = blocks.shape[1]
     lane = lax.broadcasted_iota(jnp.int32, (size, size), 1)
     sub = lax.broadcasted_iota(jnp.int32, (size, size), 0)
-    for batch in range(blocks.shape[0]):
-        pair_row, pair_column = both_ways(blocks[batch : batch + 1, :] // (2 * held))
-        before = jnp.where((pair_row == pair_column) & (lane < sub), 1.0, 0.0)
-        rank = jnp.sum(before, axis=1, keepdims=True).astype(jnp.int32)
-        away = (2 * pair_column.astype(jnp.int32)) ^ device
-        distance = 8 * ((away >> 3) & 1) + 4 * ((away >> 4) & 1) + ((away >> 1) & 3)
-        slot = rank if batch == 0 else SLOTS - 1 - rank
-        for distances, out in zip(groups, outs):
-            where = jnp.full(rank.shape, -SLOTS, jnp.int32)
-            for index, known in enumerate(distances):
-                where = jnp.where(distance == known, SLOTS * index, where)
-            slots = lax.broadcasted_iota(jnp.int32, (size, out.shape[1]), 1)
-            chosen = jnp.where(slots == where + slot, 1.0, 0.0)
-            out[batch * size : (batch + 1) * size, :] = chosen.astype(BF16)
-    counts = jnp.zeros((16, 1), F32)
-    for batch in range(blocks.shape[0]):
-        chip = blocks[batch : batch + 1, :] // (2 * held)
-        chips = lax.broadcasted_iota(jnp.int32, (16, size), 0)
-        counts = counts + jnp.sum(jnp.where(chips == chip, 1.0, 0.0), axis=1, keepdims=True)
-    fits[0] = (jnp.max(counts) <= SLOTS).astype(jnp.int32)
-
-
-def order(place, blocks, groups):
+    pair_row, pair_column = both_ways(blocks[batch : batch + 1, :] // (2 * held))
+    before = jnp.where((pair_row == pair_column) & (lane < sub), 1.0, 0.0)
+    rank = jnp.sum(before, axis=1, keepdims=True).astype(jnp.int32)
+    away = (2 * pair_column.astype(jnp.int32)) ^ device
+    distance = 8 * ((away >> 3) & 1) + 4 * ((away >> 4) & 1) + ((away >> 1) & 3)
+    slot = rank if batch == 0 else SLOTS - 1 - rank
+    for distances, out in zip(groups, outs):
+        where = jnp.full(rank.shape, -SLOTS, jnp.int32)
+        for index, known in enumerate(distances):
+            where = jnp.where(distance == known, SLOTS * index, where)
+        slots = lax.broadcasted_iota(jnp.int32, out.shape, 1)
+        out[...] = jnp.where(slots == where + slot, 1.0, 0.0).astype(BF16)
+
+
+def order(batch, place, blocks, groups):
+    rows = blocks.shape[1]
     return pl.pallas_call(
-        functools.partial(order_kernel, groups),
-        out_shape=[
-            jax.ShapeDtypeStruct((blocks.size, SLOTS * len(group)), BF16) for group in groups
-        ]
-        + [jax.ShapeDtypeStruct((1,), jnp.int32)],
+        functools.partial(order_kernel, batch, groups),
+        out_shape=[jax.ShapeDtypeStruct((rows, SLOTS * len(group)), BF16) for group in groups],
         in_specs=[SMEM, VMEM],
-        out_specs=[VMEM] * len(groups) + [SMEM],
+        out_specs=[VMEM] * len(groups),
         compiler_params=PARAMS,
         cost_estimate=pl.CostEstimate(flops=10**6, bytes_accessed=10**6, transcendentals=0),
         name="order",
@@ -197,35 +193,35 @@
 
 
 def put_in_order(chosen, pieces):
-    size = chosen.shape[0] // 2
     values = [ref[index].astype(jnp.int32) for ref in pieces for index in range(ref.shape[0])]
     high, low = split(jnp.concatenate(values, axis=0).astype(F32))
-    second = chosen[size:, :]
-    return nn(chosen[:size, :], high), nn(second, high) + nn(second, low)
-
-
-def early_kernel(chosen, *refs):
-    size = chosen.shape[0] // 2
-    refs[-1][:size, :], refs[-1][size:, :] = put_in_order(chosen, refs[:-1])
-
-
-def late_kernel(chosen, early, *refs):
-    size = chosen.shape[0] // 2
-    first, second = put_in_order(chosen, refs[:-2])
-    refs[-2][...] = ((first + early[:size, :]) * UNIT).astype(BF16)
-    refs[-1][...] = (second + early[size:, :]).astype(jnp.int32).astype(jnp.int16)
+    first, second = chosen[0][...], chosen[1][...]
+    return nn(first, high), nn(second, high) + nn(second, low)
+
+
+def early_kernel(first, second, *refs):
+    size = first.shape[0]
+    refs[-1][:size, :], refs[-1][size:, :] = put_in_order((first, second), refs[:-1])
+
+
+def late_kernel(first, second, early, *refs):
+    size = first.shape[0]
+    codes = put_in_order((first, second), refs[:-2])
+    refs[-2][...] = ((codes[0] + early[:size, :]) * UNIT).astype(BF16)
+    refs[-1][...] = (codes[1] + early[size:, :]).astype(jnp.int32).astype(jnp.int16)
 
 
 def early_rows(chosen, pieces):
+    rows = chosen[0].shape[0]
     return pl.pallas_call(
         early_kernel,
-        out_shape=jax.ShapeDtypeStruct((chosen.shape[0], pieces[0].shape[-1]), F32),
-        in_specs=[VMEM] * (1 + len(pieces)),
+        out_shape=jax.ShapeDtypeStruct((2 * rows, pieces[0].shape[-1]), F32),
+        in_specs=[VMEM] * (2 + len(pieces)),
         out_specs=VMEM,
         compiler_params=PARAMS,
         cost_estimate=pl.CostEstimate(flops=10**9, bytes_accessed=4 * 10**6, transcendentals=0),
         name="early_rows",
-    )(chosen, *pieces)
+    )(*chosen, *pieces)
 
 
 def late_rows(chosen, early, pieces):
@@ -233,11 +229,11 @@
     return pl.pallas_call(
         late_kernel,
         out_shape=[jax.ShapeDtypeStruct(shape, BF16), jax.ShapeDtypeStruct(shape, jnp.int16)],
-        in_specs=[VMEM] * (2 + len(pieces)),
+        in_specs=[VMEM] * (3 + len(pieces)),
         out_specs=[VMEM] * 2,
         compiler_params=PARAMS,
         name="late_rows",
-    )(chosen, early, *pieces)
+    )(*chosen, early, *pieces)
 
 
 def eliminate(covariance, work, inverse):
@@ -464,21 +460,23 @@
 
 
 def by_slots(place, ensemble, blocks, weights):
-    keep, send = pick(place, blocks, weights, ensemble)
+    keep, send, fits = pick(place, blocks, weights, ensemble)
     own = (keep + swap(send, CORE))[None]
     far, near = swap(own, FAR_Z), swap(own, NEAR_Z)
     near_far = swap(far, NEAR_Z)
     both = joined(own, near)
     both_x = swap(both, X)
     far_y = swap(after(far, near), Y)
-    near_far_y = swap(near_far, Y)
+    places = [order(0, place, blocks, (EARLY, LATE))]
+    near_far_y = swap(after(near_far, places[0]), Y)
     both_y = swap(after(joined(both, both_x), near_far), Y)
     far_x = swap(joined(far, far_y), X)
-    near_far_x = swap(joined(near_far, near_far_y), X)
-    early_places, late_places, fits = order(place, blocks, (EARLY, LATE))
+    places.append(order(1, place, after(blocks, far_y), (EARLY, LATE)))
+    near_far_x = swap(after(joined(near_far, near_far_y), places[1]), X)
+    early_places, late_places = zip(*places)
     pieces = [own, far, near, near_far, both_x, far_y, near_far_y, both_y, far_x]
     early = early_rows(early_places, pieces)
-    return late_rows(late_places, early, [near_far_x]), fits
+    return late_rows(late_places, early, [near_far_x]), after(fits, near)
 
 
 def add_by_swaps(value):

time: 82.4 us -> 83.3 us (1.011)
  Pallas kernels: 59 us -> 60.1 us
    pallas_call x2 -> x3, Pallas kernels: 2.75 us -> 3.44 us  [the longest x2 2.44 us: order(): pl.pallas_call(functools.partial(order_kernel, batch, groups), out_shape=...]
  transfers between devices with their start and end apart: 12 -> 12, of which waited for: 5 -> 7; matrix products, arithmetic and copies ran while one was open for 0% -> 0% of each run, Pallas kernels for 61% -> 61%
where the time goes in v9:
time: 83.3 us; the launch traced here: 83 us
  Pallas kernels  60.1 us (72%)
  starting transfers between devices  15.1 us (18%)
  waiting for transfers between devices  6.59 us (8%)
  between operations  0.96 us (1%)
    pallas_call x2, Pallas kernels, batch_call(): pl.pallas_call(kernel, out_shape=outs, in_specs=[SMEM, VMEM, VMEM, ANYWHE...  53.8 us
    ppermute x12, starting transfers between devices, swap(): return lax.ppermute(value, AXES, [(i, i ^ mask) for i in range(32)])  15.1 us
    ppermute x12, waiting for transfers between devices, swap(): return lax.ppermute(value, AXES, [(i, i ^ mask) for i in range(32)])  6.59 us
    pallas_call x1, Pallas kernels, pick(): pl.pallas_call(pick_kernel, out_shape=[jax.ShapeDtypeStruct((SLOTS, state...  2.49 us
    pallas_call x2, Pallas kernels, order(): pl.pallas_call(functools.partial(order_kernel, batch, groups), out_shape=...  2.44 us
  transfers between devices with their start and end apart: 12, of which 7 were waited for; matrix products, arithmetic and copies ran while one was open for 0% of the time, Pallas kernels for 61%

profile of v9, /device:TPU:0, one launch (start us, length us, event | category | flops | bytes accessed | tf_op | source)
XLA Modules:
  0.0 83.0 jit_solution(14072569919279164508)
XLA Ops:
  0.1 2.5 %pick.1 = (s16[56,512]{1,0:T(8,128)(2,1)S(1)}, s16[56,512]{1,0:T(8,128)(2,1)S(1)}, s32[1]{0:T(128)}) custom-call(s32[2]{0:T(128)S(1)} %pad_add_fusion.4.place, s32[2,256]{1,0:T(2,128)} %blocks.4, f32[2,4,256]{2,1,0:T(4,128)} %bitcast.5, f32[128,1024]{1,0:T(8,128)} %state_ref.3), custom_call_target="tpu_custom_call" | custom-call | tf_op jit(solution)/shard_map/pick/pallas_call | solution.py:122
  2.6 0.5 collective-permute-start.5
  3.1 0.9 %collective-permute-done.5 = s16[56,512]{1,0:T(8,128)(2,1)S(1)} collective-permute-done((s16[56,512]{1,0:T(8,128)(2,1)S(1)}, s16[56,512]{1,0:T(8,128)(2,1)S(1)}, u32[]{:S(2)}, u32[]{:S(2)}) %collective-permute-start.5) | collective-permute-done | bytes 57376 | tf_op jit(solution)/shard_map/ppermute | solution.py:447
  4.0 3.0 %collective-permute-start.6 = (s16[1,56,512]{2,1,0:T(8,128)(2,1)S(1)}, s16[1,56,512]{2,1,0:T(8,128)(2,1)S(1)}, u32[]{:S(2)}, u32[]{:S(2)}) collective-permute-start(s16[1,56,512]{2,1,0:T(8,128)(2,1)S(1)} %add_bitcast_fusion.refs_0_), channel_id=1, source_target_pairs={{0,8},{1,9},{2,10},{3,11},{4,12},{5,13},{6,14},{7,15},{8,0},{9,1},... | collective-permute-start | bytes 172040 | tf_op jit(solution)/shard_map/ppermute | solution.py:447
  7.0 2.6 %collective-permute-start.7 = (s16[1,56,512]{2,1,0:T(8,128)(2,1)S(1)}, s16[1,56,512]{2,1,0:T(8,128)(2,1)S(1)}, u32[]{:S(2)}, u32[]{:S(2)}) collective-permute-start(s16[1,56,512]{2,1,0:T(8,128)(2,1)S(1)} %add_bitcast_fusion.refs_0_), channel_id=1, source_target_pairs={{0,16},{1,17},{2,18},{3,19},{4,20},{5,21},{6,22},{7,23},{8,24},{9,... | collective-permute-start | bytes 172040 | tf_op jit(solution)/shard_map/ppermute | solution.py:447
  9.6 1.6 %collective-permute-start.10 = (s16[2,56,512]{2,1,0:T(8,128)(2,1)S(1)}, s16[2,56,512]{2,1,0:T(8,128)(2,1)S(1)}, u32[]{:S(2)}, u32[]{:S(2)}) collective-permute-start(s16[2,56,512]{2,1,0:T(8,128)(2,1)S(1)} %pad_add_fusion.1), channel_id=1, source_target_pairs={{0,4},{1,5},{2,6},{3,7},{4,0},{5,1},{6,2},{7,3},{8,12},{9,13},{10,... | collective-permute-start | bytes 344072 | tf_op jit(solution)/shard_map/ppermute | solution.py:447
  11.2 1.7 %collective-permute-done.7.refs_1_ = s16[1,56,512]{2,1,0:T(8,128)(2,1)S(1)} collective-permute-done((s16[1,56,512]{2,1,0:T(8,128)(2,1)S(1)}, s16[1,56,512]{2,1,0:T(8,128)(2,1)S(1)}, u32[]{:S(2)}, u32[]{:S(2)}) %collective-permute-start.7) | collective-permute-done | bytes 57376 | tf_op jit(solution)/shard_map/ppermute | solution.py:447
  12.9 0.3 collective-permute-start.9
  13.2 1.2 %order.2 = (bf16[256,784]{1,0:T(8,128)(2,1)S(1)}, bf16[256,112]{1,0:T(8,128)(2,1)S(1)}) custom-call(s32[2]{0:T(128)S(1)} %pad_add_fusion.4.place, s32[2,256]{1,0:T(2,128)} %blocks.4), custom_call_target="tpu_custom_call" | custom-call | flops 1000000 | bytes 1000000 | tf_op jit(solution)/shard_map/order/pallas_call | solution.py:184
  14.4 1.6 %collective-permute-start.8 = (s16[1,56,512]{2,1,0:T(8,128)(2,1)S(1)}, s16[1,56,512]{2,1,0:T(8,128)(2,1)S(1)}, u32[]{:S(2)}, u32[]{:S(2)}) collective-permute-start(s16[1,56,512]{2,1,0:T(8,128)(2,1)S(1)} %collective-permute-done.7.refs_1_), channel_id=1, source_target_pairs={{0,2},{1,3},{2,0},{3,1},{4,6},{5,7},{6,4},{7,5},{8,10},{9,11},{10,... | collective-permute-start | bytes 172040 | tf_op jit(solution)/shard_map/ppermute | solution.py:447
  16.0 1.0 %collective-permute-done.9.refs_3_ = s16[1,56,512]{2,1,0:T(8,128)(2,1)S(1)} collective-permute-done((s16[1,56,512]{2,1,0:T(8,128)(2,1)S(1)}, s16[1,56,512]{2,1,0:T(8,128)(2,1)S(1)}, u32[]{:S(2)}, u32[]{:S(2)}) %collective-permute-start.9) | collective-permute-done | bytes 57376 | tf_op jit(solution)/shard_map/ppermute | solution.py:447
  17.1 1.5 %collective-permute-start.11 = (s16[1,56,512]{2,1,0:T(8,128)(2,1)S(1)}, s16[1,56,512]{2,1,0:T(8,128)(2,1)S(1)}, u32[]{:S(2)}, u32[]{:S(2)}) collective-permute-start(s16[1,56,512]{2,1,0:T(8,128)(2,1)S(1)} %collective-permute-done.9.refs_3_), channel_id=1, source_target_pairs={{0,2},{1,3},{2,0},{3,1},{4,6},{5,7},{6,4},{7,5},{8,10},{9,11},{10,... | collective-permute-start | bytes 172040 | tf_op jit(solution)/shard_map/ppermute | solution.py:447
  18.6 0.6 collective-permute-start.12
  19.2 1.6 %collective-permute-start.13 = (s16[2,56,512]{2,1,0:T(8,128)(2,1)S(1)}, s16[2,56,512]{2,1,0:T(8,128)(2,1)S(1)}, u32[]{:S(2)}, u32[]{:S(2)}) collective-permute-start(s16[2,56,512]{2,1,0:T(8,128)(2,1)S(1)} %pad_add_fusion.2), channel_id=1, source_target_pairs={{0,4},{1,5},{2,6},{3,7},{4,0},{5,1},{6,2},{7,3},{8,12},{9,13},{10,... | collective-permute-start | bytes 344072 | tf_op jit(solution)/shard_map/ppermute | solution.py:447
  20.8 1.2 %order.3 = (bf16[256,784]{1,0:T(8,128)(2,1)S(1)}, bf16[256,112]{1,0:T(8,128)(2,1)S(1)}) custom-call(s32[2]{0:T(128)S(1)} %pad_add_fusion.4.place, s32[2,256]{1,0:T(2,128)} %blocks.4), custom_call_target="tpu_custom_call" | custom-call | flops 1000000 | bytes 1000000 | tf_op jit(solution)/shard_map/order/pallas_call | solution.py:184
  22.0 1.3 %collective-permute-start.14 = (s16[2,56,512]{2,1,0:T(8,128)(2,1)S(1)}, s16[2,56,512]{2,1,0:T(8,128)(2,1)S(1)}, u32[]{:S(2)}, u32[]{:S(2)}) collective-permute-start(s16[2,56,512]{2,1,0:T(8,128)(2,1)S(1)} %pad_add_fusion.3), channel_id=1, source_target_pairs={{0,4},{1,5},{2,6},{3,7},{4,0},{5,1},{6,2},{7,3},{8,12},{9,13},{10,... | collective-permute-start | bytes 344072 | tf_op jit(solution)/shard_map/ppermute | solution.py:447
  24.2 0.5 collective-permute-done.12.refs_7_
  24.7 1.0 %early_rows.1.early = f32[512,512]{1,0:T(8,128)S(1)} custom-call(bf16[256,784]{1,0:T(8,128)(2,1)S(1)} %get-tuple-element.49.first, bf16[256,784]{1,0:T(8,128)(2,1)S(1)} %get-tuple-element.50.second, s16[1,56,512]{2,1,0:T(8,128)(2,1)S(1)} %add_bitcast_fusion.refs_0_, s16[1,56,512]{2,1,0:T(8,128)(2,1)S(1)} %collective-permute-done.7.refs_1_, ...), custom_call_target="tpu_custom_call" | custom-call | flops 1000000000 | bytes 4000000 | tf_op jit(solution)/shard_map/early_rows/pallas_call | solution.py:216
  25.7 1.2 %collective-permute-done.14.refs_0_ = s16[2,56,512]{2,1,0:T(8,128)(2,1)S(1)} collective-permute-done((s16[2,56,512]{2,1,0:T(8,128)(2,1)S(1)}, s16[2,56,512]{2,1,0:T(8,128)(2,1)S(1)}, u32[]{:S(2)}, u32[]{:S(2)}) %collective-permute-start.14) | collective-permute-done | bytes 114720 | tf_op jit(solution)/shard_map/ppermute | solution.py:447
  26.9 0.4 late_rows.1
  27.5 0.5 collective-permute-start.15
  28.0 1.0 %collective-permute-done.16.other = bf16[256,512]{1,0:T(8,128)(2,1)S(1)} collective-permute-done((bf16[256,512]{1,0:T(8,128)(2,1)S(1)}, bf16[256,512]{1,0:T(8,128)(2,1)S(1)}, u32[]{:S(2)}, u32[]{:S(2)}) %collective-permute-start.16) | collective-permute-done | bytes 262176 | tf_op jit(solution)/shard_map/ppermute | solution.py:447
  29.0 47.4 %first_batch.1 = (bf16[256,1024]{1,0:T(8,128)(2,1)S(1)}, bf16[256,1024]{1,0:T(8,128)(2,1)S(1)}) custom-call(s32[2]{0:T(128)S(1)} %pad_add_fusion.4.place, s32[2,256]{1,0:T(2,128)S(1)} %copy-done.1, f32[2,256]{1,0:T(2,128)S(1)} %copy-done.2, bf16[2,256,1024]{2,1,0:T(8,128)(2,1)S(1)} %copy-done, bf16[256,512]{1,0:T(8,128)(2,1)S(1)} %get-tuple-element.55.own, ...), custom_call_target="tpu_custom_call" | custom-call | tf_op jit(solution)/shard_map/first_batch/pallas_call | solution.py:415
  76.4 6.4 %second_batch.1 = f32[128,1024]{1,0:T(8,128)} custom-call(s32[2]{0:T(128)S(1)} %pad_add_fusion.4.place, s32[2,256]{1,0:T(2,128)S(1)} %copy-done.1, f32[2,256]{1,0:T(2,128)S(1)} %copy-done.2, bf16[2,256,1024]{2,1,0:T(8,128)(2,1)S(1)} %copy-done, s16[256,512]{1,0:T(8,128)(2,1)S(1)} %get-tuple-element.54.own, ...), custom_call_target="tpu_custom_call" | custom-call | tf_op jit(solution)/shard_map/second_batch/pallas_call | solution.py:415
  (28 shorter events, 0.6 us)
Async XLA Ops:
  2.6 1.4 %collective-permute-start.5 = (s16[56,512]{1,0:T(8,128)(2,1)S(1)}, s16[56,512]{1,0:T(8,128)(2,1)S(1)}, u32[]{:S(2)}, u32[]{:S(2)}) collective-permute-start(s16[56,512]{1,0:T(8,128)(2,1)S(1)} %get-tuple-element.43), channel_id=1, source_target_pairs={{0,1},{1,0},{2,3},{3,2},{4,5},{5,4},{6,7},{7,6},{8,9},{9,8},{10,11... | collective-permute-start | bytes 172040 | tf_op jit(solution)/shard_map/ppermute | solution.py:447
  4.0 5.6 %collective-permute-start.6 = (s16[1,56,512]{2,1,0:T(8,128)(2,1)S(1)}, s16[1,56,512]{2,1,0:T(8,128)(2,1)S(1)}, u32[]{:S(2)}, u32[]{:S(2)}) collective-permute-start(s16[1,56,512]{2,1,0:T(8,128)(2,1)S(1)} %add_bitcast_fusion.refs_0_), channel_id=1, source_target_pairs={{0,8},{1,9},{2,10},{3,11},{4,12},{5,13},{6,14},{7,15},{8,0},{9,1},... | collective-permute-start | bytes 172040 | tf_op jit(solution)/shard_map/ppermute | solution.py:447
  7.0 5.9 %collective-permute-start.7 = (s16[1,56,512]{2,1,0:T(8,128)(2,1)S(1)}, s16[1,56,512]{2,1,0:T(8,128)(2,1)S(1)}, u32[]{:S(2)}, u32[]{:S(2)}) collective-permute-start(s16[1,56,512]{2,1,0:T(8,128)(2,1)S(1)} %add_bitcast_fusion.refs_0_), channel_id=1, source_target_pairs={{0,16},{1,17},{2,18},{3,19},{4,20},{5,21},{6,22},{7,23},{8,24},{9,... | collective-permute-start | bytes 172040 | tf_op jit(solution)/shard_map/ppermute | solution.py:447
  9.6 9.0 %collective-permute-start.10 = (s16[2,56,512]{2,1,0:T(8,128)(2,1)S(1)}, s16[2,56,512]{2,1,0:T(8,128)(2,1)S(1)}, u32[]{:S(2)}, u32[]{:S(2)}) collective-permute-start(s16[2,56,512]{2,1,0:T(8,128)(2,1)S(1)} %pad_add_fusion.1), channel_id=1, source_target_pairs={{0,4},{1,5},{2,6},{3,7},{4,0},{5,1},{6,2},{7,3},{8,12},{9,13},{10,... | collective-permute-start | bytes 344072 | tf_op jit(solution)/shard_map/ppermute | solution.py:447
  12.9 4.2 %collective-permute-start.9 = (s16[1,56,512]{2,1,0:T(8,128)(2,1)S(1)}, s16[1,56,512]{2,1,0:T(8,128)(2,1)S(1)}, u32[]{:S(2)}, u32[]{:S(2)}) collective-permute-start(s16[1,56,512]{2,1,0:T(8,128)(2,1)S(1)} %collective-permute-done.7.refs_1_), channel_id=1, source_target_pairs={{0,8},{1,9},{2,10},{3,11},{4,12},{5,13},{6,14},{7,15},{8,0},{9,1},... | collective-permute-start | bytes 172040 | tf_op jit(solution)/shard_map/ppermute | solution.py:447
  14.4 4.7 %collective-permute-start.8 = (s16[1,56,512]{2,1,0:T(8,128)(2,1)S(1)}, s16[1,56,512]{2,1,0:T(8,128)(2,1)S(1)}, u32[]{:S(2)}, u32[]{:S(2)}) collective-permute-start(s16[1,56,512]{2,1,0:T(8,128)(2,1)S(1)} %collective-permute-done.7.refs_1_), channel_id=1, source_target_pairs={{0,2},{1,3},{2,0},{3,1},{4,6},{5,7},{6,4},{7,5},{8,10},{9,11},{10,... | collective-permute-start | bytes 172040 | tf_op jit(solution)/shard_map/ppermute | solution.py:447
  17.1 4.9 %collective-permute-start.11 = (s16[1,56,512]{2,1,0:T(8,128)(2,1)S(1)}, s16[1,56,512]{2,1,0:T(8,128)(2,1)S(1)}, u32[]{:S(2)}, u32[]{:S(2)}) collective-permute-start(s16[1,56,512]{2,1,0:T(8,128)(2,1)S(1)} %collective-permute-done.9.refs_3_), channel_id=1, source_target_pairs={{0,2},{1,3},{2,0},{3,1},{4,6},{5,7},{6,4},{7,5},{8,10},{9,11},{10,... | collective-permute-start | bytes 172040 | tf_op jit(solution)/shard_map/ppermute | solution.py:447
  18.6 6.1 %collective-permute-start.12 = (s16[4,56,512]{2,1,0:T(8,128)(2,1)S(1)}, s16[4,56,512]{2,1,0:T(8,128)(2,1)S(1)}, u32[]{:S(2)}, u32[]{:S(2)}) collective-permute-start(s16[4,56,512]{2,1,0:T(8,128)(2,1)S(1)} %pad_add_fusion), channel_id=1, source_target_pairs={{0,2},{1,3},{2,0},{3,1},{4,6},{5,7},{6,4},{7,5},{8,10},{9,11},{10,... | collective-permute-start | bytes 688136 | tf_op jit(solution)/shard_map/ppermute | solution.py:447
  19.2 5.0 %collective-permute-start.13 = (s16[2,56,512]{2,1,0:T(8,128)(2,1)S(1)}, s16[2,56,512]{2,1,0:T(8,128)(2,1)S(1)}, u32[]{:S(2)}, u32[]{:S(2)}) collective-permute-start(s16[2,56,512]{2,1,0:T(8,128)(2,1)S(1)} %pad_add_fusion.2), channel_id=1, source_target_pairs={{0,4},{1,5},{2,6},{3,7},{4,0},{5,1},{6,2},{7,3},{8,12},{9,13},{10,... | collective-permute-start | bytes 344072 | tf_op jit(solution)/shard_map/ppermute | solution.py:447
  22.0 4.9 %collective-permute-start.14 = (s16[2,56,512]{2,1,0:T(8,128)(2,1)S(1)}, s16[2,56,512]{2,1,0:T(8,128)(2,1)S(1)}, u32[]{:S(2)}, u32[]{:S(2)}) collective-permute-start(s16[2,56,512]{2,1,0:T(8,128)(2,1)S(1)} %pad_add_fusion.3), channel_id=1, source_target_pairs={{0,4},{1,5},{2,6},{3,7},{4,0},{5,1},{6,2},{7,3},{8,12},{9,13},{10,... | collective-permute-start | bytes 344072 | tf_op jit(solution)/shard_map/ppermute | solution.py:447
  23.9 3.3 %copy-start.3 = (f32[128,1024]{1,0:T(8,128)S(1)}, f32[128,1024]{1,0:T(8,128)}, u32[]{:S(2)}) copy-start(f32[128,1024]{1,0:T(8,128)} %state_ref.3) | copy-start | bytes 1572868
  24.0 3.3 %copy-start.4 = (f32[2,256,4]{1,2,0:T(4,128)S(1)}, f32[2,256,4]{1,2,0:T(4,128)}, u32[]{:S(2)}) copy-start(f32[2,256,4]{1,2,0:T(4,128)} %param.10) | copy-start | bytes 24580
  24.0 3.3 %copy-start.5 = (s32[2,256]{1,0:T(2,128)S(1)}, s32[2,256]{1,0:T(2,128)}, u32[]{:S(2)}) copy-start(s32[2,256]{1,0:T(2,128)} %blocks.4) | copy-start | bytes 6148
  27.3 1.7 %copy-start = (bf16[2,256,1024]{2,1,0:T(8,128)(2,1)S(1)}, bf16[2,256,1024]{2,1,0:T(8,128)(2,1)}, u32[]{:S(2)}) copy-start(bf16[2,256,1024]{2,1,0:T(8,128)(2,1)} %noise_ref.3) | copy-start | bytes 3145732
  27.3 1.7 %copy-start.1 = (s32[2,256]{1,0:T(2,128)S(1)}, s32[2,256]{1,0:T(2,128)}, u32[]{:S(2)}) copy-start(s32[2,256]{1,0:T(2,128)} %tags.3) | copy-start | bytes 6148
  27.3 1.7 %copy-start.2 = (f32[2,256]{1,0:T(2,128)S(1)}, f32[2,256]{1,0:T(2,128)}, u32[]{:S(2)}) copy-start(f32[2,256]{1,0:T(2,128)} %values.3) | copy-start | bytes 6148
  27.4 1.6 %collective-permute-start.16 = (bf16[256,512]{1,0:T(8,128)(2,1)S(1)}, bf16[256,512]{1,0:T(8,128)(2,1)S(1)}, u32[]{:S(2)}, u32[]{:S(2)}) collective-permute-start(bf16[256,512]{1,0:T(8,128)(2,1)S(1)} %get-tuple-element.55.own), channel_id=1, source_target_pairs={{0,1},{1,0},{2,3},{3,2},{4,5},{5,4},{6,7},{7,6},{8,9},{9,8},{10,11... | collective-permute-start | bytes 786440 | tf_op jit(solution)/shard_map/ppermute | solution.py:447
  27.5 48.9 %collective-permute-start.15 = (s16[256,512]{1,0:T(8,128)(2,1)S(1)}, s16[256,512]{1,0:T(8,128)(2,1)S(1)}, u32[]{:S(2)}, u32[]{:S(2)}) collective-permute-start(s16[256,512]{1,0:T(8,128)(2,1)S(1)} %get-tuple-element.54.own), channel_id=1, source_target_pairs={{0,1},{1,0},{2,3},{3,2},{4,5},{5,4},{6,7},{7,6},{8,9},{9,8},{10,11... | collective-permute-start | bytes 786440 | tf_op jit(solution)/shard_map/ppermute | solution.py:447

commit v10 on v8

--- a/solution.py
+++ b/solution.py
@@ -404,9 +404,10 @@
     load_state.start()
     load.start()
     w, v = whitened[...], white_innov[...]
-    observed = rounded(update(both_halves(place, own, other), w, v) * UNIT)
+    codes = both_halves(place, own, other)
     load_state.wait()
-    first = update(state[...], w, v)
+    updated = update(jnp.concatenate([codes, state[...]], axis=0), w, v)
+    observed, first = rounded(updated[: codes.shape[0]] * UNIT), updated[codes.shape[0] :]
 
     def store(w, v):
         analysis[...] = update(first, w, v)

time: 82.4 us -> 84.4 us (1.024); the launches traced: 82.2 us -> 85.3 us
  Pallas kernels: 59 us -> 62.1 us
    pallas_call x2, Pallas kernels: 53.8 us -> 56.9 us  [batch_call(): pl.pallas_call(kernel, out_shape=outs, in_specs=[SMEM, VMEM, VMEM, ANYWHE...]
  transfers between devices with their start and end apart: 12 -> 12, of which waited for: 5 -> 5; matrix products, arithmetic and copies ran while one was open for 0% -> 0% of each run, Pallas kernels for 61% -> 59%
where the time goes in v10:
time: 84.4 us; the launch traced here: 85.3 us
  Pallas kernels  62.1 us (74%)
  starting transfers between devices  15.3 us (18%)
  waiting for transfers between devices  6.68 us (8%)
  between operations  0.98 us (1%)
    pallas_call x2, Pallas kernels, batch_call(): pl.pallas_call(kernel, out_shape=outs, in_specs=[SMEM, VMEM, VMEM, ANYWHE...  56.9 us
    ppermute x12, starting transfers between devices, swap(): return lax.ppermute(value, AXES, [(i, i ^ mask) for i in range(32)])  15.3 us
    ppermute x12, waiting for transfers between devices, swap(): return lax.ppermute(value, AXES, [(i, i ^ mask) for i in range(32)])  6.68 us
    pallas_call x1, Pallas kernels, pick(): pl.pallas_call(pick_kernel, out_shape=[jax.ShapeDtypeStruct((SLOTS, state...  2.05 us
    pallas_call x1, Pallas kernels, order(): pl.pallas_call(functools.partial(order_kernel, groups), out_shape=[jax.Sh...  1.74 us
  transfers between devices with their start and end apart: 12, of which 5 were waited for; matrix products, arithmetic and copies ran while one was open for 0% of the time, Pallas kernels for 59%

profile of v10, /device:TPU:0, one launch (start us, length us, event | category | flops | bytes accessed | tf_op | source)
XLA Modules:
  0.0 85.3 jit_solution(7243002767169225325)
XLA Ops:
  0.0 0.1 pad_add_fusion.4.place
  0.1 2.0 %pick.1 = (s16[56,512]{1,0:T(8,128)(2,1)S(1)}, s16[56,512]{1,0:T(8,128)(2,1)S(1)}) custom-call(s32[2]{0:T(128)S(1)} %pad_add_fusion.4.place, s32[2,256]{1,0:T(2,128)} %blocks.3, f32[2,4,256]{2,1,0:T(4,128)} %bitcast.5, f32[128,1024]{1,0:T(8,128)} %state_ref.3), custom_call_target="tpu_custom_call" | custom-call | tf_op jit(solution)/shard_map/pick/pallas_call | solution.py:116
  2.1 0.5 collective-permute-start.5
  2.7 0.9 %collective-permute-done.5 = s16[56,512]{1,0:T(8,128)(2,1)S(1)} collective-permute-done((s16[56,512]{1,0:T(8,128)(2,1)S(1)}, s16[56,512]{1,0:T(8,128)(2,1)S(1)}, u32[]{:S(2)}, u32[]{:S(2)}) %collective-permute-start.5) | collective-permute-done | bytes 57376 | tf_op jit(solution)/shard_map/ppermute | solution.py:452
  3.6 3.0 %collective-permute-start.7 = (s16[1,56,512]{2,1,0:T(8,128)(2,1)S(1)}, s16[1,56,512]{2,1,0:T(8,128)(2,1)S(1)}, u32[]{:S(2)}, u32[]{:S(2)}) collective-permute-start(s16[1,56,512]{2,1,0:T(8,128)(2,1)S(1)} %add_bitcast_fusion.refs_0_), channel_id=1, source_target_pairs={{0,8},{1,9},{2,10},{3,11},{4,12},{5,13},{6,14},{7,15},{8,0},{9,1},... | collective-permute-start | bytes 172040 | tf_op jit(solution)/shard_map/ppermute | solution.py:452
  6.5 2.6 %collective-permute-start.6 = (s16[1,56,512]{2,1,0:T(8,128)(2,1)S(1)}, s16[1,56,512]{2,1,0:T(8,128)(2,1)S(1)}, u32[]{:S(2)}, u32[]{:S(2)}) collective-permute-start(s16[1,56,512]{2,1,0:T(8,128)(2,1)S(1)} %add_bitcast_fusion.refs_0_), channel_id=1, source_target_pairs={{0,16},{1,17},{2,18},{3,19},{4,20},{5,21},{6,22},{7,23},{8,24},{9,... | collective-permute-start | bytes 172040 | tf_op jit(solution)/shard_map/ppermute | solution.py:452
  9.2 1.6 %collective-permute-start.9 = (s16[2,56,512]{2,1,0:T(8,128)(2,1)S(1)}, s16[2,56,512]{2,1,0:T(8,128)(2,1)S(1)}, u32[]{:S(2)}, u32[]{:S(2)}) collective-permute-start(s16[2,56,512]{2,1,0:T(8,128)(2,1)S(1)} %pad_add_fusion.1), channel_id=1, source_target_pairs={{0,4},{1,5},{2,6},{3,7},{4,0},{5,1},{6,2},{7,3},{8,12},{9,13},{10,... | collective-permute-start | bytes 344072 | tf_op jit(solution)/shard_map/ppermute | solution.py:452
  10.7 1.7 %collective-permute-done.6.refs_1_ = s16[1,56,512]{2,1,0:T(8,128)(2,1)S(1)} collective-permute-done((s16[1,56,512]{2,1,0:T(8,128)(2,1)S(1)}, s16[1,56,512]{2,1,0:T(8,128)(2,1)S(1)}, u32[]{:S(2)}, u32[]{:S(2)}) %collective-permute-start.6) | collective-permute-done | bytes 57376 | tf_op jit(solution)/shard_map/ppermute | solution.py:452
  12.4 0.3 collective-permute-start.8
  12.8 1.5 %collective-permute-start.10 = (s16[1,56,512]{2,1,0:T(8,128)(2,1)S(1)}, s16[1,56,512]{2,1,0:T(8,128)(2,1)S(1)}, u32[]{:S(2)}, u32[]{:S(2)}) collective-permute-start(s16[1,56,512]{2,1,0:T(8,128)(2,1)S(1)} %collective-permute-done.6.refs_1_), channel_id=1, source_target_pairs={{0,2},{1,3},{2,0},{3,1},{4,6},{5,7},{6,4},{7,5},{8,10},{9,11},{10,... | collective-permute-start | bytes 172040 | tf_op jit(solution)/shard_map/ppermute | solution.py:452
  14.3 2.3 %collective-permute-done.8.refs_3_ = s16[1,56,512]{2,1,0:T(8,128)(2,1)S(1)} collective-permute-done((s16[1,56,512]{2,1,0:T(8,128)(2,1)S(1)}, s16[1,56,512]{2,1,0:T(8,128)(2,1)S(1)}, u32[]{:S(2)}, u32[]{:S(2)}) %collective-permute-start.8) | collective-permute-done | bytes 57376 | tf_op jit(solution)/shard_map/ppermute | solution.py:452
  16.6 1.5 %collective-permute-start.11 = (s16[1,56,512]{2,1,0:T(8,128)(2,1)S(1)}, s16[1,56,512]{2,1,0:T(8,128)(2,1)S(1)}, u32[]{:S(2)}, u32[]{:S(2)}) collective-permute-start(s16[1,56,512]{2,1,0:T(8,128)(2,1)S(1)} %collective-permute-done.8.refs_3_), channel_id=1, source_target_pairs={{0,2},{1,3},{2,0},{3,1},{4,6},{5,7},{6,4},{7,5},{8,10},{9,11},{10,... | collective-permute-start | bytes 172040 | tf_op jit(solution)/shard_map/ppermute | solution.py:452
  18.2 0.6 collective-permute-start.12
  18.8 1.6 %collective-permute-start.13 = (s16[2,56,512]{2,1,0:T(8,128)(2,1)S(1)}, s16[2,56,512]{2,1,0:T(8,128)(2,1)S(1)}, u32[]{:S(2)}, u32[]{:S(2)}) collective-permute-start(s16[2,56,512]{2,1,0:T(8,128)(2,1)S(1)} %pad_add_fusion.2), channel_id=1, source_target_pairs={{0,4},{1,5},{2,6},{3,7},{4,0},{5,1},{6,2},{7,3},{8,12},{9,13},{10,... | collective-permute-start | bytes 344072 | tf_op jit(solution)/shard_map/ppermute | solution.py:452
  20.3 0.7 collective-permute-done.11.refs_6_
  21.0 1.6 %collective-permute-start.14 = (s16[2,56,512]{2,1,0:T(8,128)(2,1)S(1)}, s16[2,56,512]{2,1,0:T(8,128)(2,1)S(1)}, u32[]{:S(2)}, u32[]{:S(2)}) collective-permute-start(s16[2,56,512]{2,1,0:T(8,128)(2,1)S(1)} %pad_add_fusion.3), channel_id=1, source_target_pairs={{0,4},{1,5},{2,6},{3,7},{4,0},{5,1},{6,2},{7,3},{8,12},{9,13},{10,... | collective-permute-start | bytes 344072 | tf_op jit(solution)/shard_map/ppermute | solution.py:452
  22.6 1.7 %order.1 = (bf16[512,784]{1,0:T(8,128)(2,1)S(1)}, bf16[512,112]{1,0:T(8,128)(2,1)S(1)}, s32[1]{0:T(128)}) custom-call(s32[2]{0:T(128)S(1)} %pad_add_fusion.4.place, s32[2,256]{1,0:T(2,128)} %blocks.3), custom_call_target="tpu_custom_call" | custom-call | flops 1000000 | bytes 1000000 | tf_op jit(solution)/shard_map/order/pallas_call | solution.py:185
  25.0 1.0 %early_rows.1.early = f32[512,512]{1,0:T(8,128)S(1)} custom-call(bf16[512,784]{1,0:T(8,128)(2,1)S(1)} %get-tuple-element.37.chosen, s16[1,56,512]{2,1,0:T(8,128)(2,1)S(1)} %add_bitcast_fusion.refs_0_, s16[1,56,512]{2,1,0:T(8,128)(2,1)S(1)} %collective-permute-done.6.refs_1_, s16[1,56,512]{2,1,0:T(8,128)(2,1)S(1)} %collective-permute-done.7.refs_2_, ...), custom_call_target="tpu_custom_call" | custom-call | flops 1000000000 | bytes 4000000 | tf_op jit(solution)/shard_map/early_rows/pallas_call | solution.py:220
  26.0 0.4 late_rows.1
  26.6 0.1 collective-permute-start.16
  26.7 0.5 collective-permute-start.15
  27.2 1.0 %collective-permute-done.16.other = bf16[256,512]{1,0:T(8,128)(2,1)S(1)} collective-permute-done((bf16[256,512]{1,0:T(8,128)(2,1)S(1)}, bf16[256,512]{1,0:T(8,128)(2,1)S(1)}, u32[]{:S(2)}, u32[]{:S(2)}) %collective-permute-start.16) | collective-permute-done | bytes 262176 | tf_op jit(solution)/shard_map/ppermute | solution.py:452
  28.2 47.4 %first_batch.1 = (bf16[256,1024]{1,0:T(8,128)(2,1)S(1)}, bf16[256,1024]{1,0:T(8,128)(2,1)S(1)}) custom-call(s32[2]{0:T(128)S(1)} %pad_add_fusion.4.place, s32[2,256]{1,0:T(2,128)S(1)} %copy-done.1, f32[2,256]{1,0:T(2,128)S(1)} %copy-done.2, bf16[2,256,1024]{2,1,0:T(8,128)(2,1)S(1)} %copy-done, bf16[256,512]{1,0:T(8,128)(2,1)S(1)} %get-tuple-element.43.own, ...), custom_call_target="tpu_custom_call" | custom-call | tf_op jit(solution)/shard_map/first_batch/pallas_call | solution.py:420
  75.6 9.5 %second_batch.1 = f32[128,1024]{1,0:T(8,128)} custom-call(s32[2]{0:T(128)S(1)} %pad_add_fusion.4.place, s32[2,256]{1,0:T(2,128)S(1)} %copy-done.1, f32[2,256]{1,0:T(2,128)S(1)} %copy-done.2, bf16[2,256,1024]{2,1,0:T(8,128)(2,1)S(1)} %copy-done, s16[256,512]{1,0:T(8,128)(2,1)S(1)} %get-tuple-element.42.own, ...), custom_call_target="tpu_custom_call" | custom-call | tf_op jit(solution)/shard_map/second_batch/pallas_call | solution.py:420
  (27 shorter events, 0.2 us)
Async XLA Ops:
  2.1 1.4 %collective-permute-start.5 = (s16[56,512]{1,0:T(8,128)(2,1)S(1)}, s16[56,512]{1,0:T(8,128)(2,1)S(1)}, u32[]{:S(2)}, u32[]{:S(2)}) collective-permute-start(s16[56,512]{1,0:T(8,128)(2,1)S(1)} %get-tuple-element.39), channel_id=1, source_target_pairs={{0,1},{1,0},{2,3},{3,2},{4,5},{5,4},{6,7},{7,6},{8,9},{9,8},{10,11... | collective-permute-start | bytes 172040 | tf_op jit(solution)/shard_map/ppermute | solution.py:452
  3.6 5.6 %collective-permute-start.7 = (s16[1,56,512]{2,1,0:T(8,128)(2,1)S(1)}, s16[1,56,512]{2,1,0:T(8,128)(2,1)S(1)}, u32[]{:S(2)}, u32[]{:S(2)}) collective-permute-start(s16[1,56,512]{2,1,0:T(8,128)(2,1)S(1)} %add_bitcast_fusion.refs_0_), channel_id=1, source_target_pairs={{0,8},{1,9},{2,10},{3,11},{4,12},{5,13},{6,14},{7,15},{8,0},{9,1},... | collective-permute-start | bytes 172040 | tf_op jit(solution)/shard_map/ppermute | solution.py:452
  6.5 5.9 %collective-permute-start.6 = (s16[1,56,512]{2,1,0:T(8,128)(2,1)S(1)}, s16[1,56,512]{2,1,0:T(8,128)(2,1)S(1)}, u32[]{:S(2)}, u32[]{:S(2)}) collective-permute-start(s16[1,56,512]{2,1,0:T(8,128)(2,1)S(1)} %add_bitcast_fusion.refs_0_), channel_id=1, source_target_pairs={{0,16},{1,17},{2,18},{3,19},{4,20},{5,21},{6,22},{7,23},{8,24},{9,... | collective-permute-start | bytes 172040 | tf_op jit(solution)/shard_map/ppermute | solution.py:452
  9.2 9.0 %collective-permute-start.9 = (s16[2,56,512]{2,1,0:T(8,128)(2,1)S(1)}, s16[2,56,512]{2,1,0:T(8,128)(2,1)S(1)}, u32[]{:S(2)}, u32[]{:S(2)}) collective-permute-start(s16[2,56,512]{2,1,0:T(8,128)(2,1)S(1)} %pad_add_fusion.1), channel_id=1, source_target_pairs={{0,4},{1,5},{2,6},{3,7},{4,0},{5,1},{6,2},{7,3},{8,12},{9,13},{10,... | collective-permute-start | bytes 344072 | tf_op jit(solution)/shard_map/ppermute | solution.py:452
  12.4 4.2 %collective-permute-start.8 = (s16[1,56,512]{2,1,0:T(8,128)(2,1)S(1)}, s16[1,56,512]{2,1,0:T(8,128)(2,1)S(1)}, u32[]{:S(2)}, u32[]{:S(2)}) collective-permute-start(s16[1,56,512]{2,1,0:T(8,128)(2,1)S(1)} %collective-permute-done.6.refs_1_), channel_id=1, source_target_pairs={{0,8},{1,9},{2,10},{3,11},{4,12},{5,13},{6,14},{7,15},{8,0},{9,1},... | collective-permute-start | bytes 172040 | tf_op jit(solution)/shard_map/ppermute | solution.py:452
  12.8 6.0 %collective-permute-start.10 = (s16[1,56,512]{2,1,0:T(8,128)(2,1)S(1)}, s16[1,56,512]{2,1,0:T(8,128)(2,1)S(1)}, u32[]{:S(2)}, u32[]{:S(2)}) collective-permute-start(s16[1,56,512]{2,1,0:T(8,128)(2,1)S(1)} %collective-permute-done.6.refs_1_), channel_id=1, source_target_pairs={{0,2},{1,3},{2,0},{3,1},{4,6},{5,7},{6,4},{7,5},{8,10},{9,11},{10,... | collective-permute-start | bytes 172040 | tf_op jit(solution)/shard_map/ppermute | solution.py:452
  16.6 4.4 %collective-permute-start.11 = (s16[1,56,512]{2,1,0:T(8,128)(2,1)S(1)}, s16[1,56,512]{2,1,0:T(8,128)(2,1)S(1)}, u32[]{:S(2)}, u32[]{:S(2)}) collective-permute-start(s16[1,56,512]{2,1,0:T(8,128)(2,1)S(1)} %collective-permute-done.8.refs_3_), channel_id=1, source_target_pairs={{0,2},{1,3},{2,0},{3,1},{4,6},{5,7},{6,4},{7,5},{8,10},{9,11},{10,... | collective-permute-start | bytes 172040 | tf_op jit(solution)/shard_map/ppermute | solution.py:452
  18.2 6.8 %collective-permute-start.12 = (s16[4,56,512]{2,1,0:T(8,128)(2,1)S(1)}, s16[4,56,512]{2,1,0:T(8,128)(2,1)S(1)}, u32[]{:S(2)}, u32[]{:S(2)}) collective-permute-start(s16[4,56,512]{2,1,0:T(8,128)(2,1)S(1)} %pad_add_fusion), channel_id=1, source_target_pairs={{0,2},{1,3},{2,0},{3,1},{4,6},{5,7},{6,4},{7,5},{8,10},{9,11},{10,... | collective-permute-start | bytes 688136 | tf_op jit(solution)/shard_map/ppermute | solution.py:452
  18.8 6.2 %collective-permute-start.13 = (s16[2,56,512]{2,1,0:T(8,128)(2,1)S(1)}, s16[2,56,512]{2,1,0:T(8,128)(2,1)S(1)}, u32[]{:S(2)}, u32[]{:S(2)}) collective-permute-start(s16[2,56,512]{2,1,0:T(8,128)(2,1)S(1)} %pad_add_fusion.2), channel_id=1, source_target_pairs={{0,4},{1,5},{2,6},{3,7},{4,0},{5,1},{6,2},{7,3},{8,12},{9,13},{10,... | collective-permute-start | bytes 344072 | tf_op jit(solution)/shard_map/ppermute | solution.py:452
  21.0 5.0 %collective-permute-start.14 = (s16[2,56,512]{2,1,0:T(8,128)(2,1)S(1)}, s16[2,56,512]{2,1,0:T(8,128)(2,1)S(1)}, u32[]{:S(2)}, u32[]{:S(2)}) collective-permute-start(s16[2,56,512]{2,1,0:T(8,128)(2,1)S(1)} %pad_add_fusion.3), channel_id=1, source_target_pairs={{0,4},{1,5},{2,6},{3,7},{4,0},{5,1},{6,2},{7,3},{8,12},{9,13},{10,... | collective-permute-start | bytes 344072 | tf_op jit(solution)/shard_map/ppermute | solution.py:452
  25.0 1.4 %copy-start.3 = (f32[128,1024]{1,0:T(8,128)S(1)}, f32[128,1024]{1,0:T(8,128)}, u32[]{:S(2)}) copy-start(f32[128,1024]{1,0:T(8,128)} %state_ref.3) | copy-start | bytes 1572868
  25.0 1.4 %copy-start.4 = (f32[2,256,4]{1,2,0:T(4,128)S(1)}, f32[2,256,4]{1,2,0:T(4,128)}, u32[]{:S(2)}) copy-start(f32[2,256,4]{1,2,0:T(4,128)} %param.10) | copy-start | bytes 24580
  25.0 1.4 %copy-start.5 = (s32[2,256]{1,0:T(2,128)S(1)}, s32[2,256]{1,0:T(2,128)}, u32[]{:S(2)}) copy-start(s32[2,256]{1,0:T(2,128)} %blocks.3) | copy-start | bytes 6148
  26.5 1.7 %copy-start = (bf16[2,256,1024]{2,1,0:T(8,128)(2,1)S(1)}, bf16[2,256,1024]{2,1,0:T(8,128)(2,1)}, u32[]{:S(2)}) copy-start(bf16[2,256,1024]{2,1,0:T(8,128)(2,1)} %noise_ref.3) | copy-start | bytes 3145732
  26.5 1.7 %copy-start.1 = (s32[2,256]{1,0:T(2,128)S(1)}, s32[2,256]{1,0:T(2,128)}, u32[]{:S(2)}) copy-start(s32[2,256]{1,0:T(2,128)} %tags.3) | copy-start | bytes 6148
  26.5 1.7 %copy-start.2 = (f32[2,256]{1,0:T(2,128)S(1)}, f32[2,256]{1,0:T(2,128)}, u32[]{:S(2)}) copy-start(f32[2,256]{1,0:T(2,128)} %values.3) | copy-start | bytes 6148
  26.6 1.6 %collective-permute-start.16 = (bf16[256,512]{1,0:T(8,128)(2,1)S(1)}, bf16[256,512]{1,0:T(8,128)(2,1)S(1)}, u32[]{:S(2)}, u32[]{:S(2)}) collective-permute-start(bf16[256,512]{1,0:T(8,128)(2,1)S(1)} %get-tuple-element.43.own), channel_id=1, source_target_pairs={{0,1},{1,0},{2,3},{3,2},{4,5},{5,4},{6,7},{7,6},{8,9},{9,8},{10,11... | collective-permute-start | bytes 786440 | tf_op jit(solution)/shard_map/ppermute | solution.py:452
  26.7 48.9 %collective-permute-start.15 = (s16[256,512]{1,0:T(8,128)(2,1)S(1)}, s16[256,512]{1,0:T(8,128)(2,1)S(1)}, u32[]{:S(2)}, u32[]{:S(2)}) collective-permute-start(s16[256,512]{1,0:T(8,128)(2,1)S(1)} %get-tuple-element.42.own), channel_id=1, source_target_pairs={{0,1},{1,0},{2,3},{3,2},{4,5},{5,4},{6,7},{7,6},{8,9},{9,8},{10,11... | collective-permute-start | bytes 786440 | tf_op jit(solution)/shard_map/ppermute | solution.py:452

commit v11 on v8

--- a/solution.py
+++ b/solution.py
@@ -288,12 +288,13 @@
     def step(t):
         ts = split(t)
         error = dot3(nt, split(dot3(nn, ts, split(scaled))), ts) - eye
-        return t + nn(third_order(error).astype(BF16), ts[0]), squared(error)
+        change = third_order(error).astype(BF16)
+        return change, t + nn(change, ts[0]), squared(error)
 
     return begin, step
 
 
-def inverse_factor(covariance, work, inverse, use):
+def solve(covariance, coarse, work, inverse, apply, store):
     size = covariance.shape[0]
     lane = lax.broadcasted_iota(jnp.int32, (size, size), 1)
     sub = lax.broadcasted_iota(jnp.int32, (size, size), 0)
@@ -302,20 +303,22 @@
     scale_column = lax.rsqrt(jnp.sum(on_diagonal, axis=1, keepdims=True) * (1.0 / SCALE))
     scaled = covariance * scale_row * scale_column
     begin, step = newton(scaled)
-    t, residual = step(begin())
-    use(t * scale_row)
+    t = begin()
+    inverse[...] = t
+    for index, product in enumerate(apply(t * scale_row)):
+        coarse[index] = product
+    change, _, residual = step(t)
+    store(*[coarse[index] + nn(change, coarse[index].astype(BF16)) for index in range(2)])
 
     @pl.when(jnp.logical_not(residual <= TOLERANCE**2))
     def _():
-        inverse[...] = t
-
         def again(carry):
-            better, left = step(inverse[...])
+            _, better, left = step(inverse[...])
             inverse[...] = better
             return carry[0] + 1, left
 
         def wanted(carry):
-            return (carry[0] < 6) & jnp.logical_not(carry[1] <= (0.2 * TOLERANCE) ** 2)
+            return (carry[0] < 7) & jnp.logical_not(carry[1] <= (0.2 * TOLERANCE) ** 2)
 
         _, left = lax.while_loop(wanted, again, (0, residual))
         inverse[...] = inverse[...] * scale_row
@@ -324,10 +327,10 @@
         def _():
             eliminate(covariance, work, inverse)
 
-        use(inverse[...])
-
-
-def whiten(observed, tags, values, load, noise_ref, work, inverse, store):
+        store(*apply(inverse[...]))
+
+
+def whiten(observed, tags, values, load, noise_ref, coarse, work, inverse, store):
     members = observed.shape[1]
     size = observed.shape[0]
     mean = row_mean(observed)
@@ -339,15 +342,15 @@
     covariance = (nt(exact, exact) - mean * (mean_row * members)) * (1.0 / (members - 1))
     covariance = covariance + jnp.where(lane == sub, variance_row, 0.0)
 
-    def finish(t):
+    def apply(t):
         applied = dot2(nn, split(t), exact)
         noise = dot2(nn, split(t * jnp.sqrt(variance_row)), noise_ref[...])
         mean_part = jnp.sum(t * mean_row, axis=1, keepdims=True)
         value_part = jnp.sum(t * values, axis=1, keepdims=True)
-        store((applied - mean_part).astype(BF16), (noise + value_part - applied).astype(BF16))
+        return applied - mean_part, noise + value_part - applied
 
     load.wait()
-    inverse_factor(covariance, work, inverse, finish)
+    solve(covariance, coarse, work, inverse, apply, lambda w, v: store(w.astype(BF16), v.astype(BF16)))
 
 
 def row_sums(array):
@@ -369,7 +372,7 @@
 
 
 def first_kernel(
-    place, tags, values, noise_ref, own, other, whitened, white_innov, noise, loads, work, inverse
+    place, tags, values, noise_ref, own, other, whitened, white_innov, noise, loads, coarse, work, inverse
 ):
     load = pltpu.make_async_copy(noise_ref.at[0], noise, loads.at[0])
     load.start()
@@ -379,7 +382,7 @@
         whitened[...] = w
         white_innov[...] = v
 
-    whiten(observed, tags[:1, :], values[:1, :], load, noise, work, inverse, store)
+    whiten(observed, tags[:1, :], values[:1, :], load, noise, coarse, work, inverse, store)
 
 
 def second_kernel(
@@ -395,6 +398,7 @@
     analysis,
     noise,
     loads,
+    coarse,
     work,
     inverse,
     state,
@@ -411,7 +415,7 @@
     def store(w, v):
         analysis[...] = update(first, w, v)
 
-    whiten(observed, tags[1:2, :], values[1:2, :], load, noise, work, inverse, store)
+    whiten(observed, tags[1:2, :], values[1:2, :], load, noise, coarse, work, inverse, store)
 
 
 def batch_call(kernel, name, outs, place, tags, values, noise, *arrays, state=()):
@@ -424,6 +428,7 @@
         scratch_shapes=[
             pltpu.VMEM((rows, members), BF16),
             pltpu.SemaphoreType.DMA((2,)),
+            pltpu.VMEM((2, rows, members), F32),
             pltpu.VMEM((rows, rows), F32),
             pltpu.VMEM((rows, rows), F32),
         ]

time: 82.4 us -> 83.8 us (1.017)
  Pallas kernels: 59 us -> 60.3 us
    pallas_call x2, Pallas kernels: 53.8 us -> 55.2 us  [batch_call(): pl.pallas_call(kernel, out_shape=outs, in_specs=[SMEM, VMEM, VMEM, ANYWHE...]
where the time goes in v11:
time: 83.8 us; the launch traced here: 83.5 us
  Pallas kernels  60.3 us (72%)
  starting transfers between devices  15.3 us (18%)
  waiting for transfers between devices  6.68 us (8%)
  between operations  0.98 us (1%)
    pallas_call x2, Pallas kernels, batch_call(): pl.pallas_call(kernel, out_shape=outs, in_specs=[SMEM, VMEM, VMEM, ANYWHE...  55.2 us
    ppermute x12, starting transfers between devices, swap(): return lax.ppermute(value, AXES, [(i, i ^ mask) for i in range(32)])  15.3 us
    ppermute x12, waiting for transfers between devices, swap(): return lax.ppermute(value, AXES, [(i, i ^ mask) for i in range(32)])  6.68 us
    pallas_call x1, Pallas kernels, pick(): pl.pallas_call(pick_kernel, out_shape=[jax.ShapeDtypeStruct((SLOTS, state...  2.05 us
    pallas_call x1, Pallas kernels, order(): pl.pallas_call(functools.partial(order_kernel, groups), out_shape=[jax.Sh...  1.74 us
  transfers between devices with their start and end apart: 12, of which 5 were waited for; matrix products, arithmetic and copies ran while one was open for 0% of the time, Pallas kernels for 61%

profile of v11, /device:TPU:0, one launch (start us, length us, event | category | flops | bytes accessed | tf_op | source)
XLA Modules:
  0.0 83.5 jit_solution(1540825455240356047)
XLA Ops:
  0.0 0.1 pad_add_fusion.4.place
  0.1 2.0 %pick.1 = (s16[56,512]{1,0:T(8,128)(2,1)S(1)}, s16[56,512]{1,0:T(8,128)(2,1)S(1)}) custom-call(s32[2]{0:T(128)S(1)} %pad_add_fusion.4.place, s32[2,256]{1,0:T(2,128)} %blocks.3, f32[2,4,256]{2,1,0:T(4,128)} %bitcast.5, f32[128,1024]{1,0:T(8,128)} %state_ref.3), custom_call_target="tpu_custom_call" | custom-call | tf_op jit(solution)/shard_map/pick/pallas_call | solution.py:116
  2.1 0.5 collective-permute-start.5
  2.7 0.9 %collective-permute-done.5 = s16[56,512]{1,0:T(8,128)(2,1)S(1)} collective-permute-done((s16[56,512]{1,0:T(8,128)(2,1)S(1)}, s16[56,512]{1,0:T(8,128)(2,1)S(1)}, u32[]{:S(2)}, u32[]{:S(2)}) %collective-permute-start.5) | collective-permute-done | bytes 57376 | tf_op jit(solution)/shard_map/ppermute | solution.py:456
  3.6 3.0 %collective-permute-start.7 = (s16[1,56,512]{2,1,0:T(8,128)(2,1)S(1)}, s16[1,56,512]{2,1,0:T(8,128)(2,1)S(1)}, u32[]{:S(2)}, u32[]{:S(2)}) collective-permute-start(s16[1,56,512]{2,1,0:T(8,128)(2,1)S(1)} %add_bitcast_fusion.refs_0_), channel_id=1, source_target_pairs={{0,8},{1,9},{2,10},{3,11},{4,12},{5,13},{6,14},{7,15},{8,0},{9,1},... | collective-permute-start | bytes 172040 | tf_op jit(solution)/shard_map/ppermute | solution.py:456
  6.5 2.6 %collective-permute-start.6 = (s16[1,56,512]{2,1,0:T(8,128)(2,1)S(1)}, s16[1,56,512]{2,1,0:T(8,128)(2,1)S(1)}, u32[]{:S(2)}, u32[]{:S(2)}) collective-permute-start(s16[1,56,512]{2,1,0:T(8,128)(2,1)S(1)} %add_bitcast_fusion.refs_0_), channel_id=1, source_target_pairs={{0,16},{1,17},{2,18},{3,19},{4,20},{5,21},{6,22},{7,23},{8,24},{9,... | collective-permute-start | bytes 172040 | tf_op jit(solution)/shard_map/ppermute | solution.py:456
  9.2 1.6 %collective-permute-start.9 = (s16[2,56,512]{2,1,0:T(8,128)(2,1)S(1)}, s16[2,56,512]{2,1,0:T(8,128)(2,1)S(1)}, u32[]{:S(2)}, u32[]{:S(2)}) collective-permute-start(s16[2,56,512]{2,1,0:T(8,128)(2,1)S(1)} %pad_add_fusion.1), channel_id=1, source_target_pairs={{0,4},{1,5},{2,6},{3,7},{4,0},{5,1},{6,2},{7,3},{8,12},{9,13},{10,... | collective-permute-start | bytes 344072 | tf_op jit(solution)/shard_map/ppermute | solution.py:456
  10.7 1.7 %collective-permute-done.6.refs_1_ = s16[1,56,512]{2,1,0:T(8,128)(2,1)S(1)} collective-permute-done((s16[1,56,512]{2,1,0:T(8,128)(2,1)S(1)}, s16[1,56,512]{2,1,0:T(8,128)(2,1)S(1)}, u32[]{:S(2)}, u32[]{:S(2)}) %collective-permute-start.6) | collective-permute-done | bytes 57376 | tf_op jit(solution)/shard_map/ppermute | solution.py:456
  12.4 0.3 collective-permute-start.8
  12.8 1.5 %collective-permute-start.10 = (s16[1,56,512]{2,1,0:T(8,128)(2,1)S(1)}, s16[1,56,512]{2,1,0:T(8,128)(2,1)S(1)}, u32[]{:S(2)}, u32[]{:S(2)}) collective-permute-start(s16[1,56,512]{2,1,0:T(8,128)(2,1)S(1)} %collective-permute-done.6.refs_1_), channel_id=1, source_target_pairs={{0,2},{1,3},{2,0},{3,1},{4,6},{5,7},{6,4},{7,5},{8,10},{9,11},{10,... | collective-permute-start | bytes 172040 | tf_op jit(solution)/shard_map/ppermute | solution.py:456
  14.3 2.3 %collective-permute-done.8.refs_3_ = s16[1,56,512]{2,1,0:T(8,128)(2,1)S(1)} collective-permute-done((s16[1,56,512]{2,1,0:T(8,128)(2,1)S(1)}, s16[1,56,512]{2,1,0:T(8,128)(2,1)S(1)}, u32[]{:S(2)}, u32[]{:S(2)}) %collective-permute-start.8) | collective-permute-done | bytes 57376 | tf_op jit(solution)/shard_map/ppermute | solution.py:456
  16.6 1.5 %collective-permute-start.11 = (s16[1,56,512]{2,1,0:T(8,128)(2,1)S(1)}, s16[1,56,512]{2,1,0:T(8,128)(2,1)S(1)}, u32[]{:S(2)}, u32[]{:S(2)}) collective-permute-start(s16[1,56,512]{2,1,0:T(8,128)(2,1)S(1)} %collective-permute-done.8.refs_3_), channel_id=1, source_target_pairs={{0,2},{1,3},{2,0},{3,1},{4,6},{5,7},{6,4},{7,5},{8,10},{9,11},{10,... | collective-permute-start | bytes 172040 | tf_op jit(solution)/shard_map/ppermute | solution.py:456
  18.2 0.6 collective-permute-start.12
  18.8 1.6 %collective-permute-start.13 = (s16[2,56,512]{2,1,0:T(8,128)(2,1)S(1)}, s16[2,56,512]{2,1,0:T(8,128)(2,1)S(1)}, u32[]{:S(2)}, u32[]{:S(2)}) collective-permute-start(s16[2,56,512]{2,1,0:T(8,128)(2,1)S(1)} %pad_add_fusion.2), channel_id=1, source_target_pairs={{0,4},{1,5},{2,6},{3,7},{4,0},{5,1},{6,2},{7,3},{8,12},{9,13},{10,... | collective-permute-start | bytes 344072 | tf_op jit(solution)/shard_map/ppermute | solution.py:456
  20.3 0.7 collective-permute-done.11.refs_6_
  21.0 1.6 %collective-permute-start.14 = (s16[2,56,512]{2,1,0:T(8,128)(2,1)S(1)}, s16[2,56,512]{2,1,0:T(8,128)(2,1)S(1)}, u32[]{:S(2)}, u32[]{:S(2)}) collective-permute-start(s16[2,56,512]{2,1,0:T(8,128)(2,1)S(1)} %pad_add_fusion.3), channel_id=1, source_target_pairs={{0,4},{1,5},{2,6},{3,7},{4,0},{5,1},{6,2},{7,3},{8,12},{9,13},{10,... | collective-permute-start | bytes 344072 | tf_op jit(solution)/shard_map/ppermute | solution.py:456
  22.6 1.7 %order.1 = (bf16[512,784]{1,0:T(8,128)(2,1)S(1)}, bf16[512,112]{1,0:T(8,128)(2,1)S(1)}, s32[1]{0:T(128)}) custom-call(s32[2]{0:T(128)S(1)} %pad_add_fusion.4.place, s32[2,256]{1,0:T(2,128)} %blocks.3), custom_call_target="tpu_custom_call" | custom-call | flops 1000000 | bytes 1000000 | tf_op jit(solution)/shard_map/order/pallas_call | solution.py:185
  25.0 1.0 %early_rows.1.early = f32[512,512]{1,0:T(8,128)S(1)} custom-call(bf16[512,784]{1,0:T(8,128)(2,1)S(1)} %get-tuple-element.37.chosen, s16[1,56,512]{2,1,0:T(8,128)(2,1)S(1)} %add_bitcast_fusion.refs_0_, s16[1,56,512]{2,1,0:T(8,128)(2,1)S(1)} %collective-permute-done.6.refs_1_, s16[1,56,512]{2,1,0:T(8,128)(2,1)S(1)} %collective-permute-done.7.refs_2_, ...), custom_call_target="tpu_custom_call" | custom-call | flops 1000000000 | bytes 4000000 | tf_op jit(solution)/shard_map/early_rows/pallas_call | solution.py:220
  26.0 0.4 late_rows.1
  26.6 0.1 collective-permute-start.16
  26.7 0.5 collective-permute-start.15
  27.2 1.0 %collective-permute-done.16.other = bf16[256,512]{1,0:T(8,128)(2,1)S(1)} collective-permute-done((bf16[256,512]{1,0:T(8,128)(2,1)S(1)}, bf16[256,512]{1,0:T(8,128)(2,1)S(1)}, u32[]{:S(2)}, u32[]{:S(2)}) %collective-permute-start.16) | collective-permute-done | bytes 262176 | tf_op jit(solution)/shard_map/ppermute | solution.py:456
  28.2 48.5 %first_batch.1 = (bf16[256,1024]{1,0:T(8,128)(2,1)S(1)}, bf16[256,1024]{1,0:T(8,128)(2,1)S(1)}) custom-call(s32[2]{0:T(128)S(1)} %pad_add_fusion.4.place, s32[2,256]{1,0:T(2,128)S(1)} %copy-done.1, f32[2,256]{1,0:T(2,128)S(1)} %copy-done.2, bf16[2,256,1024]{2,1,0:T(8,128)(2,1)S(1)} %copy-done, bf16[256,512]{1,0:T(8,128)(2,1)S(1)} %get-tuple-element.43.own, ...), custom_call_target="tpu_custom_call" | custom-call | tf_op jit(solution)/shard_map/first_batch/pallas_call | solution.py:423
  76.7 6.6 %second_batch.1 = f32[128,1024]{1,0:T(8,128)} custom-call(s32[2]{0:T(128)S(1)} %pad_add_fusion.4.place, s32[2,256]{1,0:T(2,128)S(1)} %copy-done.1, f32[2,256]{1,0:T(2,128)S(1)} %copy-done.2, bf16[2,256,1024]{2,1,0:T(8,128)(2,1)S(1)} %copy-done, s16[256,512]{1,0:T(8,128)(2,1)S(1)} %get-tuple-element.42.own, ...), custom_call_target="tpu_custom_call" | custom-call | tf_op jit(solution)/shard_map/second_batch/pallas_call | solution.py:423
  (27 shorter events, 0.2 us)
Async XLA Ops:
  2.1 1.4 %collective-permute-start.5 = (s16[56,512]{1,0:T(8,128)(2,1)S(1)}, s16[56,512]{1,0:T(8,128)(2,1)S(1)}, u32[]{:S(2)}, u32[]{:S(2)}) collective-permute-start(s16[56,512]{1,0:T(8,128)(2,1)S(1)} %get-tuple-element.39), channel_id=1, source_target_pairs={{0,1},{1,0},{2,3},{3,2},{4,5},{5,4},{6,7},{7,6},{8,9},{9,8},{10,11... | collective-permute-start | bytes 172040 | tf_op jit(solution)/shard_map/ppermute | solution.py:456
  3.6 5.6 %collective-permute-start.7 = (s16[1,56,512]{2,1,0:T(8,128)(2,1)S(1)}, s16[1,56,512]{2,1,0:T(8,128)(2,1)S(1)}, u32[]{:S(2)}, u32[]{:S(2)}) collective-permute-start(s16[1,56,512]{2,1,0:T(8,128)(2,1)S(1)} %add_bitcast_fusion.refs_0_), channel_id=1, source_target_pairs={{0,8},{1,9},{2,10},{3,11},{4,12},{5,13},{6,14},{7,15},{8,0},{9,1},... | collective-permute-start | bytes 172040 | tf_op jit(solution)/shard_map/ppermute | solution.py:456
  6.5 5.9 %collective-permute-start.6 = (s16[1,56,512]{2,1,0:T(8,128)(2,1)S(1)}, s16[1,56,512]{2,1,0:T(8,128)(2,1)S(1)}, u32[]{:S(2)}, u32[]{:S(2)}) collective-permute-start(s16[1,56,512]{2,1,0:T(8,128)(2,1)S(1)} %add_bitcast_fusion.refs_0_), channel_id=1, source_target_pairs={{0,16},{1,17},{2,18},{3,19},{4,20},{5,21},{6,22},{7,23},{8,24},{9,... | collective-permute-start | bytes 172040 | tf_op jit(solution)/shard_map/ppermute | solution.py:456
  9.2 9.0 %collective-permute-start.9 = (s16[2,56,512]{2,1,0:T(8,128)(2,1)S(1)}, s16[2,56,512]{2,1,0:T(8,128)(2,1)S(1)}, u32[]{:S(2)}, u32[]{:S(2)}) collective-permute-start(s16[2,56,512]{2,1,0:T(8,128)(2,1)S(1)} %pad_add_fusion.1), channel_id=1, source_target_pairs={{0,4},{1,5},{2,6},{3,7},{4,0},{5,1},{6,2},{7,3},{8,12},{9,13},{10,... | collective-permute-start | bytes 344072 | tf_op jit(solution)/shard_map/ppermute | solution.py:456
  12.4 4.2 %collective-permute-start.8 = (s16[1,56,512]{2,1,0:T(8,128)(2,1)S(1)}, s16[1,56,512]{2,1,0:T(8,128)(2,1)S(1)}, u32[]{:S(2)}, u32[]{:S(2)}) collective-permute-start(s16[1,56,512]{2,1,0:T(8,128)(2,1)S(1)} %collective-permute-done.6.refs_1_), channel_id=1, source_target_pairs={{0,8},{1,9},{2,10},{3,11},{4,12},{5,13},{6,14},{7,15},{8,0},{9,1},... | collective-permute-start | bytes 172040 | tf_op jit(solution)/shard_map/ppermute | solution.py:456
  12.8 6.0 %collective-permute-start.10 = (s16[1,56,512]{2,1,0:T(8,128)(2,1)S(1)}, s16[1,56,512]{2,1,0:T(8,128)(2,1)S(1)}, u32[]{:S(2)}, u32[]{:S(2)}) collective-permute-start(s16[1,56,512]{2,1,0:T(8,128)(2,1)S(1)} %collective-permute-done.6.refs_1_), channel_id=1, source_target_pairs={{0,2},{1,3},{2,0},{3,1},{4,6},{5,7},{6,4},{7,5},{8,10},{9,11},{10,... | collective-permute-start | bytes 172040 | tf_op jit(solution)/shard_map/ppermute | solution.py:456
  16.6 4.4 %collective-permute-start.11 = (s16[1,56,512]{2,1,0:T(8,128)(2,1)S(1)}, s16[1,56,512]{2,1,0:T(8,128)(2,1)S(1)}, u32[]{:S(2)}, u32[]{:S(2)}) collective-permute-start(s16[1,56,512]{2,1,0:T(8,128)(2,1)S(1)} %collective-permute-done.8.refs_3_), channel_id=1, source_target_pairs={{0,2},{1,3},{2,0},{3,1},{4,6},{5,7},{6,4},{7,5},{8,10},{9,11},{10,... | collective-permute-start | bytes 172040 | tf_op jit(solution)/shard_map/ppermute | solution.py:456
  18.2 6.8 %collective-permute-start.12 = (s16[4,56,512]{2,1,0:T(8,128)(2,1)S(1)}, s16[4,56,512]{2,1,0:T(8,128)(2,1)S(1)}, u32[]{:S(2)}, u32[]{:S(2)}) collective-permute-start(s16[4,56,512]{2,1,0:T(8,128)(2,1)S(1)} %pad_add_fusion), channel_id=1, source_target_pairs={{0,2},{1,3},{2,0},{3,1},{4,6},{5,7},{6,4},{7,5},{8,10},{9,11},{10,... | collective-permute-start | bytes 688136 | tf_op jit(solution)/shard_map/ppermute | solution.py:456
  18.8 6.2 %collective-permute-start.13 = (s16[2,56,512]{2,1,0:T(8,128)(2,1)S(1)}, s16[2,56,512]{2,1,0:T(8,128)(2,1)S(1)}, u32[]{:S(2)}, u32[]{:S(2)}) collective-permute-start(s16[2,56,512]{2,1,0:T(8,128)(2,1)S(1)} %pad_add_fusion.2), channel_id=1, source_target_pairs={{0,4},{1,5},{2,6},{3,7},{4,0},{5,1},{6,2},{7,3},{8,12},{9,13},{10,... | collective-permute-start | bytes 344072 | tf_op jit(solution)/shard_map/ppermute | solution.py:456
  21.0 5.0 %collective-permute-start.14 = (s16[2,56,512]{2,1,0:T(8,128)(2,1)S(1)}, s16[2,56,512]{2,1,0:T(8,128)(2,1)S(1)}, u32[]{:S(2)}, u32[]{:S(2)}) collective-permute-start(s16[2,56,512]{2,1,0:T(8,128)(2,1)S(1)} %pad_add_fusion.3), channel_id=1, source_target_pairs={{0,4},{1,5},{2,6},{3,7},{4,0},{5,1},{6,2},{7,3},{8,12},{9,13},{10,... | collective-permute-start | bytes 344072 | tf_op jit(solution)/shard_map/ppermute | solution.py:456
  25.0 1.4 %copy-start.3 = (f32[128,1024]{1,0:T(8,128)S(1)}, f32[128,1024]{1,0:T(8,128)}, u32[]{:S(2)}) copy-start(f32[128,1024]{1,0:T(8,128)} %state_ref.3) | copy-start | bytes 1572868
  25.0 1.4 %copy-start.4 = (f32[2,256,4]{1,2,0:T(4,128)S(1)}, f32[2,256,4]{1,2,0:T(4,128)}, u32[]{:S(2)}) copy-start(f32[2,256,4]{1,2,0:T(4,128)} %param.10) | copy-start | bytes 24580
  25.0 1.4 %copy-start.5 = (s32[2,256]{1,0:T(2,128)S(1)}, s32[2,256]{1,0:T(2,128)}, u32[]{:S(2)}) copy-start(s32[2,256]{1,0:T(2,128)} %blocks.3) | copy-start | bytes 6148
  26.5 1.7 %copy-start = (bf16[2,256,1024]{2,1,0:T(8,128)(2,1)S(1)}, bf16[2,256,1024]{2,1,0:T(8,128)(2,1)}, u32[]{:S(2)}) copy-start(bf16[2,256,1024]{2,1,0:T(8,128)(2,1)} %noise_ref.3) | copy-start | bytes 3145732
  26.5 1.7 %copy-start.1 = (s32[2,256]{1,0:T(2,128)S(1)}, s32[2,256]{1,0:T(2,128)}, u32[]{:S(2)}) copy-start(s32[2,256]{1,0:T(2,128)} %tags.3) | copy-start | bytes 6148
  26.5 1.7 %copy-start.2 = (f32[2,256]{1,0:T(2,128)S(1)}, f32[2,256]{1,0:T(2,128)}, u32[]{:S(2)}) copy-start(f32[2,256]{1,0:T(2,128)} %values.3) | copy-start | bytes 6148
  26.6 1.6 %collective-permute-start.16 = (bf16[256,512]{1,0:T(8,128)(2,1)S(1)}, bf16[256,512]{1,0:T(8,128)(2,1)S(1)}, u32[]{:S(2)}, u32[]{:S(2)}) collective-permute-start(bf16[256,512]{1,0:T(8,128)(2,1)S(1)} %get-tuple-element.43.own), channel_id=1, source_target_pairs={{0,1},{1,0},{2,3},{3,2},{4,5},{5,4},{6,7},{7,6},{8,9},{9,8},{10,11... | collective-permute-start | bytes 786440 | tf_op jit(solution)/shard_map/ppermute | solution.py:456
  26.7 50.1 %collective-permute-start.15 = (s16[256,512]{1,0:T(8,128)(2,1)S(1)}, s16[256,512]{1,0:T(8,128)(2,1)S(1)}, u32[]{:S(2)}, u32[]{:S(2)}) collective-permute-start(s16[256,512]{1,0:T(8,128)(2,1)S(1)} %get-tuple-element.42.own), channel_id=1, source_target_pairs={{0,1},{1,0},{2,3},{3,2},{4,5},{5,4},{6,7},{7,6},{8,9},{9,8},{10,11... | collective-permute-start | bytes 786440 | tf_op jit(solution)/shard_map/ppermute | solution.py:456

commit v12 on v8

--- a/solution.py
+++ b/solution.py
@@ -166,13 +166,13 @@
         away = (2 * pair_column.astype(jnp.int32)) ^ device
         distance = 8 * ((away >> 3) & 1) + 4 * ((away >> 4) & 1) + ((away >> 1) & 3)
         slot = rank if batch == 0 else SLOTS - 1 - rank
-        for distances, out in zip(groups, outs):
-            where = jnp.full(rank.shape, -SLOTS, jnp.int32)
-            for index, known in enumerate(distances):
-                where = jnp.where(distance == known, SLOTS * index, where)
-            slots = lax.broadcasted_iota(jnp.int32, (size, out.shape[1]), 1)
-            chosen = jnp.where(slots == where + slot, 1.0, 0.0)
+        slot = slot + SLOTS * distance
+        begin = 0
+        for width, out in zip(groups, outs):
+            slots = lax.broadcasted_iota(jnp.int32, (size, SLOTS * width), 1) + SLOTS * begin
+            chosen = jnp.where(slots == slot, 1.0, 0.0)
             out[batch * size : (batch + 1) * size, :] = chosen.astype(BF16)
+            begin += width
     counts = jnp.zeros((16, 1), F32)
     for batch in range(blocks.shape[0]):
         chip = blocks[batch : batch + 1, :] // (2 * held)
@@ -185,7 +185,7 @@
     return pl.pallas_call(
         functools.partial(order_kernel, groups),
         out_shape=[
-            jax.ShapeDtypeStruct((blocks.size, SLOTS * len(group)), BF16) for group in groups
+            jax.ShapeDtypeStruct((blocks.size, SLOTS * width), BF16) for width in groups
         ]
         + [jax.ShapeDtypeStruct((1,), jnp.int32)],
         in_specs=[SMEM, VMEM],
@@ -196,9 +196,11 @@
     )(place, blocks)
 
 
-def put_in_order(chosen, pieces):
+def put_in_order(chosen, numbers, pieces):
     size = chosen.shape[0] // 2
-    values = [ref[index].astype(jnp.int32) for ref in pieces for index in range(ref.shape[0])]
+    blocks = [(ref, index) for ref in pieces for index in range(ref.shape[0])]
+    blocks = [blocks[where] for where in sorted(range(len(blocks)), key=lambda i: numbers[i])]
+    values = [ref[index].astype(jnp.int32) for ref, index in blocks]
     high, low = split(jnp.concatenate(values, axis=0).astype(F32))
     second = chosen[size:, :]
     return nn(chosen[:size, :], high), nn(second, high) + nn(second, low)
@@ -206,12 +208,12 @@
 
 def early_kernel(chosen, *refs):
     size = chosen.shape[0] // 2
-    refs[-1][:size, :], refs[-1][size:, :] = put_in_order(chosen, refs[:-1])
+    refs[-1][:size, :], refs[-1][size:, :] = put_in_order(chosen, EARLY, refs[:-1])
 
 
 def late_kernel(chosen, early, *refs):
     size = chosen.shape[0] // 2
-    first, second = put_in_order(chosen, refs[:-2])
+    first, second = put_in_order(chosen, LATE, refs[:-2])
     refs[-2][...] = ((first + early[:size, :]) * UNIT).astype(BF16)
     refs[-1][...] = (second + early[size:, :]).astype(jnp.int32).astype(jnp.int16)
 
@@ -475,7 +477,7 @@
     both_y = swap(after(joined(both, both_x), near_far), Y)
     far_x = swap(joined(far, far_y), X)
     near_far_x = swap(joined(near_far, near_far_y), X)
-    early_places, late_places, fits = order(place, blocks, (EARLY, LATE))
+    early_places, late_places, fits = order(place, blocks, (len(EARLY), len(LATE)))
     pieces = [own, far, near, near_far, both_x, far_y, near_far_y, both_y, far_x]
     early = early_rows(early_places, pieces)
     return late_rows(late_places, early, [near_far_x]), fits

time: 82.4 us -> 82.3 us (level)
  no operation moved by 1% of the time
where the time goes in v12:
time: 82.3 us; the launch traced here: 82.1 us
  Pallas kernels  58.9 us (72%)
  starting transfers between devices  15.3 us (19%)
  waiting for transfers between devices  6.68 us (8%)
  between operations  0.98 us (1%)
    pallas_call x2, Pallas kernels, batch_call(): pl.pallas_call(kernel, out_shape=outs, in_specs=[SMEM, VMEM, VMEM, ANYWHE...  53.8 us
    ppermute x12, starting transfers between devices, swap(): return lax.ppermute(value, AXES, [(i, i ^ mask) for i in range(32)])  15.3 us
    ppermute x12, waiting for transfers between devices, swap(): return lax.ppermute(value, AXES, [(i, i ^ mask) for i in range(32)])  6.68 us
    pallas_call x1, Pallas kernels, pick(): pl.pallas_call(pick_kernel, out_shape=[jax.ShapeDtypeStruct((SLOTS, state...  2.05 us
  transfers between devices with their start and end apart: 12, of which 5 were waited for; matrix products, arithmetic and copies ran while one was open for 0% of the time, Pallas kernels for 61%

profile of v12, /device:TPU:0, one launch (start us, length us, event | category | flops | bytes accessed | tf_op | source)
XLA Modules:
  0.0 82.1 jit_solution(11860839286133708979)
XLA Ops:
  0.0 0.1 pad_add_fusion.4.place
  0.1 2.0 %pick.1 = (s16[56,512]{1,0:T(8,128)(2,1)S(1)}, s16[56,512]{1,0:T(8,128)(2,1)S(1)}) custom-call(s32[2]{0:T(128)S(1)} %pad_add_fusion.4.place, s32[2,256]{1,0:T(2,128)} %blocks.3, f32[2,4,256]{2,1,0:T(4,128)} %bitcast.5, f32[128,1024]{1,0:T(8,128)} %state_ref.3), custom_call_target="tpu_custom_call" | custom-call | tf_op jit(solution)/shard_map/pick/pallas_call | solution.py:116
  2.1 0.5 collective-permute-start.5
  2.7 0.9 %collective-permute-done.5 = s16[56,512]{1,0:T(8,128)(2,1)S(1)} collective-permute-done((s16[56,512]{1,0:T(8,128)(2,1)S(1)}, s16[56,512]{1,0:T(8,128)(2,1)S(1)}, u32[]{:S(2)}, u32[]{:S(2)}) %collective-permute-start.5) | collective-permute-done | bytes 57376 | tf_op jit(solution)/shard_map/ppermute | solution.py:453
  3.6 3.0 %collective-permute-start.7 = (s16[1,56,512]{2,1,0:T(8,128)(2,1)S(1)}, s16[1,56,512]{2,1,0:T(8,128)(2,1)S(1)}, u32[]{:S(2)}, u32[]{:S(2)}) collective-permute-start(s16[1,56,512]{2,1,0:T(8,128)(2,1)S(1)} %add_bitcast_fusion.refs_0_), channel_id=1, source_target_pairs={{0,8},{1,9},{2,10},{3,11},{4,12},{5,13},{6,14},{7,15},{8,0},{9,1},... | collective-permute-start | bytes 172040 | tf_op jit(solution)/shard_map/ppermute | solution.py:453
  6.5 2.6 %collective-permute-start.6 = (s16[1,56,512]{2,1,0:T(8,128)(2,1)S(1)}, s16[1,56,512]{2,1,0:T(8,128)(2,1)S(1)}, u32[]{:S(2)}, u32[]{:S(2)}) collective-permute-start(s16[1,56,512]{2,1,0:T(8,128)(2,1)S(1)} %add_bitcast_fusion.refs_0_), channel_id=1, source_target_pairs={{0,16},{1,17},{2,18},{3,19},{4,20},{5,21},{6,22},{7,23},{8,24},{9,... | collective-permute-start | bytes 172040 | tf_op jit(solution)/shard_map/ppermute | solution.py:453
  9.2 1.6 %collective-permute-start.9 = (s16[2,56,512]{2,1,0:T(8,128)(2,1)S(1)}, s16[2,56,512]{2,1,0:T(8,128)(2,1)S(1)}, u32[]{:S(2)}, u32[]{:S(2)}) collective-permute-start(s16[2,56,512]{2,1,0:T(8,128)(2,1)S(1)} %pad_add_fusion.1), channel_id=1, source_target_pairs={{0,4},{1,5},{2,6},{3,7},{4,0},{5,1},{6,2},{7,3},{8,12},{9,13},{10,... | collective-permute-start | bytes 344072 | tf_op jit(solution)/shard_map/ppermute | solution.py:453
  10.7 1.7 %collective-permute-done.6.refs_1_ = s16[1,56,512]{2,1,0:T(8,128)(2,1)S(1)} collective-permute-done((s16[1,56,512]{2,1,0:T(8,128)(2,1)S(1)}, s16[1,56,512]{2,1,0:T(8,128)(2,1)S(1)}, u32[]{:S(2)}, u32[]{:S(2)}) %collective-permute-start.6) | collective-permute-done | bytes 57376 | tf_op jit(solution)/shard_map/ppermute | solution.py:453
  12.4 0.3 collective-permute-start.8
  12.8 1.5 %collective-permute-start.10 = (s16[1,56,512]{2,1,0:T(8,128)(2,1)S(1)}, s16[1,56,512]{2,1,0:T(8,128)(2,1)S(1)}, u32[]{:S(2)}, u32[]{:S(2)}) collective-permute-start(s16[1,56,512]{2,1,0:T(8,128)(2,1)S(1)} %collective-permute-done.6.refs_1_), channel_id=1, source_target_pairs={{0,2},{1,3},{2,0},{3,1},{4,6},{5,7},{6,4},{7,5},{8,10},{9,11},{10,... | collective-permute-start | bytes 172040 | tf_op jit(solution)/shard_map/ppermute | solution.py:453
  14.3 2.3 %collective-permute-done.8.refs_3_ = s16[1,56,512]{2,1,0:T(8,128)(2,1)S(1)} collective-permute-done((s16[1,56,512]{2,1,0:T(8,128)(2,1)S(1)}, s16[1,56,512]{2,1,0:T(8,128)(2,1)S(1)}, u32[]{:S(2)}, u32[]{:S(2)}) %collective-permute-start.8) | collective-permute-done | bytes 57376 | tf_op jit(solution)/shard_map/ppermute | solution.py:453
  16.6 1.5 %collective-permute-start.11 = (s16[1,56,512]{2,1,0:T(8,128)(2,1)S(1)}, s16[1,56,512]{2,1,0:T(8,128)(2,1)S(1)}, u32[]{:S(2)}, u32[]{:S(2)}) collective-permute-start(s16[1,56,512]{2,1,0:T(8,128)(2,1)S(1)} %collective-permute-done.8.refs_3_), channel_id=1, source_target_pairs={{0,2},{1,3},{2,0},{3,1},{4,6},{5,7},{6,4},{7,5},{8,10},{9,11},{10,... | collective-permute-start | bytes 172040 | tf_op jit(solution)/shard_map/ppermute | solution.py:453
  18.2 0.6 collective-permute-start.12
  18.8 1.6 %collective-permute-start.13 = (s16[2,56,512]{2,1,0:T(8,128)(2,1)S(1)}, s16[2,56,512]{2,1,0:T(8,128)(2,1)S(1)}, u32[]{:S(2)}, u32[]{:S(2)}) collective-permute-start(s16[2,56,512]{2,1,0:T(8,128)(2,1)S(1)} %pad_add_fusion.2), channel_id=1, source_target_pairs={{0,4},{1,5},{2,6},{3,7},{4,0},{5,1},{6,2},{7,3},{8,12},{9,13},{10,... | collective-permute-start | bytes 344072 | tf_op jit(solution)/shard_map/ppermute | solution.py:453
  20.3 0.7 collective-permute-done.11.refs_6_
  21.0 1.6 %collective-permute-start.14 = (s16[2,56,512]{2,1,0:T(8,128)(2,1)S(1)}, s16[2,56,512]{2,1,0:T(8,128)(2,1)S(1)}, u32[]{:S(2)}, u32[]{:S(2)}) collective-permute-start(s16[2,56,512]{2,1,0:T(8,128)(2,1)S(1)} %pad_add_fusion.3), channel_id=1, source_target_pairs={{0,4},{1,5},{2,6},{3,7},{4,0},{5,1},{6,2},{7,3},{8,12},{9,13},{10,... | collective-permute-start | bytes 344072 | tf_op jit(solution)/shard_map/ppermute | solution.py:453
  22.6 1.6 %order.1 = (bf16[512,784]{1,0:T(8,128)(2,1)S(1)}, bf16[512,112]{1,0:T(8,128)(2,1)S(1)}, s32[1]{0:T(128)}) custom-call(s32[2]{0:T(128)S(1)} %pad_add_fusion.4.place, s32[2,256]{1,0:T(2,128)} %blocks.3), custom_call_target="tpu_custom_call" | custom-call | flops 1000000 | bytes 1000000 | tf_op jit(solution)/shard_map/order/pallas_call | solution.py:185
  24.9 1.0 %early_rows.1.early = f32[512,512]{1,0:T(8,128)S(1)} custom-call(bf16[512,784]{1,0:T(8,128)(2,1)S(1)} %get-tuple-element.37.chosen, s16[1,56,512]{2,1,0:T(8,128)(2,1)S(1)} %add_bitcast_fusion.refs_0_, s16[1,56,512]{2,1,0:T(8,128)(2,1)S(1)} %collective-permute-done.6.refs_1_, s16[1,56,512]{2,1,0:T(8,128)(2,1)S(1)} %collective-permute-done.7.refs_2_, ...), custom_call_target="tpu_custom_call" | custom-call | flops 1000000000 | bytes 4000000 | tf_op jit(solution)/shard_map/early_rows/pallas_call | solution.py:222
  25.9 0.4 late_rows.1
  26.5 0.1 collective-permute-start.16
  26.5 0.5 collective-permute-start.15
  27.0 1.0 %collective-permute-done.16.other = bf16[256,512]{1,0:T(8,128)(2,1)S(1)} collective-permute-done((bf16[256,512]{1,0:T(8,128)(2,1)S(1)}, bf16[256,512]{1,0:T(8,128)(2,1)S(1)}, u32[]{:S(2)}, u32[]{:S(2)}) %collective-permute-start.16) | collective-permute-done | bytes 262176 | tf_op jit(solution)/shard_map/ppermute | solution.py:453
  28.1 47.4 %first_batch.1 = (bf16[256,1024]{1,0:T(8,128)(2,1)S(1)}, bf16[256,1024]{1,0:T(8,128)(2,1)S(1)}) custom-call(s32[2]{0:T(128)S(1)} %pad_add_fusion.4.place, s32[2,256]{1,0:T(2,128)S(1)} %copy-done.1, f32[2,256]{1,0:T(2,128)S(1)} %copy-done.2, bf16[2,256,1024]{2,1,0:T(8,128)(2,1)S(1)} %copy-done, bf16[256,512]{1,0:T(8,128)(2,1)S(1)} %get-tuple-element.43.own, ...), custom_call_target="tpu_custom_call" | custom-call | tf_op jit(solution)/shard_map/first_batch/pallas_call | solution.py:421
  75.5 6.4 %second_batch.1 = f32[128,1024]{1,0:T(8,128)} custom-call(s32[2]{0:T(128)S(1)} %pad_add_fusion.4.place, s32[2,256]{1,0:T(2,128)S(1)} %copy-done.1, f32[2,256]{1,0:T(2,128)S(1)} %copy-done.2, bf16[2,256,1024]{2,1,0:T(8,128)(2,1)S(1)} %copy-done, s16[256,512]{1,0:T(8,128)(2,1)S(1)} %get-tuple-element.42.own, ...), custom_call_target="tpu_custom_call" | custom-call | tf_op jit(solution)/shard_map/second_batch/pallas_call | solution.py:421
  (27 shorter events, 0.2 us)
Async XLA Ops:
  2.1 1.4 %collective-permute-start.5 = (s16[56,512]{1,0:T(8,128)(2,1)S(1)}, s16[56,512]{1,0:T(8,128)(2,1)S(1)}, u32[]{:S(2)}, u32[]{:S(2)}) collective-permute-start(s16[56,512]{1,0:T(8,128)(2,1)S(1)} %get-tuple-element.39), channel_id=1, source_target_pairs={{0,1},{1,0},{2,3},{3,2},{4,5},{5,4},{6,7},{7,6},{8,9},{9,8},{10,11... | collective-permute-start | bytes 172040 | tf_op jit(solution)/shard_map/ppermute | solution.py:453
  3.6 5.6 %collective-permute-start.7 = (s16[1,56,512]{2,1,0:T(8,128)(2,1)S(1)}, s16[1,56,512]{2,1,0:T(8,128)(2,1)S(1)}, u32[]{:S(2)}, u32[]{:S(2)}) collective-permute-start(s16[1,56,512]{2,1,0:T(8,128)(2,1)S(1)} %add_bitcast_fusion.refs_0_), channel_id=1, source_target_pairs={{0,8},{1,9},{2,10},{3,11},{4,12},{5,13},{6,14},{7,15},{8,0},{9,1},... | collective-permute-start | bytes 172040 | tf_op jit(solution)/shard_map/ppermute | solution.py:453
  6.5 5.9 %collective-permute-start.6 = (s16[1,56,512]{2,1,0:T(8,128)(2,1)S(1)}, s16[1,56,512]{2,1,0:T(8,128)(2,1)S(1)}, u32[]{:S(2)}, u32[]{:S(2)}) collective-permute-start(s16[1,56,512]{2,1,0:T(8,128)(2,1)S(1)} %add_bitcast_fusion.refs_0_), channel_id=1, source_target_pairs={{0,16},{1,17},{2,18},{3,19},{4,20},{5,21},{6,22},{7,23},{8,24},{9,... | collective-permute-start | bytes 172040 | tf_op jit(solution)/shard_map/ppermute | solution.py:453
  9.2 9.0 %collective-permute-start.9 = (s16[2,56,512]{2,1,0:T(8,128)(2,1)S(1)}, s16[2,56,512]{2,1,0:T(8,128)(2,1)S(1)}, u32[]{:S(2)}, u32[]{:S(2)}) collective-permute-start(s16[2,56,512]{2,1,0:T(8,128)(2,1)S(1)} %pad_add_fusion.1), channel_id=1, source_target_pairs={{0,4},{1,5},{2,6},{3,7},{4,0},{5,1},{6,2},{7,3},{8,12},{9,13},{10,... | collective-permute-start | bytes 344072 | tf_op jit(solution)/shard_map/ppermute | solution.py:453
  12.4 4.2 %collective-permute-start.8 = (s16[1,56,512]{2,1,0:T(8,128)(2,1)S(1)}, s16[1,56,512]{2,1,0:T(8,128)(2,1)S(1)}, u32[]{:S(2)}, u32[]{:S(2)}) collective-permute-start(s16[1,56,512]{2,1,0:T(8,128)(2,1)S(1)} %collective-permute-done.6.refs_1_), channel_id=1, source_target_pairs={{0,8},{1,9},{2,10},{3,11},{4,12},{5,13},{6,14},{7,15},{8,0},{9,1},... | collective-permute-start | bytes 172040 | tf_op jit(solution)/shard_map/ppermute | solution.py:453
  12.8 6.0 %collective-permute-start.10 = (s16[1,56,512]{2,1,0:T(8,128)(2,1)S(1)}, s16[1,56,512]{2,1,0:T(8,128)(2,1)S(1)}, u32[]{:S(2)}, u32[]{:S(2)}) collective-permute-start(s16[1,56,512]{2,1,0:T(8,128)(2,1)S(1)} %collective-permute-done.6.refs_1_), channel_id=1, source_target_pairs={{0,2},{1,3},{2,0},{3,1},{4,6},{5,7},{6,4},{7,5},{8,10},{9,11},{10,... | collective-permute-start | bytes 172040 | tf_op jit(solution)/shard_map/ppermute | solution.py:453
  16.6 4.4 %collective-permute-start.11 = (s16[1,56,512]{2,1,0:T(8,128)(2,1)S(1)}, s16[1,56,512]{2,1,0:T(8,128)(2,1)S(1)}, u32[]{:S(2)}, u32[]{:S(2)}) collective-permute-start(s16[1,56,512]{2,1,0:T(8,128)(2,1)S(1)} %collective-permute-done.8.refs_3_), channel_id=1, source_target_pairs={{0,2},{1,3},{2,0},{3,1},{4,6},{5,7},{6,4},{7,5},{8,10},{9,11},{10,... | collective-permute-start | bytes 172040 | tf_op jit(solution)/shard_map/ppermute | solution.py:453
  18.2 6.7 %collective-permute-start.12 = (s16[4,56,512]{2,1,0:T(8,128)(2,1)S(1)}, s16[4,56,512]{2,1,0:T(8,128)(2,1)S(1)}, u32[]{:S(2)}, u32[]{:S(2)}) collective-permute-start(s16[4,56,512]{2,1,0:T(8,128)(2,1)S(1)} %pad_add_fusion), channel_id=1, source_target_pairs={{0,2},{1,3},{2,0},{3,1},{4,6},{5,7},{6,4},{7,5},{8,10},{9,11},{10,... | collective-permute-start | bytes 688136 | tf_op jit(solution)/shard_map/ppermute | solution.py:453
  18.8 6.1 %collective-permute-start.13 = (s16[2,56,512]{2,1,0:T(8,128)(2,1)S(1)}, s16[2,56,512]{2,1,0:T(8,128)(2,1)S(1)}, u32[]{:S(2)}, u32[]{:S(2)}) collective-permute-start(s16[2,56,512]{2,1,0:T(8,128)(2,1)S(1)} %pad_add_fusion.2), channel_id=1, source_target_pairs={{0,4},{1,5},{2,6},{3,7},{4,0},{5,1},{6,2},{7,3},{8,12},{9,13},{10,... | collective-permute-start | bytes 344072 | tf_op jit(solution)/shard_map/ppermute | solution.py:453
  21.0 4.9 %collective-permute-start.14 = (s16[2,56,512]{2,1,0:T(8,128)(2,1)S(1)}, s16[2,56,512]{2,1,0:T(8,128)(2,1)S(1)}, u32[]{:S(2)}, u32[]{:S(2)}) collective-permute-start(s16[2,56,512]{2,1,0:T(8,128)(2,1)S(1)} %pad_add_fusion.3), channel_id=1, source_target_pairs={{0,4},{1,5},{2,6},{3,7},{4,0},{5,1},{6,2},{7,3},{8,12},{9,13},{10,... | collective-permute-start | bytes 344072 | tf_op jit(solution)/shard_map/ppermute | solution.py:453
  24.9 1.5 %copy-start.3 = (f32[128,1024]{1,0:T(8,128)S(1)}, f32[128,1024]{1,0:T(8,128)}, u32[]{:S(2)}) copy-start(f32[128,1024]{1,0:T(8,128)} %state_ref.3) | copy-start | bytes 1572868
  24.9 1.4 %copy-start.4 = (f32[2,256,4]{1,2,0:T(4,128)S(1)}, f32[2,256,4]{1,2,0:T(4,128)}, u32[]{:S(2)}) copy-start(f32[2,256,4]{1,2,0:T(4,128)} %param.10) | copy-start | bytes 24580
  24.9 1.4 %copy-start.5 = (s32[2,256]{1,0:T(2,128)S(1)}, s32[2,256]{1,0:T(2,128)}, u32[]{:S(2)}) copy-start(s32[2,256]{1,0:T(2,128)} %blocks.3) | copy-start | bytes 6148
  26.4 1.7 %copy-start = (bf16[2,256,1024]{2,1,0:T(8,128)(2,1)S(1)}, bf16[2,256,1024]{2,1,0:T(8,128)(2,1)}, u32[]{:S(2)}) copy-start(bf16[2,256,1024]{2,1,0:T(8,128)(2,1)} %noise_ref.3) | copy-start | bytes 3145732
  26.4 1.7 %copy-start.1 = (s32[2,256]{1,0:T(2,128)S(1)}, s32[2,256]{1,0:T(2,128)}, u32[]{:S(2)}) copy-start(s32[2,256]{1,0:T(2,128)} %tags.3) | copy-start | bytes 6148
  26.4 1.7 %copy-start.2 = (f32[2,256]{1,0:T(2,128)S(1)}, f32[2,256]{1,0:T(2,128)}, u32[]{:S(2)}) copy-start(f32[2,256]{1,0:T(2,128)} %values.3) | copy-start | bytes 6148
  26.5 1.6 %collective-permute-start.16 = (bf16[256,512]{1,0:T(8,128)(2,1)S(1)}, bf16[256,512]{1,0:T(8,128)(2,1)S(1)}, u32[]{:S(2)}, u32[]{:S(2)}) collective-permute-start(bf16[256,512]{1,0:T(8,128)(2,1)S(1)} %get-tuple-element.43.own), channel_id=1, source_target_pairs={{0,1},{1,0},{2,3},{3,2},{4,5},{5,4},{6,7},{7,6},{8,9},{9,8},{10,11... | collective-permute-start | bytes 786440 | tf_op jit(solution)/shard_map/ppermute | solution.py:453
  26.5 48.9 %collective-permute-start.15 = (s16[256,512]{1,0:T(8,128)(2,1)S(1)}, s16[256,512]{1,0:T(8,128)(2,1)S(1)}, u32[]{:S(2)}, u32[]{:S(2)}) collective-permute-start(s16[256,512]{1,0:T(8,128)(2,1)S(1)} %get-tuple-element.42.own), channel_id=1, source_target_pairs={{0,1},{1,0},{2,3},{3,2},{4,5},{5,4},{6,7},{7,6},{8,9},{9,8},{10,11... | collective-permute-start | bytes 786440 | tf_op jit(solution)/shard_map/ppermute | solution.py:453

commit v13 on v12

--- a/solution.py
+++ b/solution.py
@@ -480,7 +480,7 @@
     early_places, late_places, fits = order(place, blocks, (len(EARLY), len(LATE)))
     pieces = [own, far, near, near_far, both_x, far_y, near_far_y, both_y, far_x]
     early = early_rows(early_places, pieces)
-    return late_rows(late_places, early, [near_far_x]), fits
+    return late_rows(late_places, early, [near_far_x]), after(fits, early)
 
 
 def add_by_swaps(value):

time: 82.3 us -> 82.3 us (level)
  no operation moved by 1% of the time
where the time goes in v13:
time: 82.3 us; the launch traced here: 82.1 us
  Pallas kernels  58.9 us (72%)
  starting transfers between devices  15.3 us (19%)
  waiting for transfers between devices  6.71 us (8%)
  between operations  0.97 us (1%)
    pallas_call x2, Pallas kernels, batch_call(): pl.pallas_call(kernel, out_shape=outs, in_specs=[SMEM, VMEM, VMEM, ANYWHE...  53.8 us
    ppermute x12, starting transfers between devices, swap(): return lax.ppermute(value, AXES, [(i, i ^ mask) for i in range(32)])  15.3 us
    ppermute x12, waiting for transfers between devices, swap(): return lax.ppermute(value, AXES, [(i, i ^ mask) for i in range(32)])  6.71 us
    pallas_call x1, Pallas kernels, pick(): pl.pallas_call(pick_kernel, out_shape=[jax.ShapeDtypeStruct((SLOTS, state...  2.05 us
  transfers between devices with their start and end apart: 12, of which 5 were waited for; matrix products, arithmetic and copies ran while one was open for 0% of the time, Pallas kernels for 61%

profile of v13, /device:TPU:0, one launch (start us, length us, event | category | flops | bytes accessed | tf_op | source)
XLA Modules:
  0.0 82.1 jit_solution(14725019913075867981)
XLA Ops:
  0.0 0.1 pad_add_fusion.4.place
  0.1 2.0 %pick.1 = (s16[56,512]{1,0:T(8,128)(2,1)S(1)}, s16[56,512]{1,0:T(8,128)(2,1)S(1)}) custom-call(s32[2]{0:T(128)S(1)} %pad_add_fusion.4.place, s32[2,256]{1,0:T(2,128)} %blocks.3, f32[2,4,256]{2,1,0:T(4,128)} %bitcast.5, f32[128,1024]{1,0:T(8,128)} %state_ref.3), custom_call_target="tpu_custom_call" | custom-call | tf_op jit(solution)/shard_map/pick/pallas_call | solution.py:116
  2.1 0.5 collective-permute-start.5
  2.7 0.9 %collective-permute-done.5 = s16[56,512]{1,0:T(8,128)(2,1)S(1)} collective-permute-done((s16[56,512]{1,0:T(8,128)(2,1)S(1)}, s16[56,512]{1,0:T(8,128)(2,1)S(1)}, u32[]{:S(2)}, u32[]{:S(2)}) %collective-permute-start.5) | collective-permute-done | bytes 57376 | tf_op jit(solution)/shard_map/ppermute | solution.py:453
  3.6 3.0 %collective-permute-start.7 = (s16[1,56,512]{2,1,0:T(8,128)(2,1)S(1)}, s16[1,56,512]{2,1,0:T(8,128)(2,1)S(1)}, u32[]{:S(2)}, u32[]{:S(2)}) collective-permute-start(s16[1,56,512]{2,1,0:T(8,128)(2,1)S(1)} %add_bitcast_fusion.refs_0_), channel_id=1, source_target_pairs={{0,8},{1,9},{2,10},{3,11},{4,12},{5,13},{6,14},{7,15},{8,0},{9,1},... | collective-permute-start | bytes 172040 | tf_op jit(solution)/shard_map/ppermute | solution.py:453
  6.5 2.6 %collective-permute-start.6 = (s16[1,56,512]{2,1,0:T(8,128)(2,1)S(1)}, s16[1,56,512]{2,1,0:T(8,128)(2,1)S(1)}, u32[]{:S(2)}, u32[]{:S(2)}) collective-permute-start(s16[1,56,512]{2,1,0:T(8,128)(2,1)S(1)} %add_bitcast_fusion.refs_0_), channel_id=1, source_target_pairs={{0,16},{1,17},{2,18},{3,19},{4,20},{5,21},{6,22},{7,23},{8,24},{9,... | collective-permute-start | bytes 172040 | tf_op jit(solution)/shard_map/ppermute | solution.py:453
  9.2 1.6 %collective-permute-start.9 = (s16[2,56,512]{2,1,0:T(8,128)(2,1)S(1)}, s16[2,56,512]{2,1,0:T(8,128)(2,1)S(1)}, u32[]{:S(2)}, u32[]{:S(2)}) collective-permute-start(s16[2,56,512]{2,1,0:T(8,128)(2,1)S(1)} %pad_add_fusion.1), channel_id=1, source_target_pairs={{0,4},{1,5},{2,6},{3,7},{4,0},{5,1},{6,2},{7,3},{8,12},{9,13},{10,... | collective-permute-start | bytes 344072 | tf_op jit(solution)/shard_map/ppermute | solution.py:453
  10.7 1.7 %collective-permute-done.6.refs_1_ = s16[1,56,512]{2,1,0:T(8,128)(2,1)S(1)} collective-permute-done((s16[1,56,512]{2,1,0:T(8,128)(2,1)S(1)}, s16[1,56,512]{2,1,0:T(8,128)(2,1)S(1)}, u32[]{:S(2)}, u32[]{:S(2)}) %collective-permute-start.6) | collective-permute-done | bytes 57376 | tf_op jit(solution)/shard_map/ppermute | solution.py:453
  12.4 0.3 collective-permute-start.8
  12.8 1.5 %collective-permute-start.10 = (s16[1,56,512]{2,1,0:T(8,128)(2,1)S(1)}, s16[1,56,512]{2,1,0:T(8,128)(2,1)S(1)}, u32[]{:S(2)}, u32[]{:S(2)}) collective-permute-start(s16[1,56,512]{2,1,0:T(8,128)(2,1)S(1)} %collective-permute-done.6.refs_1_), channel_id=1, source_target_pairs={{0,2},{1,3},{2,0},{3,1},{4,6},{5,7},{6,4},{7,5},{8,10},{9,11},{10,... | collective-permute-start | bytes 172040 | tf_op jit(solution)/shard_map/ppermute | solution.py:453
  14.3 2.3 %collective-permute-done.8.refs_3_ = s16[1,56,512]{2,1,0:T(8,128)(2,1)S(1)} collective-permute-done((s16[1,56,512]{2,1,0:T(8,128)(2,1)S(1)}, s16[1,56,512]{2,1,0:T(8,128)(2,1)S(1)}, u32[]{:S(2)}, u32[]{:S(2)}) %collective-permute-start.8) | collective-permute-done | bytes 57376 | tf_op jit(solution)/shard_map/ppermute | solution.py:453
  16.6 1.5 %collective-permute-start.11 = (s16[1,56,512]{2,1,0:T(8,128)(2,1)S(1)}, s16[1,56,512]{2,1,0:T(8,128)(2,1)S(1)}, u32[]{:S(2)}, u32[]{:S(2)}) collective-permute-start(s16[1,56,512]{2,1,0:T(8,128)(2,1)S(1)} %collective-permute-done.8.refs_3_), channel_id=1, source_target_pairs={{0,2},{1,3},{2,0},{3,1},{4,6},{5,7},{6,4},{7,5},{8,10},{9,11},{10,... | collective-permute-start | bytes 172040 | tf_op jit(solution)/shard_map/ppermute | solution.py:453
  18.2 0.6 collective-permute-start.12
  18.8 1.6 %collective-permute-start.13 = (s16[2,56,512]{2,1,0:T(8,128)(2,1)S(1)}, s16[2,56,512]{2,1,0:T(8,128)(2,1)S(1)}, u32[]{:S(2)}, u32[]{:S(2)}) collective-permute-start(s16[2,56,512]{2,1,0:T(8,128)(2,1)S(1)} %pad_add_fusion.2), channel_id=1, source_target_pairs={{0,4},{1,5},{2,6},{3,7},{4,0},{5,1},{6,2},{7,3},{8,12},{9,13},{10,... | collective-permute-start | bytes 344072 | tf_op jit(solution)/shard_map/ppermute | solution.py:453
  20.3 0.7 collective-permute-done.11.refs_6_
  21.0 1.6 %collective-permute-start.14 = (s16[2,56,512]{2,1,0:T(8,128)(2,1)S(1)}, s16[2,56,512]{2,1,0:T(8,128)(2,1)S(1)}, u32[]{:S(2)}, u32[]{:S(2)}) collective-permute-start(s16[2,56,512]{2,1,0:T(8,128)(2,1)S(1)} %pad_add_fusion.3), channel_id=1, source_target_pairs={{0,4},{1,5},{2,6},{3,7},{4,0},{5,1},{6,2},{7,3},{8,12},{9,13},{10,... | collective-permute-start | bytes 344072 | tf_op jit(solution)/shard_map/ppermute | solution.py:453
  22.6 1.6 %order.1 = (bf16[512,784]{1,0:T(8,128)(2,1)S(1)}, bf16[512,112]{1,0:T(8,128)(2,1)S(1)}, s32[1]{0:T(128)}) custom-call(s32[2]{0:T(128)S(1)} %pad_add_fusion.4.place, s32[2,256]{1,0:T(2,128)} %blocks.3), custom_call_target="tpu_custom_call" | custom-call | flops 1000000 | bytes 1000000 | tf_op jit(solution)/shard_map/order/pallas_call | solution.py:185
  24.3 1.0 %early_rows.1.early = f32[512,512]{1,0:T(8,128)S(1)} custom-call(bf16[512,784]{1,0:T(8,128)(2,1)S(1)} %get-tuple-element.37.chosen, s16[1,56,512]{2,1,0:T(8,128)(2,1)S(1)} %add_bitcast_fusion.refs_0_, s16[1,56,512]{2,1,0:T(8,128)(2,1)S(1)} %collective-permute-done.6.refs_1_, s16[1,56,512]{2,1,0:T(8,128)(2,1)S(1)} %collective-permute-done.7.refs_2_, ...), custom_call_target="tpu_custom_call" | custom-call | flops 1000000000 | bytes 4000000 | tf_op jit(solution)/shard_map/early_rows/pallas_call | solution.py:222
  25.9 0.4 late_rows.1
  26.5 0.1 collective-permute-start.16
  26.5 0.5 collective-permute-start.15
  27.0 1.0 %collective-permute-done.16.other = bf16[256,512]{1,0:T(8,128)(2,1)S(1)} collective-permute-done((bf16[256,512]{1,0:T(8,128)(2,1)S(1)}, bf16[256,512]{1,0:T(8,128)(2,1)S(1)}, u32[]{:S(2)}, u32[]{:S(2)}) %collective-permute-start.16) | collective-permute-done | bytes 262176 | tf_op jit(solution)/shard_map/ppermute | solution.py:453
  28.1 47.4 %first_batch.1 = (bf16[256,1024]{1,0:T(8,128)(2,1)S(1)}, bf16[256,1024]{1,0:T(8,128)(2,1)S(1)}) custom-call(s32[2]{0:T(128)S(1)} %pad_add_fusion.4.place, s32[2,256]{1,0:T(2,128)S(1)} %copy-done.1, f32[2,256]{1,0:T(2,128)S(1)} %copy-done.2, bf16[2,256,1024]{2,1,0:T(8,128)(2,1)S(1)} %copy-done, bf16[256,512]{1,0:T(8,128)(2,1)S(1)} %get-tuple-element.45.own, ...), custom_call_target="tpu_custom_call" | custom-call | tf_op jit(solution)/shard_map/first_batch/pallas_call | solution.py:421
  75.5 6.4 %second_batch.1 = f32[128,1024]{1,0:T(8,128)} custom-call(s32[2]{0:T(128)S(1)} %pad_add_fusion.4.place, s32[2,256]{1,0:T(2,128)S(1)} %copy-done.1, f32[2,256]{1,0:T(2,128)S(1)} %copy-done.2, bf16[2,256,1024]{2,1,0:T(8,128)(2,1)S(1)} %copy-done, s16[256,512]{1,0:T(8,128)(2,1)S(1)} %get-tuple-element.44.own, ...), custom_call_target="tpu_custom_call" | custom-call | tf_op jit(solution)/shard_map/second_batch/pallas_call | solution.py:421
  (27 shorter events, 0.2 us)
Async XLA Ops:
  2.1 1.4 %collective-permute-start.5 = (s16[56,512]{1,0:T(8,128)(2,1)S(1)}, s16[56,512]{1,0:T(8,128)(2,1)S(1)}, u32[]{:S(2)}, u32[]{:S(2)}) collective-permute-start(s16[56,512]{1,0:T(8,128)(2,1)S(1)} %get-tuple-element.39), channel_id=1, source_target_pairs={{0,1},{1,0},{2,3},{3,2},{4,5},{5,4},{6,7},{7,6},{8,9},{9,8},{10,11... | collective-permute-start | bytes 172040 | tf_op jit(solution)/shard_map/ppermute | solution.py:453
  3.6 5.6 %collective-permute-start.7 = (s16[1,56,512]{2,1,0:T(8,128)(2,1)S(1)}, s16[1,56,512]{2,1,0:T(8,128)(2,1)S(1)}, u32[]{:S(2)}, u32[]{:S(2)}) collective-permute-start(s16[1,56,512]{2,1,0:T(8,128)(2,1)S(1)} %add_bitcast_fusion.refs_0_), channel_id=1, source_target_pairs={{0,8},{1,9},{2,10},{3,11},{4,12},{5,13},{6,14},{7,15},{8,0},{9,1},... | collective-permute-start | bytes 172040 | tf_op jit(solution)/shard_map/ppermute | solution.py:453
  6.5 5.9 %collective-permute-start.6 = (s16[1,56,512]{2,1,0:T(8,128)(2,1)S(1)}, s16[1,56,512]{2,1,0:T(8,128)(2,1)S(1)}, u32[]{:S(2)}, u32[]{:S(2)}) collective-permute-start(s16[1,56,512]{2,1,0:T(8,128)(2,1)S(1)} %add_bitcast_fusion.refs_0_), channel_id=1, source_target_pairs={{0,16},{1,17},{2,18},{3,19},{4,20},{5,21},{6,22},{7,23},{8,24},{9,... | collective-permute-start | bytes 172040 | tf_op jit(solution)/shard_map/ppermute | solution.py:453
  9.2 9.0 %collective-permute-start.9 = (s16[2,56,512]{2,1,0:T(8,128)(2,1)S(1)}, s16[2,56,512]{2,1,0:T(8,128)(2,1)S(1)}, u32[]{:S(2)}, u32[]{:S(2)}) collective-permute-start(s16[2,56,512]{2,1,0:T(8,128)(2,1)S(1)} %pad_add_fusion.1), channel_id=1, source_target_pairs={{0,4},{1,5},{2,6},{3,7},{4,0},{5,1},{6,2},{7,3},{8,12},{9,13},{10,... | collective-permute-start | bytes 344072 | tf_op jit(solution)/shard_map/ppermute | solution.py:453
  12.4 4.2 %collective-permute-start.8 = (s16[1,56,512]{2,1,0:T(8,128)(2,1)S(1)}, s16[1,56,512]{2,1,0:T(8,128)(2,1)S(1)}, u32[]{:S(2)}, u32[]{:S(2)}) collective-permute-start(s16[1,56,512]{2,1,0:T(8,128)(2,1)S(1)} %collective-permute-done.6.refs_1_), channel_id=1, source_target_pairs={{0,8},{1,9},{2,10},{3,11},{4,12},{5,13},{6,14},{7,15},{8,0},{9,1},... | collective-permute-start | bytes 172040 | tf_op jit(solution)/shard_map/ppermute | solution.py:453
  12.8 6.0 %collective-permute-start.10 = (s16[1,56,512]{2,1,0:T(8,128)(2,1)S(1)}, s16[1,56,512]{2,1,0:T(8,128)(2,1)S(1)}, u32[]{:S(2)}, u32[]{:S(2)}) collective-permute-start(s16[1,56,512]{2,1,0:T(8,128)(2,1)S(1)} %collective-permute-done.6.refs_1_), channel_id=1, source_target_pairs={{0,2},{1,3},{2,0},{3,1},{4,6},{5,7},{6,4},{7,5},{8,10},{9,11},{10,... | collective-permute-start | bytes 172040 | tf_op jit(solution)/shard_map/ppermute | solution.py:453
  16.6 4.4 %collective-permute-start.11 = (s16[1,56,512]{2,1,0:T(8,128)(2,1)S(1)}, s16[1,56,512]{2,1,0:T(8,128)(2,1)S(1)}, u32[]{:S(2)}, u32[]{:S(2)}) collective-permute-start(s16[1,56,512]{2,1,0:T(8,128)(2,1)S(1)} %collective-permute-done.8.refs_3_), channel_id=1, source_target_pairs={{0,2},{1,3},{2,0},{3,1},{4,6},{5,7},{6,4},{7,5},{8,10},{9,11},{10,... | collective-permute-start | bytes 172040 | tf_op jit(solution)/shard_map/ppermute | solution.py:453
  18.2 6.1 %collective-permute-start.12 = (s16[4,56,512]{2,1,0:T(8,128)(2,1)S(1)}, s16[4,56,512]{2,1,0:T(8,128)(2,1)S(1)}, u32[]{:S(2)}, u32[]{:S(2)}) collective-permute-start(s16[4,56,512]{2,1,0:T(8,128)(2,1)S(1)} %pad_add_fusion), channel_id=1, source_target_pairs={{0,2},{1,3},{2,0},{3,1},{4,6},{5,7},{6,4},{7,5},{8,10},{9,11},{10,... | collective-permute-start | bytes 688136 | tf_op jit(solution)/shard_map/ppermute | solution.py:453
  18.8 5.5 %collective-permute-start.13 = (s16[2,56,512]{2,1,0:T(8,128)(2,1)S(1)}, s16[2,56,512]{2,1,0:T(8,128)(2,1)S(1)}, u32[]{:S(2)}, u32[]{:S(2)}) collective-permute-start(s16[2,56,512]{2,1,0:T(8,128)(2,1)S(1)} %pad_add_fusion.2), channel_id=1, source_target_pairs={{0,4},{1,5},{2,6},{3,7},{4,0},{5,1},{6,2},{7,3},{8,12},{9,13},{10,... | collective-permute-start | bytes 344072 | tf_op jit(solution)/shard_map/ppermute | solution.py:453
  21.0 4.9 %collective-permute-start.14 = (s16[2,56,512]{2,1,0:T(8,128)(2,1)S(1)}, s16[2,56,512]{2,1,0:T(8,128)(2,1)S(1)}, u32[]{:S(2)}, u32[]{:S(2)}) collective-permute-start(s16[2,56,512]{2,1,0:T(8,128)(2,1)S(1)} %pad_add_fusion.3), channel_id=1, source_target_pairs={{0,4},{1,5},{2,6},{3,7},{4,0},{5,1},{6,2},{7,3},{8,12},{9,13},{10,... | collective-permute-start | bytes 344072 | tf_op jit(solution)/shard_map/ppermute | solution.py:453
  24.3 2.1 %copy-start.3 = (f32[128,1024]{1,0:T(8,128)S(1)}, f32[128,1024]{1,0:T(8,128)}, u32[]{:S(2)}) copy-start(f32[128,1024]{1,0:T(8,128)} %state_ref.3) | copy-start | bytes 1572868
  24.3 2.1 %copy-start.4 = (f32[2,256,4]{1,2,0:T(4,128)S(1)}, f32[2,256,4]{1,2,0:T(4,128)}, u32[]{:S(2)}) copy-start(f32[2,256,4]{1,2,0:T(4,128)} %param.10) | copy-start | bytes 24580
  24.3 2.1 %copy-start.5 = (s32[2,256]{1,0:T(2,128)S(1)}, s32[2,256]{1,0:T(2,128)}, u32[]{:S(2)}) copy-start(s32[2,256]{1,0:T(2,128)} %blocks.3) | copy-start | bytes 6148
  26.4 1.7 %copy-start = (bf16[2,256,1024]{2,1,0:T(8,128)(2,1)S(1)}, bf16[2,256,1024]{2,1,0:T(8,128)(2,1)}, u32[]{:S(2)}) copy-start(bf16[2,256,1024]{2,1,0:T(8,128)(2,1)} %noise_ref.3) | copy-start | bytes 3145732
  26.4 1.7 %copy-start.1 = (s32[2,256]{1,0:T(2,128)S(1)}, s32[2,256]{1,0:T(2,128)}, u32[]{:S(2)}) copy-start(s32[2,256]{1,0:T(2,128)} %tags.3) | copy-start | bytes 6148
  26.4 1.7 %copy-start.2 = (f32[2,256]{1,0:T(2,128)S(1)}, f32[2,256]{1,0:T(2,128)}, u32[]{:S(2)}) copy-start(f32[2,256]{1,0:T(2,128)} %values.3) | copy-start | bytes 6148
  26.5 1.6 %collective-permute-start.16 = (bf16[256,512]{1,0:T(8,128)(2,1)S(1)}, bf16[256,512]{1,0:T(8,128)(2,1)S(1)}, u32[]{:S(2)}, u32[]{:S(2)}) collective-permute-start(bf16[256,512]{1,0:T(8,128)(2,1)S(1)} %get-tuple-element.45.own), channel_id=1, source_target_pairs={{0,1},{1,0},{2,3},{3,2},{4,5},{5,4},{6,7},{7,6},{8,9},{9,8},{10,11... | collective-permute-start | bytes 786440 | tf_op jit(solution)/shard_map/ppermute | solution.py:453
  26.5 48.9 %collective-permute-start.15 = (s16[256,512]{1,0:T(8,128)(2,1)S(1)}, s16[256,512]{1,0:T(8,128)(2,1)S(1)}, u32[]{:S(2)}, u32[]{:S(2)}) collective-permute-start(s16[256,512]{1,0:T(8,128)(2,1)S(1)} %get-tuple-element.44.own), channel_id=1, source_target_pairs={{0,1},{1,0},{2,3},{3,2},{4,5},{5,4},{6,7},{7,6},{8,9},{9,8},{10,11... | collective-permute-start | bytes 786440 | tf_op jit(solution)/shard_map/ppermute | solution.py:453
